TPU v7x, 32 devices: a whole 2x2x4 slice. The times are simulated.
32 devices in a mesh: dp: 4 (over y, x), fsdp: 8 (over z, core).
Axes of the slice: x: 2, y: 2, z: 4, core: 2. Of those that a mesh axis runs over, the one named last changes fastest.
Arguments:
- tokens: bfloat16 [32, 1024, 768], P(('dp', 'fsdp')), may hold values from -6 to 6
- ln1_gain: bfloat16 [768], P(('dp', 'fsdp')), may hold values from 0.5 to 1.5
- ln1_bias: bfloat16 [768], P(('dp', 'fsdp')), may hold values from -1.75 to 1.75
- qkv_weight: bfloat16 [768, 2304], P(('dp', 'fsdp')), may hold values from -0.21875 to 0.21875
- qv_bias: bfloat16 [1536], P(('dp', 'fsdp')), may hold values from -3 to 3
- out_weight: bfloat16 [768, 768], P(('dp', 'fsdp')), may hold values from -1.75 to 1.75
- out_bias: bfloat16 [768], P(('dp', 'fsdp')), may hold values from -1.75 to 1.75
- ln2_gain: bfloat16 [768], P(('dp', 'fsdp')), may hold values from 0.5 to 1.5
- ln2_bias: bfloat16 [768], P(('dp', 'fsdp')), may hold values from -1.75 to 1.75
- fc_weight: bfloat16 [768, 3072], P(('dp', 'fsdp')), may hold values from -0.21875 to 0.21875
- fc_bias: bfloat16 [3072], P(('dp', 'fsdp')), may hold values from -1.75 to 1.75
- proj_weight: bfloat16 [3072, 768], P(('dp', 'fsdp')), may hold values from -0.109375 to 0.109375
- proj_bias: bfloat16 [768], P(('dp', 'fsdp')), may hold values from -1.75 to 1.75
- cotangent: bfloat16 [32, 1024, 768], P(('dp', 'fsdp')), may hold values from -6 to 6
- thought_slots: int32 [32, 2], P(('dp', 'fsdp')), may hold values from 257 to 383, as said below
- thought_count: int32 [32], P(('dp', 'fsdp')), may hold values from 1 to 2
- answer_start: int32 [32], P(('dp', 'fsdp')), may hold values from 260 to 449, as said below
Outputs:
- output: bfloat16 [32, 1024, 768], P(('dp', 'fsdp'))
- input_grad: float32 [32, 1024, 768], P(('dp', 'fsdp'))
- ln1_gain_grad: float32 [768], P(('dp', 'fsdp'))
- ln1_bias_grad: float32 [768], P(('dp', 'fsdp'))
- qkv_weight_grad: float32 [768, 2304], P(('dp', 'fsdp'))
- qv_bias_grad: float32 [1536], P(('dp', 'fsdp'))
- out_weight_grad: float32 [768, 768], P(('dp', 'fsdp'))
- out_bias_grad: float32 [768], P(('dp', 'fsdp'))
- ln2_gain_grad: float32 [768], P(('dp', 'fsdp'))
- ln2_bias_grad: float32 [768], P(('dp', 'fsdp'))
- fc_weight_grad: float32 [768, 3072], P(('dp', 'fsdp'))
- fc_bias_grad: float32 [3072], P(('dp', 'fsdp'))
- proj_weight_grad: float32 [3072, 768], P(('dp', 'fsdp'))
- proj_bias_grad: float32 [768], P(('dp', 'fsdp'))
Inputs may be any that keep to these rules, and one draw needn't show every extreme that they name: `thought_slots`: the 2 slots of a sequence are consecutive positions after its question; the position before the first slot holds the start marker. `answer_start`: A sequence's answer starts after its last thought slot and one end marker.
All inputs are finite; a program needn't handle non-finite values.
Results may differ from a plain program's by a relative error of at most 0.019.
Values may be sent and summed in bfloat16 or wider, within the bound.
No kernel may reach another device: no remote copies, remote signals or barrier semaphores. Data moves between devices by JAX's collectives and lax.ppermute only.
A program may use at most 256 MiB of HBM per device.

v0:
```python
import jax
import jax.numpy as jnp
from jax import lax
from jax.sharding import PartitionSpec as P

HD = 64
THOUGHTS = 2
PREFIX = 384


SCALE = 0.125
EPSILON = 1e-05


def fetch_weights(shards):
    return (
        lax.all_gather(shards[0], ("dp", "fsdp"), axis=0, tiled=True),
        lax.all_gather(shards[1], ("dp", "fsdp"), axis=0, tiled=True),
        lax.all_gather(shards[2], ("dp", "fsdp"), axis=0, tiled=True),
        lax.all_gather(shards[3], ("dp", "fsdp"), axis=0, tiled=True),
        lax.all_gather(shards[4], ("dp", "fsdp"), axis=0, tiled=True),
        lax.all_gather(shards[5], ("dp", "fsdp"), axis=0, tiled=True),
        lax.all_gather(shards[6], ("dp", "fsdp"), axis=0, tiled=True),
        lax.all_gather(shards[7], ("dp", "fsdp"), axis=0, tiled=True),
        lax.all_gather(shards[8], ("dp", "fsdp"), axis=0, tiled=True),
        lax.all_gather(shards[9], ("dp", "fsdp"), axis=0, tiled=True),
        lax.all_gather(shards[10], ("dp", "fsdp"), axis=0, tiled=True),
        lax.all_gather(shards[11], ("dp", "fsdp"), axis=0, tiled=True),
    )


def norm_forward(hidden, gain, bias):
    row_mean = jnp.mean(hidden, axis=-1, keepdims=True)
    centred = hidden - row_mean
    inverse = lax.rsqrt(jnp.mean(centred * centred, axis=-1, keepdims=True) + EPSILON)
    normed = centred * inverse
    return (normed * gain + bias, normed, inverse)


def norm_backward(incoming, normed, inverse, gain):
    scaled = incoming * gain
    inner = (
        scaled
        - jnp.mean(scaled, axis=-1, keepdims=True)
        - normed * jnp.mean(scaled * normed, axis=-1, keepdims=True)
    )
    return (
        inner * inverse,
        jnp.sum(incoming * normed, axis=(0, 1)),
        jnp.sum(incoming, axis=(0, 1)),
    )


def gelu_curve(values):
    return jax.nn.gelu(values, approximate=True)


def split_heads(qkv_low):
    n_rows, seq_len, triple = qkv_low.shape
    model_width = triple // 3
    head_count = model_width // HD
    queries = qkv_low[..., :model_width].reshape(n_rows, seq_len, head_count, HD)
    key_rows = qkv_low[..., model_width : 2 * model_width].reshape(n_rows, seq_len, head_count, HD)
    value_rows = qkv_low[..., 2 * model_width :].reshape(n_rows, seq_len, head_count, HD)
    return (queries, key_rows, value_rows)


def block_scores(queries, key_rows, row_begin, row_end):
    scores = (
        jnp.einsum(
            "rqhd,rkhd->rhqk",
            queries[:, row_begin:row_end],
            key_rows[:, :row_end],
            preferred_element_type=jnp.float32,
        )
        * SCALE
    )
    causal = (row_begin + lax.iota(jnp.int32, row_end - row_begin))[:, None] >= lax.iota(
        jnp.int32, row_end
    )[None, :]
    return jnp.where(causal, scores, -1e30)


def attend_blocks(queries, key_rows, value_rows):
    seq_len = queries.shape[1]
    block_rows = min(512, seq_len)
    outputs = []
    log_sums = []
    for row_begin in range(0, seq_len, block_rows):
        row_end = row_begin + block_rows
        scores = block_scores(queries, key_rows, row_begin, row_end)
        peak_row = jnp.max(scores, axis=-1, keepdims=True)
        expo_rows = jnp.exp(scores - peak_row)
        row_total = jnp.sum(expo_rows, axis=-1, keepdims=True)
        soft_low = (expo_rows / row_total).astype(jnp.bfloat16)
        outputs.append(
            jnp.einsum(
                "rhqk,rkhd->rqhd",
                soft_low,
                value_rows[:, :row_end],
                preferred_element_type=jnp.float32,
            )
        )
        log_sums.append(peak_row[..., 0] + jnp.log(row_total[..., 0]))
    return (jnp.concatenate(outputs, axis=1), jnp.concatenate(log_sums, axis=2))


def attend_backward(queries, key_rows, value_rows, log_sums, mixed_grad):
    seq_len = queries.shape[1]
    block_rows = min(512, seq_len)
    query_grads = []
    key_grad = jnp.zeros(key_rows.shape, jnp.float32)
    value_grad = jnp.zeros(value_rows.shape, jnp.float32)
    for row_begin in range(0, seq_len, block_rows):
        row_end = row_begin + block_rows
        scores = block_scores(queries, key_rows, row_begin, row_end)
        soft_rows = jnp.exp(scores - log_sums[:, :, row_begin:row_end, None])
        grad_block = mixed_grad[:, row_begin:row_end]
        prob_grad = jnp.einsum(
            "rqhd,rkhd->rhqk",
            grad_block,
            value_rows[:, :row_end],
            preferred_element_type=jnp.float32,
        )
        row_delta = jnp.sum(prob_grad * soft_rows, axis=-1, keepdims=True)
        score_grad = (soft_rows * (prob_grad - row_delta)).astype(jnp.bfloat16)
        query_grads.append(
            jnp.einsum(
                "rhqk,rkhd->rqhd",
                score_grad,
                key_rows[:, :row_end],
                preferred_element_type=jnp.float32,
            )
            * SCALE
        )
        key_grad = key_grad.at[:, :row_end].add(
            jnp.einsum(
                "rhqk,rqhd->rkhd",
                score_grad,
                queries[:, row_begin:row_end],
                preferred_element_type=jnp.float32,
            )
            * SCALE
        )
        value_grad = value_grad.at[:, :row_end].add(
            jnp.einsum(
                "rhqk,rqhd->rkhd",
                soft_rows.astype(jnp.bfloat16),
                grad_block,
                preferred_element_type=jnp.float32,
            )
        )
    return (jnp.concatenate(query_grads, axis=1), key_grad, value_grad)


def layer_forward(hidden, weights):
    (
        ln1_gain,
        ln1_bias,
        qkv_weight,
        qv_bias,
        out_weight,
        out_bias,
        ln2_gain,
        ln2_bias,
        fc_weight,
        fc_bias,
        proj_weight,
        proj_bias,
    ) = weights
    n_rows, seq_len, model_width = hidden.shape
    first, normed_one, inverse_one = norm_forward(
        hidden, ln1_gain.astype(jnp.float32), ln1_bias.astype(jnp.float32)
    )
    first_low = first.astype(jnp.bfloat16)
    bias_full = jnp.concatenate(
        [
            qv_bias[:model_width].astype(jnp.float32),
            jnp.zeros((model_width,), jnp.float32),
            qv_bias[model_width:].astype(jnp.float32),
        ]
    )
    qkv_low = (
        jnp.einsum("rsd,de->rse", first_low, qkv_weight, preferred_element_type=jnp.float32)
        + bias_full
    ).astype(jnp.bfloat16)
    queries, key_rows, value_rows = split_heads(qkv_low)
    mixed_rows, log_sums = attend_blocks(queries, key_rows, value_rows)
    mixed_low = mixed_rows.reshape(n_rows, seq_len, model_width).astype(jnp.bfloat16)
    resid = (
        hidden
        + jnp.einsum("rsd,de->rse", mixed_low, out_weight, preferred_element_type=jnp.float32)
        + out_bias.astype(jnp.float32)
    )
    second, normed_two, inverse_two = norm_forward(
        resid, ln2_gain.astype(jnp.float32), ln2_bias.astype(jnp.float32)
    )
    second_low = second.astype(jnp.bfloat16)
    pre_act = jnp.einsum(
        "rsd,df->rsf", second_low, fc_weight, preferred_element_type=jnp.float32
    ) + fc_bias.astype(jnp.float32)
    act_low = gelu_curve(pre_act).astype(jnp.bfloat16)
    result = (
        resid
        + jnp.einsum("rsf,fd->rsd", act_low, proj_weight, preferred_element_type=jnp.float32)
        + proj_bias.astype(jnp.float32)
    )
    stored = (
        normed_one,
        inverse_one,
        first_low,
        qkv_low,
        log_sums,
        mixed_low,
        normed_two,
        inverse_two,
        second_low,
        pre_act,
        act_low,
    )
    return (result, stored)


def layer_backward(upstream, stored, weights):
    (
        ln1_gain,
        ln1_bias,
        qkv_weight,
        qv_bias,
        out_weight,
        out_bias,
        ln2_gain,
        ln2_bias,
        fc_weight,
        fc_bias,
        proj_weight,
        proj_bias,
    ) = weights
    (
        normed_one,
        inverse_one,
        first_low,
        qkv_low,
        log_sums,
        mixed_low,
        normed_two,
        inverse_two,
        second_low,
        pre_act,
        act_low,
    ) = stored
    n_rows, seq_len, model_width = upstream.shape
    upstream_low = upstream.astype(jnp.bfloat16)
    proj_weight_term = jnp.einsum(
        "rsf,rsd->fd", act_low, upstream_low, preferred_element_type=jnp.float32
    )
    proj_bias_term = jnp.sum(upstream_low.astype(jnp.float32), axis=(0, 1))
    act_grad = jnp.einsum(
        "rsd,fd->rsf", upstream_low, proj_weight, preferred_element_type=jnp.float32
    )
    gelu_value, gelu_pull = jax.vjp(gelu_curve, pre_act)
    pre_grad = gelu_pull(act_grad)[0].astype(jnp.bfloat16)
    fc_weight_term = jnp.einsum(
        "rsd,rsf->df", second_low, pre_grad, preferred_element_type=jnp.float32
    )
    fc_bias_term = jnp.sum(pre_grad.astype(jnp.float32), axis=(0, 1))
    second_grad = jnp.einsum("rsf,df->rsd", pre_grad, fc_weight, preferred_element_type=jnp.float32)
    resid_part, ln2_gain_term, ln2_bias_term = norm_backward(
        second_grad, normed_two, inverse_two, ln2_gain.astype(jnp.float32)
    )
    resid_grad = upstream + resid_part
    attn_grad = resid_grad.astype(jnp.bfloat16)
    out_weight_term = jnp.einsum(
        "rsd,rse->de", mixed_low, attn_grad, preferred_element_type=jnp.float32
    )
    out_bias_term = jnp.sum(attn_grad.astype(jnp.float32), axis=(0, 1))
    mixed_grad = jnp.einsum(
        "rse,de->rsd", attn_grad, out_weight, preferred_element_type=jnp.float32
    )
    queries, key_rows, value_rows = split_heads(qkv_low)
    mixed_grad = mixed_grad.astype(jnp.bfloat16).reshape(queries.shape)
    query_grad, key_grad, value_grad = attend_backward(
        queries, key_rows, value_rows, log_sums, mixed_grad
    )
    qkv_grad = jnp.concatenate(
        [
            query_grad.reshape(n_rows, seq_len, model_width),
            key_grad.reshape(n_rows, seq_len, model_width),
            value_grad.reshape(n_rows, seq_len, model_width),
        ],
        axis=-1,
    ).astype(jnp.bfloat16)
    qkv_weight_term = jnp.einsum(
        "rsd,rse->de", first_low, qkv_grad, preferred_element_type=jnp.float32
    )
    column_sums = jnp.sum(qkv_grad.astype(jnp.float32), axis=(0, 1))
    qv_bias_term = jnp.concatenate([column_sums[:model_width], column_sums[2 * model_width :]])
    first_grad = jnp.einsum("rse,de->rsd", qkv_grad, qkv_weight, preferred_element_type=jnp.float32)
    hidden_part, ln1_gain_term, ln1_bias_term = norm_backward(
        first_grad, normed_one, inverse_one, ln1_gain.astype(jnp.float32)
    )
    terms = (
        ln1_gain_term,
        ln1_bias_term,
        qkv_weight_term,
        qv_bias_term,
        out_weight_term,
        out_bias_term,
        ln2_gain_term,
        ln2_bias_term,
        fc_weight_term,
        fc_bias_term,
        proj_weight_term,
        proj_bias_term,
    )
    return (resid_grad + hidden_part, terms)


def on_device(
    tokens,
    ln1_gain,
    ln1_bias,
    qkv_weight,
    qv_bias,
    out_weight,
    out_bias,
    ln2_gain,
    ln2_bias,
    fc_weight,
    fc_bias,
    proj_weight,
    proj_bias,
    cotangent,
    thought_slots,
    thought_count,
    answer_start,
):
    shards = (
        ln1_gain,
        ln1_bias,
        qkv_weight,
        qv_bias,
        out_weight,
        out_bias,
        ln2_gain,
        ln2_bias,
        fc_weight,
        fc_bias,
        proj_weight,
        proj_bias,
    )
    seq_len = tokens.shape[1]
    positions = lax.iota(jnp.int32, seq_len)
    hidden = tokens.astype(jnp.float32)
    stores = []
    masks = []
    for slot_index in range(THOUGHTS):
        weights = fetch_weights(shards)
        early_out, stored = layer_forward(hidden[:, :PREFIX], weights)
        slot_rows = thought_slots[:, slot_index]
        fed_rows = jnp.take_along_axis(early_out, (slot_rows - 1)[:, None, None], axis=1)
        chosen = (positions[None, :] == slot_rows[:, None]) & (slot_index < thought_count)[:, None]
        hidden = jnp.where(chosen[:, :, None], fed_rows, hidden)
        stores.append(stored)
        masks.append(chosen)
    weights = fetch_weights(shards)
    final, stored_final = layer_forward(hidden, weights)
    output = final.astype(jnp.bfloat16)
    answer_mask = positions[None, :] >= answer_start[:, None]
    answer_cot = jnp.where(answer_mask[:, :, None], cotangent.astype(jnp.float32), 0.0)
    weights = (
        lax.all_gather(ln1_gain, ("dp", "fsdp"), axis=0, tiled=True),
        lax.all_gather(ln1_bias, ("dp", "fsdp"), axis=0, tiled=True),
        lax.all_gather(qkv_weight, ("dp", "fsdp"), axis=0, tiled=True),
        lax.all_gather(qv_bias, ("dp", "fsdp"), axis=0, tiled=True),
        lax.all_gather(out_weight, ("dp", "fsdp"), axis=0, tiled=True),
        lax.all_gather(out_bias, ("dp", "fsdp"), axis=0, tiled=True),
        lax.all_gather(ln2_gain, ("dp", "fsdp"), axis=0, tiled=True),
        lax.all_gather(ln2_bias, ("dp", "fsdp"), axis=0, tiled=True),
        lax.all_gather(fc_weight, ("dp", "fsdp"), axis=0, tiled=True),
        lax.all_gather(fc_bias, ("dp", "fsdp"), axis=0, tiled=True),
        lax.all_gather(proj_weight, ("dp", "fsdp"), axis=0, tiled=True),
        lax.all_gather(proj_bias, ("dp", "fsdp"), axis=0, tiled=True),
    )
    grad_hidden, totals = layer_backward(answer_cot, stored_final, weights)
    early_positions = positions[:PREFIX]
    for slot_index in reversed(range(THOUGHTS)):
        chosen = masks[slot_index]
        slot_rows = thought_slots[:, slot_index]
        carried = jnp.sum(jnp.where(chosen[:, :, None], grad_hidden, 0.0), axis=1)
        grad_hidden = jnp.where(chosen[:, :, None], 0.0, grad_hidden)
        source_mask = early_positions[None, :] == (slot_rows - 1)[:, None]
        early_grad = jnp.where(source_mask[:, :, None], carried[:, None, :], 0.0)
        hidden_part, terms = layer_backward(early_grad, stores[slot_index], weights)
        grad_hidden = grad_hidden.at[:, :PREFIX].add(hidden_part)
        totals = tuple((total_part + new_part for total_part, new_part in zip(totals, terms)))
    partial_sums = (
        lax.psum_scatter(
            totals[0].astype(jnp.bfloat16), "dp", scatter_dimension=0, tiled=True
        ).astype(jnp.float32),
        lax.psum_scatter(
            totals[1].astype(jnp.bfloat16), "dp", scatter_dimension=0, tiled=True
        ).astype(jnp.float32),
        lax.psum_scatter(
            totals[2].astype(jnp.bfloat16), "dp", scatter_dimension=0, tiled=True
        ).astype(jnp.float32),
        lax.psum_scatter(
            totals[3].astype(jnp.bfloat16), "dp", scatter_dimension=0, tiled=True
        ).astype(jnp.float32),
        lax.psum_scatter(
            totals[4].astype(jnp.bfloat16), "dp", scatter_dimension=0, tiled=True
        ).astype(jnp.float32),
        lax.psum_scatter(
            totals[5].astype(jnp.bfloat16), "dp", scatter_dimension=0, tiled=True
        ).astype(jnp.float32),
        lax.psum_scatter(
            totals[6].astype(jnp.bfloat16), "dp", scatter_dimension=0, tiled=True
        ).astype(jnp.float32),
        lax.psum_scatter(
            totals[7].astype(jnp.bfloat16), "dp", scatter_dimension=0, tiled=True
        ).astype(jnp.float32),
        lax.psum_scatter(
            totals[8].astype(jnp.bfloat16), "dp", scatter_dimension=0, tiled=True
        ).astype(jnp.float32),
        lax.psum_scatter(
            totals[9].astype(jnp.bfloat16), "dp", scatter_dimension=0, tiled=True
        ).astype(jnp.float32),
        lax.psum_scatter(
            totals[10].astype(jnp.bfloat16), "dp", scatter_dimension=0, tiled=True
        ).astype(jnp.float32),
        lax.psum_scatter(
            totals[11].astype(jnp.bfloat16), "dp", scatter_dimension=0, tiled=True
        ).astype(jnp.float32),
    )
    summed = (
        lax.psum_scatter(
            partial_sums[0].astype(jnp.bfloat16), "fsdp", scatter_dimension=0, tiled=True
        ).astype(jnp.float32),
        lax.psum_scatter(
            partial_sums[1].astype(jnp.bfloat16), "fsdp", scatter_dimension=0, tiled=True
        ).astype(jnp.float32),
        lax.psum_scatter(
            partial_sums[2].astype(jnp.bfloat16), "fsdp", scatter_dimension=0, tiled=True
        ).astype(jnp.float32),
        lax.psum_scatter(
            partial_sums[3].astype(jnp.bfloat16), "fsdp", scatter_dimension=0, tiled=True
        ).astype(jnp.float32),
        lax.psum_scatter(
            partial_sums[4].astype(jnp.bfloat16), "fsdp", scatter_dimension=0, tiled=True
        ).astype(jnp.float32),
        lax.psum_scatter(
            partial_sums[5].astype(jnp.bfloat16), "fsdp", scatter_dimension=0, tiled=True
        ).astype(jnp.float32),
        lax.psum_scatter(
            partial_sums[6].astype(jnp.bfloat16), "fsdp", scatter_dimension=0, tiled=True
        ).astype(jnp.float32),
        lax.psum_scatter(
            partial_sums[7].astype(jnp.bfloat16), "fsdp", scatter_dimension=0, tiled=True
        ).astype(jnp.float32),
        lax.psum_scatter(
            partial_sums[8].astype(jnp.bfloat16), "fsdp", scatter_dimension=0, tiled=True
        ).astype(jnp.float32),
        lax.psum_scatter(
            partial_sums[9].astype(jnp.bfloat16), "fsdp", scatter_dimension=0, tiled=True
        ).astype(jnp.float32),
        lax.psum_scatter(
            partial_sums[10].astype(jnp.bfloat16), "fsdp", scatter_dimension=0, tiled=True
        ).astype(jnp.float32),
        lax.psum_scatter(
            partial_sums[11].astype(jnp.bfloat16), "fsdp", scatter_dimension=0, tiled=True
        ).astype(jnp.float32),
    )
    return (
        output,
        grad_hidden,
        summed[0],
        summed[1],
        summed[2],
        summed[3],
        summed[4],
        summed[5],
        summed[6],
        summed[7],
        summed[8],
        summed[9],
        summed[10],
        summed[11],
    )


def solution(mesh):
    placed = (
        P(("dp", "fsdp"), None, None),
        P(("dp", "fsdp")),
        P(("dp", "fsdp")),
        P(("dp", "fsdp"), None),
        P(("dp", "fsdp")),
        P(("dp", "fsdp"), None),
        P(("dp", "fsdp")),
        P(("dp", "fsdp")),
        P(("dp", "fsdp")),
        P(("dp", "fsdp"), None),
        P(("dp", "fsdp")),
        P(("dp", "fsdp"), None),
        P(("dp", "fsdp")),
        P(("dp", "fsdp"), None, None),
        P(("dp", "fsdp"), None),
        P(("dp", "fsdp")),
        P(("dp", "fsdp")),
    )
    return jax.shard_map(
        on_device,
        mesh=mesh,
        in_specs=placed,
        out_specs=(
            P(("dp", "fsdp"), None, None),
            P(("dp", "fsdp"), None, None),
            P(("dp", "fsdp")),
            P(("dp", "fsdp")),
            P(("dp", "fsdp"), None),
            P(("dp", "fsdp")),
            P(("dp", "fsdp"), None),
            P(("dp", "fsdp")),
            P(("dp", "fsdp")),
            P(("dp", "fsdp")),
            P(("dp", "fsdp"), None),
            P(("dp", "fsdp")),
            P(("dp", "fsdp"), None),
            P(("dp", "fsdp")),
        ),
        check_vma=False,
    )
```

profile of v0, /device:TPU:0, one launch (start us, length us, event | category | flops | bytes accessed | tf_op | source)
XLA Modules:
  0.0 906.0 jit_solution(9352381010476070721)
XLA Ops:
  20.7 42.8 %all-reduce.26 = (bf16[1536]{0:T(1024)(128)(2,1)S(1)}, bf16[768]{0:T(1024)(128)(2,1)S(1)}, bf16[768]{0:T(1024)(128)(2,1)S(1)}, bf16[3072]{0:T(1024)(128)(2,1)S(1...) all-reduce(bf16[1536]{0:T(1024)(128)(2,1)S(1)} %dynamic-update-slic, ...), channel_id=1, replica_groups=mesh['dp'=4,'fsdp'=8] {'dp','fsdp'}, use_global_device_ids=true, to_apply=%add.4 | all-reduce | flops 9216 | bytes 36864
  94.9 35.7 %all-gather.7.cloned.1.call-done = bf16[768,768]{1,0:T(8,128)(2,1)} async-done(((bf16[24,768]{1,0:T(8,128)(2,1)}), bf16[768,768]{1,0:T(8,128)(2,1)}) %all-gather.7.cloned.1.call-update) | async-done | bytes 1179664 | tf_op jit(solution)/shard_map/all_gather | solution.py:21
  134.7 61.5 %all-gather.9.cloned.1.call-done = bf16[768,3072]{1,0:T(8,128)(2,1)} async-done(((bf16[24,3072]{1,0:T(8,128)(2,1)}), bf16[768,3072]{1,0:T(8,128)(2,1)}) %all-gather.9.cloned.1.call-update) | async-done | bytes 4718608 | tf_op jit(solution)/shard_map/all_gather | solution.py:25
  203.2 58.4 %all-gather.11.cloned.1.call-done = bf16[3072,768]{1,0:T(8,128)(2,1)} async-done(((bf16[96,768]{1,0:T(8,128)(2,1)}), bf16[3072,768]{1,0:T(8,128)(2,1)}) %all-gather.11.cloned.1.call-update) | async-done | bytes 4718608 | tf_op jit(solution)/shard_map/all_gather | solution.py:27
  322.5 10.8 %fusion.15 = (f32[12,512]{1,0:T(8,128)S(1)}, f32[12,512,1024]{2,1,0:T(8,128)}) fusion(pred[512,1024]{1,0:T(8,128)(4,1)S(1)} %copy-done.27, bf16[1024,12,64]{0,2,1:T(8,128)(2,1)S(1)} %bitcast.403, bf16[1,1024,12,64]{1,3,2,0:T(8,128)(2,1)S(1)} %bitcast.410), kind=kOutput, calls=%fused_computation.34 | convolution fusion | flops 824174592 | bytes 28073984 | tf_op jit(solution)/shard_map/rqhd,rkhd->rhqk/dot_general | solution.py:70
  333.4 12.3 %fusion = f32[12,512]{1,0:T(8,128)S(1)} fusion(f32[12,512]{1,0:T(8,128)S(1)} %get-tuple-element.284, f32[12,512,1024]{2,1,0:T(8,128)} %get-tuple-element.285, pred[512,1024]{1,0:T(8,128)(4,1)S(1)} %copy-done.28), kind=kLoop, calls=%fused_computation.6 | loop fusion | flops 25159680 | bytes 25739264 | tf_op jit(solution)/shard_map/reduce_sum | solution.py:94
  348.8 9.7 %fusion.85 = bf16[12,64,512]{2,1,0:T(8,128)(2,1)} fusion(bf16[1024,12,64]{0,2,1:T(8,128)(2,1)} %bitcast.413, f32[12,512]{1,0:T(8,128)S(1)} %fusion, f32[12,512]{1,0:T(8,128)S(1)} %get-tuple-element.284, f32[12,512,1024]{2,1,0:T(8,128)S(1)} %copy-done, pred[512,1024]{1,0:T(8,128)(4,1)S(1)} %copy-done.28), kind=kOutput, calls=%fused_computation.174 | convolution fusion | flops 837156864 | bytes 28098560 | tf_op jit(solution)/shard_map/rhqk,rkhd->rqhd/dot_general | solution.py:97
  362.5 8.2 fusion.197
  370.7 16.0 %convert_reduce_fusion = (f32[3072]{0:T(1024)}, bf16[1024,3072]{1,0:T(8,128)(2,1)S(1)}) fusion(f32[1024,3072]{1,0:T(8,128)} %fusion.197, f32[3072]{0:T(1024)S(1)} %copy-done.125, bf16[3072,768]{1,0:T(8,128)(2,1)} %all-gather.11.cloned.1.call-done, bf16[1,1024,768]{2,1,0:T(8,128)(2,1)S(1)} %copy-done.66, pred[1024]{0:T(1024)(128)(4,1)S(1)} %copy-done.136), kind=kOutput, calls=%fused_computation.18 | convolution fusion | flops 4906546176 | bytes 25191424 | tf_op jit(solution)/shard_map/rsd,fd->rsf/dot_general | solution.py:258
  386.7 10.7 %fusion.54 = (f32[768]{0:T(1024)}, f32[1024]{0:T(1024)S(1)}, f32[1024,768]{1,0:T(8,128)S(1)}) fusion(f32[1,1024,768]{2,1,0:T(8,128)S(1)} %get-tuple-element.289, f32[1024]{0:T(1024)S(1)} %add_rsqrt_fusion, f32[1024]{0:T(1024)S(1)} %broadcast_multiply_fusion.4, f32[768]{0:T(1024)S(1)} %copy-done.70, bf16[1024,3072]{1,0:T(8,128)(2,1)S(1)} %get-tuple-element.307, ...), kind=kOutput, calls=%fused_computation.102 | convolution fusion | flops 4837341184 | bytes 17319936 | tf_op jit(solution)/shard_map/rsf,df->rsd/dot_general | solution.py:267
  409.4 7.1 multiply_reduce_fusion.1
  416.4 7.0 multiply_convert_fusion.1
  428.7 17.7 %multiply_reduce_fusion = (f32[12,512]{1,0:T(8,128)S(1)}, f32[12,512,1024]{2,1,0:T(8,128)}) fusion(f32[12,512]{1,0:T(8,128)S(1)} %log_add_fusion, f32[12,512,1024]{2,1,0:T(8,128)} %get-tuple-element.285, pred[512,1024]{1,0:T(8,128)(4,1)S(1)} %copy-done.29, bf16[1024,12,64]{0,2,1:T(8,128)(2,1)S(1)} %bitcast.415, bf16[1,1024,12,64]{1,3,2,0:T(8,128)(2,1)} %bitcast.466), kind=kOutput, calls=%fused_computation.1 | convolution fusion | flops 836757504 | bytes 53264384 | tf_op jit(solution)/shard_map/rqhd,rkhd->rhqk/dot_general | solution.py:119
  446.4 13.5 %fusion.52 = bf16[1,1024,12,64]{1,3,2,0:T(8,128)(2,1)} fusion(f32[1,512,12,64]{1,3,2,0:T(8,128)} %fusion.81, f32[12,512]{1,0:T(8,128)S(1)} %log_add_fusion, f32[12,512,1024]{2,1,0:T(8,128)} %get-tuple-element.285, pred[512,1024]{1,0:T(8,128)(4,1)S(1)} %copy-done.29, bf16[1,1024,12,64]{1,3,2,0:T(8,128)(2,1)} %bitcast.467), kind=kOutput, calls=%fused_computation.98 | convolution fusion | flops 832045056 | bytes 29646848 | tf_op jit(solution)/shard_map/rhqk,rqhd->rkhd/dot_general | solution.py:146
  459.9 17.2 %multiply_convert_fusion = bf16[12,512,1024]{2,1,0:T(8,128)(2,1)S(1)} fusion(f32[12,512,1024]{2,1,0:T(8,128)} %get-tuple-element.294, f32[12,512]{1,0:T(8,128)S(1)} %get-tuple-element.293, f32[12,512]{1,0:T(8,128)S(1)} %log_add_fusion, f32[12,512,1024]{2,1,0:T(8,128)} %get-tuple-element.285, pred[512,1024]{1,0:T(8,128)(4,1)S(1)} %copy-done.30), kind=kLoop, calls=%fused_computation | loop fusion | flops 37748736 | bytes 63488000 | tf_op jit(solution)/shard_map/convert_element_type | solution.py:126
  490.5 7.7 fusion.55
  503.5 7.6 convert_reduce_fusion.3
  566.8 7.5 multiply_reduce_fusion.2
  591.3 7.6 add_convert_fusion.3
  604.6 13.0 %fusion.78 = f32[3072,768]{1,0:T(8,128)} fusion(bf16[1,1024,768]{2,1,0:T(8,128)(2,1)S(1)} %copy-done.67, pred[1024]{0:T(1024)(128)(4,1)S(1)} %copy-done.137, f32[1024,3072]{1,0:T(8,128)} %fusion.197, f32[3072]{0:T(1024)S(1)} %copy-done.126), kind=kOutput, calls=%fused_computation.155 | convolution fusion | flops 4865654784 | bytes 23606272 | tf_op jit(solution)/shard_map/rsf,rsd->fd/dot_general | solution.py:254
  617.6 7.4 add_convert_fusion
  631.0 11.4 %fusion.195 = f32[768,3072]{1,0:T(8,128)} fusion(bf16[1024,3072]{1,0:T(8,128)(2,1)} %copy-done.39, f32[1,1024,768]{2,1,0:T(8,128)S(1)} %copy-done.8, f32[768]{0:T(1024)S(1)} %copy-done.75, f32[768]{0:T(1024)S(1)} %copy-done.70, f32[1024]{0:T(1024)S(1)} %copy-done.81, f32[1024]{0:T(1024)S(1)} %copy-done.79), kind=kOutput, calls=%fused_computation.373 | convolution fusion | flops 4835770368 | bytes 18888704 | tf_op jit(solution)/shard_map/rsd,rsf->df/dot_general | solution.py:263
  642.4 7.5 add_convert_fusion.1
  668.6 36.6 %reduce-scatter.21.cloned.1.call-done = bf16[768,768]{1,0:T(8,128)(2,1)} async-done(((bf16[3072,768]{1,0:T(8,128)(2,1)}), bf16[768,768]{1,0:T(8,128)(2,1)}) %reduce-scatter.21.cloned.1.call-update) | async-done | bytes 1179664 | tf_op jit(solution)/shard_map/reduce_scatter | solution.py:428
  706.8 15.8 %all-reduce.28 = (bf16[768]{0:T(1024)(128)(2,1)S(1)}, bf16[768]{0:T(1024)(128)(2,1)S(1)}, bf16[1536]{0:T(1024)(128)(2,1)S(1)}, bf16[768]{0:T(1024)(128)(2,1)S(1)...) all-reduce(bf16[768]{0:T(1024)(128)(2,1)S(1)} %add_convert_fusion.1, ...), channel_id=2, replica_groups=mesh['dp'=4,'fsdp'=8] {'dp'}, use_global_device_ids=true, to_apply=%region_41.43.clone | all-reduce | flops 9216 | bytes 36864
  723.2 14.1 %all-reduce.27 = (bf16[192]{0:T(256)(128)(2,1)S(1)}, bf16[192]{0:T(256)(128)(2,1)S(1)}, bf16[384]{0:T(512)(128)(2,1)S(1)}, bf16[192]{0:T(256)(128)(2,1)S(1)}, bf...) all-reduce(bf16[192]{0:T(256)(128)(2,1)S(1)} %dynamic-slice.70, ...), channel_id=3, replica_groups=mesh['dp'=4,'fsdp'=8] {'fsdp'}, use_global_device_ids=true, to_apply=%region_42.44.clone | all-reduce | flops 2304 | bytes 9216
  742.0 23.6 %reduce-scatter.17.cloned.1.call-done = bf16[192,3072]{1,0:T(8,128)(2,1)} async-done(((bf16[768,3072]{1,0:T(8,128)(2,1)}), bf16[192,3072]{1,0:T(8,128)(2,1)}) %reduce-scatter.17.cloned.1.call-update) | async-done | bytes 1179664 | tf_op jit(solution)/shard_map/reduce_scatter | solution.py:422
  769.4 13.0 %fusion.63 = bf16[1,1024,768]{2,1,0:T(8,128)(2,1)} fusion(f32[1,1024,768]{2,1,0:T(8,128)S(1)} %copy-done.8, bf16[3072,768]{1,0:T(8,128)(2,1)} %all-gather.11.cloned.1.call-done, f32[768]{0:T(1024)S(1)} %copy-done.104, f32[1024,3072]{1,0:T(8,128)} %fusion.197, f32[3072]{0:T(1024)S(1)} %copy-done.126), kind=kOutput, calls=%fused_computation.117 | convolution fusion | flops 4865654784 | bytes 22035456 | tf_op jit(solution)/shard_map/rsf,fd->rsd/dot_general | solution.py:205
  782.3 16.0 %reduce-scatter.15.cloned.1.call-done = bf16[24,768]{1,0:T(8,128)(2,1)} async-done(((bf16[192,768]{1,0:T(8,128)(2,1)}), bf16[24,768]{1,0:T(8,128)(2,1)}) %reduce-scatter.15.cloned.1.call-update) | async-done | bytes 36880 | tf_op jit(solution)/shard_map/reduce_scatter | solution.py:448
  799.7 31.0 %reduce-scatter.11.cloned.1.call-done = bf16[24,2304]{1,0:T(8,128)(2,1)} async-done(((bf16[192,2304]{1,0:T(8,128)(2,1)}), bf16[24,2304]{1,0:T(8,128)(2,1)}) %reduce-scatter.11.cloned.1.call-update) | async-done | bytes 110608 | tf_op jit(solution)/shard_map/reduce_scatter | solution.py:442
  832.3 31.9 %reduce-scatter.23.cloned.1.call-done = bf16[96,768]{1,0:T(8,128)(2,1)} async-done(((bf16[768,768]{1,0:T(8,128)(2,1)}), bf16[96,768]{1,0:T(8,128)(2,1)}) %reduce-scatter.23.cloned.1.call-update) | async-done | bytes 147472 | tf_op jit(solution)/shard_map/reduce_scatter | solution.py:466
  865.8 31.5 %reduce-scatter.19.cloned.1.call-done = bf16[24,3072]{1,0:T(8,128)(2,1)} async-done(((bf16[192,3072]{1,0:T(8,128)(2,1)}), bf16[24,3072]{1,0:T(8,128)(2,1)}) %reduce-scatter.19.cloned.1.call-update) | async-done | bytes 147472 | tf_op jit(solution)/shard_map/reduce_scatter | solution.py:460
  (572 shorter events, 271.2 us)
Async XLA Ops:
  7.2 68.7 %all-gather.5.cloned.1.call-start = ((), (), s32[]{:S(2)}) async-start(), calls=%async_computation.8 | async-start | bytes 3649536 | tf_op jit(solution)/shard_map/all_gather | solution.py:19
  7.9 122.7 %all-gather.7.cloned.1.call-start = ((), (), s32[]{:S(2)}) async-start(), calls=%async_computation.9 | async-start | bytes 1216512 | tf_op jit(solution)/shard_map/all_gather | solution.py:21
  8.7 187.6 %all-gather.9.cloned.1.call-start = ((), (), s32[]{:S(2)}) async-start(), calls=%async_computation.10 | async-start | bytes 4866048 | tf_op jit(solution)/shard_map/all_gather | solution.py:25
  9.4 252.2 %all-gather.11.cloned.1.call-start = ((), (), s32[]{:S(2)}) async-start(), calls=%async_computation.11 | async-start | bytes 4866048 | tf_op jit(solution)/shard_map/all_gather | solution.py:27
  10.0 645.7 %reduce-scatter.13.cloned.1.call-start = ((), (), s32[]{:S(2)}) async-start(), calls=%async_computation.14 | async-start | bytes 1474560 | tf_op jit(solution)/shard_map/reduce_scatter | solution.py:410
  69.3 61.3 %copy-start.12 = (f32[1,1024,768]{2,1,0:T(8,128)}, f32[1,1024,768]{2,1,0:T(8,128)S(1)}, u32[]{:S(2)}) copy-start(f32[1,1024,768]{2,1,0:T(8,128)S(1)} %convert_element_type.493) | copy-start | bytes 9437188
  132.8 63.5 %copy-start.108 = (f32[384]{0:T(512)}, f32[384]{0:T(512)S(1)}, u32[]{:S(2)}) copy-start(f32[384]{0:T(512)S(1)} %broadcast_multiply_fusion.16) | copy-start | bytes 4612
  134.1 62.2 %copy-start.113 = (f32[384]{0:T(512)}, f32[384]{0:T(512)S(1)}, u32[]{:S(2)}) copy-start(f32[384]{0:T(512)S(1)} %add_rsqrt_fusion.4) | copy-start | bytes 4612
  203.2 65.0 %copy-start.103 = (f32[768]{0:T(1024)S(1)}, f32[768]{0:T(1024)}, u32[]{:S(2)}) copy-start(f32[768]{0:T(1024)} %convert_element_type.512) | copy-start | bytes 9220
  203.2 65.8 %copy-start.4 = (bf16[1,1024,768]{2,1,0:T(8,128)(2,1)S(1)}, bf16[1,1024,768]{2,1,0:T(8,128)(2,1)}, u32[]{:S(2)}) copy-start(bf16[1,1024,768]{2,1,0:T(8,128)(2,1)} %param.51) | copy-start | bytes 4718596
  203.2 65.8 %copy-start.98 = (pred[1024]{0:T(1024)(128)(4,1)S(1)}, pred[1024]{0:T(1024)(128)(4,1)}, u32[]{:S(2)}) copy-start(pred[1024]{0:T(1024)(128)(4,1)} %get-tuple-element.311) | copy-start | bytes 3076
  269.0 26.6 %copy-start.86 = (f32[768]{0:T(1024)}, f32[768]{0:T(1024)S(1)}, u32[]{:S(2)}) copy-start(f32[768]{0:T(1024)S(1)} %fusion.159) | copy-start | bytes 9220
  305.9 117.5 %copy-start.9 = (bf16[1,1024,768]{1,2,0:T(8,128)(2,1)}, bf16[1,1024,768]{1,2,0:T(8,128)(2,1)S(1)}, u32[]{:S(2)}) copy-start(bf16[1,1024,768]{1,2,0:T(8,128)(2,1)S(1)} %copy.102) | copy-start | bytes 4718596
  361.9 36.4 %copy-start.7 = (f32[1,1024,768]{2,1,0:T(8,128)}, f32[1,1024,768]{2,1,0:T(8,128)S(1)}, u32[]{:S(2)}) copy-start(f32[1,1024,768]{2,1,0:T(8,128)S(1)} %get-tuple-element.289) | copy-start | bytes 9437188
  361.9 36.4 %copy-start.78 = (f32[1024]{0:T(1024)}, f32[1024]{0:T(1024)S(1)}, u32[]{:S(2)}) copy-start(f32[1024]{0:T(1024)S(1)} %broadcast_multiply_fusion.4) | copy-start | bytes 12292
  362.4 35.9 %copy-start.80 = (f32[1024]{0:T(1024)}, f32[1024]{0:T(1024)S(1)}, u32[]{:S(2)}) copy-start(f32[1024]{0:T(1024)S(1)} %add_rsqrt_fusion) | copy-start | bytes 12292
  483.4 20.1 %slice-start.15 = ((s8[4718592]{0:T(1024)(128)(4,1)}), s8[4194304]{0:T(1024)(128)(4,1)S(1)}, s32[]{:S(2)}) async-start(s8[4718592]{0:T(1024)(128)(4,1)} %bitcast.478), calls=%async_computation.35 | async-start | bytes 8388608
  525.5 19.5 %copy-start.48 = (bf16[12,64,384]{2,1,0:T(8,128)(2,1)}, bf16[12,64,384]{2,1,0:T(8,128)(2,1)S(1)}, u32[]{:S(2)}) copy-start(bf16[12,64,384]{2,1,0:T(8,128)(2,1)S(1)} %fusion.96) | copy-start | bytes 1769476
  566.3 94.1 %reduce-scatter.9.cloned.1.call-start = ((), (), s32[]{:S(2)}) async-start(), calls=%async_computation.12 | async-start | bytes 4423680 | tf_op jit(solution)/shard_map/reduce_scatter | solution.py:404
  598.9 106.2 %reduce-scatter.21.cloned.1.call-start = ((), (), s32[]{:S(2)}) async-start(), calls=%async_computation.18 | async-start | bytes 5898240 | tf_op jit(solution)/shard_map/reduce_scatter | solution.py:428
  599.5 18.1 %slice-start.11 = ((s8[4718592]{0:T(1024)(128)(4,1)}), s8[4194304]{0:T(1024)(128)(4,1)S(1)}, s32[]{:S(2)}) async-start(s8[4718592]{0:T(1024)(128)(4,1)} %bitcast.454), calls=%async_computation.31 | async-start | bytes 8388608
  625.1 140.5 %reduce-scatter.17.cloned.1.call-start = ((), (), s32[]{:S(2)}) async-start(), calls=%async_computation.16 | async-start | bytes 5898240 | tf_op jit(solution)/shard_map/reduce_scatter | solution.py:422
  649.9 148.4 %reduce-scatter.15.cloned.1.call-start = ((), (), s32[]{:S(2)}) async-start(), calls=%async_computation.15 | async-start | bytes 331776 | tf_op jit(solution)/shard_map/reduce_scatter | solution.py:448
  655.7 175.0 %reduce-scatter.11.cloned.1.call-start = ((), (), s32[]{:S(2)}) async-start(), calls=%async_computation.13 | async-start | bytes 995328 | tf_op jit(solution)/shard_map/reduce_scatter | solution.py:442
  660.4 203.8 %reduce-scatter.23.cloned.1.call-start = ((), (), s32[]{:S(2)}) async-start(), calls=%async_computation.19 | async-start | bytes 1327104 | tf_op jit(solution)/shard_map/reduce_scatter | solution.py:466
  662.5 44.2 %copy-start.115 = (f32[768]{0:T(1024)S(1)}, f32[768]{0:T(1024)}, u32[]{:S(2)}) copy-start(f32[768]{0:T(1024)} %get-tuple-element.244) | copy-start | bytes 9220
  662.5 44.2 %copy-start.119 = (f32[768]{0:T(1024)S(1)}, f32[768]{0:T(1024)}, u32[]{:S(2)}) copy-start(f32[768]{0:T(1024)} %get-tuple-element.242) | copy-start | bytes 9220
  662.6 44.2 %copy-start.131 = (f32[768]{0:T(1024)S(1)}, f32[768]{0:T(1024)}, u32[]{:S(2)}) copy-start(f32[768]{0:T(1024)} %get-tuple-element.196) | copy-start | bytes 9220
  662.6 44.2 %copy-start.116 = (f32[768]{0:T(1024)S(1)}, f32[768]{0:T(1024)}, u32[]{:S(2)}) copy-start(f32[768]{0:T(1024)} %get-tuple-element.204) | copy-start | bytes 9220
  662.6 44.2 %copy-start.128 = (f32[3072]{0:T(1024)S(1)}, f32[3072]{0:T(1024)}, u32[]{:S(2)}) copy-start(f32[3072]{0:T(1024)} %get-tuple-element.306) | copy-start | bytes 36868
  662.6 44.2 %copy-start.129 = (f32[3072]{0:T(1024)S(1)}, f32[3072]{0:T(1024)}, u32[]{:S(2)}) copy-start(f32[3072]{0:T(1024)} %get-tuple-element.308) | copy-start | bytes 36868
  705.2 192.1 %reduce-scatter.19.cloned.1.call-start = ((), (), s32[]{:S(2)}) async-start(), calls=%async_computation.17 | async-start | bytes 1327104 | tf_op jit(solution)/shard_map/reduce_scatter | solution.py:460
  (151 other events, 691.7 us)
Sparse Core Ops, SparseCore 0:
  11.0 63.4 all-gather.4
  77.6 52.9 all-gather.6
  133.6 62.5 all-gather.8
  199.1 62.4 all-gather.10
  566.4 27.3 reduce-scatter.12
  599.0 46.0 reduce-scatter.8
  648.1 57.0 reduce-scatter.20
  708.2 57.3 reduce-scatter.16
  767.8 30.4 reduce-scatter.14
  800.6 30.0 reduce-scatter.10
  833.0 31.1 reduce-scatter.22
  866.3 30.9 reduce-scatter.18
where the time goes:
time: 911 us; the launch traced here: 906 us
  waiting for transfers between devices  329 us (36%)
  matrix products  316 us (35%)
  other arithmetic  106 us (12%)
  blocking collectives  72.6 us (8%)
  local copies, waits for them, and re-layouts  58.1 us (6%)
  between operations  23.3 us (3%)
    unnamed x3, blocking collectives  72.6 us
    all_gather x1, waiting for transfers between devices, fetch_weights(): lax.all_gather(shards[8], ('dp', 'fsdp'), axis=0, tiled=True)  61.5 us
    all_gather x1, waiting for transfers between devices, fetch_weights(): lax.all_gather(shards[10], ('dp', 'fsdp'), axis=0, tiled=True)  58.4 us
    reduce_scatter x1, waiting for transfers between devices, on_device(): lax.psum_scatter(totals[10].astype(jnp.bfloat16), 'dp', scatter_dimension...  36.6 us
    dot_general x4, matrix products, attend_backward(): jnp.einsum('rqhd,rkhd->rhqk', grad_block, value_rows[:, :row_end], prefer...  36.4 us
    all_gather x1, waiting for transfers between devices, fetch_weights(): lax.all_gather(shards[4], ('dp', 'fsdp'), axis=0, tiled=True)  35.7 us
    unnamed x368, local copies, waits for them, and re-layouts  33.7 us
    convert_element_type x4, other arithmetic, attend_backward(): score_grad = (soft_rows * (prob_grad - row_delta)).astype(jnp.bfloat16)  33.4 us
  transfers between devices with their start and end apart: 12, of which 9 were waited for; matrix products, arithmetic and copies ran while one was open for 19% of the time, Pallas kernels for 0%

commit v1 on v0

v1 whole, which is shorter than its diff:
```python
import math

import jax
import jax.numpy as jnp
from jax import lax
from jax.experimental import pallas as pl
from jax.experimental.pallas import tpu as pltpu
from jax.sharding import PartitionSpec as P

HD = 64
THOUGHTS = 2
PREFIX = 384
QUESTION = 256
SCALE = 0.125
EPSILON = 1e-05
BLOCK = 256
PAIR = 2 * HD
NEG = -1e30

F32 = jnp.float32
BF16 = jnp.bfloat16
VMEM_LIMIT = 56 * 1024 * 1024


def dot(a, b):
    return lax.dot_general(a, b, (((1,), (0,)), ((), ())), preferred_element_type=F32)


def dot_nt(a, b):
    return lax.dot_general(a, b, (((1,), (1,)), ((), ())), preferred_element_type=F32)


def dot_tn(a, b):
    return lax.dot_general(a, b, (((0,), (0,)), ((), ())), preferred_element_type=F32)


def bits_of(size):
    return [1 << i for i in reversed(range(int(math.log2(size))))]


class Links:
    def __init__(self, sizes):
        self.sizes = sizes
        self.canon = [("dp", b) for b in bits_of(sizes["dp"])] + [
            ("fsdp", b) for b in bits_of(sizes["fsdp"])
        ]
        dp_bits = [("dp", b) for b in bits_of(sizes["dp"])]
        f_bits = [("fsdp", b) for b in bits_of(sizes["fsdp"])]
        self.groups = {"x": dp_bits[-1:], "y": dp_bits[:-1], "z": f_bits[:-1], "c": f_bits[-1:]}

    def order(self, text):
        out = []
        for letter in text:
            out += self.groups[letter]
        return out

    def swap(self, value, stage):
        axis, bit = stage
        return lax.ppermute(value, axis, [(i, i ^ bit) for i in range(self.sizes[axis])])

    def mine(self, stage):
        axis, bit = stage
        return (lax.axis_index(axis) & bit) != 0

    def gather(self, shard, text):
        done = []
        buf = shard
        for stage in self.order(text):
            got = self.swap(buf, stage)
            place = sum(1 for d in done if self.canon.index(d) < self.canon.index(stage))
            high = self.mine(stage)
            buf = jnp.stack([jnp.where(high, got, buf), jnp.where(high, buf, got)], axis=place)
            done.append(stage)
        return buf.reshape((-1,) + shard.shape)

    def scatter(self, value, text):
        tail = value.shape[1:]
        left = list(self.canon)
        buf = value.reshape((2,) * len(left) + tail)
        for stage in self.order(text):
            place = left.index(stage)
            high = self.mine(stage).astype(jnp.int32)
            keep = lax.dynamic_index_in_dim(buf, high, place, keepdims=False)
            send = lax.dynamic_index_in_dim(buf, 1 - high, place, keepdims=False)
            got = self.swap(send, stage)
            buf = keep.astype(F32) + got.astype(F32)
            left.remove(stage)
            if left:
                buf = buf.astype(BF16)
        return buf


def attend_kernel(q_ref, k_ref, v_ref, o_ref, lse_ref):
    seq_len = q_ref.shape[0]
    keys = k_ref[...]
    values_t = v_ref[...].T
    lane = lax.broadcasted_iota(jnp.int32, (BLOCK, PAIR), 1)
    sub = lax.broadcasted_iota(jnp.int32, (PAIR, BLOCK), 0)
    key_pos = lax.broadcasted_iota(jnp.int32, (BLOCK, BLOCK), 0)
    row_pos = lax.broadcasted_iota(jnp.int32, (BLOCK, BLOCK), 1)
    causal = key_pos <= row_pos
    for begin in range(0, seq_len, BLOCK):
        end = begin + BLOCK
        queries = q_ref[begin:end, :] * jnp.asarray(SCALE, BF16)
        parts = []
        for head in range(2):
            own = jnp.where((lane >= HD) == bool(head), queries, jnp.zeros_like(queries))
            last = jnp.where(causal, dot_nt(keys[begin:end], own), NEG)
            peak = jnp.max(last, axis=0, keepdims=True)
            if begin:
                before = dot_nt(keys[:begin], own)
                peak = jnp.maximum(peak, jnp.max(before, axis=0, keepdims=True))
            expo = jnp.exp(last - peak)
            total = jnp.sum(expo, axis=0, keepdims=True)
            mixed = dot(values_t[:, begin:end], expo.astype(BF16))
            if begin:
                expo = jnp.exp(before - peak)
                total = total + jnp.sum(expo, axis=0, keepdims=True)
                mixed = mixed + dot(values_t[:, :begin], expo.astype(BF16))
            parts.append(mixed / total)
            lse_ref[0, head : head + 1, begin:end] = peak + jnp.log(total)
        o_ref[begin:end, :] = jnp.where(sub < HD, parts[0], parts[1]).T.astype(BF16)


def attend(qkv):
    seq_len, triple = qkv.shape
    width = triple // 3
    pairs = width // PAIR
    return pl.pallas_call(
        attend_kernel,
        grid=(pairs,),
        in_specs=[
            pl.BlockSpec((seq_len, PAIR), lambda g: (0, g)),
            pl.BlockSpec((seq_len, PAIR), lambda g: (0, g + pairs)),
            pl.BlockSpec((seq_len, PAIR), lambda g: (0, g + 2 * pairs)),
        ],
        out_specs=[
            pl.BlockSpec((seq_len, PAIR), lambda g: (0, g)),
            pl.BlockSpec((1, 2, seq_len), lambda g: (g, 0, 0)),
        ],
        out_shape=[
            jax.ShapeDtypeStruct((seq_len, width), BF16),
            jax.ShapeDtypeStruct((pairs, 2, seq_len), F32),
        ],
        compiler_params=pltpu.CompilerParams(vmem_limit_bytes=VMEM_LIMIT),
        name="attention_forward",
    )(qkv, qkv, qkv)


def attend_back_kernel(q_ref, k_ref, v_ref, o_ref, lse_ref, g_ref, dq_ref, dk_ref, dv_ref):
    seq_len = q_ref.shape[0]
    first_row = seq_len - g_ref.shape[0]
    keys = k_ref[...]
    values = v_ref[...]
    keys_t = keys.T
    lane = lax.broadcasted_iota(jnp.int32, (BLOCK, PAIR), 1)
    sub = lax.broadcasted_iota(jnp.int32, (PAIR, BLOCK), 0)
    key_pos = lax.broadcasted_iota(jnp.int32, (BLOCK, BLOCK), 0)
    row_pos = lax.broadcasted_iota(jnp.int32, (BLOCK, BLOCK), 1)
    causal = key_pos <= row_pos
    dk_ref[...] = jnp.zeros_like(dk_ref)
    dv_ref[...] = jnp.zeros_like(dv_ref)
    for begin in range(first_row, seq_len, BLOCK):
        end = begin + BLOCK
        local = begin - first_row
        queries = q_ref[begin:end, :] * jnp.asarray(SCALE, BF16)
        grads = g_ref[local : local + BLOCK, :]
        product_t = (grads.astype(F32) * o_ref[begin:end, :].astype(F32)).T
        parts = []
        for head in range(2):
            chosen = (lane >= HD) == bool(head)
            own = jnp.where(chosen, queries, jnp.zeros_like(queries))
            own_grad = jnp.where(chosen, grads, jnp.zeros_like(grads))
            delta = jnp.sum(product_t[head * HD : (head + 1) * HD], axis=0, keepdims=True)
            lse = lse_ref[0, head : head + 1, begin:end]
            total = None
            for low, high in ((0, begin), (begin, end)):
                scores = dot_nt(keys[low:high], own)
                if high == end:
                    scores = jnp.where(causal, scores, NEG)
                probs = jnp.exp(scores - lse)
                prob_grad = dot_nt(values[low:high], own_grad)
                score_grad = (probs * (prob_grad - delta)).astype(BF16)
                dv_ref[low:high, :] += dot(probs.astype(BF16), own_grad)
                dk_ref[low:high, :] += dot(score_grad, own)
                part = dot(keys_t[:, low:high], score_grad)
                total = part if total is None else total + part
            parts.append(total)
        dq_ref[local : local + BLOCK, :] = jnp.where(sub < HD, parts[0], parts[1]).T * SCALE


def attend_back(qkv, mixed_low, lse, mixed_grad):
    seq_len, triple = qkv.shape
    width = triple // 3
    pairs = width // PAIR
    rows = mixed_grad.shape[0]
    return pl.pallas_call(
        attend_back_kernel,
        grid=(pairs,),
        in_specs=[
            pl.BlockSpec((seq_len, PAIR), lambda g: (0, g)),
            pl.BlockSpec((seq_len, PAIR), lambda g: (0, g + pairs)),
            pl.BlockSpec((seq_len, PAIR), lambda g: (0, g + 2 * pairs)),
            pl.BlockSpec((seq_len, PAIR), lambda g: (0, g)),
            pl.BlockSpec((1, 2, seq_len), lambda g: (g, 0, 0)),
            pl.BlockSpec((rows, PAIR), lambda g: (0, g)),
        ],
        out_specs=[
            pl.BlockSpec((rows, PAIR), lambda g: (0, g)),
            pl.BlockSpec((seq_len, PAIR), lambda g: (0, g)),
            pl.BlockSpec((seq_len, PAIR), lambda g: (0, g)),
        ],
        out_shape=[
            jax.ShapeDtypeStruct((rows, width), F32),
            jax.ShapeDtypeStruct((seq_len, width), F32),
            jax.ShapeDtypeStruct((seq_len, width), F32),
        ],
        compiler_params=pltpu.CompilerParams(vmem_limit_bytes=VMEM_LIMIT),
        name="attention_backward",
    )(qkv, qkv, qkv, mixed_low, lse, mixed_grad)


def row_norm(row, gain, bias):
    mean = jnp.mean(row, axis=-1, keepdims=True)
    centred = row - mean
    inverse = lax.rsqrt(jnp.mean(centred * centred, axis=-1, keepdims=True) + EPSILON)
    normed = centred * inverse
    return normed * gain + bias, normed, inverse


def row_norm_back(incoming, normed, inverse, gain):
    scaled = incoming * gain
    inner = (
        scaled
        - jnp.mean(scaled, axis=-1, keepdims=True)
        - normed * jnp.mean(scaled * normed, axis=-1, keepdims=True)
    )
    return inner * inverse


GELU_A = 0.7978845608028654
GELU_B = 0.044715


def gelu(pre):
    return 0.5 * pre * (1.0 + jnp.tanh(GELU_A * (pre + GELU_B * pre * pre * pre)))


def gelu_slope(pre):
    square = pre * pre
    curve = jnp.tanh(GELU_A * pre * (1.0 + GELU_B * square))
    return 0.5 * (1.0 + curve) + 0.5 * pre * (1.0 - curve * curve) * GELU_A * (
        1.0 + 3.0 * GELU_B * square
    )


def widen(row):
    return jnp.broadcast_to(row, (8, row.shape[1])).astype(BF16)


def pick(block, index):
    rows = lax.broadcasted_iota(jnp.int32, block.shape, 0)
    return jnp.sum(jnp.where(rows == index, block.astype(F32), 0.0), axis=0, keepdims=True)


def put(block, index, row):
    rows = lax.broadcasted_iota(jnp.int32, block.shape, 0)
    return jnp.where(rows == index, row.astype(block.dtype), block)


def by_head(row, heads):
    shape = (heads, row.shape[1])
    lane_head = lax.broadcasted_iota(jnp.int32, shape, 1) // HD
    return jnp.where(lane_head == lax.broadcasted_iota(jnp.int32, shape, 0), row, 0.0)


def heads_only(block):
    lane_head = lax.broadcasted_iota(jnp.int32, block.shape, 1) // HD
    own = lane_head == lax.broadcasted_iota(jnp.int32, block.shape, 0)
    return jnp.sum(jnp.where(own, block, 0.0), axis=0, keepdims=True)


HEAD_ROWS = 16


def thoughts_kernel(
    info_ref,
    tok_ref,
    qkv_ref,
    wqkv_ref,
    wout_ref,
    wfc_ref,
    wproj_ref,
    vec_ref,
    fcb_ref,
    qkvb_ref,
    hid_ref,
    qkvm_ref,
    pre_ref,
    prob_ref,
    res_ref,
):
    width = tok_ref.shape[1]
    ln1_gain, ln1_bias, out_bias, ln2_gain, ln2_bias, proj_bias = (
        vec_ref[i : i + 1, :] for i in range(6)
    )
    slot = info_ref[0]
    count = info_ref[1]
    hid_ref[...] = tok_ref[...].astype(F32)
    qkvm_ref[...] = qkv_ref[QUESTION:PREFIX, :]
    hidden_row = pick(hid_ref[...], slot - 1 - QUESTION)
    qkv_row = pick(qkvm_ref[...], slot - 1 - QUESTION)
    for step in range(THOUGHTS):
        at = slot - 1 + step
        query = by_head(qkv_row[:, :width] * SCALE, HEAD_ROWS).astype(BF16)
        scores = jnp.concatenate(
            [
                dot_nt(query, qkv_ref[:QUESTION, width : 2 * width]),
                dot_nt(query, qkvm_ref[:, width : 2 * width]),
            ],
            axis=1,
        )
        key_pos = lax.broadcasted_iota(jnp.int32, scores.shape, 1)
        scores = jnp.where(key_pos <= at, scores, NEG)
        expo = jnp.exp(scores - jnp.max(scores, axis=1, keepdims=True))
        probs = expo / jnp.sum(expo, axis=1, keepdims=True)
        prob_ref[step * HEAD_ROWS : (step + 1) * HEAD_ROWS, :] = probs
        low = probs.astype(BF16)
        mixed = heads_only(
            dot(low[:, :QUESTION], qkv_ref[:QUESTION, 2 * width :])
            + dot(low[:, QUESTION:], qkvm_ref[:, 2 * width :])
        )
        resid = hidden_row + dot(widen(mixed), wout_ref[...])[0:1] + out_bias
        res_ref[step : step + 1, :] = resid
        second, _, _ = row_norm(resid, ln2_gain, ln2_bias)
        pre = dot(widen(second), wfc_ref[...])[0:1] + fcb_ref[0:1, :]
        pre_ref[step : step + 1, :] = pre
        fed = resid + dot(widen(gelu(pre)), wproj_ref[...])[0:1] + proj_bias
        first, _, _ = row_norm(fed, ln1_gain, ln1_bias)
        qkv_row = dot(widen(first), wqkv_ref[...])[0:1] + qkvb_ref[0:1, :]
        qkv_row = qkv_row.astype(BF16).astype(F32)
        hidden_row = fed
        spot = jnp.where(step < count, slot + step - QUESTION, -1)
        hid_ref[...] = put(hid_ref[...], spot, fed)
        qkvm_ref[...] = put(qkvm_ref[...], spot, qkv_row)


def whole(array):
    zeros = (0,) * array.ndim
    return pl.BlockSpec(array.shape, lambda i, zeros=zeros: zeros)


def thoughts_forward(info, tokens, qkv, weights, vec, fc_bias, qkv_bias):
    width = tokens.shape[1]
    wqkv, wout, wfc, wproj = weights
    middle = PREFIX - QUESTION
    out_shape = [
        jax.ShapeDtypeStruct((middle, width), F32),
        jax.ShapeDtypeStruct((middle, 3 * width), BF16),
        jax.ShapeDtypeStruct((8, wfc.shape[1]), F32),
        jax.ShapeDtypeStruct((THOUGHTS * HEAD_ROWS, PREFIX), F32),
        jax.ShapeDtypeStruct((8, width), F32),
    ]
    return pl.pallas_call(
        thoughts_kernel,
        grid=(1,),
        in_specs=[
            pl.BlockSpec(memory_space=pltpu.SMEM),
            pl.BlockSpec((middle, width), lambda i: (QUESTION // middle, 0)),
            pl.BlockSpec((PREFIX, 3 * width), lambda i: (0, 0)),
            whole(wqkv),
            whole(wout),
            whole(wfc),
            whole(wproj),
            whole(vec),
            whole(fc_bias),
            whole(qkv_bias),
        ],
        out_specs=[whole(s) for s in out_shape],
        out_shape=out_shape,
        compiler_params=pltpu.CompilerParams(vmem_limit_bytes=VMEM_LIMIT),
        name="thought_rows_forward",
    )(info, tokens, qkv, wqkv, wout, wfc, wproj, vec, fc_bias, qkv_bias)


def thoughts_back_kernel(
    info_ref,
    hid_ref,
    qkv_ref,
    dk_in_ref,
    dv_in_ref,
    pre_ref,
    prob_ref,
    res_ref,
    wqkv_ref,
    wout_ref,
    wfc_ref,
    wproj_ref,
    vec_ref,
    dk_ref,
    dv_ref,
    dq_ref,
    up_ref,
    pg_ref,
    sg_ref,
    rg_ref,
):
    width = hid_ref.shape[1]
    ln1_gain, ln1_bias, _, ln2_gain, ln2_bias, _ = (vec_ref[i : i + 1, :] for i in range(6))
    slot = info_ref[0]
    count = info_ref[1]
    dk_ref[...] = dk_in_ref[...]
    dv_ref[...] = dv_in_ref[...]

    def through_first(at, query_grad):
        grad_row = jnp.concatenate(
            [query_grad, dk_ref[pl.ds(at, 1), :], dv_ref[pl.ds(at, 1), :]], axis=1
        )
        first_grad = dot_nt(widen(grad_row), wqkv_ref[...])[0:1]
        _, normed, inverse = row_norm(hid_ref[pl.ds(at - QUESTION, 1), :], ln1_gain, ln1_bias)
        return row_norm_back(first_grad, normed, inverse, ln1_gain)

    carried = through_first(slot + 1, jnp.zeros((1, width), F32))
    for step in reversed(range(THOUGHTS)):
        at = slot - 1 + step
        upstream = jnp.where(step < count, carried, 0.0)
        up_ref[step : step + 1, :] = upstream
        act_grad = dot_nt(widen(upstream), wproj_ref[...])[0:1]
        pre_grad = act_grad * gelu_slope(pre_ref[step : step + 1, :])
        pg_ref[step : step + 1, :] = pre_grad
        second_grad = dot_nt(widen(pre_grad), wfc_ref[...])[0:1]
        sg_ref[step : step + 1, :] = second_grad
        _, normed, inverse = row_norm(res_ref[step : step + 1, :], ln2_gain, ln2_bias)
        resid_grad = upstream + row_norm_back(second_grad, normed, inverse, ln2_gain)
        rg_ref[step : step + 1, :] = resid_grad
        mixed_grad = dot_nt(widen(resid_grad), wout_ref[...])[0:1]
        own_grad = by_head(mixed_grad, HEAD_ROWS).astype(BF16)
        query = by_head(pick(qkv_ref[QUESTION:PREFIX, :width], at - QUESTION) * SCALE, HEAD_ROWS)
        query = query.astype(BF16)
        probs = prob_ref[step * HEAD_ROWS : (step + 1) * HEAD_ROWS, :]
        prob_grad = dot_nt(own_grad, qkv_ref[:, 2 * width :])
        delta = jnp.sum(prob_grad * probs, axis=1, keepdims=True)
        score_grad = (probs * (prob_grad - delta)).astype(BF16)
        query_grad = heads_only(dot(score_grad, qkv_ref[:, width : 2 * width])) * SCALE
        dq_ref[step : step + 1, :] = query_grad
        dk_ref[...] += dot_tn(score_grad, query)
        dv_ref[...] += dot_tn(probs.astype(BF16), own_grad)
        if step:
            carried = resid_grad + through_first(at, query_grad)


def thoughts_back(info, hidden_mid, qkv, dk, dv, pre, probs, resid, weights, vec):
    width = hidden_mid.shape[1]
    wqkv, wout, wfc, wproj = weights
    out_shape = [
        jax.ShapeDtypeStruct((PREFIX, width), F32),
        jax.ShapeDtypeStruct((PREFIX, width), F32),
        jax.ShapeDtypeStruct((8, width), F32),
        jax.ShapeDtypeStruct((8, width), F32),
        jax.ShapeDtypeStruct((8, wfc.shape[1]), F32),
        jax.ShapeDtypeStruct((8, width), F32),
        jax.ShapeDtypeStruct((8, width), F32),
    ]
    return pl.pallas_call(
        thoughts_back_kernel,
        grid=(1,),
        in_specs=[
            pl.BlockSpec(memory_space=pltpu.SMEM),
            whole(hidden_mid),
            pl.BlockSpec((PREFIX, 3 * width), lambda i: (0, 0)),
            pl.BlockSpec((PREFIX, width), lambda i: (0, 0)),
            pl.BlockSpec((PREFIX, width), lambda i: (0, 0)),
            whole(pre),
            whole(probs),
            whole(resid),
            whole(wqkv),
            whole(wout),
            whole(wfc),
            whole(wproj),
            whole(vec),
        ],
        out_specs=[whole(s) for s in out_shape],
        out_shape=out_shape,
        compiler_params=pltpu.CompilerParams(vmem_limit_bytes=VMEM_LIMIT),
        name="thought_rows_backward",
    )(info, hidden_mid, qkv, dk, dv, pre, probs, resid, wqkv, wout, wfc, wproj, vec)


def norm_parts(hidden):
    mean = jnp.mean(hidden, axis=-1, keepdims=True)
    centred = hidden - mean
    inverse = lax.rsqrt(jnp.mean(centred * centred, axis=-1, keepdims=True) + EPSILON)
    return centred * inverse, inverse


def step_on_sequence(weights, small, tokens, cotangent, slots, count, answer_start):
    wqkv, wout, wfc, wproj = weights
    seq_len, width = tokens.shape
    vecs = {name: value.astype(F32) for name, value in small.items()}
    qkv_bias = jnp.concatenate(
        [vecs["qv_bias"][:width], jnp.zeros((width,), F32), vecs["qv_bias"][width:]]
    )
    names = ("ln1_gain", "ln1_bias", "out_bias", "ln2_gain", "ln2_bias", "proj_bias")
    vec = jnp.stack([vecs[n] for n in names] + [jnp.zeros((width,), F32)] * 2)
    info = jnp.stack([slots[0], count])

    tokens32 = tokens.astype(F32)
    normed, _ = norm_parts(tokens32)
    first_low = (normed * vecs["ln1_gain"] + vecs["ln1_bias"]).astype(BF16)
    qkv_first = (dot(first_low, wqkv) + qkv_bias).astype(BF16)
    hidden_mid, qkv_mid, pre_rows, prob_rows, res_rows = thoughts_forward(
        info, tokens, qkv_first, weights, vec, vecs["fc_bias"][None], qkv_bias[None]
    )
    qkv = lax.dynamic_update_slice(qkv_first, qkv_mid, (QUESTION, 0))
    hidden = lax.dynamic_update_slice(tokens32, hidden_mid, (QUESTION, 0))
    mixed_low, lse = attend(qkv)
    resid = hidden + dot(mixed_low, wout) + vecs["out_bias"]
    normed_two, inverse_two = norm_parts(resid)
    second_low = (normed_two * vecs["ln2_gain"] + vecs["ln2_bias"]).astype(BF16)
    pre = dot(second_low, wfc) + vecs["fc_bias"]
    act_low = gelu(pre).astype(BF16)
    final = resid + dot(act_low, wproj) + vecs["proj_bias"]
    output = final.astype(BF16)

    rows = seq_len - QUESTION
    late = QUESTION + lax.iota(jnp.int32, rows)
    upstream_low = jnp.where(
        (late >= answer_start)[:, None], cotangent[QUESTION:], jnp.zeros((), BF16)
    )
    act_grad = dot_nt(upstream_low, wproj)
    pre_grad = (act_grad * gelu_slope(pre[QUESTION:])).astype(BF16)
    second_grad = dot_nt(pre_grad, wfc)
    normed_late = normed_two[QUESTION:]
    resid_grad = upstream_low.astype(F32) + row_norm_back(
        second_grad, normed_late, inverse_two[QUESTION:], vecs["ln2_gain"]
    )
    mixed_grad = dot_nt(resid_grad.astype(BF16), wout).astype(BF16)
    query_grad, key_grad, value_grad = attend_back(qkv, mixed_low, lse, mixed_grad)
    key_early, value_early, dq_rows, up_rows, pg_rows, sg_rows, rg_rows = thoughts_back(
        info, hidden_mid, qkv, key_grad, value_grad, pre_rows, prob_rows, res_rows, weights, vec
    )
    spot = (slots[0] - 1 - QUESTION, 0)

    def insert(block, extra):
        return lax.dynamic_update_slice(block, extra[:THOUGHTS].astype(block.dtype), spot)

    upstream_low = insert(upstream_low, up_rows)
    pre_grad = insert(pre_grad, pg_rows)
    second_grad = insert(second_grad, sg_rows)
    resid_grad = insert(resid_grad, rg_rows)
    attn_grad = resid_grad.astype(BF16)
    query_grad = insert(query_grad, dq_rows)

    proj_grad = dot_tn(act_low[QUESTION:], upstream_low)
    fc_grad = dot_tn(second_low[QUESTION:], pre_grad)
    out_grad = dot_tn(mixed_low[QUESTION:], attn_grad)
    key_grad = lax.dynamic_update_slice(key_grad, key_early, (0, 0))
    value_grad = lax.dynamic_update_slice(value_grad, value_early, (0, 0))
    qkv_grad = jnp.concatenate(
        [jnp.pad(query_grad, ((QUESTION, 0), (0, 0))), key_grad, value_grad], axis=1
    ).astype(BF16)
    normed_one, inverse_one = norm_parts(hidden)
    first_low = (normed_one * vecs["ln1_gain"] + vecs["ln1_bias"]).astype(BF16)
    qkv_weight_grad = dot_tn(first_low, qkv_grad)
    first_grad = dot_nt(qkv_grad, wqkv)
    hidden_part = row_norm_back(first_grad, normed_one, inverse_one, vecs["ln1_gain"])
    positions = lax.iota(jnp.int32, seq_len)
    replaced = jnp.zeros((seq_len,), jnp.bool_)
    for step in range(THOUGHTS):
        replaced = replaced | ((positions == slots[0] + step) & (step < count))
    input_grad = jnp.where(
        replaced[:, None], 0.0, jnp.pad(resid_grad, ((QUESTION, 0), (0, 0))) + hidden_part
    )
    column_sums = jnp.sum(qkv_grad.astype(F32), axis=0)
    small_grads = {
        "ln1_gain": jnp.sum(first_grad * normed_one, axis=0),
        "ln1_bias": jnp.sum(first_grad, axis=0),
        "qv_bias": jnp.concatenate([column_sums[:width], column_sums[2 * width :]]),
        "out_bias": jnp.sum(attn_grad.astype(F32), axis=0),
        "ln2_gain": jnp.sum(second_grad * normed_late, axis=0),
        "ln2_bias": jnp.sum(second_grad, axis=0),
        "fc_bias": jnp.sum(pre_grad.astype(F32), axis=0),
        "proj_bias": jnp.sum(upstream_low.astype(F32), axis=0),
    }
    return output, input_grad, (qkv_weight_grad, out_grad, fc_grad, proj_grad), small_grads


SMALL = ("ln1_gain", "ln1_bias", "qv_bias", "out_bias", "ln2_gain", "ln2_bias", "fc_bias", "proj_bias")


def on_device(
    links,
    tokens,
    ln1_gain,
    ln1_bias,
    qkv_weight,
    qv_bias,
    out_weight,
    out_bias,
    ln2_gain,
    ln2_bias,
    fc_weight,
    fc_bias,
    proj_weight,
    proj_bias,
    cotangent,
    thought_slots,
    thought_count,
    answer_start,
):
    devices = links.sizes["dp"] * links.sizes["fsdp"]
    small_shards = dict(
        ln1_gain=ln1_gain,
        ln1_bias=ln1_bias,
        qv_bias=qv_bias,
        out_bias=out_bias,
        ln2_gain=ln2_gain,
        ln2_bias=ln2_bias,
        fc_bias=fc_bias,
        proj_bias=proj_bias,
    )
    packed = jnp.concatenate([small_shards[n] for n in SMALL])[None]
    gathered = links.gather(packed, "zxyc")[:, 0]
    small = {}
    begin = 0
    for name in SMALL:
        size = small_shards[name].shape[0]
        small[name] = gathered[:, begin : begin + size].reshape(-1)
        begin += size

    def columns(shard, orders):
        step = shard.shape[1] // len(orders)
        parts = [
            links.gather(shard[:, i * step : (i + 1) * step], text)
            for i, text in enumerate(orders)
        ]
        return jnp.concatenate(parts, axis=2).reshape(-1, shard.shape[1])

    weights = (
        columns(qkv_weight, ("zxyc", "zyxc")),
        columns(out_weight, ("xzyc",)),
        columns(fc_weight, ("zxyc", "zyxc")),
        columns(proj_weight, ("zxyc", "zyxc")),
    )
    output, input_grad, grads, small_grads = step_on_sequence(
        weights,
        small,
        tokens[0],
        cotangent[0],
        thought_slots[0],
        thought_count[0],
        answer_start[0],
    )

    def spread(grad, orders):
        rows = grad.shape[0] // devices
        step = grad.shape[1] // len(orders)
        low = grad.astype(BF16).reshape(devices, rows, grad.shape[1])
        return jnp.concatenate(
            [
                links.scatter(low[:, :, i * step : (i + 1) * step], text)
                for i, text in enumerate(orders)
            ],
            axis=1,
        )

    qkv_g, out_g, fc_g, proj_g = grads
    proj_g = spread(proj_g, ("cyxz", "cxyz"))
    fc_g = spread(fc_g, ("cyxz", "cxyz"))
    out_g = spread(out_g, ("cyzx",))
    qkv_g = spread(qkv_g, ("cyxz", "cxyz"))
    low = jnp.concatenate(
        [small_grads[n].reshape(devices, 1, -1) for n in SMALL], axis=2
    ).astype(BF16)
    flat = links.scatter(low, "cyxz")[0]
    owned = {}
    begin = 0
    for name in SMALL:
        size = small_shards[name].shape[0]
        owned[name] = flat[begin : begin + size]
        begin += size
    return (
        output[None],
        input_grad[None],
        owned["ln1_gain"],
        owned["ln1_bias"],
        qkv_g,
        owned["qv_bias"],
        out_g,
        owned["out_bias"],
        owned["ln2_gain"],
        owned["ln2_bias"],
        fc_g,
        owned["fc_bias"],
        proj_g,
        owned["proj_bias"],
    )


def solution(mesh):
    links = Links({name: mesh.shape[name] for name in ("dp", "fsdp")})
    both = ("dp", "fsdp")
    cube, matrix, vector = P(both, None, None), P(both, None), P(both)
    weight_specs = (
        vector,
        vector,
        matrix,
        vector,
        matrix,
        vector,
        vector,
        vector,
        matrix,
        vector,
        matrix,
        vector,
    )

    def per_device(*args):
        return on_device(links, *args)

    return jax.shard_map(
        per_device,
        mesh=mesh,
        in_specs=(cube,) + weight_specs + (cube, matrix, vector, vector),
        out_specs=(cube, cube) + weight_specs,
        check_vma=False,
    )
```

time: 911 us -> 559 us (0.61)
  matrix products: 316 us -> 77.8 us
  waiting for transfers between devices: 329 us -> 159 us
  Pallas kernels: 0 us -> 81.4 us
  starting transfers between devices: 1.09 us -> 80.3 us
  blocking collectives: 72.6 us -> 0 us
  other arithmetic: 106 us -> 64.7 us
  local copies, waits for them, and re-layouts: 58.1 us -> 77.6 us
  between operations: 23.3 us -> 6.36 us
    dot_general x60 -> x12, matrix products: 316 us -> 77.8 us  [the longest x4 28.7 us: dot(): lax.dot_general(a, b, (((1,), (0,)), ((), ())), preferred_element_type=F32)]
    reduce_scatter x8 -> x0, waiting for transfers between devices: 170 us -> none  [the longest x1 36.6 us: on_device(): lax.psum_scatter(totals[10].astype(jnp.bfloat16), 'dp', scatter_dimension...]
    ppermute x0 -> x80, waiting for transfers between devices: none -> 159 us  [swap(): lax.ppermute(value, axis, [(i, i ^ bit) for i in range(self.sizes[axis])])]
    all_gather x4 -> x0, waiting for transfers between devices: 156 us -> none  [the longest x1 61.5 us: fetch_weights(): lax.all_gather(shards[8], ('dp', 'fsdp'), axis=0, tiled=True)]
    pallas_call x0 -> x4, Pallas kernels: none -> 81.4 us  [the longest x1 25.8 us: attend_back(): pl.pallas_call(attend_back_kernel, grid=(pairs,), in_specs=[pl.BlockSpec(...]
    ppermute x0 -> x80, starting transfers between devices: none -> 80.3 us  [swap(): lax.ppermute(value, axis, [(i, i ^ bit) for i in range(self.sizes[axis])])]
    unnamed x3 -> x0, blocking collectives: 72.6 us -> none
    convert_element_type x33 -> x37, other arithmetic: 50.2 us -> 9.73 us  [the longest x3 3.71 us: step_on_sequence(): vecs = {name: value.astype(F32) for name, value in small.items()}]
  transfers between devices with their start and end apart: 12 -> 80, of which waited for: 9 -> 37; matrix products, arithmetic and copies ran while one was open for 19% -> 16% of each run, Pallas kernels for 0% -> 0%
where the time goes in v1:
time: 559 us; the launch traced here: 548 us
  waiting for transfers between devices  159 us (28%)
  Pallas kernels  81.4 us (15%)
  starting transfers between devices  80.3 us (14%)
  matrix products  77.8 us (14%)
  local copies, waits for them, and re-layouts  77.6 us (14%)
  other arithmetic  64.7 us (12%)
  between operations  6.36 us (1%)
    ppermute x80, waiting for transfers between devices, swap(): lax.ppermute(value, axis, [(i, i ^ bit) for i in range(self.sizes[axis])])  159 us
    ppermute x80, starting transfers between devices, swap(): lax.ppermute(value, axis, [(i, i ^ bit) for i in range(self.sizes[axis])])  80.3 us
    dot_general x4, matrix products, dot(): lax.dot_general(a, b, (((1,), (0,)), ((), ())), preferred_element_type=F32)  28.7 us
    dot_general x4, matrix products, dot_tn(): lax.dot_general(a, b, (((0,), (0,)), ((), ())), preferred_element_type=F32)  27.2 us
    pallas_call x1, Pallas kernels, attend_back(): pl.pallas_call(attend_back_kernel, grid=(pairs,), in_specs=[pl.BlockSpec(...  25.8 us
    pallas_call x1, Pallas kernels, attend(): pl.pallas_call(attend_kernel, grid=(pairs,), in_specs=[pl.BlockSpec((seq_...  23.2 us
    dot_general x4, matrix products, dot_nt(): lax.dot_general(a, b, (((1,), (1,)), ((), ())), preferred_element_type=F32)  21.9 us
    pallas_call x1, Pallas kernels, thoughts_back(): pl.pallas_call(thoughts_back_kernel, grid=(1,), in_specs=[pl.BlockSpec(me...  19.7 us
  transfers between devices with their start and end apart: 80, of which 37 were waited for; matrix products, arithmetic and copies ran while one was open for 16% of the time, Pallas kernels for 0%

profile of v1, /device:TPU:0, one launch (start us, length us, event | category | flops | bytes accessed | tf_op | source)
XLA Modules:
  0.0 547.6 jit_solution(16966571495588606346)
XLA Ops:
  0.6 5.4 concatenate.81
  6.6 4.0 collective-permute-start
  109.3 3.9 collective-permute-done.36
  126.6 3.8 collective-permute-done.27
  132.0 4.7 collective-permute-done.37
  136.9 9.3 %collective-permute-done.8 = bf16[2,2,2,24,1152]{4,3,1,2,0:T(8,128)(2,1)S(1)} collective-permute-done((bf16[2,2,2,24,1152]{4,3,1,2,0:T(8,128)(2,1)S(1)}, bf16[2,2,2,24,1152]{4,3,1,2,0:T(8,128)(2,1)S(1)}, u32[]{:S(2)}, u32[]{:S(2)}) %collective-permute-start.8) | collective-permute-done | bytes 442400 | tf_op jit(solution)/shard_map/ppermute | solution.py:59
  148.7 10.1 %collective-permute-done.23 = bf16[2,2,2,24,1536]{4,3,1,2,0:T(8,128)(2,1)S(1)} collective-permute-done((bf16[2,2,2,24,1536]{4,3,1,2,0:T(8,128)(2,1)S(1)}, bf16[2,2,2,24,1536]{4,3,1,2,0:T(8,128)(2,1)S(1)}, u32[]{:S(2)}, u32[]{:S(2)}) %collective-permute-start.23) | collective-permute-done | bytes 589856 | tf_op jit(solution)/shard_map/ppermute | solution.py:59
  158.9 11.3 %collective-permute-done.33 = bf16[2,2,2,96,384]{4,3,1,2,0:T(8,128)(2,1)S(1)} collective-permute-done((bf16[2,2,2,96,384]{4,3,1,2,0:T(8,128)(2,1)S(1)}, bf16[2,2,2,96,384]{4,3,1,2,0:T(8,128)(2,1)S(1)}, u32[]{:S(2)}, u32[]{:S(2)}) %collective-permute-start.33) | collective-permute-done | bytes 589856 | tf_op jit(solution)/shard_map/ppermute | solution.py:59
  177.4 6.1 %add_convert_fusion.qkv_ref = bf16[1024,2304]{1,0:T(8,128)(2,1)} fusion(f32[2304]{0:T(1024)S(1)} %copy-done.41, f32[768]{0:T(1024)S(1)} %copy-done.56, f32[768]{0:T(1024)S(1)} %copy-done.44, f32[1024]{0:T(1024)S(1)} %copy-done.59, f32[1024]{0:T(1024)S(1)} %copy-done.47, bf16[1,1024,768]{2,1,0:T(8,128)(2,1)S(1)} %copy-done.1, ...), kind=kOutput, calls=%fused_computation.8 | convolution fusion | flops 3640393728 | bytes 9853952 | tf_op jit(solution)/shard_map/dot_general | solution.py:26
  192.8 12.8 %thought_rows_forward.1 = (f32[128,768]{1,0:T(8,128)}, bf16[128,2304]{1,0:T(8,128)(2,1)}, f32[8,3072]{1,0:T(8,128)}, f32[32,384]{1,0:T(8,128)}, f32[8,768]{1,0:T(8,128)}) custom-call(s32[2]{0:T(128)} %pad_add_fusion.info_ref, bf16[1024,768]{1,0:T(8,128)(2,1)} %bitcast.488, bf16[1024,2304]{1,0:T(8,128)(2,1)} %add_convert_fusion.qkv_ref, ...), custom_call_target="tpu_custom_call" | custom-call | tf_op jit(solution)/shard_map/thought_rows_forward/pallas_call | solution.py:364
  207.5 23.2 %attention_forward.1 = (bf16[1024,768]{1,0:T(8,128)(2,1)}, f32[6,2,1024]{2,1,0:T(2,128)}) custom-call(bf16[1024,2304]{1,0:T(8,128)(2,1)} %constant_dynamic-update-slice_fusion.2.q_ref.k_ref.v_ref.qkv_ref, bf16[1024,2304]{1,0:T(8,128)(2,1)} %constant_dynamic-update-slice_fusion.2.q_ref.k_ref.v_ref.qkv_ref, ...), custom_call_target="tpu_custom_call" | custom-call | tf_op jit(solution)/shard_map/attention_forward/pallas_call | solution.py:129
  239.8 11.2 %fusion.4 = (bf16[1024,3072]{1,0:T(8,128)(2,1)}, f32[1024,3072]{1,0:T(8,128)}) fusion(f32[3072]{0:T(1024)S(1)} %copy-done.50, bf16[1024,768]{1,0:T(8,128)(2,1)S(1)} %get-tuple-element.56, bf16[768,1536]{1,0:T(8,128)(2,1)S(1)} %bitcast.509, bf16[768,1536]{1,0:T(8,128)(2,1)S(1)} %bitcast.506), kind=kOutput, calls=%fused_computation.5 | convolution fusion | flops 4872732672 | bytes 25178112 | tf_op jit(solution)/shard_map/dot_general | solution.py:26
  251.0 9.7 %multiply_convert_fusion = bf16[768,3072]{1,0:T(8,128)(2,1)S(1)} fusion(f32[1024,3072]{1,0:T(8,128)} %get-tuple-element.170, bf16[768,768]{1,0:T(8,128)(2,1)S(1)} %copy-done.26, bf16[3072,384]{1,0:T(8,128)(2,1)S(1)} %bitcast.503, bf16[3072,384]{1,0:T(8,128)(2,1)S(1)} %bitcast.500), kind=kOutput, calls=%fused_computation.7 | convolution fusion | flops 3675783168 | bytes 20054016 | tf_op jit(solution)/shard_map/dot_general | solution.py:30
  260.8 4.1 multiply_reduce_fusion.8
  269.7 25.8 %attention_backward.1 = (f32[768,768]{1,0:T(8,128)}, f32[1024,768]{1,0:T(8,128)}, f32[1024,768]{1,0:T(8,128)}) custom-call(bf16[1024,2304]{1,0:T(8,128)(2,1)} %constant_dynamic-update-slice_fusion.2.q_ref.k_ref.v_ref.qkv_ref, bf16[1024,2304]{1,0:T(8,128)(2,1)} %constant_dynamic-update-slice_fusion.2.q_ref.k_ref.v_ref.qkv_ref, ...), custom_call_target="tpu_custom_call" | custom-call | tf_op jit(solution)/shard_map/attention_backward/pallas_call | solution.py:197
  295.5 19.7 %thought_rows_backward.1 = (f32[384,768]{1,0:T(8,128)}, f32[384,768]{1,0:T(8,128)}, f32[8,768]{1,0:T(8,128)}, f32[8,768]{1,0:T(8,128)}, f32[8,3072]{1,0:T(8,128)}, /*index=5*/f32[8,768]{1,0:T(8,128)}, f32[8,768]{1,0:T(8,128)}) custom-call(s32[2]{0:T(128)} %pad_add_fusion.info_ref, f32[128,768]{1,0:T(8,128)} %get-tuple-element.31.hid_ref, ...), custom_call_target="tpu_custom_call" | custom-call | tf_op jit(solution)/shard_map/thought_rows_backward/pallas_call | solution.py:464
  326.1 6.0 %multiply_reduce_fusion = (bf16[768]{0:T(1024)(128)(2,1)S(1)}, f32[1024]{0:T(1024)S(1)}, f32[1024]{0:T(1024)S(1)}, bf16[768]{0:T(1024)(128)(2,1)S(1)}, f32[1024,768]{1,0:T(8,128)}) fusion(f32[1024,768]{1,0:T(8,128)S(1)} %constant_dynamic-update-slice_fusion.3, f32[1024]{0:T(1024)S(1)} %add_rsqrt_fusion, f32[1024]{0:T(1024)S(1)} %broadcast_multiply_fusion.3, ...), kind=kOutput, calls=%fused_computation.21 | convolution fusion | flops 3656905216 | bytes 14178304 | tf_op jit(solution)/shard_map/dot_general | solution.py:30
  332.1 6.0 %convolution_convert_fusion.2 = bf16[768,2304]{1,0:T(8,128)(2,1)} fusion(f32[1024,768]{1,0:T(8,128)S(1)} %constant_dynamic-update-slice_fusion.3, f32[1024]{0:T(1024)S(1)} %add_rsqrt_fusion, f32[1024]{0:T(1024)S(1)} %broadcast_multiply_fusion.3, f32[768]{0:T(1024)S(1)} %copy-done.57, f32[768]{0:T(1024)S(1)} %copy-done.44, ...), kind=kOutput, calls=%fused_computation.13 | convolution fusion | flops 3648454656 | bytes 11024384 | tf_op jit(solution)/shard_map/dot_general | solution.py:34
  348.6 8.8 %convolution_convert_fusion.1 = bf16[768,3072]{1,0:T(8,128)(2,1)} fusion(bf16[768,3072]{1,0:T(8,128)(2,1)} %dynamic_update_slice.34, bf16[1024,768]{1,0:T(8,128)(2,1)} %copy-done.31), kind=kOutput, calls=%fused_computation.12 | convolution fusion | flops 3626237952 | bytes 10616832 | tf_op jit(solution)/shard_map/dot_general | solution.py:34
  364.2 9.0 %convolution_convert_fusion = bf16[3072,768]{1,0:T(8,128)(2,1)} fusion(bf16[768,768]{1,0:T(8,128)(2,1)} %dynamic_update_slice.35, bf16[1024,3072]{1,0:T(8,128)(2,1)} %get-tuple-element.169), kind=kOutput, calls=%fused_computation.11 | convolution fusion | flops 3626237952 | bytes 10616832 | tf_op jit(solution)/shard_map/dot_general | solution.py:34
  373.2 8.1 %fusion.23 = bf16[1,1024,768]{2,1,0:T(8,128)(2,1)} fusion(f32[768]{0:T(1024)S(1)} %copy-done.55, f32[1024,768]{1,0:T(8,128)S(1)} %copy-done.7, bf16[1024,3072]{1,0:T(8,128)(2,1)} %get-tuple-element.169, bf16[3072,384]{1,0:T(8,128)(2,1)S(1)} %bitcast.504, bf16[3072,384]{1,0:T(8,128)(2,1)S(1)} %bitcast.501), kind=kOutput, calls=%fused_computation.67 | convolution fusion | flops 4843634688 | bytes 15731712 | tf_op jit(solution)/shard_map/dot_general | solution.py:26
  417.6 6.7 %collective-permute-done.56 = bf16[2,2,2,24,768]{4,3,0,2,1:T(8,128)(2,1)S(1)} collective-permute-done((bf16[2,2,2,24,768]{4,3,0,2,1:T(8,128)(2,1)S(1)}, bf16[2,2,2,24,768]{4,3,0,2,1:T(8,128)(2,1)S(1)}, u32[]{:S(2)}, u32[]{:S(2)}) %collective-permute-start.56) | collective-permute-done | bytes 294944 | tf_op jit(solution)/shard_map/ppermute | solution.py:59
  427.3 7.9 %collective-permute-done.57 = bf16[2,2,24,768]{3,2,0,1:T(8,128)(2,1)S(1)} collective-permute-done((bf16[2,2,24,768]{3,2,0,1:T(8,128)(2,1)S(1)}, bf16[2,2,24,768]{3,2,0,1:T(8,128)(2,1)S(1)}, u32[]{:S(2)}, u32[]{:S(2)}) %collective-permute-start.57) | collective-permute-done | bytes 147488 | tf_op jit(solution)/shard_map/ppermute | solution.py:59
  435.3 4.3 collective-permute-done.58
  451.7 5.3 collective-permute-done.51
  460.7 24.1 %collective-permute-done.52 = bf16[2,2,24,1152]{3,2,1,0:T(8,128)(2,1)S(1)} collective-permute-done((bf16[2,2,24,1152]{3,2,1,0:T(8,128)(2,1)S(1)}, bf16[2,2,24,1152]{3,2,1,0:T(8,128)(2,1)S(1)}, u32[]{:S(2)}, u32[]{:S(2)}) %collective-permute-start.52) | collective-permute-done | bytes 221216 | tf_op jit(solution)/shard_map/ppermute | solution.py:59
  485.5 5.2 collective-permute-done.47
  493.1 6.5 %collective-permute-done.53 = bf16[2,24,1152]{2,1,0:T(8,128)(2,1)S(1)} collective-permute-done((bf16[2,24,1152]{2,1,0:T(8,128)(2,1)S(1)}, bf16[2,24,1152]{2,1,0:T(8,128)(2,1)S(1)}, u32[]{:S(2)}, u32[]{:S(2)}) %collective-permute-start.53) | collective-permute-done | bytes 110624 | tf_op jit(solution)/shard_map/ppermute | solution.py:59
  499.7 6.9 %collective-permute-done.48 = bf16[2,24,1152]{2,1,0:T(8,128)(2,1)S(1)} collective-permute-done((bf16[2,24,1152]{2,1,0:T(8,128)(2,1)S(1)}, bf16[2,24,1152]{2,1,0:T(8,128)(2,1)S(1)}, u32[]{:S(2)}, u32[]{:S(2)}) %collective-permute-start.48) | collective-permute-done | bytes 110624 | tf_op jit(solution)/shard_map/ppermute | solution.py:59
  506.6 4.1 collective-permute-done.54
  510.8 4.1 collective-permute-done.49
  529.2 7.1 %collective-permute-done.68 = bf16[2,24,1536]{2,1,0:T(8,128)(2,1)S(1)} collective-permute-done((bf16[2,24,1536]{2,1,0:T(8,128)(2,1)S(1)}, bf16[2,24,1536]{2,1,0:T(8,128)(2,1)S(1)}, u32[]{:S(2)}, u32[]{:S(2)}) %collective-permute-start.68) | collective-permute-done | bytes 147488 | tf_op jit(solution)/shard_map/ppermute | solution.py:59
  (548 shorter events, 256.1 us)
Async XLA Ops:
  6.6 17.9 %collective-permute-start = (bf16[1,288]{1,0:T(2,128)(2,1)}, bf16[1,288]{1,0:T(2,128)(2,1)}, u32[]{:S(2)}, u32[]{:S(2)}) collective-permute-start(bf16[1,288]{1,0:T(2,128)(2,1)} %broadcast_in_dim.30), channel_id=1, source_target_pairs={{0,4},{1,5},{2,6},{3,7},{4,0},{5,1},{6,2},{7,3},{8,12},{9,13},{10,... | collective-permute-start | bytes 1736 | tf_op jit(solution)/shard_map/ppermute | solution.py:59
  12.1 71.5 %collective-permute-start.5 = (bf16[24,1152]{1,0:T(8,128)(2,1)}, bf16[24,1152]{1,0:T(8,128)(2,1)}, u32[]{:S(2)}, u32[]{:S(2)}) collective-permute-start(bf16[24,1152]{1,0:T(8,128)(2,1)} %slice.197), channel_id=1, source_target_pairs={{0,4},{1,5},{2,6},{3,7},{4,0},{5,1},{6,2},{7,3},{8,12},{9,13},{10,... | collective-permute-start | bytes 165896 | tf_op jit(solution)/shard_map/ppermute | solution.py:59
  12.1 68.2 %collective-permute-start.15 = (bf16[24,768]{1,0:T(8,128)(2,1)}, bf16[24,768]{1,0:T(8,128)(2,1)}, u32[]{:S(2)}, u32[]{:S(2)}) collective-permute-start(bf16[24,768]{1,0:T(8,128)(2,1)} %param.22), channel_id=1, source_target_pairs={{0,8},{8,0},{16,24},{24,16},{1,9},{9,1},{17,25},{25,17},{2,10},{10... | collective-permute-start | bytes 110600 | tf_op jit(solution)/shard_map/ppermute | solution.py:59
  15.5 70.9 %collective-permute-start.20 = (bf16[24,1536]{1,0:T(8,128)(2,1)}, bf16[24,1536]{1,0:T(8,128)(2,1)}, u32[]{:S(2)}, u32[]{:S(2)}) collective-permute-start(bf16[24,1536]{1,0:T(8,128)(2,1)} %slice.204), channel_id=1, source_target_pairs={{0,4},{1,5},{2,6},{3,7},{4,0},{5,1},{6,2},{7,3},{8,12},{9,13},{10,... | collective-permute-start | bytes 221192 | tf_op jit(solution)/shard_map/ppermute | solution.py:59
  19.6 70.2 %collective-permute-start.30 = (bf16[96,384]{1,0:T(8,128)(2,1)}, bf16[96,384]{1,0:T(8,128)(2,1)}, u32[]{:S(2)}, u32[]{:S(2)}) collective-permute-start(bf16[96,384]{1,0:T(8,128)(2,1)} %slice.206), channel_id=1, source_target_pairs={{0,4},{1,5},{2,6},{3,7},{4,0},{5,1},{6,2},{7,3},{8,12},{9,13},{10,... | collective-permute-start | bytes 221192 | tf_op jit(solution)/shard_map/ppermute | solution.py:59
  85.1 15.1 %collective-permute-start.6 = (bf16[2,24,1152]{2,1,0:T(8,128)(2,1)S(1)}, bf16[2,24,1152]{2,1,0:T(8,128)(2,1)S(1)}, u32[]{:S(2)}, u32[]{:S(2)}) collective-permute-start(bf16[2,24,1152]{2,1,0:T(8,128)(2,1)S(1)} %pad_maximum_fusion.38), channel_id=1, source_target_pairs={{0,2},{1,3},{2,0},{3,1},{4,6},{5,7},{6,4},{7,5},{8,10},{9,11},{10,... | collective-permute-start | bytes 331784 | tf_op jit(solution)/shard_map/ppermute | solution.py:59
  89.8 15.5 %collective-permute-start.21 = (bf16[2,24,1536]{2,1,0:T(8,128)(2,1)S(1)}, bf16[2,24,1536]{2,1,0:T(8,128)(2,1)S(1)}, u32[]{:S(2)}, u32[]{:S(2)}) collective-permute-start(bf16[2,24,1536]{2,1,0:T(8,128)(2,1)S(1)} %pad_maximum_fusion.34), channel_id=1, source_target_pairs={{0,2},{1,3},{2,0},{3,1},{4,6},{5,7},{6,4},{7,5},{8,10},{9,11},{10,... | collective-permute-start | bytes 442376 | tf_op jit(solution)/shard_map/ppermute | solution.py:59
  115.8 14.6 %collective-permute-start.27 = (bf16[2,2,24,1536]{3,2,0,1:T(8,128)(2,1)S(1)}, bf16[2,2,24,1536]{3,2,0,1:T(8,128)(2,1)S(1)}, u32[]{:S(2)}, u32[]{:S(2)}) collective-permute-start(bf16[2,2,24,1536]{3,2,0,1:T(8,128)(2,1)S(1)} %pad_maximum_fusion.25), channel_id=1, source_target_pairs={{0,16},{8,24},{16,0},{24,8},{1,17},{9,25},{17,1},{25,9},{2,18},{10... | collective-permute-start | bytes 884744 | tf_op jit(solution)/shard_map/ppermute | solution.py:59
  116.4 20.3 %collective-permute-start.37 = (bf16[2,2,96,384]{3,2,0,1:T(8,128)(2,1)S(1)}, bf16[2,2,96,384]{3,2,0,1:T(8,128)(2,1)S(1)}, u32[]{:S(2)}, u32[]{:S(2)}) collective-permute-start(bf16[2,2,96,384]{3,2,0,1:T(8,128)(2,1)S(1)} %pad_maximum_fusion.27), channel_id=1, source_target_pairs={{0,16},{8,24},{16,0},{24,8},{1,17},{9,25},{17,1},{25,9},{2,18},{10... | collective-permute-start | bytes 884744 | tf_op jit(solution)/shard_map/ppermute | solution.py:59
  119.3 26.9 %collective-permute-start.8 = (bf16[2,2,2,24,1152]{4,3,1,2,0:T(8,128)(2,1)S(1)}, bf16[2,2,2,24,1152]{4,3,1,2,0:T(8,128)(2,1)S(1)}, u32[]{:S(2)}, u32[]{:S(2)}) collective-permute-start(bf16[2,2,2,24,1152]{4,3,1,2,0:T(8,128)(2,1)S(1)} %pad_maximum_fusion.21), channel_id=1, source_target_pairs={{0,16},{8,24},{16,0},{24,8},{1,17},{9,25},{17,1},{25,9},{2,18},{10... | collective-permute-start | bytes 1327112 | tf_op jit(solution)/shard_map/ppermute | solution.py:59
  123.9 23.7 %collective-permute-start.13 = (bf16[2,2,2,24,1152]{4,3,1,2,0:T(8,128)(2,1)S(1)}, bf16[2,2,2,24,1152]{4,3,1,2,0:T(8,128)(2,1)S(1)}, u32[]{:S(2)}, u32[]{:S(2)}) collective-permute-start(bf16[2,2,2,24,1152]{4,3,1,2,0:T(8,128)(2,1)S(1)} %pad_maximum_fusion.22), channel_id=1, source_target_pairs={{0,8},{8,0},{16,24},{24,16},{1,9},{9,1},{17,25},{25,17},{2,10},{10... | collective-permute-start | bytes 1327112 | tf_op jit(solution)/shard_map/ppermute | solution.py:59
  124.9 33.9 %collective-permute-start.23 = (bf16[2,2,2,24,1536]{4,3,1,2,0:T(8,128)(2,1)S(1)}, bf16[2,2,2,24,1536]{4,3,1,2,0:T(8,128)(2,1)S(1)}, u32[]{:S(2)}, u32[]{:S(2)}) collective-permute-start(bf16[2,2,2,24,1536]{4,3,1,2,0:T(8,128)(2,1)S(1)} %pad_maximum_fusion.17), channel_id=1, source_target_pairs={{0,16},{8,24},{16,0},{24,8},{1,17},{9,25},{17,1},{25,9},{2,18},{10... | collective-permute-start | bytes 1769480 | tf_op jit(solution)/shard_map/ppermute | solution.py:59
  130.4 39.8 %collective-permute-start.33 = (bf16[2,2,2,96,384]{4,3,1,2,0:T(8,128)(2,1)S(1)}, bf16[2,2,2,96,384]{4,3,1,2,0:T(8,128)(2,1)S(1)}, u32[]{:S(2)}, u32[]{:S(2)}) collective-permute-start(bf16[2,2,2,96,384]{4,3,1,2,0:T(8,128)(2,1)S(1)} %pad_maximum_fusion.19), channel_id=1, source_target_pairs={{0,16},{8,24},{16,0},{24,8},{1,17},{9,25},{17,1},{25,9},{2,18},{10... | collective-permute-start | bytes 1769480 | tf_op jit(solution)/shard_map/ppermute | solution.py:59
  136.7 33.9 %collective-permute-start.19 = (bf16[2,2,2,2,24,768]{5,4,1,2,3,0:T(8,128)(2,1)S(1)}, bf16[2,2,2,2,24,768]{5,4,1,2,3,0:T(8,128)(2,1)S(1)}, u32[]{:S(2)}, u32[]{:S(2)}) collective-permute-start(bf16[2,2,2,2,24,768]{5,4,1,2,3,0:T(8,128)(2,1)S(1)} %pad_maximum_fusion.16), channel_id=1, source_target_pairs={{0,1},{1,0},{2,3},{3,2},{4,5},{5,4},{6,7},{7,6},{8,9},{9,8},{10,11... | collective-permute-start | bytes 1769480 | tf_op jit(solution)/shard_map/ppermute | solution.py:59
  146.2 26.4 %collective-permute-start.28 = (bf16[2,2,2,24,1536]{4,3,1,2,0:T(8,128)(2,1)S(1)}, bf16[2,2,2,24,1536]{4,3,1,2,0:T(8,128)(2,1)S(1)}, u32[]{:S(2)}, u32[]{:S(2)}) collective-permute-start(bf16[2,2,2,24,1536]{4,3,1,2,0:T(8,128)(2,1)S(1)} %pad_maximum_fusion.18), channel_id=1, source_target_pairs={{0,8},{8,0},{16,24},{24,16},{1,9},{9,1},{17,25},{25,17},{2,10},{10... | collective-permute-start | bytes 1769480 | tf_op jit(solution)/shard_map/ppermute | solution.py:59
  147.7 25.1 %collective-permute-start.38 = (bf16[2,2,2,96,384]{4,3,1,2,0:T(8,128)(2,1)S(1)}, bf16[2,2,2,96,384]{4,3,1,2,0:T(8,128)(2,1)S(1)}, u32[]{:S(2)}, u32[]{:S(2)}) collective-permute-start(bf16[2,2,2,96,384]{4,3,1,2,0:T(8,128)(2,1)S(1)} %pad_maximum_fusion.20), channel_id=1, source_target_pairs={{0,8},{8,0},{16,24},{24,16},{1,9},{9,1},{17,25},{25,17},{2,10},{10... | collective-permute-start | bytes 1769480 | tf_op jit(solution)/shard_map/ppermute | solution.py:59
  158.8 14.8 %collective-permute-start.9 = (bf16[2,2,2,2,24,1152]{5,4,2,3,0,1:T(8,128)(2,1)S(1)}, bf16[2,2,2,2,24,1152]{5,4,2,3,0,1:T(8,128)(2,1)S(1)}, u32[]{:S(2)}, u32[]{:S(2)}) collective-permute-start(bf16[2,2,2,2,24,1152]{5,4,2,3,0,1:T(8,128)(2,1)S(1)} %pad_maximum_fusion.14), channel_id=1, source_target_pairs={{0,1},{1,0},{2,3},{3,2},{4,5},{5,4},{6,7},{7,6},{8,9},{9,8},{10,11... | collective-permute-start | bytes 2654216 | tf_op jit(solution)/shard_map/ppermute | solution.py:59
  390.8 33.6 %collective-permute-start.50 = (bf16[2,2,2,2,24,1152]{5,4,3,2,0,1:T(8,128)(2,1)S(1)}, bf16[2,2,2,2,24,1152]{5,4,3,2,0,1:T(8,128)(2,1)S(1)}, u32[]{:S(2)}, u32[]{:S(2)}) collective-permute-start(bf16[2,2,2,2,24,1152]{5,4,3,2,0,1:T(8,128)(2,1)S(1)} %bitcast.530), channel_id=1, source_target_pairs={{0,1},{1,0},{2,3},{3,2},{4,5},{5,4},{6,7},{7,6},{8,9},{9,8},{10,11... | collective-permute-start | bytes 2654216 | tf_op jit(solution)/shard_map/ppermute | solution.py:59
  391.0 34.2 %collective-permute-start.45 = (bf16[2,2,2,2,24,1152]{5,4,3,2,1,0:T(8,128)(2,1)S(1)}, bf16[2,2,2,2,24,1152]{5,4,3,2,1,0:T(8,128)(2,1)S(1)}, u32[]{:S(2)}, u32[]{:S(2)}) collective-permute-start(bf16[2,2,2,2,24,1152]{5,4,3,2,1,0:T(8,128)(2,1)S(1)} %dynamic-slice_bitcast_fusion.2), channel_id=1, source_target_pairs={{0,1},{1,0},{2,3},{3,2},{4,5},{5,4},{6,7},{7,6},{8,9},{9,8},{10,11... | collective-permute-start | bytes 2654216 | tf_op jit(solution)/shard_map/ppermute | solution.py:59
  392.2 22.5 %collective-permute-start.55 = (bf16[2,2,2,2,24,768]{5,4,1,3,2,0:T(8,128)(2,1)S(1)}, bf16[2,2,2,2,24,768]{5,4,1,3,2,0:T(8,128)(2,1)S(1)}, u32[]{:S(2)}, u32[]{:S(2)}) collective-permute-start(bf16[2,2,2,2,24,768]{5,4,1,3,2,0:T(8,128)(2,1)S(1)} %bitcast.531), channel_id=1, source_target_pairs={{0,1},{1,0},{2,3},{3,2},{4,5},{5,4},{6,7},{7,6},{8,9},{9,8},{10,11... | collective-permute-start | bytes 1769480 | tf_op jit(solution)/shard_map/ppermute | solution.py:59
  393.0 52.8 %collective-permute-start.65 = (bf16[2,2,2,2,24,1536]{5,4,3,2,0,1:T(8,128)(2,1)S(1)}, bf16[2,2,2,2,24,1536]{5,4,3,2,0,1:T(8,128)(2,1)S(1)}, u32[]{:S(2)}, u32[]{:S(2)}) collective-permute-start(bf16[2,2,2,2,24,1536]{5,4,3,2,0,1:T(8,128)(2,1)S(1)} %bitcast.527), channel_id=1, source_target_pairs={{0,1},{1,0},{2,3},{3,2},{4,5},{5,4},{6,7},{7,6},{8,9},{9,8},{10,11... | collective-permute-start | bytes 3538952 | tf_op jit(solution)/shard_map/ppermute | solution.py:59
  414.1 33.8 %collective-permute-start.60 = (bf16[2,2,2,2,24,1536]{5,4,3,2,1,0:T(8,128)(2,1)S(1)}, bf16[2,2,2,2,24,1536]{5,4,3,2,1,0:T(8,128)(2,1)S(1)}, u32[]{:S(2)}, u32[]{:S(2)}) collective-permute-start(bf16[2,2,2,2,24,1536]{5,4,3,2,1,0:T(8,128)(2,1)S(1)} %dynamic-slice_bitcast_fusion.1), channel_id=1, source_target_pairs={{0,1},{1,0},{2,3},{3,2},{4,5},{5,4},{6,7},{7,6},{8,9},{9,8},{10,11... | collective-permute-start | bytes 3538952 | tf_op jit(solution)/shard_map/ppermute | solution.py:59
  424.3 24.7 %collective-permute-start.75 = (bf16[2,2,2,2,96,384]{5,4,3,2,0,1:T(8,128)(2,1)S(1)}, bf16[2,2,2,2,96,384]{5,4,3,2,0,1:T(8,128)(2,1)S(1)}, u32[]{:S(2)}, u32[]{:S(2)}) collective-permute-start(bf16[2,2,2,2,96,384]{5,4,3,2,0,1:T(8,128)(2,1)S(1)} %bitcast.528), channel_id=1, source_target_pairs={{0,1},{1,0},{2,3},{3,2},{4,5},{5,4},{6,7},{7,6},{8,9},{9,8},{10,11... | collective-permute-start | bytes 3538952 | tf_op jit(solution)/shard_map/ppermute | solution.py:59
  424.5 25.5 %collective-permute-start.70 = (bf16[2,2,2,2,96,384]{5,4,3,2,1,0:T(8,128)(2,1)S(1)}, bf16[2,2,2,2,96,384]{5,4,3,2,1,0:T(8,128)(2,1)S(1)}, u32[]{:S(2)}, u32[]{:S(2)}) collective-permute-start(bf16[2,2,2,2,96,384]{5,4,3,2,1,0:T(8,128)(2,1)S(1)} %dynamic-slice_bitcast_fusion), channel_id=1, source_target_pairs={{0,1},{1,0},{2,3},{3,2},{4,5},{5,4},{6,7},{7,6},{8,9},{9,8},{10,11... | collective-permute-start | bytes 3538952 | tf_op jit(solution)/shard_map/ppermute | solution.py:59
  447.8 67.8 %collective-permute-start.66 = (bf16[2,2,2,24,1536]{4,3,2,1,0:T(8,128)(2,1)S(1)}, bf16[2,2,2,24,1536]{4,3,2,1,0:T(8,128)(2,1)S(1)}, u32[]{:S(2)}, u32[]{:S(2)}) collective-permute-start(bf16[2,2,2,24,1536]{4,3,2,1,0:T(8,128)(2,1)S(1)} %dynamic-slice_bitcast_fusion.5), channel_id=1, source_target_pairs={{0,8},{8,0},{16,24},{24,16},{1,9},{9,1},{17,25},{25,17},{2,10},{10... | collective-permute-start | bytes 1769480 | tf_op jit(solution)/shard_map/ppermute | solution.py:59
  449.0 68.4 %collective-permute-start.61 = (bf16[2,2,2,24,1536]{4,3,2,1,0:T(8,128)(2,1)S(1)}, bf16[2,2,2,24,1536]{4,3,2,1,0:T(8,128)(2,1)S(1)}, u32[]{:S(2)}, u32[]{:S(2)}) collective-permute-start(bf16[2,2,2,24,1536]{4,3,2,1,0:T(8,128)(2,1)S(1)} %dynamic-slice_bitcast_fusion.6), channel_id=1, source_target_pairs={{0,16},{8,24},{16,0},{24,8},{1,17},{9,25},{17,1},{25,9},{2,18},{10... | collective-permute-start | bytes 1769480 | tf_op jit(solution)/shard_map/ppermute | solution.py:59
  450.0 68.4 %collective-permute-start.76 = (bf16[2,2,2,96,384]{4,3,2,1,0:T(8,128)(2,1)S(1)}, bf16[2,2,2,96,384]{4,3,2,1,0:T(8,128)(2,1)S(1)}, u32[]{:S(2)}, u32[]{:S(2)}) collective-permute-start(bf16[2,2,2,96,384]{4,3,2,1,0:T(8,128)(2,1)S(1)} %dynamic-slice_bitcast_fusion.3), channel_id=1, source_target_pairs={{0,8},{8,0},{16,24},{24,16},{1,9},{9,1},{17,25},{25,17},{2,10},{10... | collective-permute-start | bytes 1769480 | tf_op jit(solution)/shard_map/ppermute | solution.py:59
  457.0 61.9 %collective-permute-start.71 = (bf16[2,2,2,96,384]{4,3,2,1,0:T(8,128)(2,1)S(1)}, bf16[2,2,2,96,384]{4,3,2,1,0:T(8,128)(2,1)S(1)}, u32[]{:S(2)}, u32[]{:S(2)}) collective-permute-start(bf16[2,2,2,96,384]{4,3,2,1,0:T(8,128)(2,1)S(1)} %dynamic-slice_bitcast_fusion.4), channel_id=1, source_target_pairs={{0,16},{8,24},{16,0},{24,8},{1,17},{9,25},{17,1},{25,9},{2,18},{10... | collective-permute-start | bytes 1769480 | tf_op jit(solution)/shard_map/ppermute | solution.py:59
  458.9 25.8 %collective-permute-start.52 = (bf16[2,2,24,1152]{3,2,1,0:T(8,128)(2,1)S(1)}, bf16[2,2,24,1152]{3,2,1,0:T(8,128)(2,1)S(1)}, u32[]{:S(2)}, u32[]{:S(2)}) collective-permute-start(bf16[2,2,24,1152]{3,2,1,0:T(8,128)(2,1)S(1)} %dynamic-slice_bitcast_fusion.14), channel_id=1, source_target_pairs={{0,16},{8,24},{16,0},{24,8},{1,17},{9,25},{17,1},{25,9},{2,18},{10... | collective-permute-start | bytes 663560 | tf_op jit(solution)/shard_map/ppermute | solution.py:59
  524.5 14.2 %collective-permute-start.63 = (bf16[2,24,1536]{2,1,0:T(8,128)(2,1)S(1)}, bf16[2,24,1536]{2,1,0:T(8,128)(2,1)S(1)}, u32[]{:S(2)}, u32[]{:S(2)}) collective-permute-start(bf16[2,24,1536]{2,1,0:T(8,128)(2,1)S(1)} %dynamic-slice_bitcast_fusion.19), channel_id=1, source_target_pairs={{0,4},{1,5},{2,6},{3,7},{4,0},{5,1},{6,2},{7,3},{8,12},{9,13},{10,... | collective-permute-start | bytes 442376 | tf_op jit(solution)/shard_map/ppermute | solution.py:59
  526.0 14.2 %collective-permute-start.78 = (bf16[2,96,384]{2,1,0:T(8,128)(2,1)S(1)}, bf16[2,96,384]{2,1,0:T(8,128)(2,1)S(1)}, u32[]{:S(2)}, u32[]{:S(2)}) collective-permute-start(bf16[2,96,384]{2,1,0:T(8,128)(2,1)S(1)} %dynamic-slice_bitcast_fusion.16), channel_id=1, source_target_pairs={{0,4},{1,5},{2,6},{3,7},{4,0},{5,1},{6,2},{7,3},{8,12},{9,13},{10,... | collective-permute-start | bytes 442376 | tf_op jit(solution)/shard_map/ppermute | solution.py:59
  527.8 14.0 %collective-permute-start.73 = (bf16[2,96,384]{2,1,0:T(8,128)(2,1)S(1)}, bf16[2,96,384]{2,1,0:T(8,128)(2,1)S(1)}, u32[]{:S(2)}, u32[]{:S(2)}) collective-permute-start(bf16[2,96,384]{2,1,0:T(8,128)(2,1)S(1)} %dynamic-slice_bitcast_fusion.17), channel_id=1, source_target_pairs={{0,4},{1,5},{2,6},{3,7},{4,0},{5,1},{6,2},{7,3},{8,12},{9,13},{10,... | collective-permute-start | bytes 442376 | tf_op jit(solution)/shard_map/ppermute | solution.py:59
  (112 other events, 857.5 us)

commit v2 on v1

v2 whole, which is shorter than its diff:
```python
import functools
import math

import jax
import jax.numpy as jnp
from jax import lax
from jax.experimental import pallas as pl
from jax.experimental.pallas import tpu as pltpu
from jax.sharding import PartitionSpec as P

HD = 64
THOUGHTS = 2
PREFIX = 384
QUESTION = 256
SCALE = 0.125
EPSILON = 1e-05
BLOCK = 256
HEAD_ROWS = 16
WINDOW = 32
LANES = 128
PAIR = 2 * HD
NEG = -1e30

F32 = jnp.float32
BF16 = jnp.bfloat16
VMEM_LIMIT = 56 * 1024 * 1024


def cost(microseconds):
    return pl.CostEstimate(
        flops=int(microseconds * 1.15e9),
        bytes_accessed=int(microseconds * 3.6e6),
        transcendentals=0,
    )


def dot(a, b):
    return lax.dot_general(a, b, (((1,), (0,)), ((), ())), preferred_element_type=F32)


def dot_nt(a, b):
    return lax.dot_general(a, b, (((1,), (1,)), ((), ())), preferred_element_type=F32)


def dot_tn(a, b):
    return lax.dot_general(a, b, (((0,), (0,)), ((), ())), preferred_element_type=F32)


def bits_of(size):
    return [1 << i for i in reversed(range(int(math.log2(size))))]


class Links:
    def __init__(self, sizes):
        self.sizes = sizes
        self.canon = [("dp", b) for b in bits_of(sizes["dp"])] + [
            ("fsdp", b) for b in bits_of(sizes["fsdp"])
        ]
        dp_bits = [("dp", b) for b in bits_of(sizes["dp"])]
        f_bits = [("fsdp", b) for b in bits_of(sizes["fsdp"])]
        self.groups = {"x": dp_bits[-1:], "y": dp_bits[:-1], "z": f_bits[:-1], "c": f_bits[-1:]}

    def order(self, text):
        out = []
        for letter in text:
            out += self.groups[letter]
        return out

    def swap(self, value, stage):
        axis, bit = stage
        return lax.ppermute(value, axis, [(i, i ^ bit) for i in range(self.sizes[axis])])

    def mine(self, stage):
        axis, bit = stage
        return (lax.axis_index(axis) & bit) != 0

    def gather(self, shard, text, axis=0):
        return Gather(self, shard, text, axis).finish()

    def scatter(self, value, text):
        return Scatter(self, value, text)


class Gather:
    def __init__(self, links, shard, text, axis=0):
        self.links = links
        self.shape = shard.shape
        self.axis = axis
        self.todo = links.order(text)
        self.done = []
        self.buf = shard
        self.got = None

    def go(self):
        self.add()
        self.stage = self.todo.pop(0)
        self.got = self.links.swap(self.buf, self.stage)
        return self.buf

    def add(self):
        if self.got is not None:
            canon = self.links.canon
            place = sum(1 for d in self.done if canon.index(d) < canon.index(self.stage))
            high = self.links.mine(self.stage)
            pair = [jnp.where(high, self.got, self.buf), jnp.where(high, self.buf, self.got)]
            self.buf = jnp.stack(pair, axis=self.axis + place)
            self.done.append(self.stage)
            self.got = None
        return self.buf

    def finish(self):
        while self.todo:
            self.go()
        self.add()
        shape = self.shape
        return self.buf.reshape(shape[: self.axis] + (-1,) + shape[self.axis + 1 :])


class Scatter:
    def __init__(self, links, value, text):
        self.links = links
        self.left = list(links.canon)
        self.todo = list(reversed(links.order(text)))
        self.buf = value.reshape((2,) * len(self.left) + value.shape[1:])
        self.got = None

    def go(self):
        self.add()
        stage = self.todo.pop(0)
        place = self.left.index(stage)
        self.left.remove(stage)
        high = self.links.mine(stage).astype(jnp.int32)
        self.keep = lax.dynamic_index_in_dim(self.buf, high, place, keepdims=False)
        sent = lax.dynamic_index_in_dim(self.buf, 1 - high, place, keepdims=False)
        self.got = self.links.swap(sent, stage)
        return sent

    def add(self):
        if self.got is None:
            return self.buf
        self.buf = self.keep.astype(F32) + self.got.astype(F32)
        if self.left:
            self.buf = self.buf.astype(BF16)
        self.got = None
        return self.buf

    def finish(self):
        while self.todo:
            self.go()
            self.add()
        return self.buf


def join_after(swaps, *deps):
    for swap in swaps:
        swap.got = after(swap.got, *deps)
        swap.add()


def go_after(swaps, *deps):
    for swap in swaps:
        swap.buf = after(swap.buf, *deps)
    return tuple(swap.go() for swap in swaps)


def after(value, *deps):
    return lax.optimization_barrier((value, deps))[0]


def attend_kernel(info_ref, q_ref, k_ref, v_ref, o_ref, lse_ref):
    seq_len = q_ref.shape[0]
    slot = info_ref[0]
    keys = k_ref[...]
    values_t = v_ref[...].T
    lane = lax.broadcasted_iota(jnp.int32, (BLOCK, PAIR), 1)
    sub = lax.broadcasted_iota(jnp.int32, (PAIR, BLOCK), 0)
    key_pos = lax.broadcasted_iota(jnp.int32, (BLOCK, BLOCK), 0)
    row_pos = lax.broadcasted_iota(jnp.int32, (BLOCK, BLOCK), 1)
    causal = key_pos <= row_pos
    middle_pos = QUESTION + lax.broadcasted_iota(jnp.int32, (PREFIX - QUESTION, BLOCK), 0)
    is_slot = (middle_pos >= slot) & (middle_pos < slot + THOUGHTS)

    def hide(scores):
        if scores.shape[0] <= QUESTION:
            return scores
        middle = jnp.where(is_slot, NEG, scores[QUESTION:PREFIX])
        return jnp.concatenate([scores[:QUESTION], middle, scores[PREFIX:]], axis=0)

    for begin in range(0, seq_len, BLOCK):
        end = begin + BLOCK
        queries = q_ref[begin:end, :] * jnp.asarray(SCALE, BF16)
        parts = []
        for head in range(2):
            own = jnp.where((lane >= HD) == bool(head), queries, jnp.zeros_like(queries))
            scores = dot_nt(keys[:end], own)
            last = jnp.where(causal, scores[begin:], NEG)
            if begin:
                last = jnp.concatenate([scores[:begin], last], axis=0)
            scores = hide(last)
            peak = jnp.max(scores, axis=0, keepdims=True)
            expo = jnp.exp(scores - peak)
            total = jnp.sum(expo, axis=0, keepdims=True)
            mixed = dot(values_t[:, :end], expo.astype(BF16))
            parts.append(mixed / total)
            lse_ref[pl.ds(2 * pl.program_id(0) + head, 1), begin:end] = peak + jnp.log(total)
        o_ref[begin:end, :] = jnp.where(sub < HD, parts[0], parts[1]).T.astype(BF16)


def attend(info, qkv):
    _, seq_len, width = qkv.shape
    pairs = width // PAIR

    def columns(i):
        return pl.BlockSpec((None, seq_len, PAIR), lambda g, i=i: (i, 0, g))

    return pl.pallas_call(
        attend_kernel,
        grid=(pairs,),
        in_specs=[
            pl.BlockSpec(memory_space=pltpu.SMEM),
            *(columns(i) for i in range(3)),
        ],
        out_specs=[
            pl.BlockSpec((seq_len, PAIR), lambda g: (0, g)),
            pl.BlockSpec((HEAD_ROWS, seq_len), lambda g: (0, 0)),
        ],
        out_shape=[
            jax.ShapeDtypeStruct((seq_len, width), BF16),
            jax.ShapeDtypeStruct((HEAD_ROWS, seq_len), F32),
        ],
        compiler_params=pltpu.CompilerParams(vmem_limit_bytes=VMEM_LIMIT),
        cost_estimate=cost(12),
        name="attention_forward",
    )(info, qkv, qkv, qkv)


def attend_back_kernel(
    q_ref, k_ref, v_ref, o_ref, lse_ref, g_ref, out_ref, dk_acc, dv_acc
):
    seq_len = q_ref.shape[0]
    pair = pl.program_id(0)
    first_row = seq_len - g_ref.shape[0]
    keys = k_ref[...]
    values = v_ref[...]
    keys_t = keys.T
    lane = lax.broadcasted_iota(jnp.int32, (BLOCK, PAIR), 1)
    sub = lax.broadcasted_iota(jnp.int32, (PAIR, BLOCK), 0)
    key_pos = lax.broadcasted_iota(jnp.int32, (BLOCK, BLOCK), 0)
    row_pos = lax.broadcasted_iota(jnp.int32, (BLOCK, BLOCK), 1)
    causal = key_pos <= row_pos
    dk_acc[...] = jnp.zeros_like(dk_acc)
    dv_acc[...] = jnp.zeros_like(dv_acc)
    for begin in range(first_row, seq_len, BLOCK):
        end = begin + BLOCK
        local = begin - first_row
        queries = q_ref[begin:end, :] * jnp.asarray(SCALE, BF16)
        grads = g_ref[local : local + BLOCK, :]
        product_t = (grads.astype(F32) * o_ref[begin:end, :].astype(F32)).T
        parts = []
        for head in range(2):
            chosen = (lane >= HD) == bool(head)
            own = jnp.where(chosen, queries, jnp.zeros_like(queries))
            own_grad = jnp.where(chosen, grads, jnp.zeros_like(grads))
            delta = jnp.sum(product_t[head * HD : (head + 1) * HD], axis=0, keepdims=True)
            lse = lse_ref[pl.ds(2 * pair + head, 1), begin:end]
            total = None
            for low, high in ((0, begin), (begin, end)):
                scores = dot_nt(keys[low:high], own)
                if high == end:
                    scores = jnp.where(causal, scores, NEG)
                probs = jnp.exp(scores - lse)
                prob_grad = dot_nt(values[low:high], own_grad)
                score_grad = (probs * (prob_grad - delta)).astype(BF16)
                dv_acc[low:high, :] += dot(probs.astype(BF16), own_grad)
                dk_acc[low:high, :] += dot(score_grad, own)
                part = dot(keys_t[:, low:high], score_grad)
                total = part if total is None else total + part
            parts.append(total)
        mine = jnp.where(sub < HD, parts[0], parts[1]).T * SCALE
        out_ref[0, begin:end, :] = mine.astype(BF16)
    out_ref[0, :first_row, :] = jnp.zeros((first_row, PAIR), BF16)
    out_ref[1] = dk_acc[...].astype(BF16)
    out_ref[2] = dv_acc[...].astype(BF16)


def attend_back(qkv, mixed_low, lse, mixed_grad):
    _, seq_len, width = qkv.shape
    rows = mixed_grad.shape[0]

    def columns(i):
        return pl.BlockSpec((None, seq_len, PAIR), lambda g, i=i: (i, 0, g))

    late = pl.BlockSpec((rows, PAIR), lambda g: (0, g))
    return pl.pallas_call(
        attend_back_kernel,
        grid=(width // PAIR,),
        in_specs=[
            *(columns(i) for i in range(3)),
            pl.BlockSpec((seq_len, PAIR), lambda g: (0, g)),
            pl.BlockSpec((HEAD_ROWS, seq_len), lambda g: (0, 0)),
            late,
        ],
        out_specs=pl.BlockSpec((3, seq_len, PAIR), lambda g: (0, 0, g)),
        out_shape=jax.ShapeDtypeStruct((3, seq_len, width), BF16),
        scratch_shapes=[pltpu.VMEM((seq_len, PAIR), F32), pltpu.VMEM((seq_len, PAIR), F32)],
        compiler_params=pltpu.CompilerParams(vmem_limit_bytes=VMEM_LIMIT),
        cost_estimate=cost(13),
        name="attention_backward",
    )(qkv, qkv, qkv, mixed_low, lse, mixed_grad)


def add_slots_kernel(
    info_ref, q_ref, qkv_ref, o_ref, lse_ref, rows_ref, row_lse_ref, mixed_ref, out_lse_ref
):
    seq_len, width = o_ref.shape
    rows = seq_len - QUESTION
    slot = info_ref[0]
    row_pos = QUESTION + lax.broadcasted_iota(jnp.int32, (HEAD_ROWS, rows), 1)
    late_q = q_ref[QUESTION:, :]
    lse = lse_ref[:, QUESTION:]
    scores = []
    values = []
    top = lse
    for j in range(THOUGHTS):
        local = slot + j - QUESTION
        key = by_head(pick(qkv_ref[1, QUESTION:PREFIX, :], local) * SCALE, HEAD_ROWS)
        values.append(pick(qkv_ref[2, QUESTION:PREFIX, :], local))
        score = jnp.where(row_pos >= slot + j, dot_nt(key.astype(BF16), late_q), NEG)
        scores.append(score)
        top = jnp.maximum(top, score)
    whole_sum = jnp.exp(lse - top)
    for score in scores:
        whole_sum = whole_sum + jnp.exp(score - top)
    new_lse = top + jnp.log(whole_sum)
    ones = by_head(jnp.ones((1, width), F32), HEAD_ROWS).astype(BF16)
    share = jnp.exp(lse - new_lse)
    high = share.astype(BF16)
    mixed = o_ref[QUESTION:, :].astype(F32) * (
        dot_tn(high, ones) + dot_tn((share - high.astype(F32)).astype(BF16), ones)
    )
    for score, value in zip(scores, values):
        mixed = mixed + dot_tn(jnp.exp(score - new_lse).astype(BF16), ones) * value
    mixed_ref[:QUESTION, :] = o_ref[:QUESTION, :]
    mixed_ref[PREFIX:, :] = mixed[PREFIX - QUESTION :].astype(BF16)
    out_lse_ref[:, :QUESTION] = lse_ref[:, :QUESTION]
    column = lax.broadcasted_iota(jnp.int32, (HEAD_ROWS, PREFIX - QUESTION), 1)
    middle = new_lse[:, : PREFIX - QUESTION]
    block = mixed[: PREFIX - QUESTION].astype(BF16)
    for j in range(THOUGHTS):
        local = slot + j - QUESTION
        block = put(block, local, rows_ref[1 + j : 2 + j, :])
        middle = jnp.where(column == local, row_lse_ref[:, 1 + j : 2 + j], middle)
    mixed_ref[QUESTION:PREFIX, :] = block
    out_lse_ref[:, QUESTION:PREFIX] = middle
    out_lse_ref[:, PREFIX:] = new_lse[:, PREFIX - QUESTION :]


def add_slots(info, qkv, mixed_low, lse, slot_rows, slot_lse):
    seq_len, width = mixed_low.shape
    return pl.pallas_call(
        add_slots_kernel,
        grid=(1,),
        in_specs=[
            pl.BlockSpec(memory_space=pltpu.SMEM),
            pl.BlockSpec((None, seq_len, width), lambda i: (0, 0, 0)),
            pl.BlockSpec((3, PREFIX, width), lambda i: (0, 0, 0)),
            whole(mixed_low),
            whole(lse),
            whole(slot_rows),
            whole(slot_lse),
        ],
        out_specs=[whole(mixed_low), whole(lse)],
        out_shape=[
            jax.ShapeDtypeStruct(mixed_low.shape, BF16),
            jax.ShapeDtypeStruct(lse.shape, F32),
        ],
        compiler_params=pltpu.CompilerParams(vmem_limit_bytes=VMEM_LIMIT),
        cost_estimate=cost(3),
        name="attention_add_slots",
    )(info, qkv, qkv, mixed_low, lse, slot_rows, slot_lse)


def row_norm(row, gain, bias):
    mean = jnp.mean(row, axis=-1, keepdims=True)
    centred = row - mean
    inverse = lax.rsqrt(jnp.mean(centred * centred, axis=-1, keepdims=True) + EPSILON)
    normed = centred * inverse
    return normed * gain + bias, normed, inverse


def row_norm_back(incoming, normed, inverse, gain):
    scaled = incoming * gain
    inner = (
        scaled
        - jnp.mean(scaled, axis=-1, keepdims=True)
        - normed * jnp.mean(scaled * normed, axis=-1, keepdims=True)
    )
    return inner * inverse


GELU_A = 0.7978845608028654
GELU_B = 0.044715


def gelu(pre):
    return 0.5 * pre * (1.0 + jnp.tanh(GELU_A * (pre + GELU_B * pre * pre * pre)))


def gelu_slope(pre):
    square = pre * pre
    curve = jnp.tanh(GELU_A * pre * (1.0 + GELU_B * square))
    return 0.5 * (1.0 + curve) + 0.5 * pre * (1.0 - curve * curve) * GELU_A * (
        1.0 + 3.0 * GELU_B * square
    )


def widen(row):
    return jnp.broadcast_to(row, (8, row.shape[1])).astype(BF16)


def pick(block, index):
    rows = lax.broadcasted_iota(jnp.int32, block.shape, 0)
    return jnp.sum(jnp.where(rows == index, block.astype(F32), 0.0), axis=0, keepdims=True)


def put(block, index, row):
    rows = lax.broadcasted_iota(jnp.int32, block.shape, 0)
    return jnp.where(rows == index, row.astype(block.dtype), block)


def by_head(row, heads):
    shape = (heads, row.shape[1])
    lane_head = lax.broadcasted_iota(jnp.int32, shape, 1) // HD
    return jnp.where(lane_head == lax.broadcasted_iota(jnp.int32, shape, 0), row, 0.0)


def heads_only(block):
    lane_head = lax.broadcasted_iota(jnp.int32, block.shape, 1) // HD
    own = lane_head == lax.broadcasted_iota(jnp.int32, block.shape, 0)
    return jnp.sum(jnp.where(own, block, 0.0), axis=0, keepdims=True)


def through_blocks(row, ref):
    wide = widen(row)
    return jnp.concatenate([dot(wide, ref[j])[0:1] for j in range(ref.shape[0])], axis=1)


def thoughts_kernel(
    info_ref,
    tok_ref,
    qkv_ref,
    wqk_ref,
    wvo_ref,
    wfc_ref,
    wproj_ref,
    vec_ref,
    fcb_ref,
    qkvb_ref,
    hid_ref,
    qkvm_ref,
    pre_ref,
    prob_ref,
    res_ref,
    rows_ref,
    row_lse_ref,
):
    width = tok_ref.shape[1]
    blocks = wfc_ref.shape[0]
    ln1_gain, ln1_bias, out_bias, ln2_gain, ln2_bias, proj_bias = (
        vec_ref[i : i + 1, :] for i in range(6)
    )
    slot = info_ref[0]
    count = info_ref[1]
    hid_ref[...] = tok_ref[...].astype(F32)
    qkvm_ref[...] = qkv_ref[:, QUESTION:PREFIX, :]
    rows_ref[...] = jnp.zeros_like(rows_ref)
    column = lax.broadcasted_iota(jnp.int32, row_lse_ref.shape, 1)
    row_lse_ref[...] = jnp.zeros_like(row_lse_ref)
    hidden_row = pick(hid_ref[...], slot - 1 - QUESTION)
    for step in range(THOUGHTS + 1):
        at = slot - 1 + step
        qkv_row = pick(qkvm_ref[0], at - QUESTION)
        query = by_head(qkv_row * SCALE, HEAD_ROWS).astype(BF16)
        scores = jnp.concatenate(
            [
                dot_nt(query, qkv_ref[1, :QUESTION, :]),
                dot_nt(query, qkvm_ref[1]),
            ],
            axis=1,
        )
        key_pos = lax.broadcasted_iota(jnp.int32, scores.shape, 1)
        scores = jnp.where(key_pos <= at, scores, NEG)
        peak = jnp.max(scores, axis=1, keepdims=True)
        expo = jnp.exp(scores - peak)
        total = jnp.sum(expo, axis=1, keepdims=True)
        probs = expo / total
        low = probs.astype(BF16)
        mixed = heads_only(
            dot(low[:, :QUESTION], qkv_ref[2, :QUESTION, :])
            + dot(low[:, QUESTION:], qkvm_ref[2])
        )
        rows_ref[step : step + 1, :] = mixed
        row_lse_ref[...] = jnp.where(column == step, peak + jnp.log(total), row_lse_ref[...])
        if step == THOUGHTS:
            break
        prob_ref[step * HEAD_ROWS : (step + 1) * HEAD_ROWS, :] = probs
        resid = hidden_row + dot(widen(mixed), wvo_ref[1])[0:1] + out_bias
        res_ref[step : step + 1, :] = resid
        second, _, _ = row_norm(resid, ln2_gain, ln2_bias)
        pre = through_blocks(second, wfc_ref) + fcb_ref[0:1, :]
        pre_ref[step : step + 1, :] = pre
        act = gelu(pre)
        fed = resid + proj_bias
        for j in range(blocks):
            fed = fed + dot(widen(act[:, j * width : (j + 1) * width]), wproj_ref[j])[0:1]
        first, _, _ = row_norm(fed, ln1_gain, ln1_bias)
        first = widen(first)
        hidden_row = fed
        spot = jnp.where(step < count, slot + step - QUESTION, -1)
        hid_ref[...] = put(hid_ref[...], spot, fed)
        for i in range(3):
            span = slice(i * width, (i + 1) * width)
            weight = wqk_ref[i] if i < 2 else wvo_ref[0]
            new_row = dot(first, weight)[0:1] + qkvb_ref[0:1, span]
            qkvm_ref[i] = put(qkvm_ref[i], spot, new_row)


def whole(array):
    zeros = (0,) * array.ndim
    return pl.BlockSpec(array.shape, lambda i, zeros=zeros: zeros)


def weight_specs(blocks, width):
    near = pl.BlockSpec((2, width, width), lambda i: (0, 0, 0))
    return [
        near,
        near,
        pl.BlockSpec((blocks, width, width), lambda i: (0, 0, 0)),
        pl.BlockSpec((blocks, width, width), lambda i: (1, 0, 0)),
    ]


def weight_operands(weights):
    query_key, value_out, far = weights
    return query_key, value_out, far, far


def thoughts_forward(info, tokens, qkv, weights, vec, fc_bias, qkv_bias):
    width = tokens.shape[1]
    middle = PREFIX - QUESTION
    out_shape = [
        jax.ShapeDtypeStruct((middle, width), F32),
        jax.ShapeDtypeStruct((3, middle, width), BF16),
        jax.ShapeDtypeStruct((8, fc_bias.shape[1]), F32),
        jax.ShapeDtypeStruct((THOUGHTS * HEAD_ROWS, PREFIX), F32),
        jax.ShapeDtypeStruct((8, width), F32),
        jax.ShapeDtypeStruct((8, width), F32),
        jax.ShapeDtypeStruct((HEAD_ROWS, LANES), F32),
    ]
    return pl.pallas_call(
        thoughts_kernel,
        grid=(1,),
        in_specs=[
            pl.BlockSpec(memory_space=pltpu.SMEM),
            pl.BlockSpec((middle, width), lambda i: (QUESTION // middle, 0)),
            pl.BlockSpec((3, PREFIX, width), lambda i: (0, 0, 0)),
            *weight_specs(fc_bias.shape[1] // width, width),
            whole(vec),
            whole(fc_bias),
            whole(qkv_bias),
        ],
        out_specs=[whole(s) for s in out_shape],
        out_shape=out_shape,
        compiler_params=pltpu.CompilerParams(vmem_limit_bytes=VMEM_LIMIT),
        cost_estimate=cost(7),
        name="thought_rows_forward",
    )(info, tokens, qkv, *weight_operands(weights), vec, fc_bias, qkv_bias)


def thoughts_back_kernel(
    info_ref,
    hid_ref,
    qkv_ref,
    late_q_ref,
    mixed_ref,
    lse_ref,
    pre_ref,
    prob_ref,
    res_ref,
    wqk_ref,
    wvo_ref,
    wfc_ref,
    wproj_ref,
    vec_ref,
    mg_in,
    rg_in,
    sum_ref,
    fac_ref,
    mg_out,
    rg_out,
    mg_ref,
    rg_win,
    sems,
):
    width = hid_ref.shape[1]
    blocks = wfc_ref.shape[0]
    units = blocks * width
    rows = mg_ref.shape[0]
    ln1_gain, ln1_bias, _, ln2_gain, ln2_bias, _ = (vec_ref[i : i + 1, :] for i in range(6))
    slot = info_ref[0]
    count = info_ref[1]
    base = pl.multiple_of(((slot - 1 - QUESTION) // 16) * 16, 16)

    def window(ref):
        return ref.at[pl.ds(base, WINDOW)]

    loads = [
        pltpu.make_async_copy(mg_in, mg_ref, sems.at[0]),
        pltpu.make_async_copy(window(rg_in), rg_win, sems.at[1]),
    ]
    for copy in loads:
        copy.start()
    for copy in loads:
        copy.wait()

    late_q = late_q_ref[QUESTION:, :]
    mixed_grad = mg_ref[...]
    product = mixed_grad.astype(F32) * mixed_ref[QUESTION:, :].astype(F32)
    high = product.astype(BF16)
    ones = by_head(jnp.ones((1, width), F32), HEAD_ROWS).astype(BF16)
    delta = dot_nt(ones, high) + dot_nt(ones, (product - high.astype(F32)).astype(BF16))
    row_pos = QUESTION + lax.broadcasted_iota(jnp.int32, (HEAD_ROWS, rows), 1)
    lse = lse_ref[:, QUESTION:]

    def at_slot(at):
        local = at - QUESTION
        key = by_head(pick(qkv_ref[1, QUESTION:PREFIX, :], local) * SCALE, HEAD_ROWS)
        value = by_head(pick(qkv_ref[2, QUESTION:PREFIX, :], local), HEAD_ROWS)
        scores = dot_nt(key.astype(BF16), late_q)
        probs = jnp.where(row_pos >= at, jnp.exp(jnp.minimum(scores - lse, 0.0)), 0.0)
        prob_grad = dot_nt(value.astype(BF16), mixed_grad)
        score_grad = (probs * (prob_grad - delta)).astype(BF16)
        return (
            heads_only(dot(score_grad, late_q)) * SCALE,
            heads_only(dot(probs.astype(BF16), mixed_grad)),
        )

    def through_first(at, query_grad, key_grad, value_grad):
        first_grad = (
            dot_nt(widen(query_grad), wqk_ref[0])
            + dot_nt(widen(key_grad), wqk_ref[1])
            + dot_nt(widen(value_grad), wvo_ref[0])
        )[0:1]
        _, normed, inverse = row_norm(hid_ref[pl.ds(at - QUESTION, 1), :], ln1_gain, ln1_bias)
        return row_norm_back(first_grad, normed, inverse, ln1_gain)

    sum_ref[...] = jnp.zeros_like(sum_ref)
    fac_ref[...] = jnp.zeros_like(fac_ref)
    carried = through_first(slot + 1, jnp.zeros((1, width), F32), *at_slot(slot + 1))
    for step in reversed(range(THOUGHTS)):
        at = slot - 1 + step
        upstream = jnp.where(step < count, carried, 0.0)
        low = widen(upstream)
        act_grad = jnp.concatenate([dot_nt(low, wproj_ref[j])[0:1] for j in range(blocks)], axis=1)
        pre = pre_ref[step : step + 1, :]
        pre_grad = (act_grad * gelu_slope(pre)).astype(BF16).astype(F32)
        second_grad = jnp.zeros((1, width), F32)
        for j in range(blocks):
            piece = pre_grad[:, j * width : (j + 1) * width]
            second_grad = second_grad + dot_nt(widen(piece), wfc_ref[j])[0:1]
        second, normed, inverse = row_norm(res_ref[step : step + 1, :], ln2_gain, ln2_bias)
        resid_grad = upstream + row_norm_back(second_grad, normed, inverse, ln2_gain)
        mixed_row = dot_nt(widen(resid_grad), wvo_ref[1])[0:1]
        local = at - QUESTION
        rg_win[...] = put(rg_win[...], local - base, resid_grad)
        mg_ref[: PREFIX - QUESTION, :] = put(mg_ref[: PREFIX - QUESTION, :], local, mixed_row)
        up_low = upstream.astype(BF16).astype(F32)
        sum_ref[0:1, :units] += pre_grad
        sum_ref[1:2, :width] += second_grad * normed
        sum_ref[2:3, :width] += second_grad
        sum_ref[3:4, :width] += up_low
        sum_ref[4:5, :width] += resid_grad.astype(BF16).astype(F32)
        fac_ref[step : step + 1, :units] = gelu(pre)
        fac_ref[step : step + 1, units : units + width] = up_low
        fac_ref[step : step + 1, units + width : units + 2 * width] = second
        fac_ref[step : step + 1, units + 2 * width :] = pre_grad
        if step:
            own_grad = by_head(mixed_row, HEAD_ROWS).astype(BF16)
            query = by_head(pick(qkv_ref[0, QUESTION:PREFIX, :], local) * SCALE, HEAD_ROWS)
            query = query.astype(BF16)
            probs = prob_ref[step * HEAD_ROWS : (step + 1) * HEAD_ROWS, :]
            prob_grad = dot_nt(own_grad, qkv_ref[2])
            own_delta = jnp.sum(prob_grad * probs, axis=1, keepdims=True)
            score_grad = (probs * (prob_grad - own_delta)).astype(BF16)
            query_grad = heads_only(dot(score_grad, qkv_ref[1])) * SCALE
            key_grad, value_grad = at_slot(at)
            own = lax.broadcasted_iota(jnp.int32, probs.shape, 1) == at
            score_own = jnp.sum(jnp.where(own, score_grad.astype(F32), 0.0), axis=1, keepdims=True)
            prob_own = jnp.sum(jnp.where(own, probs, 0.0), axis=1, keepdims=True)
            key_grad += jnp.sum(score_own * query.astype(F32), axis=0, keepdims=True)
            value_grad += jnp.sum(prob_own * own_grad.astype(F32), axis=0, keepdims=True)
            carried = resid_grad + through_first(at, query_grad, key_grad, value_grad)
    stores = [
        pltpu.make_async_copy(mg_ref, mg_out, sems.at[0]),
        pltpu.make_async_copy(rg_win, window(rg_out), sems.at[1]),
    ]
    for copy in stores:
        copy.start()
    for copy in stores:
        copy.wait()


SUM_ROWS = ("fc_bias", "ln2_gain", "ln2_bias", "proj_bias", "out_bias")


def thoughts_back(info, hidden_mid, qkv, mixed_low, lse, saved, weights, vec, mixed_grad, resid_grad):
    width = hidden_mid.shape[1]
    blocks = weights[2].shape[0] // 2
    units = blocks * width
    seq_len = qkv.shape[1]
    anywhere = pl.BlockSpec(memory_space=pl.ANY)
    out_shape = [
        jax.ShapeDtypeStruct((8, units), F32),
        jax.ShapeDtypeStruct((8, 2 * units + 2 * width), F32),
        jax.ShapeDtypeStruct(mixed_grad.shape, BF16),
        jax.ShapeDtypeStruct(resid_grad.shape, F32),
    ]
    return pl.pallas_call(
        thoughts_back_kernel,
        grid=(1,),
        in_specs=[
            pl.BlockSpec(memory_space=pltpu.SMEM),
            whole(hidden_mid),
            pl.BlockSpec((3, PREFIX, width), lambda i: (0, 0, 0)),
            pl.BlockSpec((None, seq_len, width), lambda i: (0, 0, 0)),
            whole(mixed_low),
            whole(lse),
            *(whole(x) for x in saved),
            *weight_specs(blocks, width),
            whole(vec),
            anywhere,
            anywhere,
        ],
        out_specs=[whole(out_shape[0]), whole(out_shape[1]), anywhere, anywhere],
        out_shape=out_shape,
        input_output_aliases={14: 2, 15: 3},
        scratch_shapes=[
            pltpu.VMEM(mixed_grad.shape, BF16),
            pltpu.VMEM((WINDOW, width), F32),
            pltpu.SemaphoreType.DMA((2,)),
        ],
        compiler_params=pltpu.CompilerParams(vmem_limit_bytes=VMEM_LIMIT),
        cost_estimate=cost(12),
        name="thought_rows_backward",
    )(
        info,
        hidden_mid,
        qkv,
        qkv,
        mixed_low,
        lse,
        *saved,
        *weight_operands(weights),
        vec,
        mixed_grad,
        resid_grad,
    )


def forward_kernel(
    hid_ref, mixed_ref, wvo_ref, wfc_ref, wproj_ref, vec_ref, fcb_ref, out_ref, second_ref,
    act_ref, slope_ref, normed_ref, inverse_ref,
):
    width = hid_ref.shape[1]
    out_bias, ln2_gain, ln2_bias, proj_bias = (vec_ref[i : i + 1, :] for i in range(2, 6))
    resid = hid_ref[...] + dot(mixed_ref[...], wvo_ref[0]) + out_bias
    second, normed, inverse = row_norm(resid, ln2_gain, ln2_bias)
    low = second.astype(BF16)
    second_ref[...] = low
    normed_ref[...] = normed
    inverse_ref[...] = jnp.broadcast_to(inverse, inverse_ref.shape)
    total = resid + proj_bias
    for j in range(wfc_ref.shape[0]):
        span = slice(j * width, (j + 1) * width)
        pre = dot(low, wfc_ref[j]) + fcb_ref[:, span]
        square = pre * pre
        curve = jnp.tanh(GELU_A * pre * (1.0 + GELU_B * square))
        half = 0.5 + 0.5 * curve
        act = (pre * half).astype(BF16)
        rise = 0.5 * GELU_A + (1.5 * GELU_A * GELU_B) * square
        slope_ref[:, span] = (half + pre * rise * (1.0 - curve * curve)).astype(BF16)
        act_ref[:, span] = act
        total = total + dot(act, wproj_ref[j])
    out_ref[...] = total.astype(BF16)


def feed_forward(hidden, mixed_low, weights, vec, fc_bias):
    _, value_out, far, _ = weight_operands(weights)
    seq_len, width = hidden.shape
    units = fc_bias.shape[1]

    def rows(columns):
        return pl.BlockSpec((BLOCK, columns), lambda i: (i, 0))

    return pl.pallas_call(
        forward_kernel,
        grid=(seq_len // BLOCK,),
        in_specs=[
            rows(width),
            rows(width),
            pl.BlockSpec((1, width, width), lambda i: (1, 0, 0)),
            *weight_specs(units // width, width)[2:],
            whole(vec),
            whole(fc_bias),
        ],
        out_specs=[rows(width), rows(width), rows(units), rows(units), rows(width), rows(LANES)],
        out_shape=[
            jax.ShapeDtypeStruct((seq_len, width), BF16),
            jax.ShapeDtypeStruct((seq_len, width), BF16),
            jax.ShapeDtypeStruct((seq_len, units), BF16),
            jax.ShapeDtypeStruct((seq_len, units), BF16),
            jax.ShapeDtypeStruct((seq_len, width), F32),
            jax.ShapeDtypeStruct((seq_len, LANES), F32),
        ],
        compiler_params=pltpu.CompilerParams(vmem_limit_bytes=VMEM_LIMIT),
        cost_estimate=cost(12),
        name="feed_forward",
    )(hidden, mixed_low, value_out, far, far, vec, fc_bias)


def back_kernel(
    up_ref, slope_ref, normed_ref, inverse_ref, wvo_ref, wfc_ref, wproj_ref, vec_ref, pg_ref,
    rg_ref, mg_ref, sum_ref,
):
    width = up_ref.shape[1]
    blocks = wfc_ref.shape[0]
    units = blocks * width
    ln2_gain = vec_ref[3:4, :]

    @pl.when(pl.program_id(0) == 0)
    def _():
        sum_ref[...] = jnp.zeros_like(sum_ref)

    up = up_ref[...]
    second_grad = jnp.zeros(up.shape, F32)
    for j in range(blocks):
        span = slice(j * width, (j + 1) * width)
        pre_grad = (dot_nt(up, wproj_ref[j]) * slope_ref[:, span].astype(F32)).astype(BF16)
        pg_ref[:, span] = pre_grad
        sum_ref[0:1, span] += jnp.sum(pre_grad.astype(F32), axis=0, keepdims=True)
        second_grad = second_grad + dot_nt(pre_grad, wfc_ref[j])
    normed = normed_ref[...]
    up32 = up.astype(F32)
    resid_grad = up32 + row_norm_back(second_grad, normed, inverse_ref[:, :1], ln2_gain)
    attn_grad = resid_grad.astype(BF16)
    rg_ref[...] = resid_grad
    mg_ref[...] = dot_nt(attn_grad, wvo_ref[0]).astype(BF16)
    sum_ref[1:2, :width] += jnp.sum(second_grad * normed, axis=0, keepdims=True)
    sum_ref[2:3, :width] += jnp.sum(second_grad, axis=0, keepdims=True)
    sum_ref[3:4, :width] += jnp.sum(up32, axis=0, keepdims=True)
    sum_ref[4:5, :width] += jnp.sum(attn_grad.astype(F32), axis=0, keepdims=True)


def feed_back(upstream_low, slope, normed, inverse, weights, vec):
    _, value_out, far, _ = weight_operands(weights)
    count, width = upstream_low.shape
    units = slope.shape[1]
    skip = QUESTION // BLOCK

    def rows(columns, begin=0):
        return pl.BlockSpec((BLOCK, columns), lambda i, begin=begin: (i + begin, 0))

    sums = jax.ShapeDtypeStruct((8, units), F32)
    return pl.pallas_call(
        back_kernel,
        grid=(count // BLOCK,),
        in_specs=[
            rows(width),
            rows(units, skip),
            rows(width, skip),
            rows(LANES, skip),
            pl.BlockSpec((1, width, width), lambda i: (1, 0, 0)),
            *weight_specs(units // width, width)[2:],
            whole(vec),
        ],
        out_specs=[rows(units), rows(width), rows(width), whole(sums)],
        out_shape=[
            jax.ShapeDtypeStruct((count, units), BF16),
            jax.ShapeDtypeStruct((count, width), F32),
            jax.ShapeDtypeStruct((count, width), BF16),
            sums,
        ],
        compiler_params=pltpu.CompilerParams(vmem_limit_bytes=VMEM_LIMIT),
        cost_estimate=cost(9),
        name="feed_backward",
    )(upstream_low, slope, normed, inverse, value_out, far, far, vec)


def first_back_kernel(
    info_ref, hid_ref, grad_ref, rg_ref, wqk_ref, wvo_ref, vec_ref, in_ref, first_ref, sum_ref
):
    rows, width = hid_ref.shape
    step = pl.program_id(0)
    slot = info_ref[0]
    count = info_ref[1]

    @pl.when(step == 0)
    def _():
        sum_ref[...] = jnp.zeros_like(sum_ref)

    gain = vec_ref[0:1, :]
    first, normed, inverse = row_norm(hid_ref[...], gain, vec_ref[1:2, :])
    first_ref[...] = first.astype(BF16)
    first_grad = jnp.zeros((rows, width), F32)
    for i in range(3):
        weight = wqk_ref[i] if i < 2 else wvo_ref[0]
        first_grad = first_grad + dot_nt(grad_ref[i], weight)
        if i != 1:
            at = 2 + i // 2
            columns = jnp.sum(grad_ref[i].astype(F32), axis=0, keepdims=True)
            sum_ref[at : at + 1, :] += columns
    sum_ref[0:1, :] += jnp.sum(first_grad * normed, axis=0, keepdims=True)
    sum_ref[1:2, :] += jnp.sum(first_grad, axis=0, keepdims=True)
    late = (step >= QUESTION // BLOCK).astype(F32)
    grad = row_norm_back(first_grad, normed, inverse, gain) + late * rg_ref[...]
    position = step * rows + lax.broadcasted_iota(jnp.int32, (rows, 1), 0)
    replaced = (position >= slot) & (position < slot + jnp.minimum(count, THOUGHTS))
    in_ref[...] = jnp.where(replaced, 0.0, grad)


def first_back(info, hidden, qkv_grad, resid_grad, weights, vec):
    seq_len, width = hidden.shape
    skip = QUESTION // BLOCK
    sums = jax.ShapeDtypeStruct((8, width), F32)
    rows = pl.BlockSpec((BLOCK, width), lambda i: (i, 0))
    return pl.pallas_call(
        first_back_kernel,
        grid=(seq_len // BLOCK,),
        in_specs=[
            pl.BlockSpec(memory_space=pltpu.SMEM),
            rows,
            pl.BlockSpec((3, BLOCK, width), lambda i: (0, i, 0)),
            pl.BlockSpec((BLOCK, width), lambda i: (jnp.maximum(i - skip, 0), 0)),
            pl.BlockSpec((2, width, width), lambda i: (0, 0, 0)),
            pl.BlockSpec((1, width, width), lambda i: (0, 0, 0)),
            whole(vec),
        ],
        out_specs=[rows, rows, whole(sums)],
        out_shape=[
            jax.ShapeDtypeStruct((seq_len, width), F32),
            jax.ShapeDtypeStruct((seq_len, width), BF16),
            sums,
        ],
        compiler_params=pltpu.CompilerParams(vmem_limit_bytes=VMEM_LIMIT),
        cost_estimate=cost(5),
        name="first_norm_backward",
    )(info, hidden, qkv_grad, resid_grad, weights[0], weights[1], vec)


def first_kernel(tok_ref, wqk_ref, wvo_ref, vec_ref, qkvb_ref, qkv_ref):
    width = tok_ref.shape[1]
    first, _, _ = row_norm(tok_ref[...].astype(F32), vec_ref[0:1, :], vec_ref[1:2, :])
    first = first.astype(BF16)
    for i in range(3):
        weight = wqk_ref[i] if i < 2 else wvo_ref[0]
        span = slice(i * width, (i + 1) * width)
        qkv_ref[i] = (dot(first, weight) + qkvb_ref[:, span]).astype(BF16)


def first_forward(tokens, query_key, value_out, vec, qkv_bias):
    seq_len, width = tokens.shape
    return pl.pallas_call(
        first_kernel,
        grid=(seq_len // BLOCK,),
        in_specs=[
            pl.BlockSpec((BLOCK, width), lambda i: (i, 0)),
            pl.BlockSpec((2, width, width), lambda i: (0, 0, 0)),
            pl.BlockSpec((1, width, width), lambda i: (0, 0, 0)),
            whole(vec),
            whole(qkv_bias),
        ],
        out_specs=pl.BlockSpec((3, BLOCK, width), lambda i: (0, i, 0)),
        out_shape=jax.ShapeDtypeStruct((3, seq_len, width), BF16),
        compiler_params=pltpu.CompilerParams(vmem_limit_bytes=VMEM_LIMIT),
        cost_estimate=cost(4),
        name="first_norm_forward",
    )(tokens, query_key, value_out, vec, qkv_bias)


def group_of(blocks, own):
    each = blocks * own
    group = LANES // math.gcd(LANES, each)
    size = group * each
    row = lax.broadcasted_iota(jnp.int32, (size, size), 0)
    column = lax.broadcasted_iota(jnp.int32, (size, size), 1)
    device, block, i = row // each, row % each // own, row % own
    return group, column == block * (group * own) + device * own + i


def split_units_kernel(blocks, fc_ref, out_ref):
    own = fc_ref.shape[0]
    width = out_ref.shape[2]
    group, swap = group_of(blocks, own)
    swap = swap.astype(BF16)
    size = group * blocks * own
    span = group * own
    for g in range(width // span):
        part = dot(fc_ref[:, g * size : (g + 1) * size], swap)
        for j in range(blocks):
            piece = part[:, j * span : (j + 1) * span]
            out_ref[j, :, g * span : (g + 1) * span] = piece.astype(BF16)


def split_units(fc_shard, blocks):
    own, units = fc_shard.shape
    return pl.pallas_call(
        functools.partial(split_units_kernel, blocks),
        out_shape=jax.ShapeDtypeStruct((blocks, own, units // blocks), BF16),
        compiler_params=pltpu.CompilerParams(vmem_limit_bytes=VMEM_LIMIT),
        name="units_split",
    )(fc_shard)


def row_terms_kernel(index_ref, fac_ref, proj_ref, fc_ref, proj_out, fc_out):
    blocks, own, width = proj_ref.shape
    units = blocks * width
    shape = (width, own)
    mine = lax.broadcasted_iota(jnp.int32, shape, 0) - index_ref[0] * own
    select = (mine == lax.broadcasted_iota(jnp.int32, shape, 1)).astype(BF16)
    upstream = fac_ref[:, units : units + width]
    terms = []
    second = dot(fac_ref[:, units + width : units + 2 * width], select).astype(BF16)
    for j in range(blocks):
        act = dot(fac_ref[:, j * width : (j + 1) * width], select).astype(BF16)
        proj_out[j] = proj_ref[j] + dot_tn(act, upstream)
        begin = units + 2 * width + j * width
        terms.append(fc_ref[j] + dot_tn(second, fac_ref[:, begin : begin + width]))
    group, swap = group_of(blocks, own)
    swap = swap.astype(BF16)
    size = group * blocks * own
    span = group * own
    for g in range(width // span):
        part = jnp.concatenate([t[:, g * span : (g + 1) * span] for t in terms], axis=1)
        total = jnp.zeros_like(part)
        for _ in range(3):
            piece = part.astype(BF16)
            part = part - piece.astype(F32)
            total = total + dot_nt(piece, swap)
        fc_out[:, g * size : (g + 1) * size] = total


def row_terms(index, factors, proj_sum, fc_sum):
    blocks, own, width = fc_sum.shape
    out_shape = [
        jax.ShapeDtypeStruct(proj_sum.shape, F32),
        jax.ShapeDtypeStruct((own, blocks * width), F32),
    ]
    return pl.pallas_call(
        row_terms_kernel,
        grid=(1,),
        in_specs=[
            pl.BlockSpec(memory_space=pltpu.SMEM),
            whole(factors),
            whole(proj_sum),
            whole(fc_sum),
        ],
        out_specs=[whole(x) for x in out_shape],
        out_shape=out_shape,
        compiler_params=pltpu.CompilerParams(vmem_limit_bytes=VMEM_LIMIT),
        cost_estimate=cost(2),
        name="thought_rows_terms",
    )(index, factors, proj_sum, fc_sum)


def spread_matrix(shard, count):
    shape = (shard, shard * count)
    column = lax.broadcasted_iota(jnp.int32, shape, 1) % shard
    return (column == lax.broadcasted_iota(jnp.int32, shape, 0)).astype(BF16)


def owner_mask(shard, count):
    shape = (count, shard * count)
    owner = lax.broadcasted_iota(jnp.int32, shape, 1) // shard
    return owner == lax.broadcasted_iota(jnp.int32, shape, 0)


VECTOR_ROWS = ("ln1_gain", "ln1_bias", "out_bias", "ln2_gain", "ln2_bias", "proj_bias")


def unpack_kernel(sizes, devices, packed_ref, vec_ref, fcb_ref, qkvb_ref):
    vec_ref[...] = jnp.zeros_like(vec_ref)
    width = vec_ref.shape[1]
    for at, (name, size) in enumerate(sizes):
        if name == "fc_bias":
            own = width // devices
            for j in range(size // own):
                spread = dot(packed_ref[at][:, j * own : (j + 1) * own], spread_matrix(own, devices))
                spread = jnp.where(owner_mask(own, devices), spread, 0.0)
                span = slice(j * width, (j + 1) * width)
                fcb_ref[:, span] = jnp.sum(spread, axis=0, keepdims=True)
            continue
        block = packed_ref[at][:, :size]
        spread = dot(block, spread_matrix(size, devices))
        full = jnp.sum(jnp.where(owner_mask(size, devices), spread, 0.0), axis=0, keepdims=True)
        if name == "qv_bias":
            qkvb_ref[:, :width] = full[:, :width]
            qkvb_ref[:, width : 2 * width] = jnp.zeros((1, width), F32)
            qkvb_ref[:, 2 * width :] = full[:, width:]
        else:
            at = VECTOR_ROWS.index(name)
            vec_ref[at : at + 1, :] = full


def unpack(packed, sizes):
    devices = packed.shape[1]
    size = dict(sizes)
    width = size["ln1_gain"] * devices
    return pl.pallas_call(
        functools.partial(unpack_kernel, sizes, devices),
        out_shape=[
            jax.ShapeDtypeStruct((8, width), F32),
            jax.ShapeDtypeStruct((1, size["fc_bias"] * devices), F32),
            jax.ShapeDtypeStruct((1, 3 * width), F32),
        ],
        compiler_params=pltpu.CompilerParams(vmem_limit_bytes=VMEM_LIMIT),
        name="vectors_unpack",
    )(packed)


def pack_kernel(sizes, devices, *refs):
    out_ref = refs[-1]
    out_ref[...] = jnp.zeros_like(out_ref)
    width = refs[0].shape[1]
    for at, ((name, size), ref) in enumerate(zip(sizes, refs)):
        if name == "fc_bias":
            own = width // devices
            for j in range(size // own):
                row = jnp.broadcast_to(ref[:, j * width : (j + 1) * width], (devices, width))
                row = jnp.where(owner_mask(own, devices), row, 0.0).astype(BF16)
                piece = dot_nt(row, spread_matrix(own, devices))
                out_ref[at, :, j * own : (j + 1) * own] = piece.astype(BF16)
            continue
        row = jnp.broadcast_to(ref[...], (devices, ref.shape[1]))
        own = jnp.where(owner_mask(size, devices), row, 0.0).astype(BF16)
        out_ref[at, :, :size] = dot_nt(own, spread_matrix(size, devices)).astype(BF16)


def pack(rows, sizes, devices):
    return pl.pallas_call(
        functools.partial(pack_kernel, sizes, devices),
        out_shape=jax.ShapeDtypeStruct((len(sizes), devices, LANES), BF16),
        compiler_params=pltpu.CompilerParams(vmem_limit_bytes=VMEM_LIMIT),
        name="vectors_pack",
    )(*[rows[name] for name, _ in sizes])


def join_kernel(*refs):
    out_ref = refs[-1]
    out_ref[...] = jnp.zeros_like(out_ref)
    for at, ref in enumerate(refs[:-1]):
        out_ref[at : at + 1, : ref.shape[0]] = ref[...].astype(F32).reshape(1, ref.shape[0])


def join(vectors):
    return pl.pallas_call(
        join_kernel,
        out_shape=jax.ShapeDtypeStruct((len(vectors), LANES), F32),
        name="vectors_join",
    )(*vectors)


def part_kernel(joined_ref, *refs):
    for at, ref in enumerate(refs):
        ref[...] = joined_ref[at, : ref.shape[0]]


def part(joined, sizes):
    return pl.pallas_call(
        part_kernel,
        out_shape=[jax.ShapeDtypeStruct((size,), F32) for _, size in sizes],
        name="vectors_part",
    )(joined)


def norm_parts(hidden):
    mean = jnp.mean(hidden, axis=-1, keepdims=True)
    centred = hidden - mean
    inverse = lax.rsqrt(jnp.mean(centred * centred, axis=-1, keepdims=True) + EPSILON)
    return centred * inverse, inverse


def step_on_sequence(
    near, far, vectors, tokens, cotangent, slots, count, answer_start, devices, sizes, comm
):
    query_key, value_out = near
    vec, fc_bias, qkv_bias = vectors
    seq_len, width = tokens.shape
    info = jnp.stack([slots[0], count])

    qkv_first = first_forward(tokens, query_key, value_out, vec, qkv_bias)
    mixed_hidden, lse_hidden = attend(info, qkv_first)
    late = QUESTION + lax.iota(jnp.int32, seq_len - QUESTION)
    upstream_low = jnp.where(
        (late >= answer_start)[:, None], cotangent[QUESTION:], jnp.zeros((), BF16)
    )
    tokens32 = tokens.astype(F32)
    weights = (query_key, value_out, after(far, mixed_hidden, upstream_low, tokens32))
    hidden_mid, qkv_mid, *saved, slot_rows, slot_lse = thoughts_forward(
        info, tokens, qkv_first, weights, vec, fc_bias, qkv_bias
    )
    qkv = lax.dynamic_update_slice(qkv_first, qkv_mid, (0, QUESTION, 0))
    hidden = lax.dynamic_update_slice(tokens32, hidden_mid, (QUESTION, 0))
    mixed_low, lse = add_slots(info, qkv, mixed_hidden, lse_hidden, slot_rows, slot_lse)
    output, second_low, act_low, slope, normed_two, inverse_two = feed_forward(
        hidden, mixed_low, weights, vec, fc_bias
    )

    proj_grad = comm.order(dot_tn(act_low[QUESTION:], upstream_low).astype(BF16))
    proj_half = comm.early(proj_grad)
    pre_grad, resid_grad, mixed_grad, sums = feed_back(
        after(upstream_low, proj_grad), slope, normed_two, inverse_two, weights, vec
    )
    fc_grad = dot_tn(second_low[QUESTION:], pre_grad).astype(BF16)
    units = fc_grad.shape[1]
    fc_going = comm.scatter(
        [fc_grad[:, j * width : (j + 1) * width] for j in range(units // width)], "zyxc"
    )
    sent = fc_going.go()
    row_sums, factors, mixed_grad, resid_grad = thoughts_back(
        info,
        hidden_mid,
        qkv,
        mixed_low,
        after(lse, sent),
        saved,
        weights,
        vec,
        mixed_grad,
        resid_grad,
    )
    join_after([fc_going], row_sums)
    out_grad = dot_tn(mixed_low[QUESTION:], resid_grad.astype(BF16)).astype(BF16)
    spread = comm.factors(factors[:THOUGHTS].astype(BF16))
    sent = go_after([fc_going, spread], out_grad)
    proj_half = after(proj_half, out_grad)
    proj_going = comm.early_end(proj_half)
    lse, back_grad = after((lse, mixed_grad), sent, proj_half)
    qkv_grad = attend_back(qkv, mixed_low, lse, back_grad)
    join_after([fc_going, spread], qkv_grad)
    sent = go_after([fc_going, spread], qkv_grad)
    input_grad, first_low, first_sums = first_back(
        info, hidden, after(qkv_grad, sent), resid_grad, weights, vec
    )
    sums = sums + row_sums
    small = {name: sums[i : i + 1, :width] for i, name in enumerate(SUM_ROWS)}
    small["fc_bias"] = sums[0:1]
    small["ln1_gain"] = first_sums[0:1]
    small["ln1_bias"] = first_sums[1:2]
    small["qv_bias"] = jnp.concatenate([first_sums[2:3], first_sums[3:4]], axis=1)
    packed = pack(small, sizes, devices)
    join_after([spread], packed)
    first_low = after(first_low, go_after([spread], packed))
    qkv_weight_grad = [dot_tn(first_low, qkv_grad[i]).astype(BF16) for i in range(3)]
    join_after([fc_going, spread], *qkv_weight_grad)
    return (
        output,
        input_grad,
        (proj_going, fc_going, spread, out_grad, qkv_weight_grad, packed),
    )


SMALL = ("ln1_gain", "ln1_bias", "qv_bias", "out_bias", "ln2_gain", "ln2_bias", "fc_bias", "proj_bias")


def on_device(
    links,
    tokens,
    ln1_gain,
    ln1_bias,
    qkv_weight,
    qv_bias,
    out_weight,
    out_bias,
    ln2_gain,
    ln2_bias,
    fc_weight,
    fc_bias,
    proj_weight,
    proj_bias,
    cotangent,
    thought_slots,
    thought_count,
    answer_start,
):
    devices = links.sizes["dp"] * links.sizes["fsdp"]
    small_shards = dict(
        ln1_gain=ln1_gain,
        ln1_bias=ln1_bias,
        qv_bias=qv_bias,
        out_bias=out_bias,
        ln2_gain=ln2_gain,
        ln2_bias=ln2_bias,
        fc_bias=fc_bias,
        proj_bias=proj_bias,
    )
    sizes = tuple((n, small_shards[n].shape[0]) for n in SMALL)
    own, width = out_weight.shape
    blocks = proj_weight.shape[0] // own
    both = ("dp", "fsdp")

    far_shard = jnp.concatenate(
        [split_units(fc_weight, blocks), proj_weight.reshape(blocks, own, width)], axis=0
    )
    far = lax.all_gather(far_shard, both, axis=1, tiled=True)

    packed = join([small_shards[n] for n in SMALL]).astype(BF16)
    small = links.gather(packed, "zxyc", axis=0).reshape(devices, len(sizes), LANES)
    parts = [qkv_weight[:, i * width : (i + 1) * width] for i in range(3)] + [out_weight]
    query_key = links.gather(jnp.stack(parts[:2]), "zxyc", axis=1).reshape(2, -1, width)
    value_out = links.gather(jnp.stack(parts[2:]), "zyxc", axis=1).reshape(2, -1, width)

    class Comm:
        @staticmethod
        def order(grad):
            value = grad.reshape(blocks, links.sizes["dp"], links.sizes["fsdp"], own, width)
            return value.transpose(2, 1, 0, 3, 4).reshape(-1, width)

        @staticmethod
        def early(value):
            return lax.psum_scatter(value, "fsdp", scatter_dimension=0, tiled=True)

        @staticmethod
        def early_end(value):
            value = lax.psum_scatter(value, "dp", scatter_dimension=0, tiled=True)
            return value.reshape(blocks, own, width)

        @staticmethod
        def scatter(grads, text):
            cut = [g.reshape(devices, g.shape[0] // devices, g.shape[1]) for g in grads]
            return links.scatter(jnp.stack(cut, axis=1), text)

        @staticmethod
        def factors(rows):
            return Gather(links, rows, "zxyc")

    output, input_grad, late = step_on_sequence(
        (query_key, value_out),
        far,
        unpack(small.transpose(1, 0, 2), sizes),
        tokens[0],
        cotangent[0],
        thought_slots[0],
        thought_count[0],
        answer_start[0],
        devices,
        sizes,
        Comm,
    )
    proj_going, fc_going, spread, out_grad, qkv_grads, packed = late
    cut = [g.reshape(devices, own, width) for g in qkv_grads[:2]]
    cut.append(jnp.pad(packed.transpose(1, 0, 2), ((0, 0), (0, 0), (0, width - LANES))))
    first = links.scatter(jnp.concatenate(cut, axis=1), "zxyc")
    rest = Comm.scatter([qkv_grads[2], out_grad], "zyxc")
    swaps = [first, rest, fc_going, spread]
    terms_left = True
    done = ()
    while any(swap.todo for swap in swaps) or terms_left:
        group = [swap for swap in swaps if swap.todo]
        sent = go_after(group, *done)
        if terms_left and fc_going not in group and spread not in group:
            terms_left = False
            index = lax.axis_index(both)[None].astype(jnp.int32)
            factors = after(spread.finish(), sent).reshape(devices * THOUGHTS, -1)
            proj_g, fc_g = row_terms(index, factors, proj_going.astype(F32), fc_going.buf)
            done = (proj_g, fc_g)
        join_after(group, *done)
        done = tuple(swap.buf for swap in group)
    first, small_sum = first.buf[: 2 * own].reshape(2, own, width), first.buf[2 * own :, :LANES]
    rest = rest.buf
    proj_g = proj_g.reshape(blocks * own, width)
    qkv_g = jnp.concatenate([first[0], first[1], rest[0]], axis=1)
    out_g = rest[1]
    owned = dict(zip(SMALL, part(small_sum, sizes)))
    return (
        output[None],
        input_grad[None],
        owned["ln1_gain"],
        owned["ln1_bias"],
        qkv_g,
        owned["qv_bias"],
        out_g,
        owned["out_bias"],
        owned["ln2_gain"],
        owned["ln2_bias"],
        fc_g,
        owned["fc_bias"],
        proj_g,
        owned["proj_bias"],
    )


def solution(mesh):
    links = Links({name: mesh.shape[name] for name in ("dp", "fsdp")})
    both = ("dp", "fsdp")
    cube, matrix, vector = P(both, None, None), P(both, None), P(both)
    weight_specs = (
        vector,
        vector,
        matrix,
        vector,
        matrix,
        vector,
        vector,
        vector,
        matrix,
        vector,
        matrix,
        vector,
    )

    def per_device(*args):
        return on_device(links, *args)

    return jax.shard_map(
        per_device,
        mesh=mesh,
        in_specs=(cube,) + weight_specs + (cube, matrix, vector, vector),
        out_specs=(cube, cube) + weight_specs,
        check_vma=False,
    )
```

time: 559 us -> 383 us (0.69); the launches traced: 548 us -> 377 us
  waiting for transfers between devices: 159 us -> 64.1 us
  Pallas kernels: 81.4 us -> 169 us
  matrix products: 77.8 us -> 23.6 us
  local copies, waits for them, and re-layouts: 77.6 us -> 28.3 us
  starting transfers between devices: 80.3 us -> 41.5 us
  other arithmetic: 64.7 us -> 34.2 us
  between operations: 6.36 us -> 16.3 us
    ppermute x80 -> x35, waiting for transfers between devices: 159 us -> 64 us  [swap(): lax.ppermute(value, axis, [(i, i ^ bit) for i in range(self.sizes[axis])])]
    pallas_call x2 -> x13, Pallas kernels: 49 us -> 132 us  [the longest x1 25.6 us: attend_back(): pl.pallas_call(attend_back_kernel, grid=(width // PAIR,), in_specs=[*(col...]
    dot_general x8 -> x0, matrix products: 50.6 us -> none  [the longest x4 28.7 us: dot(): lax.dot_general(a, b, (((1,), (0,)), ((), ())), preferred_element_type=F32)]
    ppermute x80 -> x35, starting transfers between devices: 80.3 us -> 41.4 us  [swap(): lax.ppermute(value, axis, [(i, i ^ bit) for i in range(self.sizes[axis])])]
    convert_element_type x14 -> x0, local copies, waits for them, and re-layouts: 18.9 us -> none  [step_on_sequence(): vecs = {name: value.astype(F32) for name, value in small.items()}]
    reduce_sum x10 -> x0, other arithmetic: 15.7 us -> none  [the longest x3 3.57 us: norm_parts(): jnp.mean(centred * centred, axis=-1, keepdims=True) + EPSILON]
    slice x19 -> x7, local copies, waits for them, and re-layouts: 16.2 us -> 4.6 us  [the longest x1 1.48 us: step_on_sequence(): first_sums[2:3]]
    unnamed x128 -> x48, local copies, waits for them, and re-layouts: 14.3 us -> 4.21 us
  transfers between devices with their start and end apart: 80 -> 38, of which waited for: 37 -> 19; matrix products, arithmetic and copies ran while one was open for 16% -> 17% of each run, Pallas kernels for 0% -> 32%
where the time goes in v2:
time: 383 us; the launch traced here: 377 us
  Pallas kernels  169 us (44%)
  waiting for transfers between devices  64.1 us (17%)
  starting transfers between devices  41.5 us (11%)
  other arithmetic  34.2 us (9%)
  local copies, waits for them, and re-layouts  28.3 us (7%)
  matrix products  23.6 us (6%)
  between operations  16.3 us (4%)
    ppermute x35, waiting for transfers between devices, swap(): lax.ppermute(value, axis, [(i, i ^ bit) for i in range(self.sizes[axis])])  64 us
    ppermute x35, starting transfers between devices, swap(): lax.ppermute(value, axis, [(i, i ^ bit) for i in range(self.sizes[axis])])  41.4 us
    pallas_call x1, Pallas kernels, attend_back(): pl.pallas_call(attend_back_kernel, grid=(width // PAIR,), in_specs=[*(col...  25.6 us
    pallas_call x1, Pallas kernels, attend(): pl.pallas_call(attend_kernel, grid=(pairs,), in_specs=[pl.BlockSpec(memor...  25.3 us
    pallas_call x1, Pallas kernels, thoughts_back(): pl.pallas_call(thoughts_back_kernel, grid=(1,), in_specs=[pl.BlockSpec(me...  23.6 us
    dot_general x6, matrix products, dot_tn(): lax.dot_general(a, b, (((0,), (0,)), ((), ())), preferred_element_type=F32)  23.6 us
    pallas_call x1, Pallas kernels, feed_forward(): pl.pallas_call(forward_kernel, grid=(seq_len // BLOCK,), in_specs=[rows(w...  23.5 us
    pallas_call x1, Pallas kernels, feed_back(): pl.pallas_call(back_kernel, grid=(count // BLOCK,), in_specs=[rows(width)...  17.5 us
  transfers between devices with their start and end apart: 38, of which 19 were waited for; matrix products, arithmetic and copies ran while one was open for 17% of the time, Pallas kernels for 32%

profile of v2, /device:TPU:0, one launch (start us, length us, event | category | flops | bytes accessed | tf_op | source)
XLA Modules:
  0.0 377.4 jit_solution(5753197300489428035)
XLA Ops:
  7.2 2.5 units_split.1
  13.1 4.0 %collective-permute-start.5 = (bf16[2,24,768]{2,1,0:T(8,128)(2,1)S(1)}, bf16[2,24,768]{2,1,0:T(8,128)(2,1)S(1)}, u32[]{:S(2)}, u32[]{:S(2)}) collective-permute-start(bf16[2,24,768]{2,1,0:T(8,128)(2,1)S(1)} %pad_maximum_fusion.20), channel_id=1, source_target_pairs={{0,4},{1,5},{2,6},{3,7},{4,0},{5,1},{6,2},{7,3},{8,12},{9,13},{10,... | collective-permute-start | bytes 221192 | tf_op jit(solution)/shard_map/ppermute | solution.py:71
  19.3 2.9 collective-permute-start.10
  30.8 6.4 %collective-permute-done.6 = bf16[2,2,24,768]{3,2,0,1:T(8,128)(2,1)S(1)} collective-permute-done((bf16[2,2,24,768]{3,2,0,1:T(8,128)(2,1)S(1)}, bf16[2,2,24,768]{3,2,0,1:T(8,128)(2,1)S(1)}, u32[]{:S(2)}, u32[]{:S(2)}) %collective-permute-start.6) | collective-permute-done | bytes 147488 | tf_op jit(solution)/shard_map/ppermute | solution.py:71
  43.1 7.7 %collective-permute-done.2 = bf16[2,2,2,24,768]{4,3,0,1,2:T(8,128)(2,1)S(1)} collective-permute-done((bf16[2,2,2,24,768]{4,3,0,1,2:T(8,128)(2,1)S(1)}, bf16[2,2,2,24,768]{4,3,0,1,2:T(8,128)(2,1)S(1)}, u32[]{:S(2)}, u32[]{:S(2)}) %collective-permute-start.2) | collective-permute-done | bytes 294944 | tf_op jit(solution)/shard_map/ppermute | solution.py:71
  51.5 3.4 collective-permute-done.7
  58.4 7.0 %collective-permute-done.3 = bf16[2,2,2,2,24,768]{5,4,0,2,3,1:T(8,128)(2,1)S(1)} collective-permute-done((bf16[2,2,2,2,24,768]{5,4,0,2,3,1:T(8,128)(2,1)S(1)}, bf16[2,2,2,2,24,768]{5,4,0,2,3,1:T(8,128)(2,1)S(1)}, u32[]{:S(2)}, u32[]{:S(2)}) %collective-permute-start.3) | collective-permute-done | bytes 589856 | tf_op jit(solution)/shard_map/ppermute | solution.py:71
  81.5 8.7 %first_norm_forward.1.q_ref.k_ref.v_ref.qkv_ref = bf16[3,1024,768]{2,1,0:T(8,128)(2,1)} custom-call(bf16[1024,768]{1,0:T(8,128)(2,1)} %bitcast.236, bf16[2,768,768]{2,1,0:T(8,128)(2,1)} %bitcast.226, bf16[2,768,768]{2,1,0:T(8,128)(2,1)} %bitcast.230, f32[8,768]{1,0:T(8,128)} %get-tuple-element.95.vec_ref, f32[1,2304]{1,0:T(1,128)} %get-tuple-element.96.qkvb_ref), custom_call_target="tpu_custom_call" | custom-call | flops 4600000000 | bytes 14400000 | tf_op jit(solution)/shard_map/first_norm_forward/pallas_call | solution.py:972
  90.3 25.3 %attention_forward.1 = (bf16[1024,768]{1,0:T(8,128)(2,1)}, f32[16,1024]{1,0:T(8,128)}) custom-call(s32[2]{0:T(128)} %pad_add_fusion.info_ref, bf16[3,1024,768]{2,1,0:T(8,128)(2,1)} %first_norm_forward.1.q_ref.k_ref.v_ref.qkv_ref, bf16[3,1024,768]{2,1,0:T(8,128)(2,1)} %first_norm_forward.1.q_ref.k_ref.v_ref.qkv_ref, ...), custom_call_target="tpu_custom_call" | custom-call | flops 13799999488 | bytes 43200000 | tf_op jit(solution)/shard_map/attention_forward/pallas_call | solution.py:216
  115.6 14.0 %thought_rows_forward.1 = (f32[128,768]{1,0:T(8,128)}, bf16[3,128,768]{2,1,0:T(8,128)(2,1)}, f32[8,3072]{1,0:T(8,128)}, f32[32,384]{1,0:T(8,128)}, f32[8,768]{1,...) custom-call(s32[2]{0:T(128)} %pad_add_fusion.info_ref, bf16[1024,768]{1,0:T(8,128)(2,1)} %bitcast.237, ...), custom_call_target="tpu_custom_call" | custom-call | flops 8049999872 | bytes 25200000 | tf_op jit(solution)/shard_map/thought_rows_forward/pallas_call | solution.py:560
  133.4 5.9 %attention_add_slots.1 = (bf16[1024,768]{1,0:T(8,128)(2,1)}, f32[16,1024]{1,0:T(8,128)}) custom-call(s32[2]{0:T(128)} %pad_add_fusion.info_ref, bf16[3,1024,768]{2,1,0:T(8,128)(2,1)} %constant_dynamic-update-slice_fusion.q_ref.qkv_ref.late_q_ref.k_ref.v_ref, bf16[3,1024,768]{2,1,0:T(8,128)(2,1)} %constant_dynamic-update-slice_fusion.q_ref.qkv_ref.late_q_ref.k_ref.v_ref, ...), custom_call_target="tpu_custom_call" | custom-call | flops 3449999872 | bytes 10800000 | tf_op jit(solution)/shard_map/attention_add_slots/pallas_call | solution.py:360
  139.2 23.5 %feed_forward.1 = (bf16[1024,768]{1,0:T(8,128)(2,1)}, bf16[1024,768]{1,0:T(8,128)(2,1)}, bf16[1024,3072]{1,0:T(8,128)(2,1)}, bf16[1024,3072]{1,0:T(8,128)(2,1)},...) custom-call(f32[1024,768]{1,0:T(8,128)} %constant_dynamic-update-slice_fusion.1.hid_ref, ...), custom_call_target="tpu_custom_call" | custom-call | flops 13799999488 | bytes 43200000 | tf_op jit(solution)/shard_map/feed_forward/pallas_call | solution.py:805
  162.7 6.7 %convolution_convert_fusion.1 = bf16[3072,768]{1,0:T(8,128)(2,1)S(1)} fusion(bf16[768,768]{1,0:T(8,128)(2,1)S(1)} %copy-done.10, bf16[1024,3072]{1,0:T(8,128)(2,1)} %get-tuple-element.109), kind=kOutput, calls=%fused_computation.1 | convolution fusion | flops 3626237952 | bytes 10616832 | tf_op jit(solution)/shard_map/dot_general | solution.py:46
  169.5 2.7 copy.43
  172.3 17.5 %feed_backward.1 = (bf16[768,3072]{1,0:T(8,128)(2,1)}, f32[768,768]{1,0:T(8,128)}, bf16[768,768]{1,0:T(8,128)(2,1)}, f32[8,3072]{1,0:T(8,128)}) custom-call(bf16[768,768]{1,0:T(8,128)(2,1)} %bitcast_select_fusion.up_ref, bf16[1024,3072]{1,0:T(8,128)(2,1)} %get-tuple-element.111.slope_ref, f32[1024,768]{1,0:T(8,128)} %get-tuple-element.112.normed_ref, ...), custom_call_target="tpu_custom_call" | custom-call | flops 10350000128 | bytes 32400000 | tf_op jit(solution)/shard_map/feed_backward/pallas_call | solution.py:874
  189.8 6.5 %convolution_convert_fusion = bf16[768,3072]{1,0:T(8,128)(2,1)S(1)} fusion(bf16[768,3072]{1,0:T(8,128)(2,1)} %get-tuple-element.114, bf16[1024,768]{1,0:T(8,128)(2,1)S(1)} %copy-done.19), kind=kOutput, calls=%fused_computation | convolution fusion | flops 3626237952 | bytes 10616832 | tf_op jit(solution)/shard_map/dot_general | solution.py:46
  199.9 23.6 %thought_rows_backward.1 = (f32[8,3072]{1,0:T(8,128)}, f32[8,7680]{1,0:T(8,128)}, bf16[768,768]{1,0:T(8,128)(2,1)}, f32[768,768]{1,0:T(8,128)}) custom-call(s32[2]{0:T(128)} %pad_add_fusion.info_ref, f32[128,768]{1,0:T(8,128)} %get-tuple-element.100.hid_ref, ...), custom_call_target="tpu_custom_call", output_to_operand_aliasing={{2}: (14, {}), {3}: (15, {})} | custom-call | flops 13799999488 | bytes 43200000 | tf_op jit(solution)/shard_map/thought_rows_backward/pallas_call | solution.py:728
  224.6 3.9 %convolution_convert_fusion.2 = bf16[768,768]{1,0:T(8,128)(2,1)} fusion(f32[768,768]{1,0:T(8,128)} %get-tuple-element.124.rg_ref, bf16[1024,768]{1,0:T(8,128)(2,1)S(1)} %copy-done.18), kind=kOutput, calls=%fused_computation.27 | convolution fusion | flops 907149312 | bytes 4718592 | tf_op jit(solution)/shard_map/dot_general | solution.py:46
  228.5 2.9 collective-permute-start.17
  232.6 2.3 fusion
  237.8 25.6 %attention_backward.1.grad_ref = bf16[3,1024,768]{2,1,0:T(8,128)(2,1)} custom-call(bf16[3,1024,768]{2,1,0:T(8,128)(2,1)} %constant_dynamic-update-slice_fusion.q_ref.qkv_ref.late_q_ref.k_ref.v_ref, bf16[3,1024,768]{2,1,0:T(8,128)(2,1)} %constant_dynamic-update-slice_fusion.q_ref.qkv_ref.late_q_ref.k_ref.v_ref, ...), custom_call_target="tpu_custom_call" | custom-call | flops 14949999616 | bytes 46800000 | tf_op jit(solution)/shard_map/attention_backward/pallas_call | solution.py:294
  267.5 10.6 %first_norm_backward.1 = (f32[1024,768]{1,0:T(8,128)}, bf16[1024,768]{1,0:T(8,128)(2,1)}, f32[8,768]{1,0:T(8,128)}) custom-call(s32[2]{0:T(128)} %pad_add_fusion.info_ref, f32[1024,768]{1,0:T(8,128)} %constant_dynamic-update-slice_fusion.1.hid_ref, bf16[3,1024,768]{2,1,0:T(8,128)(2,1)} %attention_backward.1.grad_ref, f32[768,768]{1,0:T(8,128)} %get-tuple-element.124.rg_ref, ...), custom_call_target="tpu_custom_call" | custom-call | flops 5750000128 | bytes 18000000 | tf_op jit(solution)/shard_map/first_norm_backward/pallas_call | solution.py:936
  283.2 3.5 fusion.9
  292.8 2.6 collective-permute-done.23
  298.6 4.8 %collective-permute-done.24 = bf16[2,2,2,2,7680]{4,3,1,2,0:T(2,128)(2,1)S(1)} collective-permute-done((bf16[2,2,2,2,7680]{4,3,1,2,0:T(2,128)(2,1)S(1)}, bf16[2,2,2,2,7680]{4,3,1,2,0:T(2,128)(2,1)S(1)}, u32[]{:S(2)}, u32[]{:S(2)}) %collective-permute-start.24) | collective-permute-done | bytes 245792 | tf_op jit(solution)/shard_map/ppermute | solution.py:71
  307.2 5.4 %collective-permute-done.22 = bf16[2,4,24,768]{3,2,1,0:T(8,128)(2,1)S(1)} collective-permute-done((bf16[2,4,24,768]{3,2,1,0:T(8,128)(2,1)S(1)}, bf16[2,4,24,768]{3,2,1,0:T(8,128)(2,1)S(1)}, u32[]{:S(2)}, u32[]{:S(2)}) %collective-permute-start.22) | collective-permute-done | bytes 294944 | tf_op jit(solution)/shard_map/ppermute | solution.py:71
  318.4 2.2 collective-permute-start.27
  331.3 7.2 %collective-permute-done.26 = bf16[2,2,2,2,24,768]{5,4,3,1,2,0:T(8,128)(2,1)} collective-permute-done((bf16[2,2,2,2,24,768]{5,4,3,1,2,0:T(8,128)(2,1)}, bf16[2,2,2,2,24,768]{5,4,3,1,2,0:T(8,128)(2,1)}, u32[]{:S(2)}, u32[]{:S(2)}) %collective-permute-start.26) | collective-permute-done | bytes 589856 | tf_op jit(solution)/shard_map/ppermute | solution.py:71
  343.2 5.8 %thought_rows_terms.1 = (f32[4,24,768]{2,1,0:T(8,128)}, f32[24,3072]{1,0:T(8,128)}) custom-call(s32[1]{0:T(128)} %bitcast.92.index_ref, bf16[64,7680]{1,0:T(8,128)(2,1)} %reshape.121.fac_ref, f32[4,24,768]{2,1,0:T(8,128)} %convert.30.proj_ref, f32[4,24,768]{2,1,0:T(8,128)} %convert_add_fusion.12.fc_ref), custom_call_target="tpu_custom_call" | custom-call | flops 2300000000 | bytes 7200000 | tf_op jit(solution)/shard_map/thought_rows_terms/pallas_call | solution.py:1058
  349.8 2.2 collective-permute-done.29
  354.3 3.7 collective-permute-done.32
  362.9 2.3 collective-permute-done.34
  (221 shorter events, 107.6 us)
Async XLA Ops:
  7.2 108.4 %all-gather.2.cloned.1.call-start = ((), (), s32[]{:S(2)}) async-start(), calls=%async_computation.2 | async-start | bytes 9732096 | tf_op jit(solution)/shard_map/all_gather | solution.py:1314
  11.5 226.3 %reduce-scatter.3.cloned.1.call-start = ((), (), s32[]{:S(2)}) async-start(), calls=%async_computation.3 | async-start | bytes 5308416 | tf_op jit(solution)/shard_map/reduce_scatter | solution.py:1330
  13.1 13.7 %collective-permute-start.5 = (bf16[2,24,768]{2,1,0:T(8,128)(2,1)S(1)}, bf16[2,24,768]{2,1,0:T(8,128)(2,1)S(1)}, u32[]{:S(2)}, u32[]{:S(2)}) collective-permute-start(bf16[2,24,768]{2,1,0:T(8,128)(2,1)S(1)} %pad_maximum_fusion.20), channel_id=1, source_target_pairs={{0,4},{1,5},{2,6},{3,7},{4,0},{5,1},{6,2},{7,3},{8,12},{9,13},{10,... | collective-permute-start | bytes 221192 | tf_op jit(solution)/shard_map/ppermute | solution.py:71
  17.2 11.3 %collective-permute-start = (bf16[2,24,768]{2,1,0:T(8,128)(2,1)S(1)}, bf16[2,24,768]{2,1,0:T(8,128)(2,1)S(1)}, u32[]{:S(2)}, u32[]{:S(2)}) collective-permute-start(bf16[2,24,768]{2,1,0:T(8,128)(2,1)S(1)} %pad_maximum_fusion.19), channel_id=1, source_target_pairs={{0,4},{1,5},{2,6},{3,7},{4,0},{5,1},{6,2},{7,3},{8,12},{9,13},{10,... | collective-permute-start | bytes 221192 | tf_op jit(solution)/shard_map/ppermute | solution.py:71
  19.3 9.8 %collective-permute-start.10 = (bf16[8,128]{1,0:T(8,128)(2,1)S(1)}, bf16[8,128]{1,0:T(8,128)(2,1)S(1)}, u32[]{:S(2)}, u32[]{:S(2)}) collective-permute-start(bf16[8,128]{1,0:T(8,128)(2,1)S(1)} %convert_element_type.232), channel_id=1, source_target_pairs={{0,4},{1,5},{2,6},{3,7},{4,0},{5,1},{6,2},{7,3},{8,12},{9,13},{10,... | collective-permute-start | bytes 6152 | tf_op jit(solution)/shard_map/ppermute | solution.py:71
  26.9 10.2 %collective-permute-start.6 = (bf16[2,2,24,768]{3,2,0,1:T(8,128)(2,1)S(1)}, bf16[2,2,24,768]{3,2,0,1:T(8,128)(2,1)S(1)}, u32[]{:S(2)}, u32[]{:S(2)}) collective-permute-start(bf16[2,2,24,768]{3,2,0,1:T(8,128)(2,1)S(1)} %pad_maximum_fusion.17), channel_id=1, source_target_pairs={{0,2},{1,3},{2,0},{3,1},{4,6},{5,7},{6,4},{7,5},{8,10},{9,11},{10,... | collective-permute-start | bytes 442376 | tf_op jit(solution)/shard_map/ppermute | solution.py:71
  28.6 10.6 %collective-permute-start.1 = (bf16[2,2,24,768]{3,2,0,1:T(8,128)(2,1)S(1)}, bf16[2,2,24,768]{3,2,0,1:T(8,128)(2,1)S(1)}, u32[]{:S(2)}, u32[]{:S(2)}) collective-permute-start(bf16[2,2,24,768]{3,2,0,1:T(8,128)(2,1)S(1)} %pad_maximum_fusion.16), channel_id=1, source_target_pairs={{0,2},{1,3},{2,0},{3,1},{4,6},{5,7},{6,4},{7,5},{8,10},{9,11},{10,... | collective-permute-start | bytes 442376 | tf_op jit(solution)/shard_map/ppermute | solution.py:71
  29.2 11.7 %collective-permute-start.11 = (bf16[2,8,128]{2,1,0:T(8,128)(2,1)S(1)}, bf16[2,8,128]{2,1,0:T(8,128)(2,1)S(1)}, u32[]{:S(2)}, u32[]{:S(2)}) collective-permute-start(bf16[2,8,128]{2,1,0:T(8,128)(2,1)S(1)} %pad_maximum_fusion.27), channel_id=1, source_target_pairs={{0,2},{1,3},{2,0},{3,1},{4,6},{5,7},{6,4},{7,5},{8,10},{9,11},{10,... | collective-permute-start | bytes 12296 | tf_op jit(solution)/shard_map/ppermute | solution.py:71
  39.3 11.5 %collective-permute-start.2 = (bf16[2,2,2,24,768]{4,3,0,1,2:T(8,128)(2,1)S(1)}, bf16[2,2,2,24,768]{4,3,0,1,2:T(8,128)(2,1)S(1)}, u32[]{:S(2)}, u32[]{:S(2)}) collective-permute-start(bf16[2,2,2,24,768]{4,3,0,1,2:T(8,128)(2,1)S(1)} %pad_maximum_fusion.11), channel_id=1, source_target_pairs={{0,8},{8,0},{16,24},{24,16},{1,9},{9,1},{17,25},{25,17},{2,10},{10... | collective-permute-start | bytes 884744 | tf_op jit(solution)/shard_map/ppermute | solution.py:71
  40.9 15.7 %collective-permute-start.12 = (bf16[2,2,8,128]{3,2,0,1:T(8,128)(2,1)S(1)}, bf16[2,2,8,128]{3,2,0,1:T(8,128)(2,1)S(1)}, u32[]{:S(2)}, u32[]{:S(2)}) collective-permute-start(bf16[2,2,8,128]{3,2,0,1:T(8,128)(2,1)S(1)} %pad_maximum_fusion.25), channel_id=1, source_target_pairs={{0,8},{8,0},{16,24},{24,16},{1,9},{9,1},{17,25},{25,17},{2,10},{10... | collective-permute-start | bytes 24584 | tf_op jit(solution)/shard_map/ppermute | solution.py:71
  41.5 13.3 %collective-permute-start.7 = (bf16[2,2,2,24,768]{4,3,0,1,2:T(8,128)(2,1)S(1)}, bf16[2,2,2,24,768]{4,3,0,1,2:T(8,128)(2,1)S(1)}, u32[]{:S(2)}, u32[]{:S(2)}) collective-permute-start(bf16[2,2,2,24,768]{4,3,0,1,2:T(8,128)(2,1)S(1)} %pad_maximum_fusion.12), channel_id=1, source_target_pairs={{0,16},{8,24},{16,0},{24,8},{1,17},{9,25},{17,1},{25,9},{2,18},{10... | collective-permute-start | bytes 884744 | tf_op jit(solution)/shard_map/ppermute | solution.py:71
  50.9 14.5 %collective-permute-start.3 = (bf16[2,2,2,2,24,768]{5,4,0,2,3,1:T(8,128)(2,1)S(1)}, bf16[2,2,2,2,24,768]{5,4,0,2,3,1:T(8,128)(2,1)S(1)}, u32[]{:S(2)}, u32[]{:S(2)}) collective-permute-start(bf16[2,2,2,2,24,768]{5,4,0,2,3,1:T(8,128)(2,1)S(1)} %pad_maximum_fusion.8), channel_id=1, source_target_pairs={{0,16},{8,24},{16,0},{24,8},{1,17},{9,25},{17,1},{25,9},{2,18},{10... | collective-permute-start | bytes 1769480 | tf_op jit(solution)/shard_map/ppermute | solution.py:71
  55.0 12.9 %collective-permute-start.8 = (bf16[2,2,2,2,24,768]{5,4,0,2,3,1:T(8,128)(2,1)S(1)}, bf16[2,2,2,2,24,768]{5,4,0,2,3,1:T(8,128)(2,1)S(1)}, u32[]{:S(2)}, u32[]{:S(2)}) collective-permute-start(bf16[2,2,2,2,24,768]{5,4,0,2,3,1:T(8,128)(2,1)S(1)} %pad_maximum_fusion.9), channel_id=1, source_target_pairs={{0,8},{8,0},{16,24},{24,16},{1,9},{9,1},{17,25},{25,17},{2,10},{10... | collective-permute-start | bytes 1769480 | tf_op jit(solution)/shard_map/ppermute | solution.py:71
  56.6 12.6 %collective-permute-start.13 = (bf16[2,2,2,8,128]{4,3,1,2,0:T(8,128)(2,1)S(1)}, bf16[2,2,2,8,128]{4,3,1,2,0:T(8,128)(2,1)S(1)}, u32[]{:S(2)}, u32[]{:S(2)}) collective-permute-start(bf16[2,2,2,8,128]{4,3,1,2,0:T(8,128)(2,1)S(1)} %pad_maximum_fusion.24), channel_id=1, source_target_pairs={{0,16},{8,24},{16,0},{24,8},{1,17},{9,25},{17,1},{25,9},{2,18},{10... | collective-permute-start | bytes 49160 | tf_op jit(solution)/shard_map/ppermute | solution.py:71
  66.6 9.5 %collective-permute-start.4 = (bf16[2,2,2,2,2,24,768]{6,5,0,3,4,1,2:T(8,128)(2,1)}, bf16[2,2,2,2,2,24,768]{6,5,0,3,4,1,2:T(8,128)(2,1)S(1)}, u32[]{:S(2)}, u32[]{:S(2)}) collective-permute-start(bf16[2,2,2,2,2,24,768]{6,5,0,3,4,1,2:T(8,128)(2,1)} %pad_maximum_fusion.5), channel_id=1, source_target_pairs={{0,1},{1,0},{2,3},{3,2},{4,5},{5,4},{6,7},{7,6},{8,9},{9,8},{10,11... | collective-permute-start | bytes 3538952 | tf_op jit(solution)/shard_map/ppermute | solution.py:71
  69.1 9.1 %collective-permute-start.9 = (bf16[2,2,2,2,2,24,768]{6,5,0,3,4,1,2:T(8,128)(2,1)}, bf16[2,2,2,2,2,24,768]{6,5,0,3,4,1,2:T(8,128)(2,1)}, u32[]{:S(2)}, u32[]{:S(2)}) collective-permute-start(bf16[2,2,2,2,2,24,768]{6,5,0,3,4,1,2:T(8,128)(2,1)} %pad_maximum_fusion.6), channel_id=1, source_target_pairs={{0,1},{1,0},{2,3},{3,2},{4,5},{5,4},{6,7},{7,6},{8,9},{9,8},{10,11... | collective-permute-start | bytes 3538952 | tf_op jit(solution)/shard_map/ppermute | solution.py:71
  172.3 140.4 %reduce-scatter.5.cloned.1.call-start = ((), (), s32[]{:S(2)}) async-start(), calls=%async_computation.4 | async-start | bytes 737280 | tf_op jit(solution)/shard_map/reduce_scatter | solution.py:1334
  199.5 33.1 %collective-permute-start.15 = (bf16[2,2,2,2,4,24,768]{6,5,4,2,3,0,1:T(8,128)(2,1)}, bf16[2,2,2,2,4,24,768]{6,5,4,2,3,0,1:T(8,128)(2,1)}, u32[]{:S(2)}, u32[]{:S(2)}) collective-permute-start(bf16[2,2,2,2,4,24,768]{6,5,4,2,3,0,1:T(8,128)(2,1)} %bitcast.222), channel_id=1, source_target_pairs={{0,1},{1,0},{2,3},{3,2},{4,5},{5,4},{6,7},{7,6},{8,9},{9,8},{10,11... | collective-permute-start | bytes 7077896 | tf_op jit(solution)/shard_map/ppermute | solution.py:71
  228.5 36.1 %collective-permute-start.17 = (bf16[2,7680]{1,0:T(2,128)(2,1)S(1)}, bf16[2,7680]{1,0:T(2,128)(2,1)S(1)}, u32[]{:S(2)}, u32[]{:S(2)}) collective-permute-start(bf16[2,7680]{1,0:T(2,128)(2,1)S(1)} %slice.177), channel_id=1, source_target_pairs={{0,4},{1,5},{2,6},{3,7},{4,0},{5,1},{6,2},{7,3},{8,12},{9,13},{10,... | collective-permute-start | bytes 92168 | tf_op jit(solution)/shard_map/ppermute | solution.py:71
  236.4 27.9 %collective-permute-start.16 = (bf16[2,2,2,4,24,768]{5,4,3,1,2,0:T(8,128)(2,1)S(1)}, bf16[2,2,2,4,24,768]{5,4,3,1,2,0:T(8,128)(2,1)S(1)}, u32[]{:S(2)}, u32[]{:S(2)}) collective-permute-start(bf16[2,2,2,4,24,768]{5,4,3,1,2,0:T(8,128)(2,1)S(1)} %dynamic-slice_bitcast_fusion.2), channel_id=1, source_target_pairs={{0,8},{8,0},{16,24},{24,16},{1,9},{9,1},{17,25},{25,17},{2,10},{10... | collective-permute-start | bytes 3538952 | tf_op jit(solution)/shard_map/ppermute | solution.py:71
  264.8 18.1 %collective-permute-start.18 = (bf16[2,2,7680]{2,1,0:T(2,128)(2,1)S(1)}, bf16[2,2,7680]{2,1,0:T(2,128)(2,1)S(1)}, u32[]{:S(2)}, u32[]{:S(2)}) collective-permute-start(bf16[2,2,7680]{2,1,0:T(2,128)(2,1)S(1)} %pad_maximum_fusion.22), channel_id=1, source_target_pairs={{0,2},{1,3},{2,0},{3,1},{4,6},{5,7},{6,4},{7,5},{8,10},{9,11},{10,... | collective-permute-start | bytes 184328 | tf_op jit(solution)/shard_map/ppermute | solution.py:71
  266.0 37.8 %collective-permute-start.21 = (bf16[2,2,4,24,768]{4,3,2,0,1:T(8,128)(2,1)S(1)}, bf16[2,2,4,24,768]{4,3,2,0,1:T(8,128)(2,1)}, u32[]{:S(2)}, u32[]{:S(2)}) collective-permute-start(bf16[2,2,4,24,768]{4,3,2,0,1:T(8,128)(2,1)S(1)} %dynamic-slice_bitcast_fusion.5), channel_id=1, source_target_pairs={{0,16},{8,24},{16,0},{24,8},{1,17},{9,25},{17,1},{25,9},{2,18},{10... | collective-permute-start | bytes 1769480 | tf_op jit(solution)/shard_map/ppermute | solution.py:71
  292.8 23.4 %collective-permute-start.19 = (bf16[2,2,2,2,56,768]{5,4,2,3,1,0:T(8,128)(2,1)}, bf16[2,2,2,2,56,768]{5,4,2,3,1,0:T(8,128)(2,1)}, u32[]{:S(2)}, u32[]{:S(2)}) collective-permute-start(bf16[2,2,2,2,56,768]{5,4,2,3,1,0:T(8,128)(2,1)} %dynamic-slice_bitcast_fusion), channel_id=1, source_target_pairs={{0,1},{1,0},{2,3},{3,2},{4,5},{5,4},{6,7},{7,6},{8,9},{9,8},{10,11... | collective-permute-start | bytes 4128776 | tf_op jit(solution)/shard_map/ppermute | solution.py:71
  296.0 7.4 %collective-permute-start.24 = (bf16[2,2,2,2,7680]{4,3,1,2,0:T(2,128)(2,1)S(1)}, bf16[2,2,2,2,7680]{4,3,1,2,0:T(2,128)(2,1)S(1)}, u32[]{:S(2)}, u32[]{:S(2)}) collective-permute-start(bf16[2,2,2,2,7680]{4,3,1,2,0:T(2,128)(2,1)S(1)} %pad_maximum_fusion.14), channel_id=1, source_target_pairs={{0,16},{8,24},{16,0},{24,8},{1,17},{9,25},{17,1},{25,9},{2,18},{10... | collective-permute-start | bytes 737288 | tf_op jit(solution)/shard_map/ppermute | solution.py:71
  298.6 15.7 %collective-permute-start.20 = (bf16[2,2,2,2,2,24,768]{6,5,4,2,3,0,1:T(8,128)(2,1)}, bf16[2,2,2,2,2,24,768]{6,5,4,2,3,0,1:T(8,128)(2,1)}, u32[]{:S(2)}, u32[]{:S(2)}) collective-permute-start(bf16[2,2,2,2,2,24,768]{6,5,4,2,3,0,1:T(8,128)(2,1)} %dynamic-slice_bitcast_fusion.1), channel_id=1, source_target_pairs={{0,1},{1,0},{2,3},{3,2},{4,5},{5,4},{6,7},{7,6},{8,9},{9,8},{10,11... | collective-permute-start | bytes 3538952 | tf_op jit(solution)/shard_map/ppermute | solution.py:71
  305.0 7.5 %collective-permute-start.22 = (bf16[2,4,24,768]{3,2,1,0:T(8,128)(2,1)S(1)}, bf16[2,4,24,768]{3,2,1,0:T(8,128)(2,1)S(1)}, u32[]{:S(2)}, u32[]{:S(2)}) collective-permute-start(bf16[2,4,24,768]{3,2,1,0:T(8,128)(2,1)S(1)} %dynamic-slice_bitcast_fusion.8), channel_id=1, source_target_pairs={{0,2},{1,3},{2,0},{3,1},{4,6},{5,7},{6,4},{7,5},{8,10},{9,11},{10,... | collective-permute-start | bytes 884744 | tf_op jit(solution)/shard_map/ppermute | solution.py:71
  318.4 7.7 %collective-permute-start.27 = (bf16[4,24,768]{2,1,0:T(8,128)(2,1)S(1)}, bf16[4,24,768]{2,1,0:T(8,128)(2,1)S(1)}, u32[]{:S(2)}, u32[]{:S(2)}) collective-permute-start(bf16[4,24,768]{2,1,0:T(8,128)(2,1)S(1)} %dynamic-slice_bitcast_fusion.11), channel_id=1, source_target_pairs={{0,4},{1,5},{2,6},{3,7},{4,0},{5,1},{6,2},{7,3},{8,12},{9,13},{10,... | collective-permute-start | bytes 442376 | tf_op jit(solution)/shard_map/ppermute | solution.py:71
  321.5 18.2 %collective-permute-start.25 = (bf16[2,2,2,56,768]{4,3,1,2,0:T(8,128)(2,1)}, bf16[2,2,2,56,768]{4,3,1,2,0:T(8,128)(2,1)}, u32[]{:S(2)}, u32[]{:S(2)}) collective-permute-start(bf16[2,2,2,56,768]{4,3,1,2,0:T(8,128)(2,1)} %dynamic-slice_bitcast_fusion.3), channel_id=1, source_target_pairs={{0,16},{8,24},{16,0},{24,8},{1,17},{9,25},{17,1},{25,9},{2,18},{10... | collective-permute-start | bytes 2064392 | tf_op jit(solution)/shard_map/ppermute | solution.py:71
  322.4 16.1 %collective-permute-start.26 = (bf16[2,2,2,2,24,768]{5,4,3,1,2,0:T(8,128)(2,1)}, bf16[2,2,2,2,24,768]{5,4,3,1,2,0:T(8,128)(2,1)}, u32[]{:S(2)}, u32[]{:S(2)}) collective-permute-start(bf16[2,2,2,2,24,768]{5,4,3,1,2,0:T(8,128)(2,1)} %dynamic-slice_bitcast_fusion.4), channel_id=1, source_target_pairs={{0,8},{8,0},{16,24},{24,16},{1,9},{9,1},{17,25},{25,17},{2,10},{10... | collective-permute-start | bytes 1769480 | tf_op jit(solution)/shard_map/ppermute | solution.py:71
  341.0 8.7 %collective-permute-start.30 = (bf16[2,2,2,24,768]{4,3,2,0,1:T(8,128)(2,1)S(1)}, bf16[2,2,2,24,768]{4,3,2,0,1:T(8,128)(2,1)S(1)}, u32[]{:S(2)}, u32[]{:S(2)}) collective-permute-start(bf16[2,2,2,24,768]{4,3,2,0,1:T(8,128)(2,1)S(1)} %dynamic-slice_bitcast_fusion.7), channel_id=1, source_target_pairs={{0,16},{8,24},{16,0},{24,8},{1,17},{9,25},{17,1},{25,9},{2,18},{10... | collective-permute-start | bytes 884744 | tf_op jit(solution)/shard_map/ppermute | solution.py:71
  342.8 9.2 %collective-permute-start.29 = (bf16[2,2,56,768]{3,2,0,1:T(8,128)(2,1)S(1)}, bf16[2,2,56,768]{3,2,0,1:T(8,128)(2,1)S(1)}, u32[]{:S(2)}, u32[]{:S(2)}) collective-permute-start(bf16[2,2,56,768]{3,2,0,1:T(8,128)(2,1)S(1)} %dynamic-slice_bitcast_fusion.6), channel_id=1, source_target_pairs={{0,8},{8,0},{16,24},{24,16},{1,9},{9,1},{17,25},{25,17},{2,10},{10... | collective-permute-start | bytes 1032200 | tf_op jit(solution)/shard_map/ppermute | solution.py:71
  360.7 7.1 %collective-permute-start.33 = (bf16[56,768]{1,0:T(8,128)(2,1)S(1)}, bf16[56,768]{1,0:T(8,128)(2,1)S(1)}, u32[]{:S(2)}, u32[]{:S(2)}) collective-permute-start(bf16[56,768]{1,0:T(8,128)(2,1)S(1)} %dynamic-slice_bitcast_fusion.12), channel_id=1, source_target_pairs={{0,4},{1,5},{2,6},{3,7},{4,0},{5,1},{6,2},{7,3},{8,12},{9,13},{10,... | collective-permute-start | bytes 258056 | tf_op jit(solution)/shard_map/ppermute | solution.py:71
  (29 other events, 229.3 us)
Sparse Core Ops, SparseCore 0:
  11.8 91.9 all-gather.1
  172.4 56.1 reduce-scatter.2
  267.6 27.0 reduce-scatter.4

commit v3 on v2

--- a/solution.py
+++ b/solution.py
@@ -3,6 +3,7 @@
 
 import jax
 import jax.numpy as jnp
+import numpy as np
 from jax import lax
 from jax.experimental import pallas as pl
 from jax.experimental.pallas import tpu as pltpu
@@ -77,6 +78,18 @@
     def gather(self, shard, text, axis=0):
         return Gather(self, shard, text, axis).finish()
 
+    def chips(self, text):
+        stages = list(reversed(self.order(text)))[1:]
+        rest = [c for c in self.canon if c in stages]
+        order = []
+        for spot in range(1 << len(stages)):
+            chip = 0
+            for at, stage in enumerate(stages):
+                if spot & (1 << (len(stages) - 1 - at)):
+                    chip |= 1 << (len(rest) - 1 - rest.index(stage))
+            order.append(chip)
+        return order
+
     def scatter(self, value, text):
         return Scatter(self, value, text)
 
@@ -108,6 +121,13 @@
             self.got = None
         return self.buf
 
+    def last(self):
+        while self.todo:
+            self.go()
+        shape = self.shape
+        shape = shape[: self.axis] + (-1,) + shape[self.axis :]
+        return [self.buf.reshape(shape), self.got.reshape(shape)]
+
     def finish(self):
         while self.todo:
             self.go()
@@ -121,12 +141,23 @@
         self.links = links
         self.left = list(links.canon)
         self.todo = list(reversed(links.order(text)))
-        self.buf = value.reshape((2,) * len(self.left) + value.shape[1:])
         self.got = None
+        self.split = False
+        if isinstance(value, tuple):
+            self.split = True
+            self.left = self.todo[1:]
+            shape = (2,) * len(self.left) + value[0].shape[1:]
+            self.keep, self.buf = (v.reshape(shape) for v in value)
+        else:
+            self.buf = value.reshape((2,) * len(self.left) + value.shape[1:])
 
     def go(self):
         self.add()
         stage = self.todo.pop(0)
+        if self.split:
+            self.split = False
+            self.got = self.links.swap(self.buf, stage)
+            return self.buf
         place = self.left.index(stage)
         self.left.remove(stage)
         high = self.links.mine(stage).astype(jnp.int32)
@@ -229,7 +260,7 @@
             jax.ShapeDtypeStruct((HEAD_ROWS, seq_len), F32),
         ],
         compiler_params=pltpu.CompilerParams(vmem_limit_bytes=VMEM_LIMIT),
-        cost_estimate=cost(12),
+        cost_estimate=cost(2.0),
         name="attention_forward",
     )(info, qkv, qkv, qkv)
 
@@ -304,27 +335,197 @@
         out_shape=jax.ShapeDtypeStruct((3, seq_len, width), BF16),
         scratch_shapes=[pltpu.VMEM((seq_len, PAIR), F32), pltpu.VMEM((seq_len, PAIR), F32)],
         compiler_params=pltpu.CompilerParams(vmem_limit_bytes=VMEM_LIMIT),
-        cost_estimate=cost(13),
+        cost_estimate=cost(2.17),
         name="attention_backward",
     )(qkv, qkv, qkv, mixed_low, lse, mixed_grad)
 
 
-def add_slots_kernel(
-    info_ref, q_ref, qkv_ref, o_ref, lse_ref, rows_ref, row_lse_ref, mixed_ref, out_lse_ref
+def row_norm(row, gain, bias):
+    mean = jnp.mean(row, axis=-1, keepdims=True)
+    centred = row - mean
+    inverse = lax.rsqrt(jnp.mean(centred * centred, axis=-1, keepdims=True) + EPSILON)
+    normed = centred * inverse
+    return normed * gain + bias, normed, inverse
+
+
+def row_norm_back(incoming, normed, inverse, gain):
+    scaled = incoming * gain
+    inner = (
+        scaled
+        - jnp.mean(scaled, axis=-1, keepdims=True)
+        - normed * jnp.mean(scaled * normed, axis=-1, keepdims=True)
+    )
+    return inner * inverse
+
+
+GELU_A = 0.7978845608028654
+GELU_B = 0.044715
+
+
+def gelu(pre):
+    return 0.5 * pre * (1.0 + jnp.tanh(GELU_A * (pre + GELU_B * pre * pre * pre)))
+
+
+def gelu_slope(pre):
+    square = pre * pre
+    curve = jnp.tanh(GELU_A * pre * (1.0 + GELU_B * square))
+    return 0.5 * (1.0 + curve) + 0.5 * pre * (1.0 - curve * curve) * GELU_A * (
+        1.0 + 3.0 * GELU_B * square
+    )
+
+
+def widen(row):
+    return jnp.broadcast_to(row, (8, row.shape[1])).astype(BF16)
+
+
+def pick(block, index):
+    rows = lax.broadcasted_iota(jnp.int32, block.shape, 0)
+    return jnp.sum(jnp.where(rows == index, block.astype(F32), 0.0), axis=0, keepdims=True)
+
+
+def put(block, index, row):
+    rows = lax.broadcasted_iota(jnp.int32, block.shape, 0)
+    return jnp.where(rows == index, row.astype(block.dtype), block)
+
+
+def by_head(row, heads):
+    shape = (heads, row.shape[1])
+    lane_head = lax.broadcasted_iota(jnp.int32, shape, 1) // HD
+    return jnp.where(lane_head == lax.broadcasted_iota(jnp.int32, shape, 0), row, 0.0)
+
+
+def heads_only(block):
+    lane_head = lax.broadcasted_iota(jnp.int32, block.shape, 1) // HD
+    own = lane_head == lax.broadcasted_iota(jnp.int32, block.shape, 0)
+    return jnp.sum(jnp.where(own, block, 0.0), axis=0, keepdims=True)
+
+
+def thoughts_kernel(
+    info_ref,
+    tok_ref,
+    lse_in_ref,
+    vec_ref,
+    fcb_ref,
+    qkvb_ref,
+    near_in,
+    far_in,
+    qkv_in,
+    mixed_in,
+    hid_in,
+    lse_ref,
+    pre_ref,
+    prob_ref,
+    res_ref,
+    qkv_out,
+    mixed_out,
+    hid_out,
+    kv_ref,
+    late_q_ref,
+    mixed_ref,
+    hid_ref,
+    near_ref,
+    far_ref,
+    sems,
 ):
-    seq_len, width = o_ref.shape
-    rows = seq_len - QUESTION
+    width = tok_ref.shape[1]
+    blocks = (far_ref.shape[0] - 1) // 2
+    rows = late_q_ref.shape[0]
+    ln1_gain, ln1_bias, out_bias, ln2_gain, ln2_bias, proj_bias = (
+        vec_ref[i : i + 1, :] for i in range(6)
+    )
     slot = info_ref[0]
+    count = info_ref[1]
+
+    loads = [
+        (qkv_in.at[:, pl.ds(0, PREFIX)], kv_ref),
+        (far_in.at[pl.ds(2 * blocks, 1)], far_ref.at[pl.ds(2 * blocks, 1)]),
+        (far_in.at[pl.ds(0, blocks)], far_ref.at[pl.ds(0, blocks)]),
+        (far_in.at[pl.ds(blocks, blocks)], far_ref.at[pl.ds(blocks, blocks)]),
+        (near_in, near_ref),
+        (qkv_in.at[0, pl.ds(QUESTION, rows)], late_q_ref),
+        (mixed_in.at[pl.ds(QUESTION, rows)], mixed_ref),
+    ]
+    loads = [pltpu.make_async_copy(a, b, sems.at[i]) for i, (a, b) in enumerate(loads)]
+    for copy in loads:
+        copy.start()
+    hid_ref[...] = tok_ref[...].astype(F32)
+    hidden_row = pick(hid_ref[...], slot - 1 - QUESTION)
+    loads[0].wait()
+    slot_rows = []
+    slot_lse = []
+    for step in range(THOUGHTS + 1):
+        at = slot - 1 + step
+        qkv_row = pick(kv_ref[0, QUESTION:, :], at - QUESTION)
+        query = by_head(qkv_row * SCALE, HEAD_ROWS).astype(BF16)
+        scores = dot_nt(query, kv_ref[1])
+        key_pos = lax.broadcasted_iota(jnp.int32, scores.shape, 1)
+        scores = jnp.where(key_pos <= at, scores, NEG)
+        peak = jnp.max(scores, axis=1, keepdims=True)
+        expo = jnp.exp(scores - peak)
+        total = jnp.sum(expo, axis=1, keepdims=True)
+        probs = expo / total
+        mixed = heads_only(dot(probs.astype(BF16), kv_ref[2]))
+        if step:
+            slot_rows.append(mixed)
+            slot_lse.append(peak + jnp.log(total))
+        if step == THOUGHTS:
+            break
+        prob_ref[step * HEAD_ROWS : (step + 1) * HEAD_ROWS, :] = probs
+        if not step:
+            loads[1].wait()
+        resid = hidden_row + dot(widen(mixed), far_ref[2 * blocks])[0:1] + out_bias
+        res_ref[step : step + 1, :] = resid
+        second, _, _ = row_norm(resid, ln2_gain, ln2_bias)
+        second = widen(second)
+        if not step:
+            loads[2].wait()
+        acts = []
+        for j in range(blocks):
+            span = slice(j * width, (j + 1) * width)
+            pre = dot(second, far_ref[j])[0:1] + fcb_ref[0:1, span]
+            pre_ref[step : step + 1, span] = pre
+            acts.append(widen(gelu(pre)))
+        if not step:
+            loads[3].wait()
+        fed = resid + proj_bias
+        for j in range(blocks):
+            fed = fed + dot(acts[j], far_ref[blocks + j])[0:1]
+        first, _, _ = row_norm(fed, ln1_gain, ln1_bias)
+        first = widen(first)
+        hidden_row = fed
+        spot = jnp.where(step < count, slot + step - QUESTION, -1)
+        hid_ref[...] = put(hid_ref[...], spot, fed)
+        if not step:
+            loads[4].wait()
+        for i in range(3):
+            span = slice(i * width, (i + 1) * width)
+            new_row = dot(first, near_ref[i])[0:1] + qkvb_ref[0:1, span]
+            kv_ref[i, QUESTION:, :] = put(kv_ref[i, QUESTION:, :], spot, new_row)
+    loads[5].wait()
+    loads[6].wait()
+    stores = [
+        pltpu.make_async_copy(
+            kv_ref.at[:, pl.ds(QUESTION, PREFIX - QUESTION)],
+            qkv_out.at[:, pl.ds(QUESTION, PREFIX - QUESTION)],
+            sems.at[0],
+        ),
+        pltpu.make_async_copy(
+            hid_ref, hid_out.at[pl.ds(QUESTION, PREFIX - QUESTION)], sems.at[1]
+        ),
+    ]
+    for copy in stores:
+        copy.start()
+
     row_pos = QUESTION + lax.broadcasted_iota(jnp.int32, (HEAD_ROWS, rows), 1)
-    late_q = q_ref[QUESTION:, :]
-    lse = lse_ref[:, QUESTION:]
+    late_q = late_q_ref[...]
+    lse = lse_in_ref[:, QUESTION:]
     scores = []
     values = []
     top = lse
     for j in range(THOUGHTS):
         local = slot + j - QUESTION
-        key = by_head(pick(qkv_ref[1, QUESTION:PREFIX, :], local) * SCALE, HEAD_ROWS)
-        values.append(pick(qkv_ref[2, QUESTION:PREFIX, :], local))
+        key = by_head(pick(kv_ref[1, QUESTION:, :], local) * SCALE, HEAD_ROWS)
+        values.append(pick(kv_ref[2, QUESTION:, :], local))
         score = jnp.where(row_pos >= slot + j, dot_nt(key.astype(BF16), late_q), NEG)
         scores.append(score)
         top = jnp.maximum(top, score)
@@ -335,194 +536,33 @@
     ones = by_head(jnp.ones((1, width), F32), HEAD_ROWS).astype(BF16)
     share = jnp.exp(lse - new_lse)
     high = share.astype(BF16)
-    mixed = o_ref[QUESTION:, :].astype(F32) * (
-        dot_tn(high, ones) + dot_tn((share - high.astype(F32)).astype(BF16), ones)
-    )
-    for score, value in zip(scores, values):
-        mixed = mixed + dot_tn(jnp.exp(score - new_lse).astype(BF16), ones) * value
-    mixed_ref[:QUESTION, :] = o_ref[:QUESTION, :]
-    mixed_ref[PREFIX:, :] = mixed[PREFIX - QUESTION :].astype(BF16)
-    out_lse_ref[:, :QUESTION] = lse_ref[:, :QUESTION]
-    column = lax.broadcasted_iota(jnp.int32, (HEAD_ROWS, PREFIX - QUESTION), 1)
-    middle = new_lse[:, : PREFIX - QUESTION]
-    block = mixed[: PREFIX - QUESTION].astype(BF16)
+    low = (share - high.astype(F32)).astype(BF16)
+    weights = [jnp.exp(score - new_lse).astype(BF16) for score in scores]
+    step_rows = PREFIX - QUESTION
+    for begin in range(0, rows, step_rows):
+        span = slice(begin, begin + step_rows)
+        part = mixed_ref[span, :].astype(F32) * (
+            dot_tn(high[:, span], ones) + dot_tn(low[:, span], ones)
+        )
+        for weight, value in zip(weights, values):
+            part = part + dot_tn(weight[:, span], ones) * value
+        if not begin:
+            for j in range(THOUGHTS):
+                part = put(part, slot + j - QUESTION, slot_rows[j])
+        mixed_ref[span, :] = part.astype(BF16)
+    stores.append(
+        pltpu.make_async_copy(mixed_ref, mixed_out.at[pl.ds(QUESTION, rows)], sems.at[2])
+    )
+    stores[-1].start()
+    lse_ref[:, :QUESTION] = lse_in_ref[:, :QUESTION]
+    column = lax.broadcasted_iota(jnp.int32, (HEAD_ROWS, step_rows), 1)
+    middle = new_lse[:, :step_rows]
     for j in range(THOUGHTS):
-        local = slot + j - QUESTION
-        block = put(block, local, rows_ref[1 + j : 2 + j, :])
-        middle = jnp.where(column == local, row_lse_ref[:, 1 + j : 2 + j], middle)
-    mixed_ref[QUESTION:PREFIX, :] = block
-    out_lse_ref[:, QUESTION:PREFIX] = middle
-    out_lse_ref[:, PREFIX:] = new_lse[:, PREFIX - QUESTION :]
-
-
-def add_slots(info, qkv, mixed_low, lse, slot_rows, slot_lse):
-    seq_len, width = mixed_low.shape
-    return pl.pallas_call(
-        add_slots_kernel,
-        grid=(1,),
-        in_specs=[
-            pl.BlockSpec(memory_space=pltpu.SMEM),
-            pl.BlockSpec((None, seq_len, width), lambda i: (0, 0, 0)),
-            pl.BlockSpec((3, PREFIX, width), lambda i: (0, 0, 0)),
-            whole(mixed_low),
-            whole(lse),
-            whole(slot_rows),
-            whole(slot_lse),
-        ],
-        out_specs=[whole(mixed_low), whole(lse)],
-        out_shape=[
-            jax.ShapeDtypeStruct(mixed_low.shape, BF16),
-            jax.ShapeDtypeStruct(lse.shape, F32),
-        ],
-        compiler_params=pltpu.CompilerParams(vmem_limit_bytes=VMEM_LIMIT),
-        cost_estimate=cost(3),
-        name="attention_add_slots",
-    )(info, qkv, qkv, mixed_low, lse, slot_rows, slot_lse)
-
-
-def row_norm(row, gain, bias):
-    mean = jnp.mean(row, axis=-1, keepdims=True)
-    centred = row - mean
-    inverse = lax.rsqrt(jnp.mean(centred * centred, axis=-1, keepdims=True) + EPSILON)
-    normed = centred * inverse
-    return normed * gain + bias, normed, inverse
-
-
-def row_norm_back(incoming, normed, inverse, gain):
-    scaled = incoming * gain
-    inner = (
-        scaled
-        - jnp.mean(scaled, axis=-1, keepdims=True)
-        - normed * jnp.mean(scaled * normed, axis=-1, keepdims=True)
-    )
-    return inner * inverse
-
-
-GELU_A = 0.7978845608028654
-GELU_B = 0.044715
-
-
-def gelu(pre):
-    return 0.5 * pre * (1.0 + jnp.tanh(GELU_A * (pre + GELU_B * pre * pre * pre)))
-
-
-def gelu_slope(pre):
-    square = pre * pre
-    curve = jnp.tanh(GELU_A * pre * (1.0 + GELU_B * square))
-    return 0.5 * (1.0 + curve) + 0.5 * pre * (1.0 - curve * curve) * GELU_A * (
-        1.0 + 3.0 * GELU_B * square
-    )
-
-
-def widen(row):
-    return jnp.broadcast_to(row, (8, row.shape[1])).astype(BF16)
-
-
-def pick(block, index):
-    rows = lax.broadcasted_iota(jnp.int32, block.shape, 0)
-    return jnp.sum(jnp.where(rows == index, block.astype(F32), 0.0), axis=0, keepdims=True)
-
-
-def put(block, index, row):
-    rows = lax.broadcasted_iota(jnp.int32, block.shape, 0)
-    return jnp.where(rows == index, row.astype(block.dtype), block)
-
-
-def by_head(row, heads):
-    shape = (heads, row.shape[1])
-    lane_head = lax.broadcasted_iota(jnp.int32, shape, 1) // HD
-    return jnp.where(lane_head == lax.broadcasted_iota(jnp.int32, shape, 0), row, 0.0)
-
-
-def heads_only(block):
-    lane_head = lax.broadcasted_iota(jnp.int32, block.shape, 1) // HD
-    own = lane_head == lax.broadcasted_iota(jnp.int32, block.shape, 0)
-    return jnp.sum(jnp.where(own, block, 0.0), axis=0, keepdims=True)
-
-
-def through_blocks(row, ref):
-    wide = widen(row)
-    return jnp.concatenate([dot(wide, ref[j])[0:1] for j in range(ref.shape[0])], axis=1)
-
-
-def thoughts_kernel(
-    info_ref,
-    tok_ref,
-    qkv_ref,
-    wqk_ref,
-    wvo_ref,
-    wfc_ref,
-    wproj_ref,
-    vec_ref,
-    fcb_ref,
-    qkvb_ref,
-    hid_ref,
-    qkvm_ref,
-    pre_ref,
-    prob_ref,
-    res_ref,
-    rows_ref,
-    row_lse_ref,
-):
-    width = tok_ref.shape[1]
-    blocks = wfc_ref.shape[0]
-    ln1_gain, ln1_bias, out_bias, ln2_gain, ln2_bias, proj_bias = (
-        vec_ref[i : i + 1, :] for i in range(6)
-    )
-    slot = info_ref[0]
-    count = info_ref[1]
-    hid_ref[...] = tok_ref[...].astype(F32)
-    qkvm_ref[...] = qkv_ref[:, QUESTION:PREFIX, :]
-    rows_ref[...] = jnp.zeros_like(rows_ref)
-    column = lax.broadcasted_iota(jnp.int32, row_lse_ref.shape, 1)
-    row_lse_ref[...] = jnp.zeros_like(row_lse_ref)
-    hidden_row = pick(hid_ref[...], slot - 1 - QUESTION)
-    for step in range(THOUGHTS + 1):
-        at = slot - 1 + step
-        qkv_row = pick(qkvm_ref[0], at - QUESTION)
-        query = by_head(qkv_row * SCALE, HEAD_ROWS).astype(BF16)
-        scores = jnp.concatenate(
-            [
-                dot_nt(query, qkv_ref[1, :QUESTION, :]),
-                dot_nt(query, qkvm_ref[1]),
-            ],
-            axis=1,
-        )
-        key_pos = lax.broadcasted_iota(jnp.int32, scores.shape, 1)
-        scores = jnp.where(key_pos <= at, scores, NEG)
-        peak = jnp.max(scores, axis=1, keepdims=True)
-        expo = jnp.exp(scores - peak)
-        total = jnp.sum(expo, axis=1, keepdims=True)
-        probs = expo / total
-        low = probs.astype(BF16)
-        mixed = heads_only(
-            dot(low[:, :QUESTION], qkv_ref[2, :QUESTION, :])
-            + dot(low[:, QUESTION:], qkvm_ref[2])
-        )
-        rows_ref[step : step + 1, :] = mixed
-        row_lse_ref[...] = jnp.where(column == step, peak + jnp.log(total), row_lse_ref[...])
-        if step == THOUGHTS:
-            break
-        prob_ref[step * HEAD_ROWS : (step + 1) * HEAD_ROWS, :] = probs
-        resid = hidden_row + dot(widen(mixed), wvo_ref[1])[0:1] + out_bias
-        res_ref[step : step + 1, :] = resid
-        second, _, _ = row_norm(resid, ln2_gain, ln2_bias)
-        pre = through_blocks(second, wfc_ref) + fcb_ref[0:1, :]
-        pre_ref[step : step + 1, :] = pre
-        act = gelu(pre)
-        fed = resid + proj_bias
-        for j in range(blocks):
-            fed = fed + dot(widen(act[:, j * width : (j + 1) * width]), wproj_ref[j])[0:1]
-        first, _, _ = row_norm(fed, ln1_gain, ln1_bias)
-        first = widen(first)
-        hidden_row = fed
-        spot = jnp.where(step < count, slot + step - QUESTION, -1)
-        hid_ref[...] = put(hid_ref[...], spot, fed)
-        for i in range(3):
-            span = slice(i * width, (i + 1) * width)
-            weight = wqk_ref[i] if i < 2 else wvo_ref[0]
-            new_row = dot(first, weight)[0:1] + qkvb_ref[0:1, span]
-            qkvm_ref[i] = put(qkvm_ref[i], spot, new_row)
+        middle = jnp.where(column == slot + j - QUESTION, slot_lse[j], middle)
+    lse_ref[:, QUESTION:PREFIX] = middle
+    lse_ref[:, PREFIX:] = new_lse[:, step_rows:]
+    for copy in stores:
+        copy.wait()
 
 
 def whole(array):
@@ -530,32 +570,33 @@
     return pl.BlockSpec(array.shape, lambda i, zeros=zeros: zeros)
 
 
-def weight_specs(blocks, width):
-    near = pl.BlockSpec((2, width, width), lambda i: (0, 0, 0))
-    return [
-        near,
-        near,
-        pl.BlockSpec((blocks, width, width), lambda i: (0, 0, 0)),
-        pl.BlockSpec((blocks, width, width), lambda i: (1, 0, 0)),
-    ]
-
-
-def weight_operands(weights):
-    query_key, value_out, far = weights
-    return query_key, value_out, far, far
-
-
-def thoughts_forward(info, tokens, qkv, weights, vec, fc_bias, qkv_bias):
-    width = tokens.shape[1]
+def fc_spec(far):
+    return pl.BlockSpec((far.shape[0] // 2,) + far.shape[1:], lambda i: (0, 0, 0))
+
+
+def proj_spec(far):
+    return pl.BlockSpec((far.shape[0] // 2,) + far.shape[1:], lambda i: (1, 0, 0))
+
+
+def out_spec(far):
+    last = far.shape[0] - 1
+    return pl.BlockSpec((1,) + far.shape[1:], lambda i: (last, 0, 0))
+
+
+def thoughts_forward(info, tokens, tokens32, qkv, mixed_low, lse, weights, vec, fc_bias, qkv_bias):
+    near, far = weights
+    seq_len, width = tokens.shape
+    rows = seq_len - QUESTION
     middle = PREFIX - QUESTION
+    anywhere = pl.BlockSpec(memory_space=pl.ANY)
     out_shape = [
-        jax.ShapeDtypeStruct((middle, width), F32),
-        jax.ShapeDtypeStruct((3, middle, width), BF16),
+        jax.ShapeDtypeStruct(lse.shape, F32),
         jax.ShapeDtypeStruct((8, fc_bias.shape[1]), F32),
         jax.ShapeDtypeStruct((THOUGHTS * HEAD_ROWS, PREFIX), F32),
         jax.ShapeDtypeStruct((8, width), F32),
-        jax.ShapeDtypeStruct((8, width), F32),
-        jax.ShapeDtypeStruct((HEAD_ROWS, LANES), F32),
+        jax.ShapeDtypeStruct(qkv.shape, BF16),
+        jax.ShapeDtypeStruct(mixed_low.shape, BF16),
+        jax.ShapeDtypeStruct(tokens32.shape, F32),
     ]
     return pl.pallas_call(
         thoughts_kernel,
@@ -563,35 +604,43 @@
         in_specs=[
             pl.BlockSpec(memory_space=pltpu.SMEM),
             pl.BlockSpec((middle, width), lambda i: (QUESTION // middle, 0)),
-            pl.BlockSpec((3, PREFIX, width), lambda i: (0, 0, 0)),
-            *weight_specs(fc_bias.shape[1] // width, width),
+            whole(lse),
             whole(vec),
             whole(fc_bias),
             whole(qkv_bias),
-        ],
-        out_specs=[whole(s) for s in out_shape],
+            *[anywhere] * 5,
+        ],
+        out_specs=[*(whole(x) for x in out_shape[:4]), *[anywhere] * 3],
         out_shape=out_shape,
+        input_output_aliases={8: 4, 9: 5, 10: 6},
+        scratch_shapes=[
+            pltpu.VMEM((3, PREFIX, width), BF16),
+            pltpu.VMEM((rows, width), BF16),
+            pltpu.VMEM((rows, width), BF16),
+            pltpu.VMEM((middle, width), F32),
+            pltpu.VMEM(near.shape, BF16),
+            pltpu.VMEM(far.shape, BF16),
+            pltpu.SemaphoreType.DMA((7,)),
+        ],
         compiler_params=pltpu.CompilerParams(vmem_limit_bytes=VMEM_LIMIT),
-        cost_estimate=cost(7),
+        cost_estimate=cost(2),
         name="thought_rows_forward",
-    )(info, tokens, qkv, *weight_operands(weights), vec, fc_bias, qkv_bias)
+    )(info, tokens, lse, vec, fc_bias, qkv_bias, near, far, qkv, mixed_low, tokens32)
 
 
 def thoughts_back_kernel(
     info_ref,
     hid_ref,
     qkv_ref,
-    late_q_ref,
-    mixed_ref,
     lse_ref,
     pre_ref,
     prob_ref,
     res_ref,
-    wqk_ref,
-    wvo_ref,
-    wfc_ref,
-    wproj_ref,
     vec_ref,
+    near_in,
+    far_in,
+    qkv_in,
+    mixed_in,
     mg_in,
     rg_in,
     sum_ref,
@@ -600,10 +649,14 @@
     rg_out,
     mg_ref,
     rg_win,
+    late_q_ref,
+    mixed_ref,
+    near_ref,
+    far_ref,
     sems,
 ):
     width = hid_ref.shape[1]
-    blocks = wfc_ref.shape[0]
+    blocks = (far_ref.shape[0] - 1) // 2
     units = blocks * width
     rows = mg_ref.shape[0]
     ln1_gain, ln1_bias, _, ln2_gain, ln2_bias, _ = (vec_ref[i : i + 1, :] for i in range(6))
@@ -615,17 +668,24 @@
         return ref.at[pl.ds(base, WINDOW)]
 
     loads = [
-        pltpu.make_async_copy(mg_in, mg_ref, sems.at[0]),
-        pltpu.make_async_copy(window(rg_in), rg_win, sems.at[1]),
+        (mg_in, mg_ref),
+        (mixed_in.at[pl.ds(QUESTION, rows)], mixed_ref),
+        (qkv_in.at[0, pl.ds(QUESTION, rows)], late_q_ref),
+        (window(rg_in), rg_win),
+        (near_in, near_ref),
+        (far_in.at[pl.ds(blocks, blocks)], far_ref.at[pl.ds(blocks, blocks)]),
+        (far_in.at[pl.ds(0, blocks)], far_ref.at[pl.ds(0, blocks)]),
+        (far_in.at[pl.ds(2 * blocks, 1)], far_ref.at[pl.ds(2 * blocks, 1)]),
     ]
+    loads = [pltpu.make_async_copy(a, b, sems.at[i]) for i, (a, b) in enumerate(loads)]
     for copy in loads:
         copy.start()
-    for copy in loads:
+    for copy in loads[:4]:
         copy.wait()
 
-    late_q = late_q_ref[QUESTION:, :]
+    late_q = late_q_ref[...]
     mixed_grad = mg_ref[...]
-    product = mixed_grad.astype(F32) * mixed_ref[QUESTION:, :].astype(F32)
+    product = mixed_grad.astype(F32) * mixed_ref[...].astype(F32)
     high = product.astype(BF16)
     ones = by_head(jnp.ones((1, width), F32), HEAD_ROWS).astype(BF16)
     delta = dot_nt(ones, high) + dot_nt(ones, (product - high.astype(F32)).astype(BF16))
@@ -647,30 +707,34 @@
 
     def through_first(at, query_grad, key_grad, value_grad):
         first_grad = (
-            dot_nt(widen(query_grad), wqk_ref[0])
-            + dot_nt(widen(key_grad), wqk_ref[1])
-            + dot_nt(widen(value_grad), wvo_ref[0])
+            dot_nt(widen(query_grad), near_ref[0])
+            + dot_nt(widen(key_grad), near_ref[1])
+            + dot_nt(widen(value_grad), near_ref[2])
         )[0:1]
         _, normed, inverse = row_norm(hid_ref[pl.ds(at - QUESTION, 1), :], ln1_gain, ln1_bias)
         return row_norm_back(first_grad, normed, inverse, ln1_gain)
 
     sum_ref[...] = jnp.zeros_like(sum_ref)
     fac_ref[...] = jnp.zeros_like(fac_ref)
-    carried = through_first(slot + 1, jnp.zeros((1, width), F32), *at_slot(slot + 1))
+    slot_grads = at_slot(slot + 1)
+    loads[4].wait()
+    carried = through_first(slot + 1, jnp.zeros((1, width), F32), *slot_grads)
+    for copy in loads[5:]:
+        copy.wait()
     for step in reversed(range(THOUGHTS)):
         at = slot - 1 + step
         upstream = jnp.where(step < count, carried, 0.0)
         low = widen(upstream)
-        act_grad = jnp.concatenate([dot_nt(low, wproj_ref[j])[0:1] for j in range(blocks)], axis=1)
+        act_grad = jnp.concatenate([dot_nt(low, far_ref[blocks + j])[0:1] for j in range(blocks)], axis=1)
         pre = pre_ref[step : step + 1, :]
         pre_grad = (act_grad * gelu_slope(pre)).astype(BF16).astype(F32)
         second_grad = jnp.zeros((1, width), F32)
         for j in range(blocks):
             piece = pre_grad[:, j * width : (j + 1) * width]
-            second_grad = second_grad + dot_nt(widen(piece), wfc_ref[j])[0:1]
+            second_grad = second_grad + dot_nt(widen(piece), far_ref[j])[0:1]
         second, normed, inverse = row_norm(res_ref[step : step + 1, :], ln2_gain, ln2_bias)
         resid_grad = upstream + row_norm_back(second_grad, normed, inverse, ln2_gain)
-        mixed_row = dot_nt(widen(resid_grad), wvo_ref[1])[0:1]
+        mixed_row = dot_nt(widen(resid_grad), far_ref[2 * blocks])[0:1]
         local = at - QUESTION
         rg_win[...] = put(rg_win[...], local - base, resid_grad)
         mg_ref[: PREFIX - QUESTION, :] = put(mg_ref[: PREFIX - QUESTION, :], local, mixed_row)
@@ -713,11 +777,11 @@
 SUM_ROWS = ("fc_bias", "ln2_gain", "ln2_bias", "proj_bias", "out_bias")
 
 
-def thoughts_back(info, hidden_mid, qkv, mixed_low, lse, saved, weights, vec, mixed_grad, resid_grad):
-    width = hidden_mid.shape[1]
-    blocks = weights[2].shape[0] // 2
-    units = blocks * width
-    seq_len = qkv.shape[1]
+def thoughts_back(info, hidden, qkv, mixed_low, lse, saved, weights, vec, mixed_grad, resid_grad):
+    near, far = weights
+    width = hidden.shape[1]
+    units = far.shape[0] // 2 * width
+    middle = PREFIX - QUESTION
     anywhere = pl.BlockSpec(memory_space=pl.ANY)
     out_shape = [
         jax.ShapeDtypeStruct((8, units), F32),
@@ -730,38 +794,39 @@
         grid=(1,),
         in_specs=[
             pl.BlockSpec(memory_space=pltpu.SMEM),
-            whole(hidden_mid),
+            pl.BlockSpec((middle, width), lambda i: (QUESTION // middle, 0)),
             pl.BlockSpec((3, PREFIX, width), lambda i: (0, 0, 0)),
-            pl.BlockSpec((None, seq_len, width), lambda i: (0, 0, 0)),
-            whole(mixed_low),
             whole(lse),
             *(whole(x) for x in saved),
-            *weight_specs(blocks, width),
             whole(vec),
-            anywhere,
-            anywhere,
+            *[anywhere] * 6,
         ],
         out_specs=[whole(out_shape[0]), whole(out_shape[1]), anywhere, anywhere],
         out_shape=out_shape,
-        input_output_aliases={14: 2, 15: 3},
+        input_output_aliases={12: 2, 13: 3},
         scratch_shapes=[
             pltpu.VMEM(mixed_grad.shape, BF16),
             pltpu.VMEM((WINDOW, width), F32),
-            pltpu.SemaphoreType.DMA((2,)),
+            pltpu.VMEM(mixed_grad.shape, BF16),
+            pltpu.VMEM(mixed_grad.shape, BF16),
+            pltpu.VMEM(near.shape, BF16),
+            pltpu.VMEM(far.shape, BF16),
+            pltpu.SemaphoreType.DMA((8,)),
         ],
         compiler_params=pltpu.CompilerParams(vmem_limit_bytes=VMEM_LIMIT),
-        cost_estimate=cost(12),
+        cost_estimate=cost(2.0),
         name="thought_rows_backward",
     )(
         info,
-        hidden_mid,
+        hidden,
         qkv,
+        lse,
+        *saved,
+        vec,
+        near,
+        far,
         qkv,
         mixed_low,
-        lse,
-        *saved,
-        *weight_operands(weights),
-        vec,
         mixed_grad,
         resid_grad,
     )
@@ -769,10 +834,12 @@
 
 def forward_kernel(
     hid_ref, mixed_ref, wvo_ref, wfc_ref, wproj_ref, vec_ref, fcb_ref, out_ref, second_ref,
-    act_ref, slope_ref, normed_ref, inverse_ref,
+    act_ref, slope_ref, normed_ref, inverse_ref, first_ref,
 ):
     width = hid_ref.shape[1]
     out_bias, ln2_gain, ln2_bias, proj_bias = (vec_ref[i : i + 1, :] for i in range(2, 6))
+    first, _, _ = row_norm(hid_ref[...], vec_ref[0:1, :], vec_ref[1:2, :])
+    first_ref[...] = first.astype(BF16)
     resid = hid_ref[...] + dot(mixed_ref[...], wvo_ref[0]) + out_bias
     second, normed, inverse = row_norm(resid, ln2_gain, ln2_bias)
     low = second.astype(BF16)
@@ -795,7 +862,7 @@
 
 
 def feed_forward(hidden, mixed_low, weights, vec, fc_bias):
-    _, value_out, far, _ = weight_operands(weights)
+    far = weights[1]
     seq_len, width = hidden.shape
     units = fc_bias.shape[1]
 
@@ -808,12 +875,13 @@
         in_specs=[
             rows(width),
             rows(width),
-            pl.BlockSpec((1, width, width), lambda i: (1, 0, 0)),
-            *weight_specs(units // width, width)[2:],
+            out_spec(far),
+            fc_spec(far),
+            proj_spec(far),
             whole(vec),
             whole(fc_bias),
         ],
-        out_specs=[rows(width), rows(width), rows(units), rows(units), rows(width), rows(LANES)],
+        out_specs=[rows(n) for n in (width, width, units, units, width, LANES, width)],
         out_shape=[
             jax.ShapeDtypeStruct((seq_len, width), BF16),
             jax.ShapeDtypeStruct((seq_len, width), BF16),
@@ -821,11 +889,12 @@
             jax.ShapeDtypeStruct((seq_len, units), BF16),
             jax.ShapeDtypeStruct((seq_len, width), F32),
             jax.ShapeDtypeStruct((seq_len, LANES), F32),
+            jax.ShapeDtypeStruct((seq_len, width), BF16),
         ],
         compiler_params=pltpu.CompilerParams(vmem_limit_bytes=VMEM_LIMIT),
-        cost_estimate=cost(12),
+        cost_estimate=cost(2.0),
         name="feed_forward",
-    )(hidden, mixed_low, value_out, far, far, vec, fc_bias)
+    )(hidden, mixed_low, far, far, far, vec, fc_bias)
 
 
 def back_kernel(
@@ -862,7 +931,7 @@
 
 
 def feed_back(upstream_low, slope, normed, inverse, weights, vec):
-    _, value_out, far, _ = weight_operands(weights)
+    far = weights[1]
     count, width = upstream_low.shape
     units = slope.shape[1]
     skip = QUESTION // BLOCK
@@ -879,8 +948,9 @@
             rows(units, skip),
             rows(width, skip),
             rows(LANES, skip),
-            pl.BlockSpec((1, width, width), lambda i: (1, 0, 0)),
-            *weight_specs(units // width, width)[2:],
+            out_spec(far),
+            fc_spec(far),
+            proj_spec(far),
             whole(vec),
         ],
         out_specs=[rows(units), rows(width), rows(width), whole(sums)],
@@ -891,13 +961,13 @@
             sums,
         ],
         compiler_params=pltpu.CompilerParams(vmem_limit_bytes=VMEM_LIMIT),
-        cost_estimate=cost(9),
+        cost_estimate=cost(1.5),
         name="feed_backward",
-    )(upstream_low, slope, normed, inverse, value_out, far, far, vec)
+    )(upstream_low, slope, normed, inverse, far, far, far, vec)
 
 
 def first_back_kernel(
-    info_ref, hid_ref, grad_ref, rg_ref, wqk_ref, wvo_ref, vec_ref, in_ref, first_ref, sum_ref
+    info_ref, hid_ref, grad_ref, rg_ref, near_ref, vec_ref, in_ref, sum_ref
 ):
     rows, width = hid_ref.shape
     step = pl.program_id(0)
@@ -909,12 +979,10 @@
         sum_ref[...] = jnp.zeros_like(sum_ref)
 
     gain = vec_ref[0:1, :]
-    first, normed, inverse = row_norm(hid_ref[...], gain, vec_ref[1:2, :])
-    first_ref[...] = first.astype(BF16)
+    _, normed, inverse = row_norm(hid_ref[...], gain, vec_ref[1:2, :])
     first_grad = jnp.zeros((rows, width), F32)
     for i in range(3):
-        weight = wqk_ref[i] if i < 2 else wvo_ref[0]
-        first_grad = first_grad + dot_nt(grad_ref[i], weight)
+        first_grad = first_grad + dot_nt(grad_ref[i], near_ref[i])
         if i != 1:
             at = 2 + i // 2
             columns = jnp.sum(grad_ref[i].astype(F32), axis=0, keepdims=True)
@@ -941,71 +1009,187 @@
             rows,
             pl.BlockSpec((3, BLOCK, width), lambda i: (0, i, 0)),
             pl.BlockSpec((BLOCK, width), lambda i: (jnp.maximum(i - skip, 0), 0)),
-            pl.BlockSpec((2, width, width), lambda i: (0, 0, 0)),
-            pl.BlockSpec((1, width, width), lambda i: (0, 0, 0)),
+            whole(weights[0]),
             whole(vec),
         ],
-        out_specs=[rows, rows, whole(sums)],
+        out_specs=[rows, whole(sums)],
         out_shape=[
             jax.ShapeDtypeStruct((seq_len, width), F32),
-            jax.ShapeDtypeStruct((seq_len, width), BF16),
             sums,
         ],
         compiler_params=pltpu.CompilerParams(vmem_limit_bytes=VMEM_LIMIT),
-        cost_estimate=cost(5),
+        cost_estimate=cost(0.83),
         name="first_norm_backward",
-    )(info, hidden, qkv_grad, resid_grad, weights[0], weights[1], vec)
-
-
-def first_kernel(tok_ref, wqk_ref, wvo_ref, vec_ref, qkvb_ref, qkv_ref):
+    )(info, hidden, qkv_grad, resid_grad, weights[0], vec)
+
+
+def keep_and_send(value, core, chips, keep_ref, send_ref, at):
+    own = value.shape[0] // (2 * len(chips))
+    for spot, chip in enumerate(chips):
+        even = value[2 * chip * own : (2 * chip + 1) * own]
+        odd = value[(2 * chip + 1) * own : (2 * chip + 2) * own]
+        keep_ref[spot, at] = jnp.where(core == 0, even, odd).astype(BF16)
+        send_ref[spot, at] = jnp.where(core == 0, odd, even).astype(BF16)
+
+
+def near_terms_kernel(
+    chips_a, chips_b, core_ref, first_ref, grad_ref, mixed_ref, rg_ref, keep_a, send_a, keep_b, send_b
+):
+    core = core_ref[0]
+    first = first_ref[...]
+    for i in range(3):
+        value = dot_tn(first, grad_ref[i])
+        if i < 2:
+            keep_and_send(value, core, chips_a, keep_a, send_a, i)
+        else:
+            keep_and_send(value, core, chips_b, keep_b, send_b, 0)
+    value = dot_tn(mixed_ref[QUESTION:, :], rg_ref[...].astype(BF16))
+    keep_and_send(value, core, chips_b, keep_b, send_b, 1)
+
+
+def near_terms(core, first_low, qkv_grad, mixed_low, resid_grad, chips_a, chips_b):
+    seq_len, width = first_low.shape
+    half = jax.ShapeDtypeStruct((len(chips_a), 2, width // (2 * len(chips_a)), width), BF16)
+    return pl.pallas_call(
+        functools.partial(near_terms_kernel, chips_a, chips_b),
+        grid=(1,),
+        in_specs=[
+            pl.BlockSpec(memory_space=pltpu.SMEM),
+            whole(first_low),
+            whole(qkv_grad),
+            whole(mixed_low),
+            whole(resid_grad),
+        ],
+        out_specs=[whole(half)] * 4,
+        out_shape=[half] * 4,
+        compiler_params=pltpu.CompilerParams(vmem_limit_bytes=VMEM_LIMIT),
+        cost_estimate=cost(0.5),
+        name="near_weight_terms",
+    )(core, first_low, qkv_grad, mixed_low, resid_grad)
+
+
+def fc_terms_kernel(chips, core_ref, second_ref, pg_ref, keep_ref, send_ref):
+    value = dot_tn(second_ref[QUESTION:, :], pg_ref[...])
+    keep_and_send(value, core_ref[0], chips, keep_ref, send_ref, 0)
+
+
+def fc_terms(core, second_low, pre_grad, chips):
+    seq_len, width = second_low.shape
+    rows, units = pre_grad.shape
+    blocks = units // width
+    own = width // (2 * len(chips))
+    half = jax.ShapeDtypeStruct((len(chips), blocks, own, width), BF16)
+    out = pl.BlockSpec((len(chips), 1, own, width), lambda j: (0, j, 0, 0))
+    return pl.pallas_call(
+        functools.partial(fc_terms_kernel, chips),
+        grid=(blocks,),
+        in_specs=[
+            pl.BlockSpec(memory_space=pltpu.SMEM),
+            pl.BlockSpec((seq_len, width), lambda j: (0, 0)),
+            pl.BlockSpec((rows, width), lambda j: (0, j)),
+        ],
+        out_specs=[out, out],
+        out_shape=[half, half],
+        compiler_params=pltpu.CompilerParams(vmem_limit_bytes=VMEM_LIMIT),
+        cost_estimate=cost(0.5),
+        name="fc_weight_terms",
+    )(core, second_low, pre_grad)
+
+
+def proj_terms_kernel(outer, inner, act_ref, up_ref, out_ref):
+    value = dot_tn(act_ref[QUESTION:, :], up_ref[...])
+    rows, width = value.shape
+    value = value.reshape(outer, inner, rows // (outer * inner), width)
+    for i in range(inner):
+        out_ref[i, :, 0] = value[:, i].astype(BF16)
+
+
+def proj_terms(act_low, upstream_low, outer, inner):
+    seq_len, units = act_low.shape
+    rows, width = upstream_low.shape
+    blocks = units // width
+    shape = (inner, outer, blocks, width // (outer * inner), width)
+    return pl.pallas_call(
+        functools.partial(proj_terms_kernel, outer, inner),
+        grid=(blocks,),
+        in_specs=[
+            pl.BlockSpec((seq_len, width), lambda j: (0, j)),
+            pl.BlockSpec((rows, width), lambda j: (0, 0)),
+        ],
+        out_specs=pl.BlockSpec((inner, outer, 1) + shape[3:], lambda j: (0, 0, j, 0, 0)),
+        out_shape=jax.ShapeDtypeStruct(shape, BF16),
+        compiler_params=pltpu.CompilerParams(vmem_limit_bytes=VMEM_LIMIT),
+        cost_estimate=cost(0.5),
+        name="proj_weight_terms",
+    )(act_low, upstream_low)
+
+
+def first_kernel(
+    core_ref, tok_ref, left_mine, left_got, right_mine, right_got, vec_ref, qkvb_ref, qkv_ref,
+    near_ref, rows_ref,
+):
     width = tok_ref.shape[1]
+
+    @pl.when(pl.program_id(0) == 0)
+    def _():
+        even_is_mine = core_ref[0] == 0
+        chips, own, half = left_mine.shape[1:]
+        for i in range(3):
+            for side, (mine, got) in enumerate([(left_mine, left_got), (right_mine, right_got)]):
+                for chip in range(chips):
+                    a = mine[i, chip].astype(F32)
+                    b = got[i, chip].astype(F32)
+                    begin = 2 * chip * own
+                    rows_ref[begin : begin + own, :] = jnp.where(even_is_mine, a, b)
+                    rows_ref[begin + own : begin + 2 * own, :] = jnp.where(even_is_mine, b, a)
+                near_ref[i, :, side * half : (side + 1) * half] = rows_ref[...].astype(BF16)
+
     first, _, _ = row_norm(tok_ref[...].astype(F32), vec_ref[0:1, :], vec_ref[1:2, :])
     first = first.astype(BF16)
     for i in range(3):
-        weight = wqk_ref[i] if i < 2 else wvo_ref[0]
         span = slice(i * width, (i + 1) * width)
-        qkv_ref[i] = (dot(first, weight) + qkvb_ref[:, span]).astype(BF16)
-
-
-def first_forward(tokens, query_key, value_out, vec, qkv_bias):
+        qkv_ref[i] = (dot(first, near_ref[i]) + qkvb_ref[:, span]).astype(BF16)
+
+
+def first_forward(core, tokens, pieces, vec, qkv_bias):
     seq_len, width = tokens.shape
+    near = jax.ShapeDtypeStruct((3, width, width), BF16)
     return pl.pallas_call(
         first_kernel,
         grid=(seq_len // BLOCK,),
         in_specs=[
+            pl.BlockSpec(memory_space=pltpu.SMEM),
             pl.BlockSpec((BLOCK, width), lambda i: (i, 0)),
-            pl.BlockSpec((2, width, width), lambda i: (0, 0, 0)),
-            pl.BlockSpec((1, width, width), lambda i: (0, 0, 0)),
+            *(whole(piece) for piece in pieces),
             whole(vec),
             whole(qkv_bias),
         ],
-        out_specs=pl.BlockSpec((3, BLOCK, width), lambda i: (0, i, 0)),
-        out_shape=jax.ShapeDtypeStruct((3, seq_len, width), BF16),
+        out_specs=[pl.BlockSpec((3, BLOCK, width), lambda i: (0, i, 0)), whole(near)],
+        out_shape=[jax.ShapeDtypeStruct((3, seq_len, width), BF16), near],
+        scratch_shapes=[pltpu.VMEM((width, width // 2), F32)],
         compiler_params=pltpu.CompilerParams(vmem_limit_bytes=VMEM_LIMIT),
-        cost_estimate=cost(4),
+        cost_estimate=cost(0.67),
         name="first_norm_forward",
-    )(tokens, query_key, value_out, vec, qkv_bias)
+    )(core, tokens, *pieces, vec, qkv_bias)
 
 
 def group_of(blocks, own):
     each = blocks * own
     group = LANES // math.gcd(LANES, each)
-    size = group * each
-    row = lax.broadcasted_iota(jnp.int32, (size, size), 0)
-    column = lax.broadcasted_iota(jnp.int32, (size, size), 1)
-    device, block, i = row // each, row % each // own, row % own
-    return group, column == block * (group * own) + device * own + i
-
-
-def split_units_kernel(blocks, fc_ref, out_ref):
+    device, block, i = np.indices((group, blocks, own)).reshape(3, -1)
+    swap = np.zeros((group * each, group * each), np.float32)
+    swap[np.arange(group * each), block * (group * own) + device * own + i] = 1.0
+    return group, jnp.asarray(swap, BF16)
+
+
+def split_units_kernel(blocks, span, fc_ref, swap_ref, out_ref):
     own = fc_ref.shape[0]
-    width = out_ref.shape[2]
-    group, swap = group_of(blocks, own)
-    swap = swap.astype(BF16)
-    size = group * blocks * own
-    span = group * own
-    for g in range(width // span):
-        part = dot(fc_ref[:, g * size : (g + 1) * size], swap)
+    size = swap_ref.shape[0]
+    groups = out_ref.shape[2] // span
+    rows = [fc_ref[:, g * size : (g + 1) * size].astype(F32) for g in range(groups)]
+    swapped = dot(jnp.concatenate(rows, axis=0).astype(BF16), swap_ref[...])
+    for g in range(groups):
+        part = swapped[g * own : (g + 1) * own]
         for j in range(blocks):
             piece = part[:, j * span : (j + 1) * span]
             out_ref[j, :, g * span : (g + 1) * span] = piece.astype(BF16)
@@ -1013,15 +1197,16 @@
 
 def split_units(fc_shard, blocks):
     own, units = fc_shard.shape
+    group, swap = group_of(blocks, own)
     return pl.pallas_call(
-        functools.partial(split_units_kernel, blocks),
+        functools.partial(split_units_kernel, blocks, group * own),
         out_shape=jax.ShapeDtypeStruct((blocks, own, units // blocks), BF16),
         compiler_params=pltpu.CompilerParams(vmem_limit_bytes=VMEM_LIMIT),
         name="units_split",
-    )(fc_shard)
-
-
-def row_terms_kernel(index_ref, fac_ref, proj_ref, fc_ref, proj_out, fc_out):
+    )(fc_shard, swap)
+
+
+def row_terms_kernel(span, index_ref, fac_ref, proj_ref, fc_ref, swap_ref, proj_out, fc_out):
     blocks, own, width = proj_ref.shape
     units = blocks * width
     shape = (width, own)
@@ -1035,18 +1220,20 @@
         proj_out[j] = proj_ref[j] + dot_tn(act, upstream)
         begin = units + 2 * width + j * width
         terms.append(fc_ref[j] + dot_tn(second, fac_ref[:, begin : begin + width]))
-    group, swap = group_of(blocks, own)
-    swap = swap.astype(BF16)
-    size = group * blocks * own
-    span = group * own
-    for g in range(width // span):
-        part = jnp.concatenate([t[:, g * span : (g + 1) * span] for t in terms], axis=1)
-        total = jnp.zeros_like(part)
-        for _ in range(3):
-            piece = part.astype(BF16)
-            part = part - piece.astype(F32)
-            total = total + dot_nt(piece, swap)
-        fc_out[:, g * size : (g + 1) * size] = total
+    size = swap_ref.shape[0]
+    groups = width // span
+    rows = [
+        jnp.concatenate([t[:, g * span : (g + 1) * span] for t in terms], axis=1)
+        for g in range(groups)
+    ]
+    left = jnp.concatenate(rows, axis=0)
+    pieces = []
+    for _ in range(3):
+        pieces.append(left.astype(BF16))
+        left = left - pieces[-1].astype(F32)
+    total = sum(dot_nt(piece, swap_ref[...]) for piece in pieces)
+    for g in range(groups):
+        fc_out[:, g * size : (g + 1) * size] = total[g * own : (g + 1) * own]
 
 
 def row_terms(index, factors, proj_sum, fc_sum):
@@ -1055,21 +1242,23 @@
         jax.ShapeDtypeStruct(proj_sum.shape, F32),
         jax.ShapeDtypeStruct((own, blocks * width), F32),
     ]
+    group, swap = group_of(blocks, own)
     return pl.pallas_call(
-        row_terms_kernel,
+        functools.partial(row_terms_kernel, group * own),
         grid=(1,),
         in_specs=[
             pl.BlockSpec(memory_space=pltpu.SMEM),
             whole(factors),
             whole(proj_sum),
             whole(fc_sum),
+            whole(swap),
         ],
         out_specs=[whole(x) for x in out_shape],
         out_shape=out_shape,
         compiler_params=pltpu.CompilerParams(vmem_limit_bytes=VMEM_LIMIT),
-        cost_estimate=cost(2),
+        cost_estimate=cost(0.33),
         name="thought_rows_terms",
-    )(index, factors, proj_sum, fc_sum)
+    )(index, factors, proj_sum, fc_sum, swap)
 
 
 def spread_matrix(shard, count):
@@ -1190,45 +1379,37 @@
 
 
 def step_on_sequence(
-    near, far, vectors, tokens, cotangent, slots, count, answer_start, devices, sizes, comm
+    near_pieces, far, vectors, tokens, cotangent, slots, count, answer_start, devices, sizes, comm
 ):
-    query_key, value_out = near
     vec, fc_bias, qkv_bias = vectors
     seq_len, width = tokens.shape
     info = jnp.stack([slots[0], count])
 
-    qkv_first = first_forward(tokens, query_key, value_out, vec, qkv_bias)
+    qkv_first, near = first_forward(comm.core, tokens, near_pieces, vec, qkv_bias)
     mixed_hidden, lse_hidden = attend(info, qkv_first)
     late = QUESTION + lax.iota(jnp.int32, seq_len - QUESTION)
     upstream_low = jnp.where(
         (late >= answer_start)[:, None], cotangent[QUESTION:], jnp.zeros((), BF16)
     )
     tokens32 = tokens.astype(F32)
-    weights = (query_key, value_out, after(far, mixed_hidden, upstream_low, tokens32))
-    hidden_mid, qkv_mid, *saved, slot_rows, slot_lse = thoughts_forward(
-        info, tokens, qkv_first, weights, vec, fc_bias, qkv_bias
-    )
-    qkv = lax.dynamic_update_slice(qkv_first, qkv_mid, (0, QUESTION, 0))
-    hidden = lax.dynamic_update_slice(tokens32, hidden_mid, (QUESTION, 0))
-    mixed_low, lse = add_slots(info, qkv, mixed_hidden, lse_hidden, slot_rows, slot_lse)
-    output, second_low, act_low, slope, normed_two, inverse_two = feed_forward(
+    weights = (near, after(far, mixed_hidden, upstream_low, tokens32))
+    lse, *saved, qkv, mixed_low, hidden = thoughts_forward(
+        info, tokens, tokens32, qkv_first, mixed_hidden, lse_hidden, weights, vec, fc_bias, qkv_bias
+    )
+    output, second_low, act_low, slope, normed_two, inverse_two, first_low = feed_forward(
         hidden, mixed_low, weights, vec, fc_bias
     )
 
-    proj_grad = comm.order(dot_tn(act_low[QUESTION:], upstream_low).astype(BF16))
+    proj_grad = comm.proj_terms(act_low, upstream_low)
     proj_half = comm.early(proj_grad)
     pre_grad, resid_grad, mixed_grad, sums = feed_back(
         after(upstream_low, proj_grad), slope, normed_two, inverse_two, weights, vec
     )
-    fc_grad = dot_tn(second_low[QUESTION:], pre_grad).astype(BF16)
-    units = fc_grad.shape[1]
-    fc_going = comm.scatter(
-        [fc_grad[:, j * width : (j + 1) * width] for j in range(units // width)], "zyxc"
-    )
+    fc_going = comm.scatter(fc_terms(comm.core, second_low, pre_grad, comm.chips("zyxc")), "zyxc")
     sent = fc_going.go()
     row_sums, factors, mixed_grad, resid_grad = thoughts_back(
         info,
-        hidden_mid,
+        hidden,
         qkv,
         mixed_low,
         after(lse, sent),
@@ -1239,34 +1420,63 @@
         resid_grad,
     )
     join_after([fc_going], row_sums)
-    out_grad = dot_tn(mixed_low[QUESTION:], resid_grad.astype(BF16)).astype(BF16)
     spread = comm.factors(factors[:THOUGHTS].astype(BF16))
-    sent = go_after([fc_going, spread], out_grad)
-    proj_half = after(proj_half, out_grad)
+    sent = go_after([fc_going, spread])
+    proj_half = after(proj_half, *sent)
     proj_going = comm.early_end(proj_half)
     lse, back_grad = after((lse, mixed_grad), sent, proj_half)
     qkv_grad = attend_back(qkv, mixed_low, lse, back_grad)
     join_after([fc_going, spread], qkv_grad)
     sent = go_after([fc_going, spread], qkv_grad)
-    input_grad, first_low, first_sums = first_back(
-        info, hidden, after(qkv_grad, sent), resid_grad, weights, vec
-    )
-    sums = sums + row_sums
+    first_low = after(first_low, *sent)
+    terms = near_terms(
+        comm.core,
+        first_low,
+        qkv_grad,
+        mixed_low,
+        resid_grad,
+        comm.chips("zxyc"),
+        comm.chips("zyxc"),
+    )
+    first = comm.scatter(terms[:2], "zxyc")
+    rest = comm.scatter(terms[2:], "zyxc")
+
+    sent = go_after([first, rest])
+    join_after([spread], *sent)
+    go_after([spread])
+    join_after([first, rest, fc_going])
+    sent = go_after([first, rest, fc_going], spread.buf)
+    input_grad, first_sums = first_back(info, hidden, after(qkv_grad, *sent), resid_grad, weights, vec)
+    join_after([first, rest, fc_going], input_grad)
+    sent = go_after([first, rest, fc_going])
+    sums = after(sums, *sent) + row_sums
     small = {name: sums[i : i + 1, :width] for i, name in enumerate(SUM_ROWS)}
     small["fc_bias"] = sums[0:1]
     small["ln1_gain"] = first_sums[0:1]
     small["ln1_bias"] = first_sums[1:2]
     small["qv_bias"] = jnp.concatenate([first_sums[2:3], first_sums[3:4]], axis=1)
-    packed = pack(small, sizes, devices)
-    join_after([spread], packed)
-    first_low = after(first_low, go_after([spread], packed))
-    qkv_weight_grad = [dot_tn(first_low, qkv_grad[i]).astype(BF16) for i in range(3)]
-    join_after([fc_going, spread], *qkv_weight_grad)
-    return (
-        output,
-        input_grad,
-        (proj_going, fc_going, spread, out_grad, qkv_weight_grad, packed),
-    )
+    vectors_going = comm.scatter_vectors(pack(small, sizes, devices))
+    go_after([vectors_going])
+    join_after([vectors_going])
+    join_after([spread], vectors_going.buf)
+    going = [first, rest, fc_going, spread, vectors_going]
+    sent = go_after([spread, vectors_going])
+    join_after(going, *sent)
+    proj_g = fc_g = None
+    while any(swap.todo for swap in going) or proj_g is None:
+        group = [swap for swap in going if swap.todo]
+        sent = go_after(group)
+        done = ()
+        behind = len(vectors_going.todo)
+        if behind and behind >= max(len(swap.todo) for swap in going) and len(group) > 1:
+            join_after([vectors_going], *sent)
+            sent = go_after([vectors_going])
+        if proj_g is None and fc_going not in group and spread not in group:
+            factors = after(spread.finish(), *sent)
+            proj_g, fc_g = comm.terms(factors, proj_going, fc_going.buf)
+            done = (proj_g, fc_g)
+        join_after(group, *done)
+    return output, input_grad, first.buf, rest.buf, proj_g, fc_g, vectors_going.buf
 
 
 SMALL = ("ln1_gain", "ln1_bias", "qv_bias", "out_bias", "ln2_gain", "ln2_bias", "fc_bias", "proj_bias")
@@ -1309,25 +1519,39 @@
     both = ("dp", "fsdp")
 
     far_shard = jnp.concatenate(
-        [split_units(fc_weight, blocks), proj_weight.reshape(blocks, own, width)], axis=0
+        [
+            split_units(fc_weight, blocks),
+            proj_weight.reshape(blocks, own, width),
+            out_weight[None],
+        ],
+        axis=0,
     )
     far = lax.all_gather(far_shard, both, axis=1, tiled=True)
 
     packed = join([small_shards[n] for n in SMALL]).astype(BF16)
     small = links.gather(packed, "zxyc", axis=0).reshape(devices, len(sizes), LANES)
-    parts = [qkv_weight[:, i * width : (i + 1) * width] for i in range(3)] + [out_weight]
-    query_key = links.gather(jnp.stack(parts[:2]), "zxyc", axis=1).reshape(2, -1, width)
-    value_out = links.gather(jnp.stack(parts[2:]), "zyxc", axis=1).reshape(2, -1, width)
+    half = width // 2
+    near_pieces = []
+    for side, text in enumerate(("zxyc", "zyxc")):
+        part_columns = [
+            qkv_weight[:, i * width + side * half : i * width + (side + 1) * half] for i in range(3)
+        ]
+        ring = Gather(links, jnp.stack(part_columns), text, axis=1)
+        near_pieces += ring.last()
 
     class Comm:
+        chips = links.chips
+        core = (lax.axis_index("fsdp") % 2)[None].astype(jnp.int32)
+
         @staticmethod
-        def order(grad):
-            value = grad.reshape(blocks, links.sizes["dp"], links.sizes["fsdp"], own, width)
-            return value.transpose(2, 1, 0, 3, 4).reshape(-1, width)
+        def proj_terms(act_low, upstream_low):
+            return proj_terms(act_low, upstream_low, links.sizes["dp"], links.sizes["fsdp"])
 
         @staticmethod
         def early(value):
-            return lax.psum_scatter(value, "fsdp", scatter_dimension=0, tiled=True)
+            return lax.psum_scatter(
+                value.reshape(-1, width), "fsdp", scatter_dimension=0, tiled=True
+            )
 
         @staticmethod
         def early_end(value):
@@ -1335,16 +1559,25 @@
             return value.reshape(blocks, own, width)
 
         @staticmethod
-        def scatter(grads, text):
-            cut = [g.reshape(devices, g.shape[0] // devices, g.shape[1]) for g in grads]
-            return links.scatter(jnp.stack(cut, axis=1), text)
+        def scatter(halves, text):
+            return links.scatter(tuple(halves), text)
 
         @staticmethod
         def factors(rows):
             return Gather(links, rows, "zxyc")
 
-    output, input_grad, late = step_on_sequence(
-        (query_key, value_out),
+        @staticmethod
+        def scatter_vectors(value):
+            return links.scatter(value.transpose(1, 0, 2), "zxyc")
+
+        @staticmethod
+        def terms(factors, proj_sum, fc_sum):
+            index = lax.axis_index(both)[None].astype(jnp.int32)
+            factors = factors.reshape(devices * THOUGHTS, -1)
+            return row_terms(index, factors, proj_sum.astype(F32), fc_sum)
+
+    output, input_grad, first, rest, proj_g, fc_g, vector_sums = step_on_sequence(
+        near_pieces,
         far,
         unpack(small.transpose(1, 0, 2), sizes),
         tokens[0],
@@ -1356,31 +1589,10 @@
         sizes,
         Comm,
     )
-    proj_going, fc_going, spread, out_grad, qkv_grads, packed = late
-    cut = [g.reshape(devices, own, width) for g in qkv_grads[:2]]
-    cut.append(jnp.pad(packed.transpose(1, 0, 2), ((0, 0), (0, 0), (0, width - LANES))))
-    first = links.scatter(jnp.concatenate(cut, axis=1), "zxyc")
-    rest = Comm.scatter([qkv_grads[2], out_grad], "zyxc")
-    swaps = [first, rest, fc_going, spread]
-    terms_left = True
-    done = ()
-    while any(swap.todo for swap in swaps) or terms_left:
-        group = [swap for swap in swaps if swap.todo]
-        sent = go_after(group, *done)
-        if terms_left and fc_going not in group and spread not in group:
-            terms_left = False
-            index = lax.axis_index(both)[None].astype(jnp.int32)
-            factors = after(spread.finish(), sent).reshape(devices * THOUGHTS, -1)
-            proj_g, fc_g = row_terms(index, factors, proj_going.astype(F32), fc_going.buf)
-            done = (proj_g, fc_g)
-        join_after(group, *done)
-        done = tuple(swap.buf for swap in group)
-    first, small_sum = first.buf[: 2 * own].reshape(2, own, width), first.buf[2 * own :, :LANES]
-    rest = rest.buf
     proj_g = proj_g.reshape(blocks * own, width)
     qkv_g = jnp.concatenate([first[0], first[1], rest[0]], axis=1)
     out_g = rest[1]
-    owned = dict(zip(SMALL, part(small_sum, sizes)))
+    owned = dict(zip(SMALL, part(vector_sums, sizes)))
     return (
         output[None],
         input_grad[None],

time: 383 us -> 348 us (0.909); the launches traced: 377 us -> 349 us
  Pallas kernels: 169 us -> 199 us
  matrix products: 23.6 us -> 0 us
  waiting for transfers between devices: 64.1 us -> 45.5 us
  local copies, waits for them, and re-layouts: 28.3 us -> 16.1 us
  other arithmetic: 34.2 us -> 23.2 us
  starting transfers between devices: 41.5 us -> 48.9 us
    dot_general x6 -> x0, matrix products: 23.6 us -> none  [dot_tn(): lax.dot_general(a, b, (((0,), (0,)), ((), ())), preferred_element_type=F32)]
    ppermute x35 -> x40, waiting for transfers between devices: 64 us -> 45.4 us  [swap(): lax.ppermute(value, axis, [(i, i ^ bit) for i in range(self.sizes[axis])])]
    pallas_call x3 -> x5, Pallas kernels: 14.2 us -> 32.5 us  [the longest x1 10.2 us: near_terms(): pl.pallas_call(functools.partial(near_terms_kernel, chips_a, chips_b), gr...]
    pallas_call x1, Pallas kernels: 23.5 us -> 35.2 us  [feed_forward(): pl.pallas_call(forward_kernel, grid=(seq_len // BLOCK,), in_specs=[rows(w...]
    ppermute x35 -> x40, starting transfers between devices: 41.4 us -> 48.7 us  [swap(): lax.ppermute(value, axis, [(i, i ^ bit) for i in range(self.sizes[axis])])]
    convert_element_type x12 -> x16, other arithmetic: 10.6 us -> 5.43 us  [add(): self.buf = self.buf.astype(BF16)]
    another operation x39 -> x35, other arithmetic: 11.8 us -> 7.24 us  [add(): self.buf = jnp.stack(pair, axis=self.axis + place)]
    squeeze x14 -> x16, local copies, waits for them, and re-layouts: 4.42 us -> 0.41 us  [go(): sent = lax.dynamic_index_in_dim(self.buf, 1 - high, place, keepdims=False)]
  transfers between devices with their start and end apart: 38 -> 43, of which waited for: 19 -> 16; matrix products, arithmetic and copies ran while one was open for 17% -> 10% of each run, Pallas kernels for 32% -> 39%
where the time goes in v3:
time: 348 us; the launch traced here: 349 us
  Pallas kernels  199 us (57%)
  starting transfers between devices  48.9 us (14%)
  waiting for transfers between devices  45.5 us (13%)
  other arithmetic  23.2 us (7%)
  local copies, waits for them, and re-layouts  16.1 us (5%)
  between operations  16 us (5%)
    ppermute x40, starting transfers between devices, swap(): lax.ppermute(value, axis, [(i, i ^ bit) for i in range(self.sizes[axis])])  48.7 us
    ppermute x40, waiting for transfers between devices, swap(): lax.ppermute(value, axis, [(i, i ^ bit) for i in range(self.sizes[axis])])  45.4 us
    pallas_call x1, Pallas kernels, feed_forward(): pl.pallas_call(forward_kernel, grid=(seq_len // BLOCK,), in_specs=[rows(w...  35.2 us
    pallas_call x1, Pallas kernels, attend_back(): pl.pallas_call(attend_back_kernel, grid=(width // PAIR,), in_specs=[*(col...  26 us
    pallas_call x1, Pallas kernels, attend(): pl.pallas_call(attend_kernel, grid=(pairs,), in_specs=[pl.BlockSpec(memor...  25.3 us
    pallas_call x1, Pallas kernels, thoughts_back(): pl.pallas_call(thoughts_back_kernel, grid=(1,), in_specs=[pl.BlockSpec(me...  20.3 us
    pallas_call x1, Pallas kernels, feed_back(): pl.pallas_call(back_kernel, grid=(count // BLOCK,), in_specs=[rows(width)...  17.4 us
    pallas_call x1, Pallas kernels, thoughts_forward(): pl.pallas_call(thoughts_kernel, grid=(1,), in_specs=[pl.BlockSpec(memory_...  15.2 us
  transfers between devices with their start and end apart: 43, of which 16 were waited for; matrix products, arithmetic and copies ran while one was open for 10% of the time, Pallas kernels for 39%

profile of v3, /device:TPU:0, one launch (start us, length us, event | category | flops | bytes accessed | tf_op | source)
XLA Modules:
  0.0 348.8 jit_solution(5599918006679831947)
XLA Ops:
  7.2 2.2 units_split.1
  13.3 4.0 %collective-permute-start.10 = (bf16[8,128]{1,0:T(8,128)(2,1)S(1)}, bf16[8,128]{1,0:T(8,128)(2,1)S(1)}, u32[]{:S(2)}, u32[]{:S(2)}) collective-permute-start(bf16[8,128]{1,0:T(8,128)(2,1)S(1)} %convert_element_type.267), channel_id=1, source_target_pairs={{0,4},{1,5},{2,6},{3,7},{4,0},{5,1},{6,2},{7,3},{8,12},{9,13},{10,... | collective-permute-start | bytes 6152 | tf_op jit(solution)/shard_map/ppermute | solution.py:72
  17.5 3.0 collective-permute-start.5
  24.7 2.5 collective-permute-done.11
  30.8 3.3 collective-permute-done.1
  34.1 2.2 collective-permute-done.6
  40.0 2.4 collective-permute-done.7
  42.5 2.1 collective-permute-start.8
  44.6 3.0 collective-permute-done.2
  49.8 12.8 %collective-permute-done.8 = bf16[3,2,2,2,24,384]{5,4,0,2,3,1:T(8,128)(2,1)S(1)} collective-permute-done((bf16[3,2,2,2,24,384]{5,4,0,2,3,1:T(8,128)(2,1)S(1)}, bf16[3,2,2,2,24,384]{5,4,0,2,3,1:T(8,128)(2,1)S(1)}, u32[]{:S(2)}, u32[]{:S(2)}) %collective-permute-start.8) | collective-permute-done | bytes 442400 | tf_op jit(solution)/shard_map/ppermute | solution.py:72
  76.3 10.6 %first_norm_forward.1 = (bf16[3,1024,768]{2,1,0:T(8,128)(2,1)}, bf16[3,768,768]{2,1,0:T(8,128)(2,1)}) custom-call(s32[1]{0:T(128)} %bitcast.2.core_ref, bf16[1024,768]{1,0:T(8,128)(2,1)} %bitcast.223, bf16[3,16,24,384]{3,2,1,0:T(8,128)(2,1)} %bitcast.226, bf16[3,16,24,384]{3,2,1,0:T(8,128)(2,1)} %bitcast.228, bf16[3,16,24,384]{3,2,1,0:T(8,128)(2,1)} %bitcast.225, ...), custom_call_target="tpu_custom_call" | custom-call | flops 770499968 | bytes 2412000 | tf_op jit(solution)/shard_map/first_norm_forward/pallas_call | solution.py:1157
  86.9 25.3 %attention_forward.1 = (bf16[1024,768]{1,0:T(8,128)(2,1)}, f32[16,1024]{1,0:T(8,128)}) custom-call(s32[2]{0:T(128)} %pad_add_fusion.info_ref, bf16[3,1024,768]{2,1,0:T(8,128)(2,1)} %get-tuple-element.95.q_ref.k_ref.v_ref.qkv_in, bf16[3,1024,768]{2,1,0:T(8,128)(2,1)} %get-tuple-element.95.q_ref.k_ref.v_ref.qkv_in, ...), custom_call_target="tpu_custom_call" | custom-call | flops 2300000000 | bytes 7200000 | tf_op jit(solution)/shard_map/attention_forward/pallas_call | solution.py:247
  112.2 15.2 %thought_rows_forward.1 = (f32[16,1024]{1,0:T(8,128)}, f32[8,3072]{1,0:T(8,128)}, f32[32,384]{1,0:T(8,128)}, f32[8,768]{1,0:T(8,128)}, bf16[3,1024,768]{2,1,0:T(...) custom-call(s32[2]{0:T(128)} %pad_add_fusion.info_ref, ...), custom_call_target="tpu_custom_call", output_to_operand_aliasing={{4}: (8, {}), {5}: (9, {}), {6}: (10, {})} | custom-call | flops 2300000000 | bytes 7200000 | tf_op jit(solution)/shard_map/thought_rows_forward/pallas_call | solution.py:601
  127.4 35.2 %feed_forward.1 = (bf16[1024,768]{1,0:T(8,128)(2,1)}, bf16[1024,768]{1,0:T(8,128)(2,1)}, bf16[1024,3072]{1,0:T(8,128)(2,1)}, bf16[1024,3072]{1,0:T(8,128)(2,1)},...) custom-call(f32[1024,768]{1,0:T(8,128)} %get-tuple-element.101.hid_ref, ...), custom_call_target="tpu_custom_call" | custom-call | flops 2300000000 | bytes 7200000 | tf_op jit(solution)/shard_map/feed_forward/pallas_call | solution.py:872
  162.7 8.2 %proj_weight_terms.1 = bf16[8,4,4,24,768]{4,3,2,1,0:T(8,128)(2,1)} custom-call(bf16[1024,3072]{1,0:T(8,128)(2,1)} %get-tuple-element.107.act_ref, bf16[768,768]{1,0:T(8,128)(2,1)} %bitcast_select_fusion.up_ref), custom_call_target="tpu_custom_call" | custom-call | flops 575000000 | bytes 1800000 | tf_op jit(solution)/shard_map/proj_weight_terms/pallas_call | solution.py:1112
  170.9 17.4 %feed_backward.1 = (bf16[768,3072]{1,0:T(8,128)(2,1)}, f32[768,768]{1,0:T(8,128)}, bf16[768,768]{1,0:T(8,128)(2,1)}, f32[8,3072]{1,0:T(8,128)}) custom-call(bf16[768,768]{1,0:T(8,128)(2,1)} %bitcast_select_fusion.up_ref, bf16[1024,3072]{1,0:T(8,128)(2,1)} %get-tuple-element.109.slope_ref, f32[1024,768]{1,0:T(8,128)} %get-tuple-element.110.normed_ref, ...), custom_call_target="tpu_custom_call" | custom-call | flops 1724999936 | bytes 5400000 | tf_op jit(solution)/shard_map/feed_backward/pallas_call | solution.py:943
  188.4 8.1 %fc_weight_terms.1 = (bf16[16,4,24,768]{3,2,1,0:T(8,128)(2,1)}, bf16[16,4,24,768]{3,2,1,0:T(8,128)(2,1)}) custom-call(s32[1]{0:T(128)} %bitcast.2.core_ref, bf16[1024,768]{1,0:T(8,128)(2,1)} %get-tuple-element.106.second_ref, bf16[768,3072]{1,0:T(8,128)(2,1)} %get-tuple-element.112.pg_ref), custom_call_target="tpu_custom_call" | custom-call | flops 575000000 | bytes 1800000 | tf_op jit(solution)/shard_map/fc_weight_terms/pallas_call | solution.py:1083
  196.6 20.3 %thought_rows_backward.1 = (f32[8,3072]{1,0:T(8,128)}, f32[8,7680]{1,0:T(8,128)}, bf16[768,768]{1,0:T(8,128)(2,1)}, f32[768,768]{1,0:T(8,128)}) custom-call(s32[2]{0:T(128)} %pad_add_fusion.info_ref, f32[1024,768]{1,0:T(8,128)} %get-tuple-element.101.hid_ref, ...), custom_call_target="tpu_custom_call", output_to_operand_aliasing={{2}: (12, {}), {3}: (13, {})} | custom-call | flops 2300000000 | bytes 7200000 | tf_op jit(solution)/shard_map/thought_rows_backward/pallas_call | solution.py:792
  218.4 2.4 fusion
  224.4 2.7 collective-permute-start.17
  227.1 26.0 %attention_backward.1.grad_ref = bf16[3,1024,768]{2,1,0:T(8,128)(2,1)} custom-call(bf16[3,1024,768]{2,1,0:T(8,128)(2,1)} %get-tuple-element.104.qkv_ref.qkv_in.q_ref.k_ref.v_ref, bf16[3,1024,768]{2,1,0:T(8,128)(2,1)} %get-tuple-element.104.qkv_ref.qkv_in.q_ref.k_ref.v_ref, bf16[3,1024,768]{2,1,0:T(8,128)(2,1)} %get-tuple-element.104.qkv_ref.qkv_in.q_ref.k_ref.v_ref, ...), custom_call_target="tpu_custom_call" | custom-call | flops 2495500032 | bytes 7812000 | tf_op jit(solution)/shard_map/attention_backward/pallas_call | solution.py:325
  255.7 3.0 collective-permute-start.19
  258.9 10.2 %near_weight_terms.1 = (bf16[16,2,24,768]{3,2,1,0:T(8,128)(2,1)}, bf16[16,2,24,768]{3,2,1,0:T(8,128)(2,1)}, bf16[16,2,24,768]{3,2,1,0:T(8,128)(2,1)}, bf16[16,2,24,768]{3,2,1,0:T(8,128)(2,1)}) custom-call(s32[1]{0:T(128)} %bitcast.2.core_ref, bf16[1024,768]{1,0:T(8,128)(2,1)} %get-tuple-element.133.first_ref, ...), custom_call_target="tpu_custom_call" | custom-call | flops 575000000 | bytes 1800000 | tf_op jit(solution)/shard_map/near_weight_terms/pallas_call | solution.py:1053
  269.9 2.5 collective-permute-done.21
  274.6 2.6 collective-permute-start.23
  278.2 10.4 %first_norm_backward.1 = (f32[1024,768]{1,0:T(8,128)}, f32[8,768]{1,0:T(8,128)}) custom-call(s32[2]{0:T(128)} %pad_add_fusion.info_ref, f32[1024,768]{1,0:T(8,128)} %get-tuple-element.101.hid_ref, bf16[3,1024,768]{2,1,0:T(8,128)(2,1)} %attention_backward.1.grad_ref, f32[768,768]{1,0:T(8,128)} %get-tuple-element.134.rg_ref, ...), custom_call_target="tpu_custom_call" | custom-call | flops 954499968 | bytes 2988000 | tf_op jit(solution)/shard_map/first_norm_backward/pallas_call | solution.py:1004
  307.1 3.9 %collective-permute-done.26 = bf16[2,2,2,8,128]{4,3,1,2,0:T(8,128)(2,1)S(1)} collective-permute-done((bf16[2,2,2,8,128]{4,3,1,2,0:T(8,128)(2,1)S(1)}, bf16[2,2,2,8,128]{4,3,1,2,0:T(8,128)(2,1)S(1)}, u32[]{:S(2)}, u32[]{:S(2)}) %collective-permute-start.26) | collective-permute-done | bytes 16416 | tf_op jit(solution)/shard_map/ppermute | solution.py:72
  312.1 3.1 collective-permute-done.31
  321.5 3.5 collective-permute-done.36
  325.0 2.7 collective-permute-done.35
  328.5 2.3 collective-permute-start.39
  335.0 3.8 %thought_rows_terms.1 = (f32[4,24,768]{2,1,0:T(8,128)}, f32[24,3072]{1,0:T(8,128)}) custom-call(s32[1]{0:T(128)} %bitcast.91.index_ref, bf16[64,7680]{1,0:T(8,128)(2,1)} %reshape.127.fac_ref, f32[4,24,768]{2,1,0:T(8,128)} %convert.42.proj_ref, f32[4,24,768]{2,1,0:T(8,128)} %convert_add_fusion.10.fc_ref, bf16[384,384]{1,0:T(8,128)(2,1)} %constant.133.clone.swap_ref), custom_call_target="tpu_custom_call" | custom-call | flops 379500000 | bytes 1188000 | tf_op jit(solution)/shard_map/thought_rows_terms/pallas_call | solution.py:1246
  (198 shorter events, 75.8 us)
Async XLA Ops:
  7.2 105.0 %all-gather.2.cloned.1.call-start = ((), (), s32[]{:S(2)}) async-start(), calls=%async_computation.2 | async-start | bytes 10948608 | tf_op jit(solution)/shard_map/all_gather | solution.py:1529
  11.2 215.8 %reduce-scatter.3.cloned.1.call-start = ((), (), s32[]{:S(2)}) async-start(), calls=%async_computation.3 | async-start | bytes 5308416 | tf_op jit(solution)/shard_map/reduce_scatter | solution.py:1552
  13.3 9.7 %collective-permute-start.10 = (bf16[8,128]{1,0:T(8,128)(2,1)S(1)}, bf16[8,128]{1,0:T(8,128)(2,1)S(1)}, u32[]{:S(2)}, u32[]{:S(2)}) collective-permute-start(bf16[8,128]{1,0:T(8,128)(2,1)S(1)} %convert_element_type.267), channel_id=1, source_target_pairs={{0,4},{1,5},{2,6},{3,7},{4,0},{5,1},{6,2},{7,3},{8,12},{9,13},{10,... | collective-permute-start | bytes 6152 | tf_op jit(solution)/shard_map/ppermute | solution.py:72
  17.4 9.8 %collective-permute-start = (bf16[3,24,384]{2,1,0:T(8,128)(2,1)S(1)}, bf16[3,24,384]{2,1,0:T(8,128)(2,1)S(1)}, u32[]{:S(2)}, u32[]{:S(2)}) collective-permute-start(bf16[3,24,384]{2,1,0:T(8,128)(2,1)S(1)} %pad_maximum_fusion.16), channel_id=1, source_target_pairs={{0,4},{1,5},{2,6},{3,7},{4,0},{5,1},{6,2},{7,3},{8,12},{9,13},{10,... | collective-permute-start | bytes 165896 | tf_op jit(solution)/shard_map/ppermute | solution.py:72
  17.5 10.9 %collective-permute-start.5 = (bf16[3,24,384]{2,1,0:T(8,128)(2,1)S(1)}, bf16[3,24,384]{2,1,0:T(8,128)(2,1)S(1)}, u32[]{:S(2)}, u32[]{:S(2)}) collective-permute-start(bf16[3,24,384]{2,1,0:T(8,128)(2,1)S(1)} %pad_maximum_fusion.17), channel_id=1, source_target_pairs={{0,4},{1,5},{2,6},{3,7},{4,0},{5,1},{6,2},{7,3},{8,12},{9,13},{10,... | collective-permute-start | bytes 165896 | tf_op jit(solution)/shard_map/ppermute | solution.py:72
  28.5 7.8 %collective-permute-start.6 = (bf16[3,2,24,384]{3,2,0,1:T(8,128)(2,1)S(1)}, bf16[3,2,24,384]{3,2,0,1:T(8,128)(2,1)S(1)}, u32[]{:S(2)}, u32[]{:S(2)}) collective-permute-start(bf16[3,2,24,384]{3,2,0,1:T(8,128)(2,1)S(1)} %pad_maximum_fusion.13), channel_id=1, source_target_pairs={{0,2},{1,3},{2,0},{3,1},{4,6},{5,7},{6,4},{7,5},{8,10},{9,11},{10,... | collective-permute-start | bytes 331784 | tf_op jit(solution)/shard_map/ppermute | solution.py:72
  29.5 8.9 %collective-permute-start.12 = (bf16[2,2,8,128]{3,2,0,1:T(8,128)(2,1)S(1)}, bf16[2,2,8,128]{3,2,0,1:T(8,128)(2,1)S(1)}, u32[]{:S(2)}, u32[]{:S(2)}) collective-permute-start(bf16[2,2,8,128]{3,2,0,1:T(8,128)(2,1)S(1)} %pad_maximum_fusion.20), channel_id=1, source_target_pairs={{0,8},{8,0},{16,24},{24,16},{1,9},{9,1},{17,25},{25,17},{2,10},{10... | collective-permute-start | bytes 24584 | tf_op jit(solution)/shard_map/ppermute | solution.py:72
  38.4 9.2 %collective-permute-start.2 = (bf16[3,2,2,24,384]{4,3,0,1,2:T(8,128)(2,1)S(1)}, bf16[3,2,2,24,384]{4,3,0,1,2:T(8,128)(2,1)S(1)}, u32[]{:S(2)}, u32[]{:S(2)}) collective-permute-start(bf16[3,2,2,24,384]{4,3,0,1,2:T(8,128)(2,1)S(1)} %pad_maximum_fusion.8), channel_id=1, source_target_pairs={{0,8},{8,0},{16,24},{24,16},{1,9},{9,1},{17,25},{25,17},{2,10},{10... | collective-permute-start | bytes 663560 | tf_op jit(solution)/shard_map/ppermute | solution.py:72
  42.5 20.1 %collective-permute-start.8 = (bf16[3,2,2,2,24,384]{5,4,0,2,3,1:T(8,128)(2,1)S(1)}, bf16[3,2,2,2,24,384]{5,4,0,2,3,1:T(8,128)(2,1)S(1)}, u32[]{:S(2)}, u32[]{:S(2)}) collective-permute-start(bf16[3,2,2,2,24,384]{5,4,0,2,3,1:T(8,128)(2,1)S(1)} %pad_maximum_fusion.5), channel_id=1, source_target_pairs={{0,8},{8,0},{16,24},{24,16},{1,9},{9,1},{17,25},{25,17},{2,10},{10... | collective-permute-start | bytes 1327112 | tf_op jit(solution)/shard_map/ppermute | solution.py:72
  47.7 15.2 %collective-permute-start.3 = (bf16[3,2,2,2,24,384]{5,4,0,2,3,1:T(8,128)(2,1)S(1)}, bf16[3,2,2,2,24,384]{5,4,0,2,3,1:T(8,128)(2,1)S(1)}, u32[]{:S(2)}, u32[]{:S(2)}) collective-permute-start(bf16[3,2,2,2,24,384]{5,4,0,2,3,1:T(8,128)(2,1)S(1)} %pad_maximum_fusion.4), channel_id=1, source_target_pairs={{0,16},{8,24},{16,0},{24,8},{1,17},{9,25},{17,1},{25,9},{2,18},{10... | collective-permute-start | bytes 1327112 | tf_op jit(solution)/shard_map/ppermute | solution.py:72
  47.8 18.3 %collective-permute-start.13 = (bf16[2,2,2,8,128]{4,3,1,2,0:T(8,128)(2,1)S(1)}, bf16[2,2,2,8,128]{4,3,1,2,0:T(8,128)(2,1)S(1)}, u32[]{:S(2)}, u32[]{:S(2)}) collective-permute-start(bf16[2,2,2,8,128]{4,3,1,2,0:T(8,128)(2,1)S(1)} %pad_maximum_fusion.19), channel_id=1, source_target_pairs={{0,16},{8,24},{16,0},{24,8},{1,17},{9,25},{17,1},{25,9},{2,18},{10... | collective-permute-start | bytes 49160 | tf_op jit(solution)/shard_map/ppermute | solution.py:72
  62.8 11.4 %collective-permute-start.9 = (bf16[3,2,2,2,2,24,384]{6,5,0,3,4,1,2:T(8,128)(2,1)S(1)}, bf16[3,2,2,2,2,24,384]{6,5,0,3,4,1,2:T(8,128)(2,1)S(1)}, u32[]{:S(2)}, u32[]{:S(2)}) collective-permute-start(bf16[3,2,2,2,2,24,384]{6,5,0,3,4,1,2:T(8,128)(2,1)S(1)} %pad_maximum_fusion.2), channel_id=1, source_target_pairs={{0,1},{1,0},{2,3},{3,2},{4,5},{5,4},{6,7},{7,6},{8,9},{9,8},{10,11... | collective-permute-start | bytes 2654216 | tf_op jit(solution)/shard_map/ppermute | solution.py:72
  63.2 12.1 %collective-permute-start.4 = (bf16[3,2,2,2,2,24,384]{6,5,0,3,4,2,1:T(8,128)(2,1)S(1)}, bf16[3,2,2,2,2,24,384]{6,5,0,3,4,2,1:T(8,128)(2,1)S(1)}, u32[]{:S(2)}, u32[]{:S(2)}) collective-permute-start(bf16[3,2,2,2,2,24,384]{6,5,0,3,4,2,1:T(8,128)(2,1)S(1)} %pad_maximum_fusion.1), channel_id=1, source_target_pairs={{0,1},{1,0},{2,3},{3,2},{4,5},{5,4},{6,7},{7,6},{8,9},{9,8},{10,11... | collective-permute-start | bytes 2654216 | tf_op jit(solution)/shard_map/ppermute | solution.py:72
  170.9 128.2 %reduce-scatter.5.cloned.1.call-start = ((), (), s32[]{:S(2)}) async-start(), calls=%async_computation.4 | async-start | bytes 737280 | tf_op jit(solution)/shard_map/reduce_scatter | solution.py:1558
  196.4 20.5 %collective-permute-start.15 = (bf16[2,2,2,2,4,24,768]{6,5,4,3,2,1,0:T(8,128)(2,1)}, bf16[2,2,2,2,4,24,768]{6,5,4,3,2,1,0:T(8,128)(2,1)S(1)}, u32[]{:S(2)}, u32[]{:S(2)}) collective-permute-start(bf16[2,2,2,2,4,24,768]{6,5,4,3,2,1,0:T(8,128)(2,1)} %bitcast.240), channel_id=1, source_target_pairs={{0,1},{1,0},{2,3},{3,2},{4,5},{5,4},{6,7},{7,6},{8,9},{9,8},{10,11... | collective-permute-start | bytes 7077896 | tf_op jit(solution)/shard_map/ppermute | solution.py:72
  220.9 32.3 %collective-permute-start.16 = (bf16[2,2,2,4,24,768]{5,4,3,2,1,0:T(8,128)(2,1)S(1)}, bf16[2,2,2,4,24,768]{5,4,3,2,1,0:T(8,128)(2,1)}, u32[]{:S(2)}, u32[]{:S(2)}) collective-permute-start(bf16[2,2,2,4,24,768]{5,4,3,2,1,0:T(8,128)(2,1)S(1)} %dynamic-slice_bitcast_fusion), channel_id=1, source_target_pairs={{0,8},{8,0},{16,24},{24,16},{1,9},{9,1},{17,25},{25,17},{2,10},{10... | collective-permute-start | bytes 3538952 | tf_op jit(solution)/shard_map/ppermute | solution.py:72
  224.4 30.4 %collective-permute-start.17 = (bf16[2,7680]{1,0:T(2,128)(2,1)}, bf16[2,7680]{1,0:T(2,128)(2,1)}, u32[]{:S(2)}, u32[]{:S(2)}) collective-permute-start(bf16[2,7680]{1,0:T(2,128)(2,1)} %slice.119), channel_id=1, source_target_pairs={{0,4},{1,5},{2,6},{3,7},{4,0},{5,1},{6,2},{7,3},{8,12},{9,13},{10,... | collective-permute-start | bytes 92168 | tf_op jit(solution)/shard_map/ppermute | solution.py:72
  255.7 13.9 %collective-permute-start.19 = (bf16[2,2,7680]{2,1,0:T(2,128)(2,1)S(1)}, bf16[2,2,7680]{2,1,0:T(2,128)(2,1)S(1)}, u32[]{:S(2)}, u32[]{:S(2)}) collective-permute-start(bf16[2,2,7680]{2,1,0:T(2,128)(2,1)S(1)} %pad_maximum_fusion.15), channel_id=1, source_target_pairs={{0,2},{1,3},{2,0},{3,1},{4,6},{5,7},{6,4},{7,5},{8,10},{9,11},{10,... | collective-permute-start | bytes 184328 | tf_op jit(solution)/shard_map/ppermute | solution.py:72
  258.7 13.7 %collective-permute-start.21 = (bf16[2,2,4,24,768]{4,3,2,1,0:T(8,128)(2,1)S(1)}, bf16[2,2,4,24,768]{4,3,2,1,0:T(8,128)(2,1)S(1)}, u32[]{:S(2)}, u32[]{:S(2)}) collective-permute-start(bf16[2,2,4,24,768]{4,3,2,1,0:T(8,128)(2,1)S(1)} %dynamic-slice_bitcast_fusion.3), channel_id=1, source_target_pairs={{0,16},{8,24},{16,0},{24,8},{1,17},{9,25},{17,1},{25,9},{2,18},{10... | collective-permute-start | bytes 1769480 | tf_op jit(solution)/shard_map/ppermute | solution.py:72
  272.6 16.0 %collective-permute-start.24 = (bf16[2,4,24,768]{3,2,1,0:T(8,128)(2,1)S(1)}, bf16[2,4,24,768]{3,2,1,0:T(8,128)(2,1)S(1)}, u32[]{:S(2)}, u32[]{:S(2)}) collective-permute-start(bf16[2,4,24,768]{3,2,1,0:T(8,128)(2,1)S(1)} %dynamic-slice_bitcast_fusion.6), channel_id=1, source_target_pairs={{0,2},{1,3},{2,0},{3,1},{4,6},{5,7},{6,4},{7,5},{8,10},{9,11},{10,... | collective-permute-start | bytes 884744 | tf_op jit(solution)/shard_map/ppermute | solution.py:72
  274.6 16.2 %collective-permute-start.23 = (bf16[2,2,2,2,24,768]{5,4,3,2,1,0:T(8,128)(2,1)S(1)}, bf16[2,2,2,2,24,768]{5,4,3,2,1,0:T(8,128)(2,1)S(1)}, u32[]{:S(2)}, u32[]{:S(2)}) collective-permute-start(bf16[2,2,2,2,24,768]{5,4,3,2,1,0:T(8,128)(2,1)S(1)} %dynamic-slice_bitcast_fusion.1), channel_id=1, source_target_pairs={{0,8},{8,0},{16,24},{24,16},{1,9},{9,1},{17,25},{25,17},{2,10},{10... | collective-permute-start | bytes 1769480 | tf_op jit(solution)/shard_map/ppermute | solution.py:72
  277.3 14.8 %collective-permute-start.22 = (bf16[2,2,2,2,24,768]{5,4,3,2,1,0:T(8,128)(2,1)S(1)}, bf16[2,2,2,2,24,768]{5,4,3,2,1,0:T(8,128)(2,1)S(1)}, u32[]{:S(2)}, u32[]{:S(2)}) collective-permute-start(bf16[2,2,2,2,24,768]{5,4,3,2,1,0:T(8,128)(2,1)S(1)} %dynamic-slice_bitcast_fusion.2), channel_id=1, source_target_pairs={{0,16},{8,24},{16,0},{24,8},{1,17},{9,25},{17,1},{25,9},{2,18},{10... | collective-permute-start | bytes 1769480 | tf_op jit(solution)/shard_map/ppermute | solution.py:72
  297.4 9.7 %collective-permute-start.37 = (bf16[4,24,768]{2,1,0:T(8,128)(2,1)S(1)}, bf16[4,24,768]{2,1,0:T(8,128)(2,1)S(1)}, u32[]{:S(2)}, u32[]{:S(2)}) collective-permute-start(bf16[4,24,768]{2,1,0:T(8,128)(2,1)S(1)} %dynamic-slice_bitcast_fusion.9), channel_id=1, source_target_pairs={{0,4},{1,5},{2,6},{3,7},{4,0},{5,1},{6,2},{7,3},{8,12},{9,13},{10,... | collective-permute-start | bytes 442376 | tf_op jit(solution)/shard_map/ppermute | solution.py:72
  300.7 15.5 %collective-permute-start.30 = (bf16[2,2,2,24,768]{4,3,2,1,0:T(8,128)(2,1)S(1)}, bf16[2,2,2,24,768]{4,3,2,1,0:T(8,128)(2,1)S(1)}, u32[]{:S(2)}, u32[]{:S(2)}) collective-permute-start(bf16[2,2,2,24,768]{4,3,2,1,0:T(8,128)(2,1)S(1)} %dynamic-slice_bitcast_fusion.4), channel_id=1, source_target_pairs={{0,16},{8,24},{16,0},{24,8},{1,17},{9,25},{17,1},{25,9},{2,18},{10... | collective-permute-start | bytes 884744 | tf_op jit(solution)/shard_map/ppermute | solution.py:72
  301.9 14.4 %collective-permute-start.29 = (bf16[2,2,2,24,768]{4,3,2,1,0:T(8,128)(2,1)S(1)}, bf16[2,2,2,24,768]{4,3,2,1,0:T(8,128)(2,1)S(1)}, u32[]{:S(2)}, u32[]{:S(2)}) collective-permute-start(bf16[2,2,2,24,768]{4,3,2,1,0:T(8,128)(2,1)S(1)} %dynamic-slice_bitcast_fusion.5), channel_id=1, source_target_pairs={{0,8},{8,0},{16,24},{24,16},{1,9},{9,1},{17,25},{25,17},{2,10},{10... | collective-permute-start | bytes 884744 | tf_op jit(solution)/shard_map/ppermute | solution.py:72
  303.7 7.3 %collective-permute-start.26 = (bf16[2,2,2,8,128]{4,3,1,2,0:T(8,128)(2,1)S(1)}, bf16[2,2,2,8,128]{4,3,1,2,0:T(8,128)(2,1)S(1)}, u32[]{:S(2)}, u32[]{:S(2)}) collective-permute-start(bf16[2,2,2,8,128]{4,3,1,2,0:T(8,128)(2,1)S(1)} %dynamic-slice_bitcast_fusion.12), channel_id=1, source_target_pairs={{0,16},{8,24},{16,0},{24,8},{1,17},{9,25},{17,1},{25,9},{2,18},{10... | collective-permute-start | bytes 49160 | tf_op jit(solution)/shard_map/ppermute | solution.py:72
  304.4 10.7 %collective-permute-start.31 = (bf16[2,2,2,2,7680]{4,3,1,2,0:T(2,128)(2,1)S(1)}, bf16[2,2,2,2,7680]{4,3,1,2,0:T(2,128)(2,1)S(1)}, u32[]{:S(2)}, u32[]{:S(2)}) collective-permute-start(bf16[2,2,2,2,7680]{4,3,1,2,0:T(2,128)(2,1)S(1)} %pad_maximum_fusion.7), channel_id=1, source_target_pairs={{0,16},{8,24},{16,0},{24,8},{1,17},{9,25},{17,1},{25,9},{2,18},{10... | collective-permute-start | bytes 737288 | tf_op jit(solution)/shard_map/ppermute | solution.py:72
  318.3 12.5 %collective-permute-start.34 = (bf16[2,2,2,2,2,7680]{5,4,2,3,1,0:T(2,128)(2,1)S(1)}, bf16[2,2,2,2,2,7680]{5,4,2,3,1,0:T(2,128)(2,1)S(1)}, u32[]{:S(2)}, u32[]{:S(2)}) collective-permute-start(bf16[2,2,2,2,2,7680]{5,4,2,3,1,0:T(2,128)(2,1)S(1)} %pad_maximum_fusion.3), channel_id=1, source_target_pairs={{0,1},{1,0},{2,3},{3,2},{4,5},{5,4},{6,7},{7,6},{8,9},{9,8},{10,11... | collective-permute-start | bytes 1474568 | tf_op jit(solution)/shard_map/ppermute | solution.py:72
  319.4 8.4 %collective-permute-start.35 = (bf16[2,2,24,768]{3,2,1,0:T(8,128)(2,1)S(1)}, bf16[2,2,24,768]{3,2,1,0:T(8,128)(2,1)S(1)}, u32[]{:S(2)}, u32[]{:S(2)}) collective-permute-start(bf16[2,2,24,768]{3,2,1,0:T(8,128)(2,1)S(1)} %dynamic-slice_bitcast_fusion.8), channel_id=1, source_target_pairs={{0,2},{1,3},{2,0},{3,1},{4,6},{5,7},{6,4},{7,5},{8,10},{9,11},{10,... | collective-permute-start | bytes 442376 | tf_op jit(solution)/shard_map/ppermute | solution.py:72
  320.4 19.2 %collective-permute-start.33 = (bf16[8,128]{1,0:T(8,128)(2,1)S(1)}, bf16[8,128]{1,0:T(8,128)(2,1)S(1)}, u32[]{:S(2)}, u32[]{:S(2)}) collective-permute-start(bf16[8,128]{1,0:T(8,128)(2,1)S(1)} %fusion.31), channel_id=1, source_target_pairs={{0,4},{1,5},{2,6},{3,7},{4,0},{5,1},{6,2},{7,3},{8,12},{9,13},{10,... | collective-permute-start | bytes 6152 | tf_op jit(solution)/shard_map/ppermute | solution.py:72
  327.8 11.0 %collective-permute-start.38 = (bf16[2,24,768]{2,1,0:T(8,128)(2,1)S(1)}, bf16[2,24,768]{2,1,0:T(8,128)(2,1)S(1)}, u32[]{:S(2)}, u32[]{:S(2)}) collective-permute-start(bf16[2,24,768]{2,1,0:T(8,128)(2,1)S(1)} %dynamic-slice_bitcast_fusion.11), channel_id=1, source_target_pairs={{0,4},{1,5},{2,6},{3,7},{4,0},{5,1},{6,2},{7,3},{8,12},{9,13},{10,... | collective-permute-start | bytes 221192 | tf_op jit(solution)/shard_map/ppermute | solution.py:72
  328.5 10.4 %collective-permute-start.39 = (bf16[2,24,768]{2,1,0:T(8,128)(2,1)S(1)}, bf16[2,24,768]{2,1,0:T(8,128)(2,1)S(1)}, u32[]{:S(2)}, u32[]{:S(2)}) collective-permute-start(bf16[2,24,768]{2,1,0:T(8,128)(2,1)S(1)} %dynamic-slice_bitcast_fusion.10), channel_id=1, source_target_pairs={{0,4},{1,5},{2,6},{3,7},{4,0},{5,1},{6,2},{7,3},{8,12},{9,13},{10,... | collective-permute-start | bytes 221192 | tf_op jit(solution)/shard_map/ppermute | solution.py:72
  (23 other events, 123.6 us)
Sparse Core Ops, SparseCore 0:
  11.3 100.1 all-gather.1
  171.0 55.6 reduce-scatter.2
  229.6 25.4 reduce-scatter.4

commit v4 on v3

--- a/solution.py
+++ b/solution.py
@@ -19,6 +19,7 @@
 HEAD_ROWS = 16
 WINDOW = 32
 LANES = 128
+FACTOR_ROWS = 32
 PAIR = 2 * HD
 NEG = -1e30
 
@@ -120,6 +121,13 @@
             self.done.append(self.stage)
             self.got = None
         return self.buf
+
+    def hold(self, *deps):
+        self.buf = after(self.buf, *deps)
+
+    def join(self, *deps):
+        self.got = after(self.got, *deps)
+        self.add()
 
     def last(self):
         while self.todo:
@@ -152,45 +160,46 @@
             self.buf = value.reshape((2,) * len(self.left) + value.shape[1:])
 
     def go(self):
-        self.add()
         stage = self.todo.pop(0)
         if self.split:
             self.split = False
-            self.got = self.links.swap(self.buf, stage)
-            return self.buf
-        place = self.left.index(stage)
-        self.left.remove(stage)
-        high = self.links.mine(stage).astype(jnp.int32)
-        self.keep = lax.dynamic_index_in_dim(self.buf, high, place, keepdims=False)
-        sent = lax.dynamic_index_in_dim(self.buf, 1 - high, place, keepdims=False)
+            sent = self.buf
+        else:
+            place = self.left.index(stage)
+            self.left.remove(stage)
+            high = self.links.mine(stage).astype(jnp.int32)
+            parts = [self.buf] if self.got is None else [self.keep, self.got]
+
+            def half(side):
+                cut = [lax.dynamic_index_in_dim(p, side, place, keepdims=False) for p in parts]
+                return cut[0] if len(cut) == 1 else cut[0].astype(F32) + cut[1].astype(F32)
+
+            sent = half(1 - high).astype(BF16)
+            self.keep = half(high)
         self.got = self.links.swap(sent, stage)
         return sent
 
-    def add(self):
+    def hold(self, *deps):
         if self.got is None:
-            return self.buf
-        self.buf = self.keep.astype(F32) + self.got.astype(F32)
-        if self.left:
-            self.buf = self.buf.astype(BF16)
-        self.got = None
-        return self.buf
+            self.buf = after(self.buf, *deps)
+        else:
+            self.got = after(self.got, *deps)
+
+    def join(self, *deps):
+        self.got = after(self.got, *deps)
 
     def finish(self):
-        while self.todo:
-            self.go()
-            self.add()
-        return self.buf
+        return self.keep.astype(F32) + self.got.astype(F32)
 
 
 def join_after(swaps, *deps):
     for swap in swaps:
-        swap.got = after(swap.got, *deps)
-        swap.add()
+        swap.join(*deps)
 
 
 def go_after(swaps, *deps):
     for swap in swaps:
-        swap.buf = after(swap.buf, *deps)
+        swap.hold(*deps)
     return tuple(swap.go() for swap in swaps)
 
 
@@ -715,7 +724,7 @@
         return row_norm_back(first_grad, normed, inverse, ln1_gain)
 
     sum_ref[...] = jnp.zeros_like(sum_ref)
-    fac_ref[...] = jnp.zeros_like(fac_ref)
+    fac = {}
     slot_grads = at_slot(slot + 1)
     loads[4].wait()
     carried = through_first(slot + 1, jnp.zeros((1, width), F32), *slot_grads)
@@ -744,10 +753,12 @@
         sum_ref[2:3, :width] += second_grad
         sum_ref[3:4, :width] += up_low
         sum_ref[4:5, :width] += resid_grad.astype(BF16).astype(F32)
-        fac_ref[step : step + 1, :units] = gelu(pre)
-        fac_ref[step : step + 1, units : units + width] = up_low
-        fac_ref[step : step + 1, units + width : units + 2 * width] = second
-        fac_ref[step : step + 1, units + 2 * width :] = pre_grad
+        act = gelu(pre)
+        rows_here = [act[:, j * width : (j + 1) * width] for j in range(blocks)]
+        rows_here += [up_low, second]
+        rows_here += [pre_grad[:, j * width : (j + 1) * width] for j in range(blocks)]
+        for j, row in enumerate(rows_here):
+            fac[THOUGHTS * j + step] = row
         if step:
             own_grad = by_head(mixed_row, HEAD_ROWS).astype(BF16)
             query = by_head(pick(qkv_ref[0, QUESTION:PREFIX, :], local) * SCALE, HEAD_ROWS)
@@ -764,6 +775,8 @@
             key_grad += jnp.sum(score_own * query.astype(F32), axis=0, keepdims=True)
             value_grad += jnp.sum(prob_own * own_grad.astype(F32), axis=0, keepdims=True)
             carried = resid_grad + through_first(at, query_grad, key_grad, value_grad)
+    padding = [jnp.zeros((1, width), F32)] * (fac_ref.shape[0] - len(fac))
+    fac_ref[...] = jnp.concatenate([fac[i] for i in range(len(fac))] + padding, axis=0).astype(BF16)
     stores = [
         pltpu.make_async_copy(mg_ref, mg_out, sems.at[0]),
         pltpu.make_async_copy(rg_win, window(rg_out), sems.at[1]),
@@ -785,7 +798,7 @@
     anywhere = pl.BlockSpec(memory_space=pl.ANY)
     out_shape = [
         jax.ShapeDtypeStruct((8, units), F32),
-        jax.ShapeDtypeStruct((8, 2 * units + 2 * width), F32),
+        jax.ShapeDtypeStruct((FACTOR_ROWS, width), BF16),
         jax.ShapeDtypeStruct(mixed_grad.shape, BF16),
         jax.ShapeDtypeStruct(resid_grad.shape, F32),
     ]
@@ -832,22 +845,29 @@
     )
 
 
-def forward_kernel(
-    hid_ref, mixed_ref, wvo_ref, wfc_ref, wproj_ref, vec_ref, fcb_ref, out_ref, second_ref,
-    act_ref, slope_ref, normed_ref, inverse_ref, first_ref,
+def feed_kernel(
+    hid_ref, mixed_ref, up_ref, wout_ref, wfc_ref, wproj_ref, vec_ref, fcb_ref, out_ref, first_ref,
+    second_ref, act_ref, pg_ref, rg_ref, mg_ref, sum_ref, slope_ref,
 ):
     width = hid_ref.shape[1]
+    blocks = wfc_ref.shape[0]
+    step = pl.program_id(0)
+    skip = QUESTION // BLOCK
     out_bias, ln2_gain, ln2_bias, proj_bias = (vec_ref[i : i + 1, :] for i in range(2, 6))
-    first, _, _ = row_norm(hid_ref[...], vec_ref[0:1, :], vec_ref[1:2, :])
-    first_ref[...] = first.astype(BF16)
-    resid = hid_ref[...] + dot(mixed_ref[...], wvo_ref[0]) + out_bias
+
+    @pl.when(step == 0)
+    def _():
+        sum_ref[...] = jnp.zeros_like(sum_ref)
+
+    hidden = hid_ref[...]
+    _, first_normed, _ = row_norm(hidden, vec_ref[0:1, :], vec_ref[1:2, :])
+    first_ref[...] = first_normed.astype(BF16)
+    resid = hidden + dot(mixed_ref[...], wout_ref[0]) + out_bias
     second, normed, inverse = row_norm(resid, ln2_gain, ln2_bias)
     low = second.astype(BF16)
     second_ref[...] = low
-    normed_ref[...] = normed
-    inverse_ref[...] = jnp.broadcast_to(inverse, inverse_ref.shape)
     total = resid + proj_bias
-    for j in range(wfc_ref.shape[0]):
+    for j in range(blocks):
         span = slice(j * width, (j + 1) * width)
         pre = dot(low, wfc_ref[j]) + fcb_ref[:, span]
         square = pre * pre
@@ -860,135 +880,92 @@
         total = total + dot(act, wproj_ref[j])
     out_ref[...] = total.astype(BF16)
 
-
-def feed_forward(hidden, mixed_low, weights, vec, fc_bias):
+    @pl.when(step >= skip)
+    def _():
+        up = up_ref[...]
+        second_grad = jnp.zeros(up.shape, F32)
+        for j in range(blocks):
+            span = slice(j * width, (j + 1) * width)
+            slope = slope_ref[:, span].astype(F32)
+            pre_grad = (dot_nt(up, wproj_ref[j]) * slope).astype(BF16)
+            pg_ref[:, span] = pre_grad
+            sum_ref[0:1, span] += jnp.sum(pre_grad.astype(F32), axis=0, keepdims=True)
+            second_grad = second_grad + dot_nt(pre_grad, wfc_ref[j])
+        up32 = up.astype(F32)
+        resid_grad = up32 + row_norm_back(second_grad, normed, inverse, ln2_gain)
+        attn_grad = resid_grad.astype(BF16)
+        rg_ref[...] = resid_grad
+        mg_ref[...] = dot_nt(attn_grad, wout_ref[0]).astype(BF16)
+        sum_ref[1:2, :width] += jnp.sum(second_grad * normed, axis=0, keepdims=True)
+        sum_ref[2:3, :width] += jnp.sum(second_grad, axis=0, keepdims=True)
+        sum_ref[3:4, :width] += jnp.sum(up32, axis=0, keepdims=True)
+        sum_ref[4:5, :width] += jnp.sum(attn_grad.astype(F32), axis=0, keepdims=True)
+
+
+def feed(hidden, mixed_low, upstream_low, weights, vec, fc_bias):
     far = weights[1]
     seq_len, width = hidden.shape
+    late = seq_len - QUESTION
     units = fc_bias.shape[1]
+    skip = QUESTION // BLOCK
 
     def rows(columns):
         return pl.BlockSpec((BLOCK, columns), lambda i: (i, 0))
 
+    def late_rows(columns):
+        return pl.BlockSpec((BLOCK, columns), lambda i: (jnp.maximum(i - skip, 0), 0))
+
+    sums = jax.ShapeDtypeStruct((8, units), F32)
     return pl.pallas_call(
-        forward_kernel,
+        feed_kernel,
         grid=(seq_len // BLOCK,),
         in_specs=[
             rows(width),
             rows(width),
+            late_rows(width),
             out_spec(far),
             fc_spec(far),
             proj_spec(far),
             whole(vec),
             whole(fc_bias),
         ],
-        out_specs=[rows(n) for n in (width, width, units, units, width, LANES, width)],
+        out_specs=[
+            rows(width),
+            rows(width),
+            late_rows(width),
+            late_rows(units),
+            late_rows(units),
+            late_rows(width),
+            late_rows(width),
+            whole(sums),
+        ],
         out_shape=[
             jax.ShapeDtypeStruct((seq_len, width), BF16),
             jax.ShapeDtypeStruct((seq_len, width), BF16),
-            jax.ShapeDtypeStruct((seq_len, units), BF16),
-            jax.ShapeDtypeStruct((seq_len, units), BF16),
-            jax.ShapeDtypeStruct((seq_len, width), F32),
-            jax.ShapeDtypeStruct((seq_len, LANES), F32),
-            jax.ShapeDtypeStruct((seq_len, width), BF16),
-        ],
+            jax.ShapeDtypeStruct((late, width), BF16),
+            jax.ShapeDtypeStruct((late, units), BF16),
+            jax.ShapeDtypeStruct((late, units), BF16),
+            jax.ShapeDtypeStruct((late, width), F32),
+            jax.ShapeDtypeStruct((late, width), BF16),
+            sums,
+        ],
+        scratch_shapes=[pltpu.VMEM((BLOCK, units), BF16)],
         compiler_params=pltpu.CompilerParams(vmem_limit_bytes=VMEM_LIMIT),
-        cost_estimate=cost(2.0),
-        name="feed_forward",
-    )(hidden, mixed_low, far, far, far, vec, fc_bias)
-
-
-def back_kernel(
-    up_ref, slope_ref, normed_ref, inverse_ref, wvo_ref, wfc_ref, wproj_ref, vec_ref, pg_ref,
-    rg_ref, mg_ref, sum_ref,
-):
-    width = up_ref.shape[1]
-    blocks = wfc_ref.shape[0]
-    units = blocks * width
-    ln2_gain = vec_ref[3:4, :]
-
-    @pl.when(pl.program_id(0) == 0)
-    def _():
-        sum_ref[...] = jnp.zeros_like(sum_ref)
-
-    up = up_ref[...]
-    second_grad = jnp.zeros(up.shape, F32)
-    for j in range(blocks):
-        span = slice(j * width, (j + 1) * width)
-        pre_grad = (dot_nt(up, wproj_ref[j]) * slope_ref[:, span].astype(F32)).astype(BF16)
-        pg_ref[:, span] = pre_grad
-        sum_ref[0:1, span] += jnp.sum(pre_grad.astype(F32), axis=0, keepdims=True)
-        second_grad = second_grad + dot_nt(pre_grad, wfc_ref[j])
-    normed = normed_ref[...]
-    up32 = up.astype(F32)
-    resid_grad = up32 + row_norm_back(second_grad, normed, inverse_ref[:, :1], ln2_gain)
-    attn_grad = resid_grad.astype(BF16)
-    rg_ref[...] = resid_grad
-    mg_ref[...] = dot_nt(attn_grad, wvo_ref[0]).astype(BF16)
-    sum_ref[1:2, :width] += jnp.sum(second_grad * normed, axis=0, keepdims=True)
-    sum_ref[2:3, :width] += jnp.sum(second_grad, axis=0, keepdims=True)
-    sum_ref[3:4, :width] += jnp.sum(up32, axis=0, keepdims=True)
-    sum_ref[4:5, :width] += jnp.sum(attn_grad.astype(F32), axis=0, keepdims=True)
-
-
-def feed_back(upstream_low, slope, normed, inverse, weights, vec):
-    far = weights[1]
-    count, width = upstream_low.shape
-    units = slope.shape[1]
-    skip = QUESTION // BLOCK
-
-    def rows(columns, begin=0):
-        return pl.BlockSpec((BLOCK, columns), lambda i, begin=begin: (i + begin, 0))
-
-    sums = jax.ShapeDtypeStruct((8, units), F32)
-    return pl.pallas_call(
-        back_kernel,
-        grid=(count // BLOCK,),
-        in_specs=[
-            rows(width),
-            rows(units, skip),
-            rows(width, skip),
-            rows(LANES, skip),
-            out_spec(far),
-            fc_spec(far),
-            proj_spec(far),
-            whole(vec),
-        ],
-        out_specs=[rows(units), rows(width), rows(width), whole(sums)],
-        out_shape=[
-            jax.ShapeDtypeStruct((count, units), BF16),
-            jax.ShapeDtypeStruct((count, width), F32),
-            jax.ShapeDtypeStruct((count, width), BF16),
-            sums,
-        ],
-        compiler_params=pltpu.CompilerParams(vmem_limit_bytes=VMEM_LIMIT),
-        cost_estimate=cost(1.5),
-        name="feed_backward",
-    )(upstream_low, slope, normed, inverse, far, far, far, vec)
-
-
-def first_back_kernel(
-    info_ref, hid_ref, grad_ref, rg_ref, near_ref, vec_ref, in_ref, sum_ref
-):
+        cost_estimate=cost(3),
+        name="feed_forward_and_back",
+    )(hidden, mixed_low, upstream_low, far, far, far, vec, fc_bias)
+
+
+def first_back_kernel(info_ref, hid_ref, grad_ref, rg_ref, near_ref, vec_ref, in_ref):
     rows, width = hid_ref.shape
     step = pl.program_id(0)
     slot = info_ref[0]
     count = info_ref[1]
-
-    @pl.when(step == 0)
-    def _():
-        sum_ref[...] = jnp.zeros_like(sum_ref)
-
     gain = vec_ref[0:1, :]
     _, normed, inverse = row_norm(hid_ref[...], gain, vec_ref[1:2, :])
     first_grad = jnp.zeros((rows, width), F32)
     for i in range(3):
         first_grad = first_grad + dot_nt(grad_ref[i], near_ref[i])
-        if i != 1:
-            at = 2 + i // 2
-            columns = jnp.sum(grad_ref[i].astype(F32), axis=0, keepdims=True)
-            sum_ref[at : at + 1, :] += columns
-    sum_ref[0:1, :] += jnp.sum(first_grad * normed, axis=0, keepdims=True)
-    sum_ref[1:2, :] += jnp.sum(first_grad, axis=0, keepdims=True)
     late = (step >= QUESTION // BLOCK).astype(F32)
     grad = row_norm_back(first_grad, normed, inverse, gain) + late * rg_ref[...]
     position = step * rows + lax.broadcasted_iota(jnp.int32, (rows, 1), 0)
@@ -999,7 +976,6 @@
 def first_back(info, hidden, qkv_grad, resid_grad, weights, vec):
     seq_len, width = hidden.shape
     skip = QUESTION // BLOCK
-    sums = jax.ShapeDtypeStruct((8, width), F32)
     rows = pl.BlockSpec((BLOCK, width), lambda i: (i, 0))
     return pl.pallas_call(
         first_back_kernel,
@@ -1012,15 +988,20 @@
             whole(weights[0]),
             whole(vec),
         ],
-        out_specs=[rows, whole(sums)],
-        out_shape=[
-            jax.ShapeDtypeStruct((seq_len, width), F32),
-            sums,
-        ],
+        out_specs=rows,
+        out_shape=jax.ShapeDtypeStruct((seq_len, width), F32),
         compiler_params=pltpu.CompilerParams(vmem_limit_bytes=VMEM_LIMIT),
         cost_estimate=cost(0.83),
         name="first_norm_backward",
     )(info, hidden, qkv_grad, resid_grad, weights[0], vec)
+
+
+def in_pieces(value, count=3):
+    pieces = []
+    for _ in range(count):
+        pieces.append(value.astype(BF16))
+        value = value - pieces[-1].astype(F32)
+    return pieces
 
 
 def keep_and_send(value, core, chips, keep_ref, send_ref, at):
@@ -1033,48 +1014,81 @@
 
 
 def near_terms_kernel(
-    chips_a, chips_b, core_ref, first_ref, grad_ref, mixed_ref, rg_ref, keep_a, send_a, keep_b, send_b
+    sizes, chips_a, chips_b, core_ref, normed_ref, grad_ref, mixed_ref, rg_ref, near_ref, vec_ref,
+    feed_sum_ref, row_sum_ref, keep_a, send_a, keep_b, send_b, packed_ref,
 ):
     core = core_ref[0]
-    first = first_ref[...]
+    width = normed_ref.shape[1]
+    columns = vec_ref[...].T
+    gain, bias = columns[:, 0:1], columns[:, 1:2]
+    normed_t = normed_ref[...].T
+    gain_terms = jnp.zeros((width, width), F32)
+    bias_rows = jnp.zeros((16, width), F32)
+    column_sums = []
     for i in range(3):
-        value = dot_tn(first, grad_ref[i])
+        inner = dot(normed_t, grad_ref[i])
+        sums = jnp.sum(grad_ref[i].astype(F32), axis=0, keepdims=True)
+        value = inner * gain + bias * sums
         if i < 2:
             keep_and_send(value, core, chips_a, keep_a, send_a, i)
         else:
             keep_and_send(value, core, chips_b, keep_b, send_b, 0)
+        gain_terms = gain_terms + inner * near_ref[i].astype(F32)
+        pieces = in_pieces(jnp.broadcast_to(sums, (8, width)), 2)
+        bias_rows = bias_rows + dot_nt(jnp.concatenate(pieces, axis=0), near_ref[i])
+        column_sums.append(sums)
+    ones = jnp.ones((16, width), BF16)
+    totals = feed_sum_ref[...] + row_sum_ref[...]
+    small = {name: totals[i : i + 1, :width] for i, name in enumerate(SUM_ROWS)}
+    small["fc_bias"] = totals[0:1]
+    small["ln1_gain"] = sum(dot_nt(ones, piece) for piece in in_pieces(gain_terms, 2))[0:1]
+    small["ln1_bias"] = bias_rows[0:1] + bias_rows[8:9]
+    small["qv_bias"] = jnp.concatenate([column_sums[0], column_sums[2]], axis=1)
+    pack(small, sizes, 2 * len(chips_a), packed_ref)
     value = dot_tn(mixed_ref[QUESTION:, :], rg_ref[...].astype(BF16))
     keep_and_send(value, core, chips_b, keep_b, send_b, 1)
 
 
-def near_terms(core, first_low, qkv_grad, mixed_low, resid_grad, chips_a, chips_b):
-    seq_len, width = first_low.shape
+def near_terms(
+    core, normed_low, qkv_grad, mixed_low, resid_grad, near, vec, feed_sums, row_sums, sizes, chips_a, chips_b
+):
+    seq_len, width = normed_low.shape
     half = jax.ShapeDtypeStruct((len(chips_a), 2, width // (2 * len(chips_a)), width), BF16)
+    packed = jax.ShapeDtypeStruct((len(sizes), 2 * len(chips_a), LANES), BF16)
+    out_shape = [half] * 4 + [packed]
     return pl.pallas_call(
-        functools.partial(near_terms_kernel, chips_a, chips_b),
+        functools.partial(near_terms_kernel, sizes, chips_a, chips_b),
         grid=(1,),
         in_specs=[
             pl.BlockSpec(memory_space=pltpu.SMEM),
-            whole(first_low),
+            whole(normed_low),
             whole(qkv_grad),
             whole(mixed_low),
             whole(resid_grad),
-        ],
-        out_specs=[whole(half)] * 4,
-        out_shape=[half] * 4,
+            whole(near),
+            whole(vec),
+            whole(feed_sums),
+            whole(row_sums),
+        ],
+        out_specs=[whole(x) for x in out_shape],
+        out_shape=out_shape,
         compiler_params=pltpu.CompilerParams(vmem_limit_bytes=VMEM_LIMIT),
         cost_estimate=cost(0.5),
         name="near_weight_terms",
-    )(core, first_low, qkv_grad, mixed_low, resid_grad)
-
-
-def fc_terms_kernel(chips, core_ref, second_ref, pg_ref, keep_ref, send_ref):
-    value = dot_tn(second_ref[QUESTION:, :], pg_ref[...])
+    )(core, normed_low, qkv_grad, mixed_low, resid_grad, near, vec, feed_sums, row_sums)
+
+
+def fc_terms_kernel(chips, core_ref, second_ref, pg_ref, keep_ref, send_ref, second_t):
+    @pl.when(pl.program_id(0) == 0)
+    def _():
+        second_t[...] = second_ref[...].T
+
+    value = dot(second_t[...], pg_ref[...])
     keep_and_send(value, core_ref[0], chips, keep_ref, send_ref, 0)
 
 
 def fc_terms(core, second_low, pre_grad, chips):
-    seq_len, width = second_low.shape
+    width = second_low.shape[1]
     rows, units = pre_grad.shape
     blocks = units // width
     own = width // (2 * len(chips))
@@ -1085,11 +1099,12 @@
         grid=(blocks,),
         in_specs=[
             pl.BlockSpec(memory_space=pltpu.SMEM),
-            pl.BlockSpec((seq_len, width), lambda j: (0, 0)),
+            pl.BlockSpec((rows, width), lambda j: (0, 0)),
             pl.BlockSpec((rows, width), lambda j: (0, j)),
         ],
         out_specs=[out, out],
         out_shape=[half, half],
+        scratch_shapes=[pltpu.VMEM((width, rows), BF16)],
         compiler_params=pltpu.CompilerParams(vmem_limit_bytes=VMEM_LIMIT),
         cost_estimate=cost(0.5),
         name="fc_weight_terms",
@@ -1097,7 +1112,7 @@
 
 
 def proj_terms_kernel(outer, inner, act_ref, up_ref, out_ref):
-    value = dot_tn(act_ref[QUESTION:, :], up_ref[...])
+    value = dot_tn(act_ref[...], up_ref[...])
     rows, width = value.shape
     value = value.reshape(outer, inner, rows // (outer * inner), width)
     for i in range(inner):
@@ -1105,7 +1120,7 @@
 
 
 def proj_terms(act_low, upstream_low, outer, inner):
-    seq_len, units = act_low.shape
+    units = act_low.shape[1]
     rows, width = upstream_low.shape
     blocks = units // width
     shape = (inner, outer, blocks, width // (outer * inner), width)
@@ -1113,7 +1128,7 @@
         functools.partial(proj_terms_kernel, outer, inner),
         grid=(blocks,),
         in_specs=[
-            pl.BlockSpec((seq_len, width), lambda j: (0, j)),
+            pl.BlockSpec((rows, width), lambda j: (0, j)),
             pl.BlockSpec((rows, width), lambda j: (0, 0)),
         ],
         out_specs=pl.BlockSpec((inner, outer, 1) + shape[3:], lambda j: (0, 0, j, 0, 0)),
@@ -1208,18 +1223,20 @@
 
 def row_terms_kernel(span, index_ref, fac_ref, proj_ref, fc_ref, swap_ref, proj_out, fc_out):
     blocks, own, width = proj_ref.shape
-    units = blocks * width
     shape = (width, own)
     mine = lax.broadcasted_iota(jnp.int32, shape, 0) - index_ref[0] * own
     select = (mine == lax.broadcasted_iota(jnp.int32, shape, 1)).astype(BF16)
-    upstream = fac_ref[:, units : units + width]
+
+    def factor(j):
+        return jnp.concatenate([fac_ref[THOUGHTS * j + i] for i in range(THOUGHTS)], axis=0)
+
+    upstream = factor(blocks)
     terms = []
-    second = dot(fac_ref[:, units + width : units + 2 * width], select).astype(BF16)
+    second = dot(factor(blocks + 1), select).astype(BF16)
     for j in range(blocks):
-        act = dot(fac_ref[:, j * width : (j + 1) * width], select).astype(BF16)
-        proj_out[j] = proj_ref[j] + dot_tn(act, upstream)
-        begin = units + 2 * width + j * width
-        terms.append(fc_ref[j] + dot_tn(second, fac_ref[:, begin : begin + width]))
+        act = dot(factor(j), select).astype(BF16)
+        proj_out[j] = proj_ref[j].astype(F32) + dot_tn(act, upstream)
+        terms.append(fc_ref[j] + dot_tn(second, factor(blocks + 2 + j)))
     size = swap_ref.shape[0]
     groups = width // span
     rows = [
@@ -1227,11 +1244,7 @@
         for g in range(groups)
     ]
     left = jnp.concatenate(rows, axis=0)
-    pieces = []
-    for _ in range(3):
-        pieces.append(left.astype(BF16))
-        left = left - pieces[-1].astype(F32)
-    total = sum(dot_nt(piece, swap_ref[...]) for piece in pieces)
+    total = sum(dot_nt(piece, swap_ref[...]) for piece in in_pieces(left))
     for g in range(groups):
         fc_out[:, g * size : (g + 1) * size] = total[g * own : (g + 1) * own]
 
@@ -1316,31 +1329,17 @@
     )(packed)
 
 
-def pack_kernel(sizes, devices, *refs):
-    out_ref = refs[-1]
+def pack(rows, sizes, devices, out_ref):
     out_ref[...] = jnp.zeros_like(out_ref)
-    width = refs[0].shape[1]
-    for at, ((name, size), ref) in enumerate(zip(sizes, refs)):
-        if name == "fc_bias":
-            own = width // devices
-            for j in range(size // own):
-                row = jnp.broadcast_to(ref[:, j * width : (j + 1) * width], (devices, width))
-                row = jnp.where(owner_mask(own, devices), row, 0.0).astype(BF16)
-                piece = dot_nt(row, spread_matrix(own, devices))
-                out_ref[at, :, j * own : (j + 1) * own] = piece.astype(BF16)
-            continue
-        row = jnp.broadcast_to(ref[...], (devices, ref.shape[1]))
-        own = jnp.where(owner_mask(size, devices), row, 0.0).astype(BF16)
-        out_ref[at, :, :size] = dot_nt(own, spread_matrix(size, devices)).astype(BF16)
-
-
-def pack(rows, sizes, devices):
-    return pl.pallas_call(
-        functools.partial(pack_kernel, sizes, devices),
-        out_shape=jax.ShapeDtypeStruct((len(sizes), devices, LANES), BF16),
-        compiler_params=pltpu.CompilerParams(vmem_limit_bytes=VMEM_LIMIT),
-        name="vectors_pack",
-    )(*[rows[name] for name, _ in sizes])
+    width = rows["ln1_gain"].shape[1]
+    for at, (name, size) in enumerate(sizes):
+        own = width // devices if name == "fc_bias" else size
+        span = own * devices
+        for j in range(size // own):
+            row = jnp.broadcast_to(rows[name][:, j * span : (j + 1) * span], (devices, span))
+            row = jnp.where(owner_mask(own, devices), row, 0.0).astype(BF16)
+            piece = dot_nt(row, spread_matrix(own, devices)).astype(BF16)
+            out_ref[at, :, j * own : (j + 1) * own] = piece
 
 
 def join_kernel(*refs):
@@ -1371,13 +1370,6 @@
     )(joined)
 
 
-def norm_parts(hidden):
-    mean = jnp.mean(hidden, axis=-1, keepdims=True)
-    centred = hidden - mean
-    inverse = lax.rsqrt(jnp.mean(centred * centred, axis=-1, keepdims=True) + EPSILON)
-    return centred * inverse, inverse
-
-
 def step_on_sequence(
     near_pieces, far, vectors, tokens, cotangent, slots, count, answer_start, devices, sizes, comm
 ):
@@ -1396,23 +1388,21 @@
     lse, *saved, qkv, mixed_low, hidden = thoughts_forward(
         info, tokens, tokens32, qkv_first, mixed_hidden, lse_hidden, weights, vec, fc_bias, qkv_bias
     )
-    output, second_low, act_low, slope, normed_two, inverse_two, first_low = feed_forward(
-        hidden, mixed_low, weights, vec, fc_bias
+    output, normed_low, second_low, act_low, pre_grad, resid_grad, mixed_grad, sums = feed(
+        hidden, mixed_low, upstream_low, weights, vec, fc_bias
     )
 
     proj_grad = comm.proj_terms(act_low, upstream_low)
     proj_half = comm.early(proj_grad)
-    pre_grad, resid_grad, mixed_grad, sums = feed_back(
-        after(upstream_low, proj_grad), slope, normed_two, inverse_two, weights, vec
-    )
-    fc_going = comm.scatter(fc_terms(comm.core, second_low, pre_grad, comm.chips("zyxc")), "zyxc")
-    sent = fc_going.go()
+    halves = fc_terms(comm.core, after(second_low, proj_grad), pre_grad, comm.chips("zyxc"))
+    fc_going = comm.scatter(halves, "zyxc")
+    sent = go_after([fc_going])
     row_sums, factors, mixed_grad, resid_grad = thoughts_back(
         info,
         hidden,
         qkv,
         mixed_low,
-        after(lse, sent),
+        after(lse, *sent),
         saved,
         weights,
         vec,
@@ -1420,63 +1410,59 @@
         resid_grad,
     )
     join_after([fc_going], row_sums)
-    spread = comm.factors(factors[:THOUGHTS].astype(BF16))
+    spread = comm.factors(factors)
     sent = go_after([fc_going, spread])
-    proj_half = after(proj_half, *sent)
-    proj_going = comm.early_end(proj_half)
-    lse, back_grad = after((lse, mixed_grad), sent, proj_half)
+    lse, back_grad = after((lse, mixed_grad), *sent)
     qkv_grad = attend_back(qkv, mixed_low, lse, back_grad)
     join_after([fc_going, spread], qkv_grad)
-    sent = go_after([fc_going, spread], qkv_grad)
-    first_low = after(first_low, *sent)
-    terms = near_terms(
+    proj_half = after(proj_half, qkv_grad)
+    proj_going = comm.early_end(proj_half)
+    sent = (*go_after([fc_going, spread]), proj_half)
+    *terms, packed = near_terms(
         comm.core,
-        first_low,
+        after(normed_low, *sent),
         qkv_grad,
         mixed_low,
         resid_grad,
+        near,
+        vec,
+        sums,
+        row_sums,
+        sizes,
         comm.chips("zxyc"),
         comm.chips("zyxc"),
     )
     first = comm.scatter(terms[:2], "zxyc")
     rest = comm.scatter(terms[2:], "zyxc")
-
-    sent = go_after([first, rest])
+    vectors_going = comm.scatter_vectors(packed)
+
+    sent = go_after([first, rest, vectors_going])
     join_after([spread], *sent)
-    go_after([spread])
-    join_after([first, rest, fc_going])
-    sent = go_after([first, rest, fc_going], spread.buf)
-    input_grad, first_sums = first_back(info, hidden, after(qkv_grad, *sent), resid_grad, weights, vec)
-    join_after([first, rest, fc_going], input_grad)
-    sent = go_after([first, rest, fc_going])
-    sums = after(sums, *sent) + row_sums
-    small = {name: sums[i : i + 1, :width] for i, name in enumerate(SUM_ROWS)}
-    small["fc_bias"] = sums[0:1]
-    small["ln1_gain"] = first_sums[0:1]
-    small["ln1_bias"] = first_sums[1:2]
-    small["qv_bias"] = jnp.concatenate([first_sums[2:3], first_sums[3:4]], axis=1)
-    vectors_going = comm.scatter_vectors(pack(small, sizes, devices))
-    go_after([vectors_going])
-    join_after([vectors_going])
-    join_after([spread], vectors_going.buf)
-    going = [first, rest, fc_going, spread, vectors_going]
-    sent = go_after([spread, vectors_going])
+    sent = go_after([spread])
+    going = [first, rest, vectors_going, fc_going, spread]
     join_after(going, *sent)
+    sent = go_after(going)
+    input_grad = first_back(info, hidden, after(qkv_grad, *sent), resid_grad, weights, vec)
+    join_after(going, input_grad)
     proj_g = fc_g = None
     while any(swap.todo for swap in going) or proj_g is None:
         group = [swap for swap in going if swap.todo]
         sent = go_after(group)
-        done = ()
-        behind = len(vectors_going.todo)
-        if behind and behind >= max(len(swap.todo) for swap in going) and len(group) > 1:
-            join_after([vectors_going], *sent)
-            sent = go_after([vectors_going])
+        done = sent
         if proj_g is None and fc_going not in group and spread not in group:
-            factors = after(spread.finish(), *sent)
-            proj_g, fc_g = comm.terms(factors, proj_going, fc_going.buf)
+            factors, fc_sum = after((spread.finish(), fc_going.finish()), *sent)
+            proj_g, fc_g = comm.terms(factors, proj_going, fc_sum)
             done = (proj_g, fc_g)
         join_after(group, *done)
-    return output, input_grad, first.buf, rest.buf, proj_g, fc_g, vectors_going.buf
+    return (
+        output,
+        input_grad,
+        first.finish(),
+        rest.finish(),
+        proj_g,
+        fc_g,
+        vectors_going.finish(),
+    )
 
 
 SMALL = ("ln1_gain", "ln1_bias", "qv_bias", "out_bias", "ln2_gain", "ln2_bias", "fc_bias", "proj_bias")
@@ -1573,8 +1559,8 @@
         @staticmethod
         def terms(factors, proj_sum, fc_sum):
             index = lax.axis_index(both)[None].astype(jnp.int32)
-            factors = factors.reshape(devices * THOUGHTS, -1)
-            return row_terms(index, factors, proj_sum.astype(F32), fc_sum)
+            factors = factors.reshape(devices, FACTOR_ROWS, width).transpose(1, 0, 2)
+            return row_terms(index, factors, proj_sum, fc_sum)
 
     output, input_grad, first, rest, proj_g, fc_g, vector_sums = step_on_sequence(
         near_pieces,

time: 348 us -> 324 us (0.931); the launches traced: 349 us -> 320 us
  Pallas kernels: 199 us -> 184 us
  other arithmetic: 23.2 us -> 17.6 us
  local copies, waits for them, and re-layouts: 16.1 us -> 11.3 us
  starting transfers between devices: 48.9 us -> 44.7 us
    pallas_call x4 -> x2, Pallas kernels: 64.6 us -> 49.5 us  [the longest x1 35.3 us: feed(): pl.pallas_call(feed_kernel, grid=(seq_len // BLOCK,), in_specs=[rows(widt...]
    convert_element_type x17 -> x6, other arithmetic: 7.07 us -> 0.1 us  [go(): sent = half(1 - high).astype(BF16)]
    add x5 -> x14, other arithmetic: 1.4 us -> 7.76 us  [the longest x10 6.35 us: half(): return cut[0] if len(cut) == 1 else cut[0].astype(F32) + cut[1].astype(F32)]
    another operation x35, other arithmetic: 7.24 us -> 2.8 us  [add(): self.buf = jnp.stack(pair, axis=self.axis + place)]
    slice x4 -> x0, local copies, waits for them, and re-layouts: 4.28 us -> none  [the longest x1 1.58 us: step_on_sequence(): spread = comm.factors(factors[:THOUGHTS].astype(BF16))]
    ppermute x40, starting transfers between devices: 48.7 us -> 44.6 us  [swap(): lax.ppermute(value, axis, [(i, i ^ bit) for i in range(self.sizes[axis])])]
  transfers between devices with their start and end apart: 43 -> 43, of which waited for: 16 -> 13; matrix products, arithmetic and copies ran while one was open for 10% -> 7% of each run, Pallas kernels for 39% -> 39%
where the time goes in v4:
time: 324 us; the launch traced here: 320 us
  Pallas kernels  184 us (57%)
  waiting for transfers between devices  46.2 us (14%)
  starting transfers between devices  44.7 us (14%)
  other arithmetic  17.6 us (5%)
  between operations  15.9 us (5%)
  local copies, waits for them, and re-layouts  11.3 us (3%)
    ppermute x40, waiting for transfers between devices, swap(): lax.ppermute(value, axis, [(i, i ^ bit) for i in range(self.sizes[axis])])  46.2 us
    ppermute x40, starting transfers between devices, swap(): lax.ppermute(value, axis, [(i, i ^ bit) for i in range(self.sizes[axis])])  44.6 us
    pallas_call x1, Pallas kernels, feed(): pl.pallas_call(feed_kernel, grid=(seq_len // BLOCK,), in_specs=[rows(widt...  35.3 us
    pallas_call x1, Pallas kernels, attend_back(): pl.pallas_call(attend_back_kernel, grid=(width // PAIR,), in_specs=[*(col...  25.6 us
    pallas_call x1, Pallas kernels, attend(): pl.pallas_call(attend_kernel, grid=(pairs,), in_specs=[pl.BlockSpec(memor...  25.3 us
    pallas_call x1, Pallas kernels, thoughts_back(): pl.pallas_call(thoughts_back_kernel, grid=(1,), in_specs=[pl.BlockSpec(me...  20.3 us
    pallas_call x1, Pallas kernels, thoughts_forward(): pl.pallas_call(thoughts_kernel, grid=(1,), in_specs=[pl.BlockSpec(memory_...  15.2 us
    pallas_call x1, Pallas kernels, near_terms(): pl.pallas_call(functools.partial(near_terms_kernel, sizes, chips_a, chips...  14.2 us
  transfers between devices with their start and end apart: 43, of which 13 were waited for; matrix products, arithmetic and copies ran while one was open for 7% of the time, Pallas kernels for 39%

profile of v4, /device:TPU:0, one launch (start us, length us, event | category | flops | bytes accessed | tf_op | source)
XLA Modules:
  0.0 319.7 jit_solution(10805610980975447634)
XLA Ops:
  7.2 2.2 units_split.1
  13.3 4.0 %collective-permute-start.10 = (bf16[8,128]{1,0:T(8,128)(2,1)S(1)}, bf16[8,128]{1,0:T(8,128)(2,1)S(1)}, u32[]{:S(2)}, u32[]{:S(2)}) collective-permute-start(bf16[8,128]{1,0:T(8,128)(2,1)S(1)} %convert_element_type.306), channel_id=1, source_target_pairs={{0,4},{1,5},{2,6},{3,7},{4,0},{5,1},{6,2},{7,3},{8,12},{9,13},{10,... | collective-permute-start | bytes 6152 | tf_op jit(solution)/shard_map/ppermute | solution.py:73
  17.5 3.0 collective-permute-start.5
  20.5 2.0 bitcast_convert_fusion.hid_in
  24.8 2.5 collective-permute-done.11
  31.0 3.2 %collective-permute-done.1 = bf16[3,2,24,384]{3,2,0,1:T(8,128)(2,1)S(1)} collective-permute-done((bf16[3,2,24,384]{3,2,0,1:T(8,128)(2,1)S(1)}, bf16[3,2,24,384]{3,2,0,1:T(8,128)(2,1)S(1)}, u32[]{:S(2)}, u32[]{:S(2)}) %collective-permute-start.1) | collective-permute-done | bytes 110624 | tf_op jit(solution)/shard_map/ppermute | solution.py:73
  34.2 2.2 collective-permute-done.6
  40.2 2.4 collective-permute-done.7
  42.7 2.3 collective-permute-start.8
  44.9 3.0 collective-permute-done.2
  48.2 2.0 collective-permute-start.13
  50.2 12.9 %collective-permute-done.8 = bf16[3,2,2,2,24,384]{5,4,0,2,3,1:T(8,128)(2,1)S(1)} collective-permute-done((bf16[3,2,2,2,24,384]{5,4,0,2,3,1:T(8,128)(2,1)S(1)}, bf16[3,2,2,2,24,384]{5,4,0,2,3,1:T(8,128)(2,1)S(1)}, u32[]{:S(2)}, u32[]{:S(2)}) %collective-permute-start.8) | collective-permute-done | bytes 442400 | tf_op jit(solution)/shard_map/ppermute | solution.py:73
  77.2 10.3 %first_norm_forward.1 = (bf16[3,1024,768]{2,1,0:T(8,128)(2,1)}, bf16[3,768,768]{2,1,0:T(8,128)(2,1)}) custom-call(s32[1]{0:T(128)} %bitcast.2.core_ref, bf16[1024,768]{1,0:T(8,128)(2,1)} %bitcast.298, bf16[3,16,24,384]{3,2,1,0:T(8,128)(2,1)} %bitcast.303, bf16[3,16,24,384]{3,2,1,0:T(8,128)(2,1)} %bitcast.305, bf16[3,16,24,384]{3,2,1,0:T(8,128)(2,1)} %bitcast.302, ...), custom_call_target="tpu_custom_call" | custom-call | flops 770499968 | bytes 2412000 | tf_op jit(solution)/shard_map/first_norm_forward/pallas_call | solution.py:1172
  87.5 25.3 %attention_forward.1 = (bf16[1024,768]{1,0:T(8,128)(2,1)}, f32[16,1024]{1,0:T(8,128)}) custom-call(s32[2]{0:T(128)} %pad_add_fusion.info_ref, bf16[3,1024,768]{2,1,0:T(8,128)(2,1)} %get-tuple-element.94.q_ref.k_ref.v_ref.qkv_in, bf16[3,1024,768]{2,1,0:T(8,128)(2,1)} %get-tuple-element.94.q_ref.k_ref.v_ref.qkv_in, ...), custom_call_target="tpu_custom_call" | custom-call | flops 2300000000 | bytes 7200000 | tf_op jit(solution)/shard_map/attention_forward/pallas_call | solution.py:256
  112.8 15.2 %thought_rows_forward.1 = (f32[16,1024]{1,0:T(8,128)}, f32[8,3072]{1,0:T(8,128)}, f32[32,384]{1,0:T(8,128)}, f32[8,768]{1,0:T(8,128)}, bf16[3,1024,768]{2,1,0:T(...) custom-call(s32[2]{0:T(128)} %pad_add_fusion.info_ref, ...), custom_call_target="tpu_custom_call", output_to_operand_aliasing={{4}: (8, {}), {5}: (9, {}), {6}: (10, {})} | custom-call | flops 2300000000 | bytes 7200000 | tf_op jit(solution)/shard_map/thought_rows_forward/pallas_call | solution.py:610
  128.0 35.3 %feed_forward_and_back.1 = (bf16[1024,768]{1,0:T(8,128)(2,1)}, bf16[1024,768]{1,0:T(8,128)(2,1)}, bf16[768,768]{1,0:T(8,128)(2,1)}, bf16[768,3072]{1,0:T(8,128)(...) custom-call(f32[1024,768]{1,0:T(8,128)} %get-tuple-element.100.hid_ref, ...), custom_call_target="tpu_custom_call" | custom-call | flops 3449999872 | bytes 10800000 | tf_op jit(solution)/shard_map/feed_forward_and_back/pallas_call | solution.py:919
  163.3 7.9 %proj_weight_terms.1 = bf16[8,4,4,24,768]{4,3,2,1,0:T(8,128)(2,1)} custom-call(bf16[768,3072]{1,0:T(8,128)(2,1)} %get-tuple-element.106.act_ref, bf16[768,768]{1,0:T(8,128)(2,1)} %bitcast_select_fusion.up_ref), custom_call_target="tpu_custom_call" | custom-call | flops 575000000 | bytes 1800000 | tf_op jit(solution)/shard_map/proj_weight_terms/pallas_call | solution.py:1127
  171.3 8.8 %fc_weight_terms.1 = (bf16[16,4,24,768]{3,2,1,0:T(8,128)(2,1)}, bf16[16,4,24,768]{3,2,1,0:T(8,128)(2,1)}) custom-call(s32[1]{0:T(128)} %bitcast.2.core_ref, bf16[768,768]{1,0:T(8,128)(2,1)} %get-tuple-element.107.second_ref, bf16[768,3072]{1,0:T(8,128)(2,1)} %get-tuple-element.108.pg_ref), custom_call_target="tpu_custom_call" | custom-call | flops 575000000 | bytes 1800000 | tf_op jit(solution)/shard_map/fc_weight_terms/pallas_call | solution.py:1097
  180.4 20.3 %thought_rows_backward.1 = (f32[8,3072]{1,0:T(8,128)}, bf16[32,768]{1,0:T(8,128)(2,1)}, bf16[768,768]{1,0:T(8,128)(2,1)}, f32[768,768]{1,0:T(8,128)}) custom-call(s32[2]{0:T(128)} %pad_add_fusion.info_ref, f32[1024,768]{1,0:T(8,128)} %get-tuple-element.100.hid_ref, ...), custom_call_target="tpu_custom_call", output_to_operand_aliasing={{2}: (12, {}), {3}: (13, {})} | custom-call | flops 2300000000 | bytes 7200000 | tf_op jit(solution)/shard_map/thought_rows_backward/pallas_call | solution.py:805
  202.1 2.3 convert_add_fusion
  205.9 2.6 collective-permute-start.17
  208.5 25.6 %attention_backward.1.grad_ref = bf16[3,1024,768]{2,1,0:T(8,128)(2,1)} custom-call(bf16[3,1024,768]{2,1,0:T(8,128)(2,1)} %get-tuple-element.103.qkv_ref.qkv_in.q_ref.k_ref.v_ref, bf16[3,1024,768]{2,1,0:T(8,128)(2,1)} %get-tuple-element.103.qkv_ref.qkv_in.q_ref.k_ref.v_ref, bf16[3,1024,768]{2,1,0:T(8,128)(2,1)} %get-tuple-element.103.qkv_ref.qkv_in.q_ref.k_ref.v_ref, ...), custom_call_target="tpu_custom_call" | custom-call | flops 2495500032 | bytes 7812000 | tf_op jit(solution)/shard_map/attention_backward/pallas_call | solution.py:334
  234.2 2.3 bitcast_add_fusion
  238.5 14.2 %near_weight_terms.1 = (bf16[16,2,24,768]{3,2,1,0:T(8,128)(2,1)}, bf16[16,2,24,768]{3,2,1,0:T(8,128)(2,1)}, bf16[16,2,24,768]{3,2,1,0:T(8,128)(2,1)}, bf16[16,2,...) custom-call(s32[1]{0:T(128)} %bitcast.2.core_ref, bf16[1024,768]{1,0:T(8,128)(2,1)} %get-tuple-element.127.normed_ref, ...), custom_call_target="tpu_custom_call" | custom-call | flops 575000000 | bytes 1800000 | tf_op jit(solution)/shard_map/near_weight_terms/pallas_call | solution.py:1059
  256.5 5.6 %collective-permute-done.23 = bf16[2,2,32,768]{3,2,0,1:T(8,128)(2,1)S(1)} collective-permute-done((bf16[2,2,32,768]{3,2,0,1:T(8,128)(2,1)S(1)}, bf16[2,2,32,768]{3,2,0,1:T(8,128)(2,1)S(1)}, u32[]{:S(2)}, u32[]{:S(2)}) %collective-permute-start.23) | collective-permute-done | bytes 196640 | tf_op jit(solution)/shard_map/ppermute | solution.py:73
  267.8 10.4 %first_norm_backward.1 = f32[1024,768]{1,0:T(8,128)} custom-call(s32[2]{0:T(128)} %pad_add_fusion.info_ref, f32[1024,768]{1,0:T(8,128)} %get-tuple-element.100.hid_ref, bf16[3,1024,768]{2,1,0:T(8,128)(2,1)} %attention_backward.1.grad_ref, f32[768,768]{1,0:T(8,128)} %get-tuple-element.128.rg_ref, bf16[3,768,768]{2,1,0:T(8,128)(2,1)} %get-tuple-element.97.near_in.near_ref, ...), custom_call_target="tpu_custom_call" | custom-call | flops 954499968 | bytes 2988000 | tf_op jit(solution)/shard_map/first_norm_backward/pallas_call | solution.py:980
  281.2 6.2 %collective-permute-done.26 = bf16[2,2,2,2,24,768]{5,4,3,2,1,0:T(8,128)(2,1)S(1)} collective-permute-done((bf16[2,2,2,2,24,768]{5,4,3,2,1,0:T(8,128)(2,1)S(1)}, bf16[2,2,2,2,24,768]{5,4,3,2,1,0:T(8,128)(2,1)S(1)}, u32[]{:S(2)}, u32[]{:S(2)}) %collective-permute-start.26) | collective-permute-done | bytes 589856 | tf_op jit(solution)/shard_map/ppermute | solution.py:73
  291.8 2.5 collective-permute-done.33
  296.5 2.0 copy.64
  298.5 4.0 %thought_rows_terms.1 = (f32[4,24,768]{2,1,0:T(8,128)}, f32[24,3072]{1,0:T(8,128)}) custom-call(s32[1]{0:T(128)} %bitcast.89.index_ref, bf16[32,32,768]{2,1,0:T(8,128)(2,1)} %bitcast.301, bf16[4,24,768]{2,1,0:T(8,128)(2,1)} %bitcast.313, f32[4,24,768]{2,1,0:T(8,128)} %bitcast_add_fusion.12.fc_ref, bf16[384,384]{1,0:T(8,128)(2,1)} %constant.301.clone.swap_ref), custom_call_target="tpu_custom_call" | custom-call | flops 379500000 | bytes 1188000 | tf_op jit(solution)/shard_map/thought_rows_terms/pallas_call | solution.py:1259
  303.3 2.3 collective-permute-start.38
  309.2 2.3 collective-permute-done.39
  (171 shorter events, 56.6 us)
Async XLA Ops:
  7.2 105.6 %all-gather.2.cloned.1.call-start = ((), (), s32[]{:S(2)}) async-start(), calls=%async_computation.2 | async-start | bytes 10948608 | tf_op jit(solution)/shard_map/all_gather | solution.py:1515
  11.2 227.2 %reduce-scatter.3.cloned.1.call-start = ((), (), s32[]{:S(2)}) async-start(), calls=%async_computation.3 | async-start | bytes 5308416 | tf_op jit(solution)/shard_map/reduce_scatter | solution.py:1538
  13.3 9.8 %collective-permute-start.10 = (bf16[8,128]{1,0:T(8,128)(2,1)S(1)}, bf16[8,128]{1,0:T(8,128)(2,1)S(1)}, u32[]{:S(2)}, u32[]{:S(2)}) collective-permute-start(bf16[8,128]{1,0:T(8,128)(2,1)S(1)} %convert_element_type.306), channel_id=1, source_target_pairs={{0,4},{1,5},{2,6},{3,7},{4,0},{5,1},{6,2},{7,3},{8,12},{9,13},{10,... | collective-permute-start | bytes 6152 | tf_op jit(solution)/shard_map/ppermute | solution.py:73
  17.4 9.9 %collective-permute-start = (bf16[3,24,384]{2,1,0:T(8,128)(2,1)S(1)}, bf16[3,24,384]{2,1,0:T(8,128)(2,1)S(1)}, u32[]{:S(2)}, u32[]{:S(2)}) collective-permute-start(bf16[3,24,384]{2,1,0:T(8,128)(2,1)S(1)} %pad_maximum_fusion.16), channel_id=1, source_target_pairs={{0,4},{1,5},{2,6},{3,7},{4,0},{5,1},{6,2},{7,3},{8,12},{9,13},{10,... | collective-permute-start | bytes 165896 | tf_op jit(solution)/shard_map/ppermute | solution.py:73
  17.5 11.0 %collective-permute-start.5 = (bf16[3,24,384]{2,1,0:T(8,128)(2,1)S(1)}, bf16[3,24,384]{2,1,0:T(8,128)(2,1)S(1)}, u32[]{:S(2)}, u32[]{:S(2)}) collective-permute-start(bf16[3,24,384]{2,1,0:T(8,128)(2,1)S(1)} %pad_maximum_fusion.17), channel_id=1, source_target_pairs={{0,4},{1,5},{2,6},{3,7},{4,0},{5,1},{6,2},{7,3},{8,12},{9,13},{10,... | collective-permute-start | bytes 165896 | tf_op jit(solution)/shard_map/ppermute | solution.py:73
  29.5 8.9 %collective-permute-start.12 = (bf16[2,2,8,128]{3,2,0,1:T(8,128)(2,1)S(1)}, bf16[2,2,8,128]{3,2,0,1:T(8,128)(2,1)S(1)}, u32[]{:S(2)}, u32[]{:S(2)}) collective-permute-start(bf16[2,2,8,128]{3,2,0,1:T(8,128)(2,1)S(1)} %pad_maximum_fusion.20), channel_id=1, source_target_pairs={{0,8},{8,0},{16,24},{24,16},{1,9},{9,1},{17,25},{25,17},{2,10},{10... | collective-permute-start | bytes 24584 | tf_op jit(solution)/shard_map/ppermute | solution.py:73
  38.5 9.4 %collective-permute-start.2 = (bf16[3,2,2,24,384]{4,3,0,1,2:T(8,128)(2,1)S(1)}, bf16[3,2,2,24,384]{4,3,0,1,2:T(8,128)(2,1)S(1)}, u32[]{:S(2)}, u32[]{:S(2)}) collective-permute-start(bf16[3,2,2,24,384]{4,3,0,1,2:T(8,128)(2,1)S(1)} %pad_maximum_fusion.8), channel_id=1, source_target_pairs={{0,8},{8,0},{16,24},{24,16},{1,9},{9,1},{17,25},{25,17},{2,10},{10... | collective-permute-start | bytes 663560 | tf_op jit(solution)/shard_map/ppermute | solution.py:73
  42.7 20.5 %collective-permute-start.8 = (bf16[3,2,2,2,24,384]{5,4,0,2,3,1:T(8,128)(2,1)S(1)}, bf16[3,2,2,2,24,384]{5,4,0,2,3,1:T(8,128)(2,1)S(1)}, u32[]{:S(2)}, u32[]{:S(2)}) collective-permute-start(bf16[3,2,2,2,24,384]{5,4,0,2,3,1:T(8,128)(2,1)S(1)} %pad_maximum_fusion.5), channel_id=1, source_target_pairs={{0,8},{8,0},{16,24},{24,16},{1,9},{9,1},{17,25},{25,17},{2,10},{10... | collective-permute-start | bytes 1327112 | tf_op jit(solution)/shard_map/ppermute | solution.py:73
  48.1 15.3 %collective-permute-start.3 = (bf16[3,2,2,2,24,384]{5,4,0,2,3,1:T(8,128)(2,1)S(1)}, bf16[3,2,2,2,24,384]{5,4,0,2,3,1:T(8,128)(2,1)S(1)}, u32[]{:S(2)}, u32[]{:S(2)}) collective-permute-start(bf16[3,2,2,2,24,384]{5,4,0,2,3,1:T(8,128)(2,1)S(1)} %pad_maximum_fusion.4), channel_id=1, source_target_pairs={{0,16},{8,24},{16,0},{24,8},{1,17},{9,25},{17,1},{25,9},{2,18},{10... | collective-permute-start | bytes 1327112 | tf_op jit(solution)/shard_map/ppermute | solution.py:73
  48.2 18.7 %collective-permute-start.13 = (bf16[2,2,2,8,128]{4,3,1,2,0:T(8,128)(2,1)S(1)}, bf16[2,2,2,8,128]{4,3,1,2,0:T(8,128)(2,1)S(1)}, u32[]{:S(2)}, u32[]{:S(2)}) collective-permute-start(bf16[2,2,2,8,128]{4,3,1,2,0:T(8,128)(2,1)S(1)} %pad_maximum_fusion.19), channel_id=1, source_target_pairs={{0,16},{8,24},{16,0},{24,8},{1,17},{9,25},{17,1},{25,9},{2,18},{10... | collective-permute-start | bytes 49160 | tf_op jit(solution)/shard_map/ppermute | solution.py:73
  63.3 11.8 %collective-permute-start.9 = (bf16[3,2,2,2,2,24,384]{6,5,0,3,4,1,2:T(8,128)(2,1)S(1)}, bf16[3,2,2,2,2,24,384]{6,5,0,3,4,1,2:T(8,128)(2,1)S(1)}, u32[]{:S(2)}, u32[]{:S(2)}) collective-permute-start(bf16[3,2,2,2,2,24,384]{6,5,0,3,4,1,2:T(8,128)(2,1)S(1)} %pad_maximum_fusion.2), channel_id=1, source_target_pairs={{0,1},{1,0},{2,3},{3,2},{4,5},{5,4},{6,7},{7,6},{8,9},{9,8},{10,11... | collective-permute-start | bytes 2654216 | tf_op jit(solution)/shard_map/ppermute | solution.py:73
  63.7 12.4 %collective-permute-start.4 = (bf16[3,2,2,2,2,24,384]{6,5,0,3,4,2,1:T(8,128)(2,1)S(1)}, bf16[3,2,2,2,2,24,384]{6,5,0,3,4,2,1:T(8,128)(2,1)S(1)}, u32[]{:S(2)}, u32[]{:S(2)}) collective-permute-start(bf16[3,2,2,2,2,24,384]{6,5,0,3,4,2,1:T(8,128)(2,1)S(1)} %pad_maximum_fusion.1), channel_id=1, source_target_pairs={{0,1},{1,0},{2,3},{3,2},{4,5},{5,4},{6,7},{7,6},{8,9},{9,8},{10,11... | collective-permute-start | bytes 2654216 | tf_op jit(solution)/shard_map/ppermute | solution.py:73
  171.2 127.3 %reduce-scatter.5.cloned.1.call-start = ((), (), s32[]{:S(2)}) async-start(), calls=%async_computation.4 | async-start | bytes 737280 | tf_op jit(solution)/shard_map/reduce_scatter | solution.py:1544
  180.0 20.7 %collective-permute-start.15 = (bf16[2,2,2,2,4,24,768]{6,5,4,3,2,1,0:T(8,128)(2,1)}, bf16[2,2,2,2,4,24,768]{6,5,4,3,2,1,0:T(8,128)(2,1)S(1)}, u32[]{:S(2)}, u32[]{:S(2)}) collective-permute-start(bf16[2,2,2,2,4,24,768]{6,5,4,3,2,1,0:T(8,128)(2,1)} %bitcast.317), channel_id=1, source_target_pairs={{0,1},{1,0},{2,3},{3,2},{4,5},{5,4},{6,7},{7,6},{8,9},{9,8},{10,11... | collective-permute-start | bytes 7077896 | tf_op jit(solution)/shard_map/ppermute | solution.py:73
  204.4 29.7 %collective-permute-start.16 = (bf16[2,2,2,4,24,768]{5,4,3,2,1,0:T(8,128)(2,1)S(1)}, bf16[2,2,2,4,24,768]{5,4,3,2,1,0:T(8,128)(2,1)}, u32[]{:S(2)}, u32[]{:S(2)}) collective-permute-start(bf16[2,2,2,4,24,768]{5,4,3,2,1,0:T(8,128)(2,1)S(1)} %get-tuple-element.171), channel_id=1, source_target_pairs={{0,8},{8,0},{16,24},{24,16},{1,9},{9,1},{17,25},{25,17},{2,10},{10... | collective-permute-start | bytes 3538952 | tf_op jit(solution)/shard_map/ppermute | solution.py:73
  205.9 28.2 %collective-permute-start.17 = (bf16[32,768]{1,0:T(8,128)(2,1)}, bf16[32,768]{1,0:T(8,128)(2,1)S(1)}, u32[]{:S(2)}, u32[]{:S(2)}) collective-permute-start(bf16[32,768]{1,0:T(8,128)(2,1)} %get-tuple-element.120), channel_id=1, source_target_pairs={{0,4},{1,5},{2,6},{3,7},{4,0},{5,1},{6,2},{7,3},{8,12},{9,13},{10,... | collective-permute-start | bytes 147464 | tf_op jit(solution)/shard_map/ppermute | solution.py:73
  236.5 18.6 %collective-permute-start.22 = (bf16[2,2,4,24,768]{4,3,2,1,0:T(8,128)(2,1)}, bf16[2,2,4,24,768]{4,3,2,1,0:T(8,128)(2,1)S(1)}, u32[]{:S(2)}, u32[]{:S(2)}) collective-permute-start(bf16[2,2,4,24,768]{4,3,2,1,0:T(8,128)(2,1)} %get-tuple-element.173), channel_id=1, source_target_pairs={{0,16},{8,24},{16,0},{24,8},{1,17},{9,25},{17,1},{25,9},{2,18},{10... | collective-permute-start | bytes 1769480 | tf_op jit(solution)/shard_map/ppermute | solution.py:73
  237.2 17.1 %collective-permute-start.19 = (bf16[2,32,768]{2,1,0:T(8,128)(2,1)S(1)}, bf16[2,32,768]{2,1,0:T(8,128)(2,1)S(1)}, u32[]{:S(2)}, u32[]{:S(2)}) collective-permute-start(bf16[2,32,768]{2,1,0:T(8,128)(2,1)S(1)} %pad_maximum_fusion.14), channel_id=1, source_target_pairs={{0,2},{1,3},{2,0},{3,1},{4,6},{5,7},{6,4},{7,5},{8,10},{9,11},{10,... | collective-permute-start | bytes 294920 | tf_op jit(solution)/shard_map/ppermute | solution.py:73
  253.7 10.7 %collective-permute-start.20 = (bf16[2,2,2,2,2,24,768]{6,5,4,3,2,1,0:T(8,128)(2,1)}, bf16[2,2,2,2,2,24,768]{6,5,4,3,2,1,0:T(8,128)(2,1)S(1)}, u32[]{:S(2)}, u32[]{:S(2)}) collective-permute-start(bf16[2,2,2,2,2,24,768]{6,5,4,3,2,1,0:T(8,128)(2,1)} %bitcast.320), channel_id=1, source_target_pairs={{0,1},{1,0},{2,3},{3,2},{4,5},{5,4},{6,7},{7,6},{8,9},{9,8},{10,11... | collective-permute-start | bytes 3538952 | tf_op jit(solution)/shard_map/ppermute | solution.py:73
  254.2 10.2 %collective-permute-start.18 = (bf16[2,2,2,2,2,24,768]{6,5,4,3,2,1,0:T(8,128)(2,1)}, bf16[2,2,2,2,2,24,768]{6,5,4,3,2,1,0:T(8,128)(2,1)S(1)}, u32[]{:S(2)}, u32[]{:S(2)}) collective-permute-start(bf16[2,2,2,2,2,24,768]{6,5,4,3,2,1,0:T(8,128)(2,1)} %bitcast.319), channel_id=1, source_target_pairs={{0,1},{1,0},{2,3},{3,2},{4,5},{5,4},{6,7},{7,6},{8,9},{9,8},{10,11... | collective-permute-start | bytes 3538952 | tf_op jit(solution)/shard_map/ppermute | solution.py:73
  256.0 22.5 %collective-permute-start.28 = (bf16[2,4,24,768]{3,2,1,0:T(8,128)(2,1)}, bf16[2,4,24,768]{3,2,1,0:T(8,128)(2,1)S(1)}, u32[]{:S(2)}, u32[]{:S(2)}) collective-permute-start(bf16[2,4,24,768]{3,2,1,0:T(8,128)(2,1)} %get-tuple-element.183), channel_id=1, source_target_pairs={{0,2},{1,3},{2,0},{3,1},{4,6},{5,7},{6,4},{7,5},{8,10},{9,11},{10,... | collective-permute-start | bytes 884744 | tf_op jit(solution)/shard_map/ppermute | solution.py:73
  262.2 16.0 %collective-permute-start.29 = (bf16[2,2,2,32,768]{4,3,1,2,0:T(8,128)(2,1)S(1)}, bf16[2,2,2,32,768]{4,3,1,2,0:T(8,128)(2,1)S(1)}, u32[]{:S(2)}, u32[]{:S(2)}) collective-permute-start(bf16[2,2,2,32,768]{4,3,1,2,0:T(8,128)(2,1)S(1)} %pad_maximum_fusion.6), channel_id=1, source_target_pairs={{0,16},{8,24},{16,0},{24,8},{1,17},{9,25},{17,1},{25,9},{2,18},{10... | collective-permute-start | bytes 1179656 | tf_op jit(solution)/shard_map/ppermute | solution.py:73
  262.9 15.5 %collective-permute-start.24 = (bf16[2,2,2,8,128]{4,3,1,2,0:T(8,128)(2,1)S(1)}, bf16[2,2,2,8,128]{4,3,1,2,0:T(8,128)(2,1)S(1)}, u32[]{:S(2)}, u32[]{:S(2)}) collective-permute-start(bf16[2,2,2,8,128]{4,3,1,2,0:T(8,128)(2,1)S(1)} %get-tuple-element.231), channel_id=1, source_target_pairs={{0,16},{8,24},{16,0},{24,8},{1,17},{9,25},{17,1},{25,9},{2,18},{10... | collective-permute-start | bytes 49160 | tf_op jit(solution)/shard_map/ppermute | solution.py:73
  264.7 15.4 %collective-permute-start.27 = (bf16[2,2,2,2,24,768]{5,4,3,2,1,0:T(8,128)(2,1)S(1)}, bf16[2,2,2,2,24,768]{5,4,3,2,1,0:T(8,128)(2,1)S(1)}, u32[]{:S(2)}, u32[]{:S(2)}) collective-permute-start(bf16[2,2,2,2,24,768]{5,4,3,2,1,0:T(8,128)(2,1)S(1)} %get-tuple-element.175), channel_id=1, source_target_pairs={{0,8},{8,0},{16,24},{24,16},{1,9},{9,1},{17,25},{25,17},{2,10},{10... | collective-permute-start | bytes 1769480 | tf_op jit(solution)/shard_map/ppermute | solution.py:73
  266.4 21.0 %collective-permute-start.26 = (bf16[2,2,2,2,24,768]{5,4,3,2,1,0:T(8,128)(2,1)S(1)}, bf16[2,2,2,2,24,768]{5,4,3,2,1,0:T(8,128)(2,1)S(1)}, u32[]{:S(2)}, u32[]{:S(2)}) collective-permute-start(bf16[2,2,2,2,24,768]{5,4,3,2,1,0:T(8,128)(2,1)S(1)} %get-tuple-element.177), channel_id=1, source_target_pairs={{0,16},{8,24},{16,0},{24,8},{1,17},{9,25},{17,1},{25,9},{2,18},{10... | collective-permute-start | bytes 1769480 | tf_op jit(solution)/shard_map/ppermute | solution.py:73
  278.5 11.2 %collective-permute-start.31 = (bf16[2,2,2,2,32,768]{5,4,2,3,1,0:T(8,128)(2,1)S(1)}, bf16[2,2,2,2,32,768]{5,4,2,3,1,0:T(8,128)(2,1)S(1)}, u32[]{:S(2)}, u32[]{:S(2)}) collective-permute-start(bf16[2,2,2,2,32,768]{5,4,2,3,1,0:T(8,128)(2,1)S(1)} %pad_maximum_fusion.3), channel_id=1, source_target_pairs={{0,1},{1,0},{2,3},{3,2},{4,5},{5,4},{6,7},{7,6},{8,9},{9,8},{10,11... | collective-permute-start | bytes 2359304 | tf_op jit(solution)/shard_map/ppermute | solution.py:73
  278.6 10.3 %collective-permute-start.32 = (bf16[4,24,768]{2,1,0:T(8,128)(2,1)S(1)}, bf16[4,24,768]{2,1,0:T(8,128)(2,1)S(1)}, u32[]{:S(2)}, u32[]{:S(2)}) collective-permute-start(bf16[4,24,768]{2,1,0:T(8,128)(2,1)S(1)} %fusion.14), channel_id=1, source_target_pairs={{0,4},{1,5},{2,6},{3,7},{4,0},{5,1},{6,2},{7,3},{8,12},{9,13},{10,... | collective-permute-start | bytes 442376 | tf_op jit(solution)/shard_map/ppermute | solution.py:73
  279.0 9.8 %collective-permute-start.25 = (bf16[2,2,8,128]{3,2,0,1:T(8,128)(2,1)S(1)}, bf16[2,2,8,128]{3,2,0,1:T(8,128)(2,1)S(1)}, u32[]{:S(2)}, u32[]{:S(2)}) collective-permute-start(bf16[2,2,8,128]{3,2,0,1:T(8,128)(2,1)S(1)} %get-tuple-element.228), channel_id=1, source_target_pairs={{0,8},{8,0},{16,24},{24,16},{1,9},{9,1},{17,25},{25,17},{2,10},{10... | collective-permute-start | bytes 24584 | tf_op jit(solution)/shard_map/ppermute | solution.py:73
  280.3 11.5 %collective-permute-start.34 = (bf16[2,2,2,24,768]{4,3,2,1,0:T(8,128)(2,1)S(1)}, bf16[2,2,2,24,768]{4,3,2,1,0:T(8,128)(2,1)S(1)}, u32[]{:S(2)}, u32[]{:S(2)}) collective-permute-start(bf16[2,2,2,24,768]{4,3,2,1,0:T(8,128)(2,1)S(1)} %get-tuple-element.179), channel_id=1, source_target_pairs={{0,16},{8,24},{16,0},{24,8},{1,17},{9,25},{17,1},{25,9},{2,18},{10... | collective-permute-start | bytes 884744 | tf_op jit(solution)/shard_map/ppermute | solution.py:73
  288.9 13.7 %collective-permute-start.30 = (bf16[2,8,128]{2,1,0:T(8,128)(2,1)S(1)}, bf16[2,8,128]{2,1,0:T(8,128)(2,1)S(1)}, u32[]{:S(2)}, u32[]{:S(2)}) collective-permute-start(bf16[2,8,128]{2,1,0:T(8,128)(2,1)S(1)} %get-tuple-element.234), channel_id=1, source_target_pairs={{0,2},{1,3},{2,0},{3,1},{4,6},{5,7},{6,4},{7,5},{8,10},{9,11},{10,... | collective-permute-start | bytes 12296 | tf_op jit(solution)/shard_map/ppermute | solution.py:73
  294.3 8.9 %collective-permute-start.37 = (bf16[2,2,24,768]{3,2,1,0:T(8,128)(2,1)S(1)}, bf16[2,2,24,768]{3,2,1,0:T(8,128)(2,1)S(1)}, u32[]{:S(2)}, u32[]{:S(2)}) collective-permute-start(bf16[2,2,24,768]{3,2,1,0:T(8,128)(2,1)S(1)} %get-tuple-element.187), channel_id=1, source_target_pairs={{0,2},{1,3},{2,0},{3,1},{4,6},{5,7},{6,4},{7,5},{8,10},{9,11},{10,... | collective-permute-start | bytes 442376 | tf_op jit(solution)/shard_map/ppermute | solution.py:73
  294.7 8.6 %collective-permute-start.36 = (bf16[2,2,24,768]{3,2,1,0:T(8,128)(2,1)S(1)}, bf16[2,2,24,768]{3,2,1,0:T(8,128)(2,1)S(1)}, u32[]{:S(2)}, u32[]{:S(2)}) collective-permute-start(bf16[2,2,24,768]{3,2,1,0:T(8,128)(2,1)S(1)} %get-tuple-element.189), channel_id=1, source_target_pairs={{0,2},{1,3},{2,0},{3,1},{4,6},{5,7},{6,4},{7,5},{8,10},{9,11},{10,... | collective-permute-start | bytes 442376 | tf_op jit(solution)/shard_map/ppermute | solution.py:73
  (22 other events, 155.7 us)
Sparse Core Ops, SparseCore 0:
  11.3 100.1 all-gather.1
  171.3 56.1 reduce-scatter.2
  238.6 25.5 reduce-scatter.4

commit v5 on v4

--- a/solution.py
+++ b/solution.py
@@ -19,7 +19,7 @@
 HEAD_ROWS = 16
 WINDOW = 32
 LANES = 128
-FACTOR_ROWS = 32
+FACTOR_ROWS = 24
 PAIR = 2 * HD
 NEG = -1e30
 
@@ -91,6 +91,18 @@
             order.append(chip)
         return order
 
+    def spots(self, text):
+        stages = [c for c in reversed(self.order(text)) if c not in self.groups["c"]]
+        rest = [c for c in self.canon if c in stages]
+        order = []
+        for spot in range(1 << len(stages)):
+            chip = 0
+            for at, stage in enumerate(stages):
+                if spot & (1 << (len(stages) - 1 - at)):
+                    chip |= 1 << (len(rest) - 1 - rest.index(stage))
+            order.append(chip)
+        return order
+
     def scatter(self, value, text):
         return Scatter(self, value, text)
 
@@ -130,11 +142,14 @@
         self.add()
 
     def last(self):
-        while self.todo:
-            self.go()
-        shape = self.shape
-        shape = shape[: self.axis] + (-1,) + shape[self.axis :]
-        return [self.buf.reshape(shape), self.got.reshape(shape)]
+        for stage in self.todo:
+            if self.got is not None:
+                high = self.links.mine(self.stage)
+                pair = [jnp.where(high, self.got, self.buf), jnp.where(high, self.buf, self.got)]
+                self.buf = jnp.concatenate(pair, axis=0)
+            self.stage = stage
+            self.got = self.links.swap(self.buf, stage)
+        return [self.buf, self.got]
 
     def finish(self):
         while self.todo:
@@ -698,21 +713,31 @@
     high = product.astype(BF16)
     ones = by_head(jnp.ones((1, width), F32), HEAD_ROWS).astype(BF16)
     delta = dot_nt(ones, high) + dot_nt(ones, (product - high.astype(F32)).astype(BF16))
-    row_pos = QUESTION + lax.broadcasted_iota(jnp.int32, (HEAD_ROWS, rows), 1)
     lse = lse_ref[:, QUESTION:]
 
-    def at_slot(at):
-        local = at - QUESTION
-        key = by_head(pick(qkv_ref[1, QUESTION:PREFIX, :], local) * SCALE, HEAD_ROWS)
-        value = by_head(pick(qkv_ref[2, QUESTION:PREFIX, :], local), HEAD_ROWS)
-        scores = dot_nt(key.astype(BF16), late_q)
-        probs = jnp.where(row_pos >= at, jnp.exp(jnp.minimum(scores - lse, 0.0)), 0.0)
-        prob_grad = dot_nt(value.astype(BF16), mixed_grad)
-        score_grad = (probs * (prob_grad - delta)).astype(BF16)
-        return (
-            heads_only(dot(score_grad, late_q)) * SCALE,
-            heads_only(dot(probs.astype(BF16), mixed_grad)),
-        )
+    def columns(block, scale):
+        rows_here = [
+            by_head(pick(block, slot + j - QUESTION) * scale, HEAD_ROWS) for j in range(THOUGHTS)
+        ]
+        return jnp.concatenate(rows_here, axis=0).astype(BF16)
+
+    def twice(block):
+        return jnp.concatenate([block] * THOUGHTS, axis=0)
+
+    slot_pos = jnp.concatenate(
+        [jnp.full((HEAD_ROWS, rows), QUESTION - j, jnp.int32) for j in range(THOUGHTS)], axis=0
+    )
+    seen = slot_pos + lax.broadcasted_iota(jnp.int32, slot_pos.shape, 1) >= slot
+    scores = dot_nt(columns(qkv_ref[1, QUESTION:PREFIX, :], SCALE), late_q)
+    probs = jnp.where(seen, jnp.exp(jnp.minimum(scores - twice(lse), 0.0)), 0.0)
+    prob_grad = dot_nt(columns(qkv_ref[2, QUESTION:PREFIX, :], 1.0), mixed_grad)
+    score_grad = (probs * (prob_grad - twice(delta))).astype(BF16)
+    slot_keys = dot(score_grad, late_q)
+    slot_values = dot(probs.astype(BF16), mixed_grad)
+    slot_grads = []
+    for j in range(THOUGHTS):
+        span = slice(j * HEAD_ROWS, (j + 1) * HEAD_ROWS)
+        slot_grads.append((heads_only(slot_keys[span]) * SCALE, heads_only(slot_values[span])))
 
     def through_first(at, query_grad, key_grad, value_grad):
         first_grad = (
@@ -725,9 +750,8 @@
 
     sum_ref[...] = jnp.zeros_like(sum_ref)
     fac = {}
-    slot_grads = at_slot(slot + 1)
     loads[4].wait()
-    carried = through_first(slot + 1, jnp.zeros((1, width), F32), *slot_grads)
+    carried = through_first(slot + 1, jnp.zeros((1, width), F32), *slot_grads[1])
     for copy in loads[5:]:
         copy.wait()
     for step in reversed(range(THOUGHTS)):
@@ -768,7 +792,7 @@
             own_delta = jnp.sum(prob_grad * probs, axis=1, keepdims=True)
             score_grad = (probs * (prob_grad - own_delta)).astype(BF16)
             query_grad = heads_only(dot(score_grad, qkv_ref[1])) * SCALE
-            key_grad, value_grad = at_slot(at)
+            key_grad, value_grad = slot_grads[0]
             own = lax.broadcasted_iota(jnp.int32, probs.shape, 1) == at
             score_own = jnp.sum(jnp.where(own, score_grad.astype(F32), 0.0), axis=1, keepdims=True)
             prob_own = jnp.sum(jnp.where(own, probs, 0.0), axis=1, keepdims=True)
@@ -1140,7 +1164,7 @@
 
 
 def first_kernel(
-    core_ref, tok_ref, left_mine, left_got, right_mine, right_got, vec_ref, qkvb_ref, qkv_ref,
+    orders, core_ref, tok_ref, left_mine, left_got, right_mine, right_got, vec_ref, qkvb_ref, qkv_ref,
     near_ref, rows_ref,
 ):
     width = tok_ref.shape[1]
@@ -1148,12 +1172,12 @@
     @pl.when(pl.program_id(0) == 0)
     def _():
         even_is_mine = core_ref[0] == 0
-        chips, own, half = left_mine.shape[1:]
+        own, half = left_mine.shape[2:]
         for i in range(3):
             for side, (mine, got) in enumerate([(left_mine, left_got), (right_mine, right_got)]):
-                for chip in range(chips):
-                    a = mine[i, chip].astype(F32)
-                    b = got[i, chip].astype(F32)
+                for spot, chip in enumerate(orders[side]):
+                    a = mine[spot, i].astype(F32)
+                    b = got[spot, i].astype(F32)
                     begin = 2 * chip * own
                     rows_ref[begin : begin + own, :] = jnp.where(even_is_mine, a, b)
                     rows_ref[begin + own : begin + 2 * own, :] = jnp.where(even_is_mine, b, a)
@@ -1166,11 +1190,11 @@
         qkv_ref[i] = (dot(first, near_ref[i]) + qkvb_ref[:, span]).astype(BF16)
 
 
-def first_forward(core, tokens, pieces, vec, qkv_bias):
+def first_forward(core, tokens, pieces, orders, vec, qkv_bias):
     seq_len, width = tokens.shape
     near = jax.ShapeDtypeStruct((3, width, width), BF16)
     return pl.pallas_call(
-        first_kernel,
+        functools.partial(first_kernel, orders),
         grid=(seq_len // BLOCK,),
         in_specs=[
             pl.BlockSpec(memory_space=pltpu.SMEM),
@@ -1197,10 +1221,10 @@
     return group, jnp.asarray(swap, BF16)
 
 
-def split_units_kernel(blocks, span, fc_ref, swap_ref, out_ref):
-    own = fc_ref.shape[0]
+def far_shard_kernel(blocks, span, fc_ref, proj_ref, out_w_ref, swap_ref, out_ref):
+    own, width = out_w_ref.shape
     size = swap_ref.shape[0]
-    groups = out_ref.shape[2] // span
+    groups = width // span
     rows = [fc_ref[:, g * size : (g + 1) * size].astype(F32) for g in range(groups)]
     swapped = dot(jnp.concatenate(rows, axis=0).astype(BF16), swap_ref[...])
     for g in range(groups):
@@ -1208,17 +1232,21 @@
         for j in range(blocks):
             piece = part[:, j * span : (j + 1) * span]
             out_ref[j, :, g * span : (g + 1) * span] = piece.astype(BF16)
-
-
-def split_units(fc_shard, blocks):
-    own, units = fc_shard.shape
+    for j in range(blocks):
+        out_ref[blocks + j] = proj_ref[j]
+    out_ref[2 * blocks] = out_w_ref[...]
+
+
+def join_far(fc_shard, proj_shard, out_shard):
+    own, width = out_shard.shape
+    blocks = fc_shard.shape[1] // width
     group, swap = group_of(blocks, own)
     return pl.pallas_call(
-        functools.partial(split_units_kernel, blocks, group * own),
-        out_shape=jax.ShapeDtypeStruct((blocks, own, units // blocks), BF16),
+        functools.partial(far_shard_kernel, blocks, group * own),
+        out_shape=jax.ShapeDtypeStruct((2 * blocks + 1, own, width), BF16),
         compiler_params=pltpu.CompilerParams(vmem_limit_bytes=VMEM_LIMIT),
-        name="units_split",
-    )(fc_shard, swap)
+        name="far_shard",
+    )(fc_shard, proj_shard.reshape(blocks, own, width), out_shard, swap)
 
 
 def row_terms_kernel(span, index_ref, fac_ref, proj_ref, fc_ref, swap_ref, proj_out, fc_out):
@@ -1377,7 +1405,9 @@
     seq_len, width = tokens.shape
     info = jnp.stack([slots[0], count])
 
-    qkv_first, near = first_forward(comm.core, tokens, near_pieces, vec, qkv_bias)
+    qkv_first, near = first_forward(
+        comm.core, tokens, near_pieces, comm.near_orders, vec, qkv_bias
+    )
     mixed_hidden, lse_hidden = attend(info, qkv_first)
     late = QUESTION + lax.iota(jnp.int32, seq_len - QUESTION)
     upstream_low = jnp.where(
@@ -1436,13 +1466,15 @@
     rest = comm.scatter(terms[2:], "zyxc")
     vectors_going = comm.scatter_vectors(packed)
 
-    sent = go_after([first, rest, vectors_going])
-    join_after([spread], *sent)
-    sent = go_after([spread])
-    going = [first, rest, vectors_going, fc_going, spread]
+    join_after([fc_going, spread], packed)
+
+    going = [first, rest, vectors_going]
+    sent = go_after(going, fc_going.got, spread.buf)
+    sent += go_after([fc_going, spread], *sent)
     join_after(going, *sent)
     sent = go_after(going)
     input_grad = first_back(info, hidden, after(qkv_grad, *sent), resid_grad, weights, vec)
+    going += [fc_going, spread]
     join_after(going, input_grad)
     proj_g = fc_g = None
     while any(swap.todo for swap in going) or proj_g is None:
@@ -1504,29 +1536,24 @@
     blocks = proj_weight.shape[0] // own
     both = ("dp", "fsdp")
 
-    far_shard = jnp.concatenate(
-        [
-            split_units(fc_weight, blocks),
-            proj_weight.reshape(blocks, own, width),
-            out_weight[None],
-        ],
-        axis=0,
-    )
+    far_shard = join_far(fc_weight, proj_weight, out_weight)
     far = lax.all_gather(far_shard, both, axis=1, tiled=True)
 
     packed = join([small_shards[n] for n in SMALL]).astype(BF16)
     small = links.gather(packed, "zxyc", axis=0).reshape(devices, len(sizes), LANES)
     half = width // 2
     near_pieces = []
-    for side, text in enumerate(("zxyc", "zyxc")):
+    near_texts = ("zxyc", "zyxc")
+    for side, text in enumerate(near_texts):
         part_columns = [
             qkv_weight[:, i * width + side * half : i * width + (side + 1) * half] for i in range(3)
         ]
-        ring = Gather(links, jnp.stack(part_columns), text, axis=1)
+        ring = Gather(links, jnp.stack(part_columns)[None], text)
         near_pieces += ring.last()
 
     class Comm:
         chips = links.chips
+        near_orders = [links.spots(text) for text in near_texts]
         core = (lax.axis_index("fsdp") % 2)[None].astype(jnp.int32)
 
         @staticmethod
@@ -1550,7 +1577,7 @@
 
         @staticmethod
         def factors(rows):
-            return Gather(links, rows, "zxyc")
+            return Gather(links, rows, "zyxc")
 
         @staticmethod
         def scatter_vectors(value):

time: 324 us -> 319 us (0.985)
  waiting for transfers between devices: 46.2 us -> 37.8 us
  other arithmetic: 17.6 us -> 21.1 us
    ppermute x40, waiting for transfers between devices: 46.2 us -> 37.7 us  [swap(): lax.ppermute(value, axis, [(i, i ^ bit) for i in range(self.sizes[axis])])]
where the time goes in v5:
time: 319 us; the launch traced here: 315 us
  Pallas kernels  184 us (58%)
  starting transfers between devices  46.4 us (15%)
  waiting for transfers between devices  37.8 us (12%)
  other arithmetic  21.1 us (7%)
  between operations  15.9 us (5%)
  local copies, waits for them, and re-layouts  9.7 us (3%)
    ppermute x40, starting transfers between devices, swap(): lax.ppermute(value, axis, [(i, i ^ bit) for i in range(self.sizes[axis])])  46.3 us
    ppermute x40, waiting for transfers between devices, swap(): lax.ppermute(value, axis, [(i, i ^ bit) for i in range(self.sizes[axis])])  37.7 us
    pallas_call x1, Pallas kernels, feed(): pl.pallas_call(feed_kernel, grid=(seq_len // BLOCK,), in_specs=[rows(widt...  35.3 us
    pallas_call x1, Pallas kernels, attend_back(): pl.pallas_call(attend_back_kernel, grid=(width // PAIR,), in_specs=[*(col...  25.7 us
    pallas_call x1, Pallas kernels, attend(): pl.pallas_call(attend_kernel, grid=(pairs,), in_specs=[pl.BlockSpec(memor...  25.3 us
    pallas_call x1, Pallas kernels, thoughts_back(): pl.pallas_call(thoughts_back_kernel, grid=(1,), in_specs=[pl.BlockSpec(me...  19.3 us
    pallas_call x1, Pallas kernels, thoughts_forward(): pl.pallas_call(thoughts_kernel, grid=(1,), in_specs=[pl.BlockSpec(memory_...  15.2 us
    pallas_call x1, Pallas kernels, near_terms(): pl.pallas_call(functools.partial(near_terms_kernel, sizes, chips_a, chips...  14.2 us
  transfers between devices with their start and end apart: 43, of which 13 were waited for; matrix products, arithmetic and copies ran while one was open for 7% of the time, Pallas kernels for 39%

profile of v5, /device:TPU:0, one launch (start us, length us, event | category | flops | bytes accessed | tf_op | source)
XLA Modules:
  0.0 314.9 jit_solution(7011096631771326808)
XLA Ops:
  7.2 2.3 far_shard.1
  11.7 4.0 %collective-permute-start.10 = (bf16[8,128]{1,0:T(8,128)(2,1)S(1)}, bf16[8,128]{1,0:T(8,128)(2,1)S(1)}, u32[]{:S(2)}, u32[]{:S(2)}) collective-permute-start(bf16[8,128]{1,0:T(8,128)(2,1)S(1)} %convert_element_type.306), channel_id=1, source_target_pairs={{0,4},{1,5},{2,6},{3,7},{4,0},{5,1},{6,2},{7,3},{8,12},{9,13},{10,... | collective-permute-start | bytes 6152 | tf_op jit(solution)/shard_map/ppermute | solution.py:73
  15.9 3.0 collective-permute-start.5
  18.9 2.0 bitcast_convert_fusion.hid_in
  23.2 2.0 collective-permute-done.11
  29.0 3.9 %collective-permute-done.1 = bf16[2,3,24,384]{3,2,1,0:T(8,128)(2,1)S(1)} collective-permute-done((bf16[2,3,24,384]{3,2,1,0:T(8,128)(2,1)S(1)}, bf16[2,3,24,384]{3,2,1,0:T(8,128)(2,1)S(1)}, u32[]{:S(2)}, u32[]{:S(2)}) %collective-permute-start.1) | collective-permute-done | bytes 110624 | tf_op jit(solution)/shard_map/ppermute | solution.py:73
  32.9 3.5 %collective-permute-done.6 = bf16[2,3,24,384]{3,2,1,0:T(8,128)(2,1)S(1)} collective-permute-done((bf16[2,3,24,384]{3,2,1,0:T(8,128)(2,1)S(1)}, bf16[2,3,24,384]{3,2,1,0:T(8,128)(2,1)S(1)}, u32[]{:S(2)}, u32[]{:S(2)}) %collective-permute-start.6) | collective-permute-done | bytes 110624 | tf_op jit(solution)/shard_map/ppermute | solution.py:73
  36.5 1.7 collective-permute-start.7
  39.8 2.7 collective-permute-done.7
  44.2 3.6 %collective-permute-done.2 = bf16[4,3,24,384]{3,2,1,0:T(8,128)(2,1)S(1)} collective-permute-done((bf16[4,3,24,384]{3,2,1,0:T(8,128)(2,1)S(1)}, bf16[4,3,24,384]{3,2,1,0:T(8,128)(2,1)S(1)}, u32[]{:S(2)}, u32[]{:S(2)}) %collective-permute-start.2) | collective-permute-done | bytes 221216 | tf_op jit(solution)/shard_map/ppermute | solution.py:73
  48.0 2.0 collective-permute-start.13
  50.0 12.8 %collective-permute-done.8 = bf16[8,3,24,384]{3,2,1,0:T(8,128)(2,1)S(1)} collective-permute-done((bf16[8,3,24,384]{3,2,1,0:T(8,128)(2,1)S(1)}, bf16[8,3,24,384]{3,2,1,0:T(8,128)(2,1)S(1)}, u32[]{:S(2)}, u32[]{:S(2)}) %collective-permute-start.8) | collective-permute-done | bytes 442400 | tf_op jit(solution)/shard_map/ppermute | solution.py:73
  71.2 1.8 vectors_unpack.1
  74.2 11.3 %first_norm_forward.1 = (bf16[3,1024,768]{2,1,0:T(8,128)(2,1)}, bf16[3,768,768]{2,1,0:T(8,128)(2,1)}) custom-call(s32[1]{0:T(128)} %bitcast.2.core_ref, bf16[1024,768]{1,0:T(8,128)(2,1)} %bitcast.273, bf16[16,3,24,384]{3,2,1,0:T(8,128)(2,1)} %copy-done.2, bf16[16,3,24,384]{3,2,1,0:T(8,128)(2,1)} %copy-done.9, bf16[16,3,24,384]{3,2,1,0:T(8,128)(2,1)} %copy-done.1, ...), custom_call_target="tpu_custom_call" | custom-call | flops 770499968 | bytes 2412000 | tf_op jit(solution)/shard_map/first_norm_forward/pallas_call | solution.py:1196
  85.5 25.3 %attention_forward.1 = (bf16[1024,768]{1,0:T(8,128)(2,1)}, f32[16,1024]{1,0:T(8,128)}) custom-call(s32[2]{0:T(128)} %pad_add_fusion.info_ref, bf16[3,1024,768]{2,1,0:T(8,128)(2,1)} %get-tuple-element.99.q_ref.k_ref.v_ref.qkv_in, bf16[3,1024,768]{2,1,0:T(8,128)(2,1)} %get-tuple-element.99.q_ref.k_ref.v_ref.qkv_in, ...), custom_call_target="tpu_custom_call" | custom-call | flops 2300000000 | bytes 7200000 | tf_op jit(solution)/shard_map/attention_forward/pallas_call | solution.py:271
  110.9 15.2 %thought_rows_forward.1 = (f32[16,1024]{1,0:T(8,128)}, f32[8,3072]{1,0:T(8,128)}, f32[32,384]{1,0:T(8,128)}, f32[8,768]{1,0:T(8,128)}, bf16[3,1024,768]{2,1,0:T(...) custom-call(s32[2]{0:T(128)} %pad_add_fusion.info_ref, ...), custom_call_target="tpu_custom_call", output_to_operand_aliasing={{4}: (8, {}), {5}: (9, {}), {6}: (10, {})} | custom-call | flops 2300000000 | bytes 7200000 | tf_op jit(solution)/shard_map/thought_rows_forward/pallas_call | solution.py:625
  126.0 35.3 %feed_forward_and_back.1 = (bf16[1024,768]{1,0:T(8,128)(2,1)}, bf16[1024,768]{1,0:T(8,128)(2,1)}, bf16[768,768]{1,0:T(8,128)(2,1)}, bf16[768,3072]{1,0:T(8,128)(...) custom-call(f32[1024,768]{1,0:T(8,128)} %get-tuple-element.105.hid_ref, ...), custom_call_target="tpu_custom_call" | custom-call | flops 3449999872 | bytes 10800000 | tf_op jit(solution)/shard_map/feed_forward_and_back/pallas_call | solution.py:943
  161.3 7.9 %proj_weight_terms.1 = bf16[8,4,4,24,768]{4,3,2,1,0:T(8,128)(2,1)} custom-call(bf16[768,3072]{1,0:T(8,128)(2,1)} %get-tuple-element.111.act_ref, bf16[768,768]{1,0:T(8,128)(2,1)} %bitcast_select_fusion.up_ref), custom_call_target="tpu_custom_call" | custom-call | flops 575000000 | bytes 1800000 | tf_op jit(solution)/shard_map/proj_weight_terms/pallas_call | solution.py:1151
  169.3 8.8 %fc_weight_terms.1 = (bf16[16,4,24,768]{3,2,1,0:T(8,128)(2,1)}, bf16[16,4,24,768]{3,2,1,0:T(8,128)(2,1)}) custom-call(s32[1]{0:T(128)} %bitcast.2.core_ref, bf16[768,768]{1,0:T(8,128)(2,1)} %get-tuple-element.112.second_ref, bf16[768,3072]{1,0:T(8,128)(2,1)} %get-tuple-element.113.pg_ref), custom_call_target="tpu_custom_call" | custom-call | flops 575000000 | bytes 1800000 | tf_op jit(solution)/shard_map/fc_weight_terms/pallas_call | solution.py:1121
  178.4 19.3 %thought_rows_backward.1 = (f32[8,3072]{1,0:T(8,128)}, bf16[24,768]{1,0:T(8,128)(2,1)}, bf16[768,768]{1,0:T(8,128)(2,1)}, f32[768,768]{1,0:T(8,128)}) custom-call(s32[2]{0:T(128)} %pad_add_fusion.info_ref, f32[1024,768]{1,0:T(8,128)} %get-tuple-element.105.hid_ref, ...), custom_call_target="tpu_custom_call", output_to_operand_aliasing={{2}: (12, {}), {3}: (13, {})} | custom-call | flops 2300000000 | bytes 7200000 | tf_op jit(solution)/shard_map/thought_rows_backward/pallas_call | solution.py:829
  199.2 2.2 convert_add_fusion
  204.5 25.7 %attention_backward.1.grad_ref = bf16[3,1024,768]{2,1,0:T(8,128)(2,1)} custom-call(bf16[3,1024,768]{2,1,0:T(8,128)(2,1)} %get-tuple-element.108.qkv_ref.qkv_in.q_ref.k_ref.v_ref, bf16[3,1024,768]{2,1,0:T(8,128)(2,1)} %get-tuple-element.108.qkv_ref.qkv_in.q_ref.k_ref.v_ref, bf16[3,1024,768]{2,1,0:T(8,128)(2,1)} %get-tuple-element.108.qkv_ref.qkv_in.q_ref.k_ref.v_ref, ...), custom_call_target="tpu_custom_call" | custom-call | flops 2495500032 | bytes 7812000 | tf_op jit(solution)/shard_map/attention_backward/pallas_call | solution.py:349
  230.2 2.3 bitcast_add_fusion
  235.0 14.2 %near_weight_terms.1 = (bf16[16,2,24,768]{3,2,1,0:T(8,128)(2,1)}, bf16[16,2,24,768]{3,2,1,0:T(8,128)(2,1)}, bf16[16,2,24,768]{3,2,1,0:T(8,128)(2,1)}, bf16[16,2,...) custom-call(s32[1]{0:T(128)} %bitcast.2.core_ref, bf16[1024,768]{1,0:T(8,128)(2,1)} %get-tuple-element.132.normed_ref, ...), custom_call_target="tpu_custom_call" | custom-call | flops 575000000 | bytes 1800000 | tf_op jit(solution)/shard_map/near_weight_terms/pallas_call | solution.py:1083
  252.8 2.1 collective-permute-start.28
  254.9 2.0 bitcast_add_fusion.4
  261.4 10.6 %first_norm_backward.1 = f32[1024,768]{1,0:T(8,128)} custom-call(s32[2]{0:T(128)} %pad_add_fusion.info_ref, f32[1024,768]{1,0:T(8,128)} %get-tuple-element.105.hid_ref, bf16[3,1024,768]{2,1,0:T(8,128)(2,1)} %attention_backward.1.grad_ref, f32[768,768]{1,0:T(8,128)} %get-tuple-element.133.rg_ref, bf16[3,768,768]{2,1,0:T(8,128)(2,1)} %get-tuple-element.102.near_in.near_ref, ...), custom_call_target="tpu_custom_call" | custom-call | flops 954499968 | bytes 2988000 | tf_op jit(solution)/shard_map/first_norm_backward/pallas_call | solution.py:1004
  277.6 2.2 collective-permute-start.31
  280.6 4.1 %collective-permute-done.32 = bf16[2,2,2,24,768]{4,3,1,2,0:T(8,128)(2,1)S(1)} collective-permute-done((bf16[2,2,2,24,768]{4,3,1,2,0:T(8,128)(2,1)S(1)}, bf16[2,2,2,24,768]{4,3,1,2,0:T(8,128)(2,1)S(1)}, u32[]{:S(2)}, u32[]{:S(2)}) %collective-permute-start.32) | collective-permute-done | bytes 294944 | tf_op jit(solution)/shard_map/ppermute | solution.py:73
  287.4 3.2 %collective-permute-done.30 = bf16[2,2,2,24,768]{4,3,2,1,0:T(8,128)(2,1)S(1)} collective-permute-done((bf16[2,2,2,24,768]{4,3,2,1,0:T(8,128)(2,1)S(1)}, bf16[2,2,2,24,768]{4,3,2,1,0:T(8,128)(2,1)S(1)}, u32[]{:S(2)}, u32[]{:S(2)}) %collective-permute-start.30) | collective-permute-done | bytes 294944 | tf_op jit(solution)/shard_map/ppermute | solution.py:73
  296.1 2.0 collective-permute-start.38
  300.8 3.8 %thought_rows_terms.1 = (f32[4,24,768]{2,1,0:T(8,128)}, f32[24,3072]{1,0:T(8,128)}) custom-call(s32[1]{0:T(128)} %bitcast.79.index_ref, bf16[24,32,768]{2,1,0:T(8,128)(2,1)} %bitcast.275, bf16[4,24,768]{2,1,0:T(8,128)(2,1)} %bitcast.284, f32[4,24,768]{2,1,0:T(8,128)} %bitcast_add_fusion.10.fc_ref, bf16[384,384]{1,0:T(8,128)(2,1)} %constant.301.clone.swap_ref), custom_call_target="tpu_custom_call" | custom-call | flops 379500000 | bytes 1188000 | tf_op jit(solution)/shard_map/thought_rows_terms/pallas_call | solution.py:1287
  (181 shorter events, 56.2 us)
Async XLA Ops:
  7.2 103.7 %all-gather.2.cloned.1.call-start = ((), (), s32[]{:S(2)}) async-start(), calls=%async_computation.2 | async-start | bytes 10948608 | tf_op jit(solution)/shard_map/all_gather | solution.py:1540
  9.6 225.4 %reduce-scatter.3.cloned.1.call-start = ((), (), s32[]{:S(2)}) async-start(), calls=%async_computation.3 | async-start | bytes 5308416 | tf_op jit(solution)/shard_map/reduce_scatter | solution.py:1565
  11.7 9.8 %collective-permute-start.10 = (bf16[8,128]{1,0:T(8,128)(2,1)S(1)}, bf16[8,128]{1,0:T(8,128)(2,1)S(1)}, u32[]{:S(2)}, u32[]{:S(2)}) collective-permute-start(bf16[8,128]{1,0:T(8,128)(2,1)S(1)} %convert_element_type.306), channel_id=1, source_target_pairs={{0,4},{1,5},{2,6},{3,7},{4,0},{5,1},{6,2},{7,3},{8,12},{9,13},{10,... | collective-permute-start | bytes 6152 | tf_op jit(solution)/shard_map/ppermute | solution.py:73
  15.8 9.5 %collective-permute-start = (bf16[1,3,24,384]{3,2,1,0:T(8,128)(2,1)S(1)}, bf16[1,3,24,384]{3,2,1,0:T(8,128)(2,1)S(1)}, u32[]{:S(2)}, u32[]{:S(2)}) collective-permute-start(bf16[1,3,24,384]{3,2,1,0:T(8,128)(2,1)S(1)} %maximum_bitcast_fusion), channel_id=1, source_target_pairs={{0,4},{1,5},{2,6},{3,7},{4,0},{5,1},{6,2},{7,3},{8,12},{9,13},{10,... | collective-permute-start | bytes 165896 | tf_op jit(solution)/shard_map/ppermute | solution.py:73
  15.9 11.1 %collective-permute-start.5 = (bf16[1,3,24,384]{3,2,1,0:T(8,128)(2,1)S(1)}, bf16[1,3,24,384]{3,2,1,0:T(8,128)(2,1)S(1)}, u32[]{:S(2)}, u32[]{:S(2)}) collective-permute-start(bf16[1,3,24,384]{3,2,1,0:T(8,128)(2,1)S(1)} %maximum_bitcast_fusion.1), channel_id=1, source_target_pairs={{0,4},{1,5},{2,6},{3,7},{4,0},{5,1},{6,2},{7,3},{8,12},{9,13},{10,... | collective-permute-start | bytes 165896 | tf_op jit(solution)/shard_map/ppermute | solution.py:73
  27.0 9.4 %collective-permute-start.6 = (bf16[2,3,24,384]{3,2,1,0:T(8,128)(2,1)S(1)}, bf16[2,3,24,384]{3,2,1,0:T(8,128)(2,1)S(1)}, u32[]{:S(2)}, u32[]{:S(2)}) collective-permute-start(bf16[2,3,24,384]{3,2,1,0:T(8,128)(2,1)S(1)} %pad_maximum_fusion.12), channel_id=1, source_target_pairs={{0,2},{1,3},{2,0},{3,1},{4,6},{5,7},{6,4},{7,5},{8,10},{9,11},{10,... | collective-permute-start | bytes 331784 | tf_op jit(solution)/shard_map/ppermute | solution.py:73
  27.5 10.7 %collective-permute-start.12 = (bf16[2,2,8,128]{3,2,0,1:T(8,128)(2,1)S(1)}, bf16[2,2,8,128]{3,2,0,1:T(8,128)(2,1)S(1)}, u32[]{:S(2)}, u32[]{:S(2)}) collective-permute-start(bf16[2,2,8,128]{3,2,0,1:T(8,128)(2,1)S(1)} %pad_maximum_fusion.17), channel_id=1, source_target_pairs={{0,8},{8,0},{16,24},{24,16},{1,9},{9,1},{17,25},{25,17},{2,10},{10... | collective-permute-start | bytes 24584 | tf_op jit(solution)/shard_map/ppermute | solution.py:73
  38.2 9.6 %collective-permute-start.2 = (bf16[4,3,24,384]{3,2,1,0:T(8,128)(2,1)S(1)}, bf16[4,3,24,384]{3,2,1,0:T(8,128)(2,1)S(1)}, u32[]{:S(2)}, u32[]{:S(2)}) collective-permute-start(bf16[4,3,24,384]{3,2,1,0:T(8,128)(2,1)S(1)} %pad_maximum_fusion.7), channel_id=1, source_target_pairs={{0,8},{8,0},{16,24},{24,16},{1,9},{9,1},{17,25},{25,17},{2,10},{10... | collective-permute-start | bytes 663560 | tf_op jit(solution)/shard_map/ppermute | solution.py:73
  42.6 20.2 %collective-permute-start.8 = (bf16[8,3,24,384]{3,2,1,0:T(8,128)(2,1)S(1)}, bf16[8,3,24,384]{3,2,1,0:T(8,128)(2,1)S(1)}, u32[]{:S(2)}, u32[]{:S(2)}) collective-permute-start(bf16[8,3,24,384]{3,2,1,0:T(8,128)(2,1)S(1)} %pad_maximum_fusion.5), channel_id=1, source_target_pairs={{0,8},{8,0},{16,24},{24,16},{1,9},{9,1},{17,25},{25,17},{2,10},{10... | collective-permute-start | bytes 1327112 | tf_op jit(solution)/shard_map/ppermute | solution.py:73
  47.9 15.2 %collective-permute-start.3 = (bf16[8,3,24,384]{3,2,1,0:T(8,128)(2,1)S(1)}, bf16[8,3,24,384]{3,2,1,0:T(8,128)(2,1)S(1)}, u32[]{:S(2)}, u32[]{:S(2)}) collective-permute-start(bf16[8,3,24,384]{3,2,1,0:T(8,128)(2,1)S(1)} %pad_maximum_fusion.4), channel_id=1, source_target_pairs={{0,16},{8,24},{16,0},{24,8},{1,17},{9,25},{17,1},{25,9},{2,18},{10... | collective-permute-start | bytes 1327112 | tf_op jit(solution)/shard_map/ppermute | solution.py:73
  48.0 18.6 %collective-permute-start.13 = (bf16[2,2,2,8,128]{4,3,1,2,0:T(8,128)(2,1)S(1)}, bf16[2,2,2,8,128]{4,3,1,2,0:T(8,128)(2,1)S(1)}, u32[]{:S(2)}, u32[]{:S(2)}) collective-permute-start(bf16[2,2,2,8,128]{4,3,1,2,0:T(8,128)(2,1)S(1)} %pad_maximum_fusion.16), channel_id=1, source_target_pairs={{0,16},{8,24},{16,0},{24,8},{1,17},{9,25},{17,1},{25,9},{2,18},{10... | collective-permute-start | bytes 49160 | tf_op jit(solution)/shard_map/ppermute | solution.py:73
  63.0 10.0 %collective-permute-start.9 = (bf16[16,3,24,384]{3,2,1,0:T(8,128)(2,1)S(1)}, bf16[16,3,24,384]{3,2,1,0:T(8,128)(2,1)S(1)}, u32[]{:S(2)}, u32[]{:S(2)}) collective-permute-start(bf16[16,3,24,384]{3,2,1,0:T(8,128)(2,1)S(1)} %pad_maximum_fusion.2.right_mine), channel_id=1, source_target_pairs={{0,1},{1,0},{2,3},{3,2},{4,5},{5,4},{6,7},{7,6},{8,9},{9,8},{10,11... | collective-permute-start | bytes 2654216 | tf_op jit(solution)/shard_map/ppermute | solution.py:73
  64.0 9.1 %collective-permute-start.4 = (bf16[16,3,24,384]{3,2,1,0:T(8,128)(2,1)S(1)}, bf16[16,3,24,384]{3,2,1,0:T(8,128)(2,1)S(1)}, u32[]{:S(2)}, u32[]{:S(2)}) collective-permute-start(bf16[16,3,24,384]{3,2,1,0:T(8,128)(2,1)S(1)} %pad_maximum_fusion.1.left_mine), channel_id=1, source_target_pairs={{0,1},{1,0},{2,3},{3,2},{4,5},{5,4},{6,7},{7,6},{8,9},{9,8},{10,11... | collective-permute-start | bytes 2654216 | tf_op jit(solution)/shard_map/ppermute | solution.py:73
  169.2 131.6 %reduce-scatter.5.cloned.1.call-start = ((), (), s32[]{:S(2)}) async-start(), calls=%async_computation.4 | async-start | bytes 737280 | tf_op jit(solution)/shard_map/reduce_scatter | solution.py:1571
  178.1 19.6 %collective-permute-start.15 = (bf16[2,2,2,2,4,24,768]{6,5,4,3,2,1,0:T(8,128)(2,1)}, bf16[2,2,2,2,4,24,768]{6,5,4,3,2,1,0:T(8,128)(2,1)S(1)}, u32[]{:S(2)}, u32[]{:S(2)}) collective-permute-start(bf16[2,2,2,2,4,24,768]{6,5,4,3,2,1,0:T(8,128)(2,1)} %bitcast.287), channel_id=1, source_target_pairs={{0,1},{1,0},{2,3},{3,2},{4,5},{5,4},{6,7},{7,6},{8,9},{9,8},{10,11... | collective-permute-start | bytes 7077896 | tf_op jit(solution)/shard_map/ppermute | solution.py:73
  201.4 28.8 %collective-permute-start.16 = (bf16[2,2,2,4,24,768]{5,4,3,2,1,0:T(8,128)(2,1)S(1)}, bf16[2,2,2,4,24,768]{5,4,3,2,1,0:T(8,128)(2,1)}, u32[]{:S(2)}, u32[]{:S(2)}) collective-permute-start(bf16[2,2,2,4,24,768]{5,4,3,2,1,0:T(8,128)(2,1)S(1)} %get-tuple-element.181), channel_id=1, source_target_pairs={{0,8},{8,0},{16,24},{24,16},{1,9},{9,1},{17,25},{25,17},{2,10},{10... | collective-permute-start | bytes 3538952 | tf_op jit(solution)/shard_map/ppermute | solution.py:73
  203.0 27.2 %collective-permute-start.17 = (bf16[24,768]{1,0:T(8,128)(2,1)}, bf16[24,768]{1,0:T(8,128)(2,1)S(1)}, u32[]{:S(2)}, u32[]{:S(2)}) collective-permute-start(bf16[24,768]{1,0:T(8,128)(2,1)} %get-tuple-element.125), channel_id=1, source_target_pairs={{0,4},{1,5},{2,6},{3,7},{4,0},{5,1},{6,2},{7,3},{8,12},{9,13},{10,... | collective-permute-start | bytes 110600 | tf_op jit(solution)/shard_map/ppermute | solution.py:73
  232.5 16.7 %collective-permute-start.18 = (bf16[2,2,4,24,768]{4,3,2,1,0:T(8,128)(2,1)}, bf16[2,2,4,24,768]{4,3,2,1,0:T(8,128)(2,1)S(1)}, u32[]{:S(2)}, u32[]{:S(2)}) collective-permute-start(bf16[2,2,4,24,768]{4,3,2,1,0:T(8,128)(2,1)} %get-tuple-element.183), channel_id=1, source_target_pairs={{0,16},{8,24},{16,0},{24,8},{1,17},{9,25},{17,1},{25,9},{2,18},{10... | collective-permute-start | bytes 1769480 | tf_op jit(solution)/shard_map/ppermute | solution.py:73
  233.5 15.7 %collective-permute-start.19 = (bf16[2,24,768]{2,1,0:T(8,128)(2,1)S(1)}, bf16[2,24,768]{2,1,0:T(8,128)(2,1)S(1)}, u32[]{:S(2)}, u32[]{:S(2)}) collective-permute-start(bf16[2,24,768]{2,1,0:T(8,128)(2,1)S(1)} %pad_maximum_fusion.13), channel_id=1, source_target_pairs={{0,2},{1,3},{2,0},{3,1},{4,6},{5,7},{6,4},{7,5},{8,10},{9,11},{10,... | collective-permute-start | bytes 221192 | tf_op jit(solution)/shard_map/ppermute | solution.py:73
  252.8 19.2 %collective-permute-start.28 = (bf16[2,2,24,768]{3,2,0,1:T(8,128)(2,1)}, bf16[2,2,24,768]{3,2,0,1:T(8,128)(2,1)}, u32[]{:S(2)}, u32[]{:S(2)}) collective-permute-start(bf16[2,2,24,768]{3,2,0,1:T(8,128)(2,1)} %pad_maximum_fusion.10), channel_id=1, source_target_pairs={{0,16},{8,24},{16,0},{24,8},{1,17},{9,25},{17,1},{25,9},{2,18},{10... | collective-permute-start | bytes 442376 | tf_op jit(solution)/shard_map/ppermute | solution.py:73
  256.9 17.3 %collective-permute-start.27 = (bf16[2,4,24,768]{3,2,1,0:T(8,128)(2,1)}, bf16[2,4,24,768]{3,2,1,0:T(8,128)(2,1)}, u32[]{:S(2)}, u32[]{:S(2)}) collective-permute-start(bf16[2,4,24,768]{3,2,1,0:T(8,128)(2,1)} %get-tuple-element.193), channel_id=1, source_target_pairs={{0,2},{1,3},{2,0},{3,1},{4,6},{5,7},{6,4},{7,5},{8,10},{9,11},{10,... | collective-permute-start | bytes 884744 | tf_op jit(solution)/shard_map/ppermute | solution.py:73
  257.7 16.5 %collective-permute-start.23 = (bf16[2,2,2,8,128]{4,3,1,2,0:T(8,128)(2,1)S(1)}, bf16[2,2,2,8,128]{4,3,1,2,0:T(8,128)(2,1)S(1)}, u32[]{:S(2)}, u32[]{:S(2)}) collective-permute-start(bf16[2,2,2,8,128]{4,3,1,2,0:T(8,128)(2,1)S(1)} %get-tuple-element.233), channel_id=1, source_target_pairs={{0,16},{8,24},{16,0},{24,8},{1,17},{9,25},{17,1},{25,9},{2,18},{10... | collective-permute-start | bytes 49160 | tf_op jit(solution)/shard_map/ppermute | solution.py:73
  258.6 18.8 %collective-permute-start.26 = (bf16[2,2,2,2,24,768]{5,4,3,2,1,0:T(8,128)(2,1)S(1)}, bf16[2,2,2,2,24,768]{5,4,3,2,1,0:T(8,128)(2,1)S(1)}, u32[]{:S(2)}, u32[]{:S(2)}) collective-permute-start(bf16[2,2,2,2,24,768]{5,4,3,2,1,0:T(8,128)(2,1)S(1)} %get-tuple-element.185), channel_id=1, source_target_pairs={{0,8},{8,0},{16,24},{24,16},{1,9},{9,1},{17,25},{25,17},{2,10},{10... | collective-permute-start | bytes 1769480 | tf_op jit(solution)/shard_map/ppermute | solution.py:73
  260.1 17.4 %collective-permute-start.25 = (bf16[2,2,2,2,24,768]{5,4,3,2,1,0:T(8,128)(2,1)S(1)}, bf16[2,2,2,2,24,768]{5,4,3,2,1,0:T(8,128)(2,1)S(1)}, u32[]{:S(2)}, u32[]{:S(2)}) collective-permute-start(bf16[2,2,2,2,24,768]{5,4,3,2,1,0:T(8,128)(2,1)S(1)} %get-tuple-element.187), channel_id=1, source_target_pairs={{0,16},{8,24},{16,0},{24,8},{1,17},{9,25},{17,1},{25,9},{2,18},{10... | collective-permute-start | bytes 1769480 | tf_op jit(solution)/shard_map/ppermute | solution.py:73
  273.0 11.6 %collective-permute-start.32 = (bf16[2,2,2,24,768]{4,3,1,2,0:T(8,128)(2,1)S(1)}, bf16[2,2,2,24,768]{4,3,1,2,0:T(8,128)(2,1)S(1)}, u32[]{:S(2)}, u32[]{:S(2)}) collective-permute-start(bf16[2,2,2,24,768]{4,3,1,2,0:T(8,128)(2,1)S(1)} %pad_maximum_fusion.6), channel_id=1, source_target_pairs={{0,8},{8,0},{16,24},{24,16},{1,9},{9,1},{17,25},{25,17},{2,10},{10... | collective-permute-start | bytes 884744 | tf_op jit(solution)/shard_map/ppermute | solution.py:73
  274.2 10.6 %collective-permute-start.24 = (bf16[2,2,8,128]{3,2,0,1:T(8,128)(2,1)S(1)}, bf16[2,2,8,128]{3,2,0,1:T(8,128)(2,1)S(1)}, u32[]{:S(2)}, u32[]{:S(2)}) collective-permute-start(bf16[2,2,8,128]{3,2,0,1:T(8,128)(2,1)S(1)} %get-tuple-element.238), channel_id=1, source_target_pairs={{0,8},{8,0},{16,24},{24,16},{1,9},{9,1},{17,25},{25,17},{2,10},{10... | collective-permute-start | bytes 24584 | tf_op jit(solution)/shard_map/ppermute | solution.py:73
  276.1 8.9 %collective-permute-start.35 = (bf16[4,24,768]{2,1,0:T(8,128)(2,1)S(1)}, bf16[4,24,768]{2,1,0:T(8,128)(2,1)S(1)}, u32[]{:S(2)}, u32[]{:S(2)}) collective-permute-start(bf16[4,24,768]{2,1,0:T(8,128)(2,1)S(1)} %fusion.14), channel_id=1, source_target_pairs={{0,4},{1,5},{2,6},{3,7},{4,0},{5,1},{6,2},{7,3},{8,12},{9,13},{10,... | collective-permute-start | bytes 442376 | tf_op jit(solution)/shard_map/ppermute | solution.py:73
  280.0 10.7 %collective-permute-start.30 = (bf16[2,2,2,24,768]{4,3,2,1,0:T(8,128)(2,1)S(1)}, bf16[2,2,2,24,768]{4,3,2,1,0:T(8,128)(2,1)S(1)}, u32[]{:S(2)}, u32[]{:S(2)}) collective-permute-start(bf16[2,2,2,24,768]{4,3,2,1,0:T(8,128)(2,1)S(1)} %get-tuple-element.191), channel_id=1, source_target_pairs={{0,8},{8,0},{16,24},{24,16},{1,9},{9,1},{17,25},{25,17},{2,10},{10... | collective-permute-start | bytes 884744 | tf_op jit(solution)/shard_map/ppermute | solution.py:73
  285.0 14.2 %collective-permute-start.34 = (bf16[2,2,2,2,24,768]{5,4,2,3,0,1:T(8,128)(2,1)S(1)}, bf16[2,2,2,2,24,768]{5,4,2,3,0,1:T(8,128)(2,1)S(1)}, u32[]{:S(2)}, u32[]{:S(2)}) collective-permute-start(bf16[2,2,2,2,24,768]{5,4,2,3,0,1:T(8,128)(2,1)S(1)} %pad_maximum_fusion.3), channel_id=1, source_target_pairs={{0,1},{1,0},{2,3},{3,2},{4,5},{5,4},{6,7},{7,6},{8,9},{9,8},{10,11... | collective-permute-start | bytes 1769480 | tf_op jit(solution)/shard_map/ppermute | solution.py:73
  285.0 8.9 %collective-permute-start.29 = (bf16[2,8,128]{2,1,0:T(8,128)(2,1)S(1)}, bf16[2,8,128]{2,1,0:T(8,128)(2,1)S(1)}, u32[]{:S(2)}, u32[]{:S(2)}) collective-permute-start(bf16[2,8,128]{2,1,0:T(8,128)(2,1)S(1)} %get-tuple-element.242), channel_id=1, source_target_pairs={{0,2},{1,3},{2,0},{3,1},{4,6},{5,7},{6,4},{7,5},{8,10},{9,11},{10,... | collective-permute-start | bytes 12296 | tf_op jit(solution)/shard_map/ppermute | solution.py:73
  286.4 8.8 %collective-permute-start.37 = (bf16[2,2,24,768]{3,2,1,0:T(8,128)(2,1)S(1)}, bf16[2,2,24,768]{3,2,1,0:T(8,128)(2,1)S(1)}, u32[]{:S(2)}, u32[]{:S(2)}) collective-permute-start(bf16[2,2,24,768]{3,2,1,0:T(8,128)(2,1)S(1)} %get-tuple-element.197), channel_id=1, source_target_pairs={{0,2},{1,3},{2,0},{3,1},{4,6},{5,7},{6,4},{7,5},{8,10},{9,11},{10,... | collective-permute-start | bytes 442376 | tf_op jit(solution)/shard_map/ppermute | solution.py:73
  293.9 11.7 %collective-permute-start.33 = (bf16[8,128]{1,0:T(8,128)(2,1)S(1)}, bf16[8,128]{1,0:T(8,128)(2,1)S(1)}, u32[]{:S(2)}, u32[]{:S(2)}) collective-permute-start(bf16[8,128]{1,0:T(8,128)(2,1)S(1)} %fusion.43), channel_id=1, source_target_pairs={{0,4},{1,5},{2,6},{3,7},{4,0},{5,1},{6,2},{7,3},{8,12},{9,13},{10,... | collective-permute-start | bytes 6152 | tf_op jit(solution)/shard_map/ppermute | solution.py:73
  (30 other events, 153.1 us)
Sparse Core Ops, SparseCore 0:
  11.2 99.5 all-gather.1
  169.4 55.6 reduce-scatter.2
  252.9 27.3 reduce-scatter.4

commit v6 on v5

--- a/solution.py
+++ b/solution.py
@@ -228,7 +228,6 @@
     keys = k_ref[...]
     values_t = v_ref[...].T
     lane = lax.broadcasted_iota(jnp.int32, (BLOCK, PAIR), 1)
-    sub = lax.broadcasted_iota(jnp.int32, (PAIR, BLOCK), 0)
     key_pos = lax.broadcasted_iota(jnp.int32, (BLOCK, BLOCK), 0)
     row_pos = lax.broadcasted_iota(jnp.int32, (BLOCK, BLOCK), 1)
     causal = key_pos <= row_pos
@@ -255,10 +254,10 @@
             peak = jnp.max(scores, axis=0, keepdims=True)
             expo = jnp.exp(scores - peak)
             total = jnp.sum(expo, axis=0, keepdims=True)
-            mixed = dot(values_t[:, :end], expo.astype(BF16))
+            mixed = dot(values_t[head * HD : (head + 1) * HD, :end], expo.astype(BF16))
             parts.append(mixed / total)
             lse_ref[pl.ds(2 * pl.program_id(0) + head, 1), begin:end] = peak + jnp.log(total)
-        o_ref[begin:end, :] = jnp.where(sub < HD, parts[0], parts[1]).T.astype(BF16)
+        o_ref[begin:end, :] = jnp.concatenate(parts, axis=0).T.astype(BF16)
 
 
 def attend(info, qkv):
@@ -299,7 +298,6 @@
     values = v_ref[...]
     keys_t = keys.T
     lane = lax.broadcasted_iota(jnp.int32, (BLOCK, PAIR), 1)
-    sub = lax.broadcasted_iota(jnp.int32, (PAIR, BLOCK), 0)
     key_pos = lax.broadcasted_iota(jnp.int32, (BLOCK, BLOCK), 0)
     row_pos = lax.broadcasted_iota(jnp.int32, (BLOCK, BLOCK), 1)
     causal = key_pos <= row_pos
@@ -311,27 +309,30 @@
         queries = q_ref[begin:end, :] * jnp.asarray(SCALE, BF16)
         grads = g_ref[local : local + BLOCK, :]
         product_t = (grads.astype(F32) * o_ref[begin:end, :].astype(F32)).T
-        parts = []
+        owns, own_grads, probs_low, score_grads, parts = [], [], [], [], []
         for head in range(2):
             chosen = (lane >= HD) == bool(head)
             own = jnp.where(chosen, queries, jnp.zeros_like(queries))
             own_grad = jnp.where(chosen, grads, jnp.zeros_like(grads))
-            delta = jnp.sum(product_t[head * HD : (head + 1) * HD], axis=0, keepdims=True)
+            rows_here = slice(head * HD, (head + 1) * HD)
+            delta = jnp.sum(product_t[rows_here], axis=0, keepdims=True)
             lse = lse_ref[pl.ds(2 * pair + head, 1), begin:end]
-            total = None
-            for low, high in ((0, begin), (begin, end)):
-                scores = dot_nt(keys[low:high], own)
-                if high == end:
-                    scores = jnp.where(causal, scores, NEG)
-                probs = jnp.exp(scores - lse)
-                prob_grad = dot_nt(values[low:high], own_grad)
-                score_grad = (probs * (prob_grad - delta)).astype(BF16)
-                dv_acc[low:high, :] += dot(probs.astype(BF16), own_grad)
-                dk_acc[low:high, :] += dot(score_grad, own)
-                part = dot(keys_t[:, low:high], score_grad)
-                total = part if total is None else total + part
-            parts.append(total)
-        mine = jnp.where(sub < HD, parts[0], parts[1]).T * SCALE
+            scores = dot_nt(keys[:end], own)
+            last = jnp.where(causal, scores[begin:], NEG)
+            scores = jnp.concatenate([scores[:begin], last], axis=0) if begin else last
+            probs = jnp.exp(scores - lse)
+            prob_grad = dot_nt(values[:end], own_grad)
+            score_grad = (probs * (prob_grad - delta)).astype(BF16)
+            parts.append(dot(keys_t[rows_here, :end], score_grad))
+            owns.append(own)
+            own_grads.append(own_grad)
+            probs_low.append(probs.astype(BF16))
+            score_grads.append(score_grad)
+        dv_acc[:end, :] += dot(
+            jnp.concatenate(probs_low, axis=1), jnp.concatenate(own_grads, axis=0)
+        )
+        dk_acc[:end, :] += dot(jnp.concatenate(score_grads, axis=1), jnp.concatenate(owns, axis=0))
+        mine = jnp.concatenate(parts, axis=0).T * SCALE
         out_ref[0, begin:end, :] = mine.astype(BF16)
     out_ref[0, :first_row, :] = jnp.zeros((first_row, PAIR), BF16)
     out_ref[1] = dk_acc[...].astype(BF16)
@@ -1039,38 +1040,49 @@
 
 def near_terms_kernel(
     sizes, chips_a, chips_b, core_ref, normed_ref, grad_ref, mixed_ref, rg_ref, near_ref, vec_ref,
-    feed_sum_ref, row_sum_ref, keep_a, send_a, keep_b, send_b, packed_ref,
+    feed_sum_ref, row_sum_ref, place_a, owner_a, place_b, owner_b, keep_a, send_a, keep_b, send_b,
+    packed_ref, normed_t, gain_ref, bias_ref, column_ref,
 ):
     core = core_ref[0]
+    step = pl.program_id(0)
     width = normed_ref.shape[1]
-    columns = vec_ref[...].T
-    gain, bias = columns[:, 0:1], columns[:, 1:2]
-    normed_t = normed_ref[...].T
-    gain_terms = jnp.zeros((width, width), F32)
-    bias_rows = jnp.zeros((16, width), F32)
-    column_sums = []
-    for i in range(3):
-        inner = dot(normed_t, grad_ref[i])
-        sums = jnp.sum(grad_ref[i].astype(F32), axis=0, keepdims=True)
-        value = inner * gain + bias * sums
-        if i < 2:
-            keep_and_send(value, core, chips_a, keep_a, send_a, i)
-        else:
-            keep_and_send(value, core, chips_b, keep_b, send_b, 0)
-        gain_terms = gain_terms + inner * near_ref[i].astype(F32)
+
+    @pl.when(step == 0)
+    def _():
+        normed_t[...] = normed_ref[...].T
+        gain_ref[...] = jnp.zeros_like(gain_ref)
+        bias_ref[...] = jnp.zeros_like(bias_ref)
+
+    def term():
+        columns = vec_ref[...].T
+        inner = dot(normed_t[...], grad_ref[...])
+        sums = jnp.sum(grad_ref[...].astype(F32), axis=0, keepdims=True)
+        gain_ref[...] += inner * near_ref[...].astype(F32)
         pieces = in_pieces(jnp.broadcast_to(sums, (8, width)), 2)
-        bias_rows = bias_rows + dot_nt(jnp.concatenate(pieces, axis=0), near_ref[i])
-        column_sums.append(sums)
-    ones = jnp.ones((16, width), BF16)
-    totals = feed_sum_ref[...] + row_sum_ref[...]
-    small = {name: totals[i : i + 1, :width] for i, name in enumerate(SUM_ROWS)}
-    small["fc_bias"] = totals[0:1]
-    small["ln1_gain"] = sum(dot_nt(ones, piece) for piece in in_pieces(gain_terms, 2))[0:1]
-    small["ln1_bias"] = bias_rows[0:1] + bias_rows[8:9]
-    small["qv_bias"] = jnp.concatenate([column_sums[0], column_sums[2]], axis=1)
-    pack(small, sizes, 2 * len(chips_a), packed_ref)
-    value = dot_tn(mixed_ref[QUESTION:, :], rg_ref[...].astype(BF16))
-    keep_and_send(value, core, chips_b, keep_b, send_b, 1)
+        bias_ref[...] += dot_nt(jnp.concatenate(pieces, axis=0), near_ref[...])
+        column_ref[pl.ds(step, 1), :] = sums
+        return inner * columns[:, 0:1] + columns[:, 1:2] * sums
+
+    @pl.when(step < 2)
+    def _():
+        keep_and_send(term(), core, chips_a, keep_a, send_a, 0)
+
+    @pl.when(step == 2)
+    def _():
+        keep_and_send(term(), core, chips_b, keep_b, send_b, 0)
+
+    @pl.when(step == 3)
+    def _():
+        value = dot_tn(mixed_ref[QUESTION:, :], rg_ref[...].astype(BF16))
+        keep_and_send(value, core, chips_b, keep_b, send_b, 0)
+        ones = jnp.ones((16, width), BF16)
+        totals = feed_sum_ref[...] + row_sum_ref[...]
+        small = {name: totals[i : i + 1, :width] for i, name in enumerate(SUM_ROWS)}
+        small["fc_bias"] = totals[0:1]
+        small["ln1_gain"] = sum(dot_nt(ones, p) for p in in_pieces(gain_ref[...], 2))[0:1]
+        small["ln1_bias"] = bias_ref[0:1, :] + bias_ref[8:9, :]
+        small["qv_bias"] = jnp.concatenate([column_ref[0:1, :], column_ref[2:3, :]], axis=1)
+        pack(small, sizes, 2 * len(chips_a), (place_a, owner_a, place_b, owner_b), packed_ref)
 
 
 def near_terms(
@@ -1078,28 +1090,40 @@
 ):
     seq_len, width = normed_low.shape
     half = jax.ShapeDtypeStruct((len(chips_a), 2, width // (2 * len(chips_a)), width), BF16)
-    packed = jax.ShapeDtypeStruct((len(sizes), 2 * len(chips_a), LANES), BF16)
+    piece = (len(chips_a), 1) + half.shape[2:]
+    left = pl.BlockSpec(piece, lambda i: (0, jnp.minimum(i, 1), 0, 0))
+    right = pl.BlockSpec(piece, lambda i: (0, jnp.maximum(i - 2, 0), 0, 0))
+    devices = 2 * len(chips_a)
+    maps = lane_maps(width // devices, devices)
+    packed = jax.ShapeDtypeStruct((len(sizes), devices, LANES), BF16)
     out_shape = [half] * 4 + [packed]
     return pl.pallas_call(
         functools.partial(near_terms_kernel, sizes, chips_a, chips_b),
-        grid=(1,),
+        grid=(4,),
         in_specs=[
             pl.BlockSpec(memory_space=pltpu.SMEM),
             whole(normed_low),
-            whole(qkv_grad),
+            pl.BlockSpec((None, seq_len, width), lambda i: (jnp.minimum(i, 2), 0, 0)),
             whole(mixed_low),
             whole(resid_grad),
-            whole(near),
+            pl.BlockSpec((None, width, width), lambda i: (jnp.minimum(i, 2), 0, 0)),
             whole(vec),
             whole(feed_sums),
             whole(row_sums),
-        ],
-        out_specs=[whole(x) for x in out_shape],
+            *(whole(x) for x in maps),
+        ],
+        out_specs=[left, left, right, right, whole(packed)],
         out_shape=out_shape,
+        scratch_shapes=[
+            pltpu.VMEM((width, seq_len), BF16),
+            pltpu.VMEM((width, width), F32),
+            pltpu.VMEM((16, width), F32),
+            pltpu.VMEM((8, width), F32),
+        ],
         compiler_params=pltpu.CompilerParams(vmem_limit_bytes=VMEM_LIMIT),
         cost_estimate=cost(0.5),
         name="near_weight_terms",
-    )(core, normed_low, qkv_grad, mixed_low, resid_grad, near, vec, feed_sums, row_sums)
+    )(core, normed_low, qkv_grad, mixed_low, resid_grad, near, vec, feed_sums, row_sums, *maps)
 
 
 def fc_terms_kernel(chips, core_ref, second_ref, pg_ref, keep_ref, send_ref, second_t):
@@ -1302,51 +1326,54 @@
     )(index, factors, proj_sum, fc_sum, swap)
 
 
-def spread_matrix(shard, count):
-    shape = (shard, shard * count)
-    column = lax.broadcasted_iota(jnp.int32, shape, 1) % shard
-    return (column == lax.broadcasted_iota(jnp.int32, shape, 0)).astype(BF16)
-
-
-def owner_mask(shard, count):
-    shape = (count, shard * count)
-    owner = lax.broadcasted_iota(jnp.int32, shape, 1) // shard
-    return owner == lax.broadcasted_iota(jnp.int32, shape, 0)
+def lane_maps(own, devices):
+    maps = []
+    for size in (own, 2 * own):
+        column = np.arange(size * devices)
+        maps.append(jnp.asarray(column[None, :] % size == np.arange(size)[:, None], BF16))
+        maps.append(jnp.asarray(column[None, :] // size == np.arange(devices)[:, None], F32))
+    return maps
+
+
+def lane_pieces(sizes, own):
+    pieces = []
+    for at, (name, size) in enumerate(sizes):
+        wide = size == 2 * own
+        step = 2 * own if wide else own
+        pieces += [(at, name, begin, 2 * int(wide), step) for begin in range(0, size, step)]
+    return pieces
 
 
 VECTOR_ROWS = ("ln1_gain", "ln1_bias", "out_bias", "ln2_gain", "ln2_bias", "proj_bias")
 
 
-def unpack_kernel(sizes, devices, packed_ref, vec_ref, fcb_ref, qkvb_ref):
+def unpack_kernel(
+    sizes, own, packed_ref, place_a, owner_a, place_b, owner_b, vec_ref, fcb_ref, qkvb_ref
+):
+    maps = (place_a, owner_a, place_b, owner_b)
     vec_ref[...] = jnp.zeros_like(vec_ref)
     width = vec_ref.shape[1]
-    for at, (name, size) in enumerate(sizes):
+    for at, name, begin, which, size in lane_pieces(sizes, own):
+        spread = dot(packed_ref[at][:, begin : begin + size], maps[which][...])
+        full = jnp.sum(spread * maps[which + 1][...], axis=0, keepdims=True)
         if name == "fc_bias":
-            own = width // devices
-            for j in range(size // own):
-                spread = dot(packed_ref[at][:, j * own : (j + 1) * own], spread_matrix(own, devices))
-                spread = jnp.where(owner_mask(own, devices), spread, 0.0)
-                span = slice(j * width, (j + 1) * width)
-                fcb_ref[:, span] = jnp.sum(spread, axis=0, keepdims=True)
-            continue
-        block = packed_ref[at][:, :size]
-        spread = dot(block, spread_matrix(size, devices))
-        full = jnp.sum(jnp.where(owner_mask(size, devices), spread, 0.0), axis=0, keepdims=True)
-        if name == "qv_bias":
+            fcb_ref[:, begin // own * width : (begin // own + 1) * width] = full
+        elif name == "qv_bias":
             qkvb_ref[:, :width] = full[:, :width]
             qkvb_ref[:, width : 2 * width] = jnp.zeros((1, width), F32)
             qkvb_ref[:, 2 * width :] = full[:, width:]
         else:
-            at = VECTOR_ROWS.index(name)
-            vec_ref[at : at + 1, :] = full
+            row = VECTOR_ROWS.index(name)
+            vec_ref[row : row + 1, :] = full
 
 
 def unpack(packed, sizes):
     devices = packed.shape[1]
     size = dict(sizes)
-    width = size["ln1_gain"] * devices
+    own = size["ln1_gain"]
+    width = own * devices
     return pl.pallas_call(
-        functools.partial(unpack_kernel, sizes, devices),
+        functools.partial(unpack_kernel, sizes, own),
         out_shape=[
             jax.ShapeDtypeStruct((8, width), F32),
             jax.ShapeDtypeStruct((1, size["fc_bias"] * devices), F32),
@@ -1354,20 +1381,24 @@
         ],
         compiler_params=pltpu.CompilerParams(vmem_limit_bytes=VMEM_LIMIT),
         name="vectors_unpack",
-    )(packed)
-
-
-def pack(rows, sizes, devices, out_ref):
+    )(packed, *lane_maps(own, devices))
+
+
+def pack(rows, sizes, devices, maps, out_ref):
     out_ref[...] = jnp.zeros_like(out_ref)
     width = rows["ln1_gain"].shape[1]
-    for at, (name, size) in enumerate(sizes):
-        own = width // devices if name == "fc_bias" else size
-        span = own * devices
-        for j in range(size // own):
-            row = jnp.broadcast_to(rows[name][:, j * span : (j + 1) * span], (devices, span))
-            row = jnp.where(owner_mask(own, devices), row, 0.0).astype(BF16)
-            piece = dot_nt(row, spread_matrix(own, devices)).astype(BF16)
-            out_ref[at, :, j * own : (j + 1) * own] = piece
+    own = width // devices
+    pieces = lane_pieces(sizes, own)
+    for which in sorted({piece[3] for piece in pieces}):
+        group = [piece for piece in pieces if piece[3] == which]
+        stack = []
+        for _, name, begin, _, size in group:
+            span = size * devices
+            first = begin // size * span
+            stack.append((rows[name][:, first : first + span] * maps[which + 1][...]).astype(BF16))
+        done = dot_nt(jnp.concatenate(stack, axis=0), maps[which][...]).astype(BF16)
+        for i, (at, _, begin, _, size) in enumerate(group):
+            out_ref[at, :, begin : begin + size] = done[i * devices : (i + 1) * devices]
 
 
 def join_kernel(*refs):

time: 319 us -> 319 us (level)
  transfers between devices with their start and end apart: 43 -> 43, of which waited for: 13 -> 12; matrix products, arithmetic and copies ran while one was open for 7% -> 7% of each run, Pallas kernels for 39% -> 38%
where the time goes in v6:
time: 319 us; the launch traced here: 314 us
  Pallas kernels  182 us (57%)
  starting transfers between devices  46.5 us (15%)
  waiting for transfers between devices  38.8 us (12%)
  other arithmetic  21.1 us (7%)
  between operations  15.8 us (5%)
  local copies, waits for them, and re-layouts  9.69 us (3%)
    ppermute x40, starting transfers between devices, swap(): lax.ppermute(value, axis, [(i, i ^ bit) for i in range(self.sizes[axis])])  46.4 us
    ppermute x40, waiting for transfers between devices, swap(): lax.ppermute(value, axis, [(i, i ^ bit) for i in range(self.sizes[axis])])  38.7 us
    pallas_call x1, Pallas kernels, feed(): pl.pallas_call(feed_kernel, grid=(seq_len // BLOCK,), in_specs=[rows(widt...  35.2 us
    pallas_call x1, Pallas kernels, attend(): pl.pallas_call(attend_kernel, grid=(pairs,), in_specs=[pl.BlockSpec(memor...  25.5 us
    pallas_call x1, Pallas kernels, attend_back(): pl.pallas_call(attend_back_kernel, grid=(width // PAIR,), in_specs=[*(col...  24.7 us
    pallas_call x1, Pallas kernels, thoughts_back(): pl.pallas_call(thoughts_back_kernel, grid=(1,), in_specs=[pl.BlockSpec(me...  19.3 us
    pallas_call x1, Pallas kernels, thoughts_forward(): pl.pallas_call(thoughts_kernel, grid=(1,), in_specs=[pl.BlockSpec(memory_...  15.2 us
    pallas_call x1, Pallas kernels, near_terms(): pl.pallas_call(functools.partial(near_terms_kernel, sizes, chips_a, chips...  13.7 us
  transfers between devices with their start and end apart: 43, of which 12 were waited for; matrix products, arithmetic and copies ran while one was open for 7% of the time, Pallas kernels for 38%

profile of v6, /device:TPU:0, one launch (start us, length us, event | category | flops | bytes accessed | tf_op | source)
XLA Modules:
  0.0 314.3 jit_solution(6040577629076962183)
XLA Ops:
  7.2 2.3 far_shard.1
  11.7 4.0 %collective-permute-start.10 = (bf16[8,128]{1,0:T(8,128)(2,1)S(1)}, bf16[8,128]{1,0:T(8,128)(2,1)S(1)}, u32[]{:S(2)}, u32[]{:S(2)}) collective-permute-start(bf16[8,128]{1,0:T(8,128)(2,1)S(1)} %convert_element_type.306), channel_id=1, source_target_pairs={{0,4},{1,5},{2,6},{3,7},{4,0},{5,1},{6,2},{7,3},{8,12},{9,13},{10,... | collective-permute-start | bytes 6152 | tf_op jit(solution)/shard_map/ppermute | solution.py:73
  15.9 3.0 collective-permute-start.5
  18.9 2.0 bitcast_convert_fusion.hid_in
  23.2 2.0 collective-permute-done.11
  29.0 3.9 %collective-permute-done.1 = bf16[2,3,24,384]{3,2,1,0:T(8,128)(2,1)S(1)} collective-permute-done((bf16[2,3,24,384]{3,2,1,0:T(8,128)(2,1)S(1)}, bf16[2,3,24,384]{3,2,1,0:T(8,128)(2,1)S(1)}, u32[]{:S(2)}, u32[]{:S(2)}) %collective-permute-start.1) | collective-permute-done | bytes 110624 | tf_op jit(solution)/shard_map/ppermute | solution.py:73
  32.9 3.5 %collective-permute-done.6 = bf16[2,3,24,384]{3,2,1,0:T(8,128)(2,1)S(1)} collective-permute-done((bf16[2,3,24,384]{3,2,1,0:T(8,128)(2,1)S(1)}, bf16[2,3,24,384]{3,2,1,0:T(8,128)(2,1)S(1)}, u32[]{:S(2)}, u32[]{:S(2)}) %collective-permute-start.6) | collective-permute-done | bytes 110624 | tf_op jit(solution)/shard_map/ppermute | solution.py:73
  36.5 1.7 collective-permute-start.7
  39.8 2.7 collective-permute-done.7
  44.2 3.6 %collective-permute-done.2 = bf16[4,3,24,384]{3,2,1,0:T(8,128)(2,1)S(1)} collective-permute-done((bf16[4,3,24,384]{3,2,1,0:T(8,128)(2,1)S(1)}, bf16[4,3,24,384]{3,2,1,0:T(8,128)(2,1)S(1)}, u32[]{:S(2)}, u32[]{:S(2)}) %collective-permute-start.2) | collective-permute-done | bytes 221216 | tf_op jit(solution)/shard_map/ppermute | solution.py:73
  48.0 2.0 collective-permute-start.13
  50.0 12.8 %collective-permute-done.8 = bf16[8,3,24,384]{3,2,1,0:T(8,128)(2,1)S(1)} collective-permute-done((bf16[8,3,24,384]{3,2,1,0:T(8,128)(2,1)S(1)}, bf16[8,3,24,384]{3,2,1,0:T(8,128)(2,1)S(1)}, u32[]{:S(2)}, u32[]{:S(2)}) %collective-permute-start.8) | collective-permute-done | bytes 442400 | tf_op jit(solution)/shard_map/ppermute | solution.py:73
  71.2 2.0 vectors_unpack.1
  74.5 11.0 %first_norm_forward.1 = (bf16[3,1024,768]{2,1,0:T(8,128)(2,1)}, bf16[3,768,768]{2,1,0:T(8,128)(2,1)}) custom-call(s32[1]{0:T(128)} %bitcast.2.core_ref, bf16[1024,768]{1,0:T(8,128)(2,1)} %bitcast.273, bf16[16,3,24,384]{3,2,1,0:T(8,128)(2,1)} %copy-done.2, bf16[16,3,24,384]{3,2,1,0:T(8,128)(2,1)} %copy-done.9, bf16[16,3,24,384]{3,2,1,0:T(8,128)(2,1)} %copy-done.1, ...), custom_call_target="tpu_custom_call" | custom-call | flops 770499968 | bytes 2412000 | tf_op jit(solution)/shard_map/first_norm_forward/pallas_call | solution.py:1220
  85.5 25.5 %attention_forward.1 = (bf16[1024,768]{1,0:T(8,128)(2,1)}, f32[16,1024]{1,0:T(8,128)}) custom-call(s32[2]{0:T(128)} %pad_add_fusion.info_ref, bf16[3,1024,768]{2,1,0:T(8,128)(2,1)} %get-tuple-element.99.q_ref.k_ref.v_ref.qkv_in, bf16[3,1024,768]{2,1,0:T(8,128)(2,1)} %get-tuple-element.99.q_ref.k_ref.v_ref.qkv_in, ...), custom_call_target="tpu_custom_call" | custom-call | flops 2300000000 | bytes 7200000 | tf_op jit(solution)/shard_map/attention_forward/pallas_call | solution.py:270
  111.0 15.2 %thought_rows_forward.1 = (f32[16,1024]{1,0:T(8,128)}, f32[8,3072]{1,0:T(8,128)}, f32[32,384]{1,0:T(8,128)}, f32[8,768]{1,0:T(8,128)}, bf16[3,1024,768]{2,1,0:T(...) custom-call(s32[2]{0:T(128)} %pad_add_fusion.info_ref, ...), custom_call_target="tpu_custom_call", output_to_operand_aliasing={{4}: (8, {}), {5}: (9, {}), {6}: (10, {})} | custom-call | flops 2300000000 | bytes 7200000 | tf_op jit(solution)/shard_map/thought_rows_forward/pallas_call | solution.py:626
  126.2 35.2 %feed_forward_and_back.1 = (bf16[1024,768]{1,0:T(8,128)(2,1)}, bf16[1024,768]{1,0:T(8,128)(2,1)}, bf16[768,768]{1,0:T(8,128)(2,1)}, bf16[768,3072]{1,0:T(8,128)(...) custom-call(f32[1024,768]{1,0:T(8,128)} %get-tuple-element.105.hid_ref, ...), custom_call_target="tpu_custom_call" | custom-call | flops 3449999872 | bytes 10800000 | tf_op jit(solution)/shard_map/feed_forward_and_back/pallas_call | solution.py:944
  161.4 7.9 %proj_weight_terms.1 = bf16[8,4,4,24,768]{4,3,2,1,0:T(8,128)(2,1)} custom-call(bf16[768,3072]{1,0:T(8,128)(2,1)} %get-tuple-element.111.act_ref, bf16[768,768]{1,0:T(8,128)(2,1)} %bitcast_select_fusion.up_ref), custom_call_target="tpu_custom_call" | custom-call | flops 575000000 | bytes 1800000 | tf_op jit(solution)/shard_map/proj_weight_terms/pallas_call | solution.py:1175
  169.4 8.7 %fc_weight_terms.1 = (bf16[16,4,24,768]{3,2,1,0:T(8,128)(2,1)}, bf16[16,4,24,768]{3,2,1,0:T(8,128)(2,1)}) custom-call(s32[1]{0:T(128)} %bitcast.2.core_ref, bf16[768,768]{1,0:T(8,128)(2,1)} %get-tuple-element.112.second_ref, bf16[768,3072]{1,0:T(8,128)(2,1)} %get-tuple-element.113.pg_ref), custom_call_target="tpu_custom_call" | custom-call | flops 575000000 | bytes 1800000 | tf_op jit(solution)/shard_map/fc_weight_terms/pallas_call | solution.py:1145
  178.4 19.3 %thought_rows_backward.1 = (f32[8,3072]{1,0:T(8,128)}, bf16[24,768]{1,0:T(8,128)(2,1)}, bf16[768,768]{1,0:T(8,128)(2,1)}, f32[768,768]{1,0:T(8,128)}) custom-call(s32[2]{0:T(128)} %pad_add_fusion.info_ref, f32[1024,768]{1,0:T(8,128)} %get-tuple-element.105.hid_ref, ...), custom_call_target="tpu_custom_call", output_to_operand_aliasing={{2}: (12, {}), {3}: (13, {})} | custom-call | flops 2300000000 | bytes 7200000 | tf_op jit(solution)/shard_map/thought_rows_backward/pallas_call | solution.py:830
  199.1 2.3 convert_add_fusion
  201.4 1.7 collective-permute-start.16
  204.3 24.7 %attention_backward.1.grad_ref = bf16[3,1024,768]{2,1,0:T(8,128)(2,1)} custom-call(bf16[3,1024,768]{2,1,0:T(8,128)(2,1)} %get-tuple-element.108.qkv_ref.qkv_in.q_ref.k_ref.v_ref, bf16[3,1024,768]{2,1,0:T(8,128)(2,1)} %get-tuple-element.108.qkv_ref.qkv_in.q_ref.k_ref.v_ref, bf16[3,1024,768]{2,1,0:T(8,128)(2,1)} %get-tuple-element.108.qkv_ref.qkv_in.q_ref.k_ref.v_ref, ...), custom_call_target="tpu_custom_call" | custom-call | flops 2495500032 | bytes 7812000 | tf_op jit(solution)/shard_map/attention_backward/pallas_call | solution.py:350
  229.7 2.3 bitcast_add_fusion
  234.6 13.7 %near_weight_terms.1 = (bf16[16,2,24,768]{3,2,1,0:T(8,128)(2,1)}, bf16[16,2,24,768]{3,2,1,0:T(8,128)(2,1)}, bf16[16,2,24,768]{3,2,1,0:T(8,128)(2,1)}, bf16[16,2,...) custom-call(s32[1]{0:T(128)} %bitcast.2.core_ref, bf16[1024,768]{1,0:T(8,128)(2,1)} %get-tuple-element.132.normed_ref, ...), custom_call_target="tpu_custom_call" | custom-call | flops 575000000 | bytes 1800000 | tf_op jit(solution)/shard_map/near_weight_terms/pallas_call | solution.py:1100
  253.6 2.0 bitcast_add_fusion.4
  260.8 10.4 %first_norm_backward.1 = f32[1024,768]{1,0:T(8,128)} custom-call(s32[2]{0:T(128)} %pad_add_fusion.info_ref, f32[1024,768]{1,0:T(8,128)} %get-tuple-element.105.hid_ref, bf16[3,1024,768]{2,1,0:T(8,128)(2,1)} %attention_backward.1.grad_ref, f32[768,768]{1,0:T(8,128)} %get-tuple-element.133.rg_ref, bf16[3,768,768]{2,1,0:T(8,128)(2,1)} %get-tuple-element.102.near_in.near_ref, ...), custom_call_target="tpu_custom_call" | custom-call | flops 954499968 | bytes 2988000 | tf_op jit(solution)/shard_map/first_norm_backward/pallas_call | solution.py:1005
  275.3 1.8 collective-permute-start.35
  279.5 4.8 %collective-permute-done.32 = bf16[2,2,2,24,768]{4,3,1,2,0:T(8,128)(2,1)S(1)} collective-permute-done((bf16[2,2,2,24,768]{4,3,1,2,0:T(8,128)(2,1)S(1)}, bf16[2,2,2,24,768]{4,3,1,2,0:T(8,128)(2,1)S(1)}, u32[]{:S(2)}, u32[]{:S(2)}) %collective-permute-start.32) | collective-permute-done | bytes 294944 | tf_op jit(solution)/shard_map/ppermute | solution.py:73
  286.7 3.5 %collective-permute-done.30 = bf16[2,2,2,24,768]{4,3,2,1,0:T(8,128)(2,1)S(1)} collective-permute-done((bf16[2,2,2,24,768]{4,3,2,1,0:T(8,128)(2,1)S(1)}, bf16[2,2,2,24,768]{4,3,2,1,0:T(8,128)(2,1)S(1)}, u32[]{:S(2)}, u32[]{:S(2)}) %collective-permute-start.30) | collective-permute-done | bytes 294944 | tf_op jit(solution)/shard_map/ppermute | solution.py:73
  293.3 1.8 collective-permute-start.33
  300.4 3.8 %thought_rows_terms.1 = (f32[4,24,768]{2,1,0:T(8,128)}, f32[24,3072]{1,0:T(8,128)}) custom-call(s32[1]{0:T(128)} %bitcast.79.index_ref, bf16[24,32,768]{2,1,0:T(8,128)(2,1)} %bitcast.275, bf16[4,24,768]{2,1,0:T(8,128)(2,1)} %bitcast.284, f32[4,24,768]{2,1,0:T(8,128)} %bitcast_add_fusion.10.fc_ref, bf16[384,384]{1,0:T(8,128)(2,1)} %constant.309.clone.swap_ref), custom_call_target="tpu_custom_call" | custom-call | flops 379500000 | bytes 1188000 | tf_op jit(solution)/shard_map/thought_rows_terms/pallas_call | solution.py:1311
  (181 shorter events, 57.3 us)
Async XLA Ops:
  7.2 103.8 %all-gather.2.cloned.1.call-start = ((), (), s32[]{:S(2)}) async-start(), calls=%async_computation.2 | async-start | bytes 10948608 | tf_op jit(solution)/shard_map/all_gather | solution.py:1571
  9.6 225.0 %reduce-scatter.3.cloned.1.call-start = ((), (), s32[]{:S(2)}) async-start(), calls=%async_computation.3 | async-start | bytes 5308416 | tf_op jit(solution)/shard_map/reduce_scatter | solution.py:1596
  11.7 9.8 %collective-permute-start.10 = (bf16[8,128]{1,0:T(8,128)(2,1)S(1)}, bf16[8,128]{1,0:T(8,128)(2,1)S(1)}, u32[]{:S(2)}, u32[]{:S(2)}) collective-permute-start(bf16[8,128]{1,0:T(8,128)(2,1)S(1)} %convert_element_type.306), channel_id=1, source_target_pairs={{0,4},{1,5},{2,6},{3,7},{4,0},{5,1},{6,2},{7,3},{8,12},{9,13},{10,... | collective-permute-start | bytes 6152 | tf_op jit(solution)/shard_map/ppermute | solution.py:73
  15.8 9.5 %collective-permute-start = (bf16[1,3,24,384]{3,2,1,0:T(8,128)(2,1)S(1)}, bf16[1,3,24,384]{3,2,1,0:T(8,128)(2,1)S(1)}, u32[]{:S(2)}, u32[]{:S(2)}) collective-permute-start(bf16[1,3,24,384]{3,2,1,0:T(8,128)(2,1)S(1)} %maximum_bitcast_fusion), channel_id=1, source_target_pairs={{0,4},{1,5},{2,6},{3,7},{4,0},{5,1},{6,2},{7,3},{8,12},{9,13},{10,... | collective-permute-start | bytes 165896 | tf_op jit(solution)/shard_map/ppermute | solution.py:73
  15.9 11.1 %collective-permute-start.5 = (bf16[1,3,24,384]{3,2,1,0:T(8,128)(2,1)S(1)}, bf16[1,3,24,384]{3,2,1,0:T(8,128)(2,1)S(1)}, u32[]{:S(2)}, u32[]{:S(2)}) collective-permute-start(bf16[1,3,24,384]{3,2,1,0:T(8,128)(2,1)S(1)} %maximum_bitcast_fusion.1), channel_id=1, source_target_pairs={{0,4},{1,5},{2,6},{3,7},{4,0},{5,1},{6,2},{7,3},{8,12},{9,13},{10,... | collective-permute-start | bytes 165896 | tf_op jit(solution)/shard_map/ppermute | solution.py:73
  27.0 9.4 %collective-permute-start.6 = (bf16[2,3,24,384]{3,2,1,0:T(8,128)(2,1)S(1)}, bf16[2,3,24,384]{3,2,1,0:T(8,128)(2,1)S(1)}, u32[]{:S(2)}, u32[]{:S(2)}) collective-permute-start(bf16[2,3,24,384]{3,2,1,0:T(8,128)(2,1)S(1)} %pad_maximum_fusion.12), channel_id=1, source_target_pairs={{0,2},{1,3},{2,0},{3,1},{4,6},{5,7},{6,4},{7,5},{8,10},{9,11},{10,... | collective-permute-start | bytes 331784 | tf_op jit(solution)/shard_map/ppermute | solution.py:73
  27.5 10.7 %collective-permute-start.12 = (bf16[2,2,8,128]{3,2,0,1:T(8,128)(2,1)S(1)}, bf16[2,2,8,128]{3,2,0,1:T(8,128)(2,1)S(1)}, u32[]{:S(2)}, u32[]{:S(2)}) collective-permute-start(bf16[2,2,8,128]{3,2,0,1:T(8,128)(2,1)S(1)} %pad_maximum_fusion.17), channel_id=1, source_target_pairs={{0,8},{8,0},{16,24},{24,16},{1,9},{9,1},{17,25},{25,17},{2,10},{10... | collective-permute-start | bytes 24584 | tf_op jit(solution)/shard_map/ppermute | solution.py:73
  38.2 9.6 %collective-permute-start.2 = (bf16[4,3,24,384]{3,2,1,0:T(8,128)(2,1)S(1)}, bf16[4,3,24,384]{3,2,1,0:T(8,128)(2,1)S(1)}, u32[]{:S(2)}, u32[]{:S(2)}) collective-permute-start(bf16[4,3,24,384]{3,2,1,0:T(8,128)(2,1)S(1)} %pad_maximum_fusion.7), channel_id=1, source_target_pairs={{0,8},{8,0},{16,24},{24,16},{1,9},{9,1},{17,25},{25,17},{2,10},{10... | collective-permute-start | bytes 663560 | tf_op jit(solution)/shard_map/ppermute | solution.py:73
  42.6 20.2 %collective-permute-start.8 = (bf16[8,3,24,384]{3,2,1,0:T(8,128)(2,1)S(1)}, bf16[8,3,24,384]{3,2,1,0:T(8,128)(2,1)S(1)}, u32[]{:S(2)}, u32[]{:S(2)}) collective-permute-start(bf16[8,3,24,384]{3,2,1,0:T(8,128)(2,1)S(1)} %pad_maximum_fusion.5), channel_id=1, source_target_pairs={{0,8},{8,0},{16,24},{24,16},{1,9},{9,1},{17,25},{25,17},{2,10},{10... | collective-permute-start | bytes 1327112 | tf_op jit(solution)/shard_map/ppermute | solution.py:73
  47.9 15.2 %collective-permute-start.3 = (bf16[8,3,24,384]{3,2,1,0:T(8,128)(2,1)S(1)}, bf16[8,3,24,384]{3,2,1,0:T(8,128)(2,1)S(1)}, u32[]{:S(2)}, u32[]{:S(2)}) collective-permute-start(bf16[8,3,24,384]{3,2,1,0:T(8,128)(2,1)S(1)} %pad_maximum_fusion.4), channel_id=1, source_target_pairs={{0,16},{8,24},{16,0},{24,8},{1,17},{9,25},{17,1},{25,9},{2,18},{10... | collective-permute-start | bytes 1327112 | tf_op jit(solution)/shard_map/ppermute | solution.py:73
  48.0 18.6 %collective-permute-start.13 = (bf16[2,2,2,8,128]{4,3,1,2,0:T(8,128)(2,1)S(1)}, bf16[2,2,2,8,128]{4,3,1,2,0:T(8,128)(2,1)S(1)}, u32[]{:S(2)}, u32[]{:S(2)}) collective-permute-start(bf16[2,2,2,8,128]{4,3,1,2,0:T(8,128)(2,1)S(1)} %pad_maximum_fusion.16), channel_id=1, source_target_pairs={{0,16},{8,24},{16,0},{24,8},{1,17},{9,25},{17,1},{25,9},{2,18},{10... | collective-permute-start | bytes 49160 | tf_op jit(solution)/shard_map/ppermute | solution.py:73
  63.0 10.2 %collective-permute-start.9 = (bf16[16,3,24,384]{3,2,1,0:T(8,128)(2,1)S(1)}, bf16[16,3,24,384]{3,2,1,0:T(8,128)(2,1)S(1)}, u32[]{:S(2)}, u32[]{:S(2)}) collective-permute-start(bf16[16,3,24,384]{3,2,1,0:T(8,128)(2,1)S(1)} %pad_maximum_fusion.2.right_mine), channel_id=1, source_target_pairs={{0,1},{1,0},{2,3},{3,2},{4,5},{5,4},{6,7},{7,6},{8,9},{9,8},{10,11... | collective-permute-start | bytes 2654216 | tf_op jit(solution)/shard_map/ppermute | solution.py:73
  64.0 9.3 %collective-permute-start.4 = (bf16[16,3,24,384]{3,2,1,0:T(8,128)(2,1)S(1)}, bf16[16,3,24,384]{3,2,1,0:T(8,128)(2,1)S(1)}, u32[]{:S(2)}, u32[]{:S(2)}) collective-permute-start(bf16[16,3,24,384]{3,2,1,0:T(8,128)(2,1)S(1)} %pad_maximum_fusion.1.left_mine), channel_id=1, source_target_pairs={{0,1},{1,0},{2,3},{3,2},{4,5},{5,4},{6,7},{7,6},{8,9},{9,8},{10,11... | collective-permute-start | bytes 2654216 | tf_op jit(solution)/shard_map/ppermute | solution.py:73
  169.4 131.1 %reduce-scatter.5.cloned.1.call-start = ((), (), s32[]{:S(2)}) async-start(), calls=%async_computation.4 | async-start | bytes 737280 | tf_op jit(solution)/shard_map/reduce_scatter | solution.py:1602
  178.1 19.6 %collective-permute-start.15 = (bf16[2,2,2,2,4,24,768]{6,5,4,3,2,1,0:T(8,128)(2,1)}, bf16[2,2,2,2,4,24,768]{6,5,4,3,2,1,0:T(8,128)(2,1)S(1)}, u32[]{:S(2)}, u32[]{:S(2)}) collective-permute-start(bf16[2,2,2,2,4,24,768]{6,5,4,3,2,1,0:T(8,128)(2,1)} %bitcast.287), channel_id=1, source_target_pairs={{0,1},{1,0},{2,3},{3,2},{4,5},{5,4},{6,7},{7,6},{8,9},{9,8},{10,11... | collective-permute-start | bytes 7077896 | tf_op jit(solution)/shard_map/ppermute | solution.py:73
  201.4 28.3 %collective-permute-start.16 = (bf16[2,2,2,4,24,768]{5,4,3,2,1,0:T(8,128)(2,1)S(1)}, bf16[2,2,2,4,24,768]{5,4,3,2,1,0:T(8,128)(2,1)}, u32[]{:S(2)}, u32[]{:S(2)}) collective-permute-start(bf16[2,2,2,4,24,768]{5,4,3,2,1,0:T(8,128)(2,1)S(1)} %get-tuple-element.181), channel_id=1, source_target_pairs={{0,8},{8,0},{16,24},{24,16},{1,9},{9,1},{17,25},{25,17},{2,10},{10... | collective-permute-start | bytes 3538952 | tf_op jit(solution)/shard_map/ppermute | solution.py:73
  203.1 25.9 %collective-permute-start.17 = (bf16[24,768]{1,0:T(8,128)(2,1)}, bf16[24,768]{1,0:T(8,128)(2,1)S(1)}, u32[]{:S(2)}, u32[]{:S(2)}) collective-permute-start(bf16[24,768]{1,0:T(8,128)(2,1)} %get-tuple-element.125), channel_id=1, source_target_pairs={{0,4},{1,5},{2,6},{3,7},{4,0},{5,1},{6,2},{7,3},{8,12},{9,13},{10,... | collective-permute-start | bytes 110600 | tf_op jit(solution)/shard_map/ppermute | solution.py:73
  232.1 16.3 %collective-permute-start.18 = (bf16[2,2,4,24,768]{4,3,2,1,0:T(8,128)(2,1)}, bf16[2,2,4,24,768]{4,3,2,1,0:T(8,128)(2,1)S(1)}, u32[]{:S(2)}, u32[]{:S(2)}) collective-permute-start(bf16[2,2,4,24,768]{4,3,2,1,0:T(8,128)(2,1)} %get-tuple-element.183), channel_id=1, source_target_pairs={{0,16},{8,24},{16,0},{24,8},{1,17},{9,25},{17,1},{25,9},{2,18},{10... | collective-permute-start | bytes 1769480 | tf_op jit(solution)/shard_map/ppermute | solution.py:73
  233.2 15.1 %collective-permute-start.19 = (bf16[2,24,768]{2,1,0:T(8,128)(2,1)S(1)}, bf16[2,24,768]{2,1,0:T(8,128)(2,1)S(1)}, u32[]{:S(2)}, u32[]{:S(2)}) collective-permute-start(bf16[2,24,768]{2,1,0:T(8,128)(2,1)S(1)} %pad_maximum_fusion.13), channel_id=1, source_target_pairs={{0,2},{1,3},{2,0},{3,1},{4,6},{5,7},{6,4},{7,5},{8,10},{9,11},{10,... | collective-permute-start | bytes 221192 | tf_op jit(solution)/shard_map/ppermute | solution.py:73
  251.9 19.2 %collective-permute-start.28 = (bf16[2,2,24,768]{3,2,0,1:T(8,128)(2,1)}, bf16[2,2,24,768]{3,2,0,1:T(8,128)(2,1)}, u32[]{:S(2)}, u32[]{:S(2)}) collective-permute-start(bf16[2,2,24,768]{3,2,0,1:T(8,128)(2,1)} %pad_maximum_fusion.10), channel_id=1, source_target_pairs={{0,16},{8,24},{16,0},{24,8},{1,17},{9,25},{17,1},{25,9},{2,18},{10... | collective-permute-start | bytes 442376 | tf_op jit(solution)/shard_map/ppermute | solution.py:73
  255.6 17.5 %collective-permute-start.27 = (bf16[2,4,24,768]{3,2,1,0:T(8,128)(2,1)}, bf16[2,4,24,768]{3,2,1,0:T(8,128)(2,1)}, u32[]{:S(2)}, u32[]{:S(2)}) collective-permute-start(bf16[2,4,24,768]{3,2,1,0:T(8,128)(2,1)} %get-tuple-element.193), channel_id=1, source_target_pairs={{0,2},{1,3},{2,0},{3,1},{4,6},{5,7},{6,4},{7,5},{8,10},{9,11},{10,... | collective-permute-start | bytes 884744 | tf_op jit(solution)/shard_map/ppermute | solution.py:73
  256.4 16.7 %collective-permute-start.23 = (bf16[2,2,2,8,128]{4,3,1,2,0:T(8,128)(2,1)S(1)}, bf16[2,2,2,8,128]{4,3,1,2,0:T(8,128)(2,1)S(1)}, u32[]{:S(2)}, u32[]{:S(2)}) collective-permute-start(bf16[2,2,2,8,128]{4,3,1,2,0:T(8,128)(2,1)S(1)} %get-tuple-element.233), channel_id=1, source_target_pairs={{0,16},{8,24},{16,0},{24,8},{1,17},{9,25},{17,1},{25,9},{2,18},{10... | collective-permute-start | bytes 49160 | tf_op jit(solution)/shard_map/ppermute | solution.py:73
  257.9 19.2 %collective-permute-start.26 = (bf16[2,2,2,2,24,768]{5,4,3,2,1,0:T(8,128)(2,1)S(1)}, bf16[2,2,2,2,24,768]{5,4,3,2,1,0:T(8,128)(2,1)S(1)}, u32[]{:S(2)}, u32[]{:S(2)}) collective-permute-start(bf16[2,2,2,2,24,768]{5,4,3,2,1,0:T(8,128)(2,1)S(1)} %get-tuple-element.185), channel_id=1, source_target_pairs={{0,8},{8,0},{16,24},{24,16},{1,9},{9,1},{17,25},{25,17},{2,10},{10... | collective-permute-start | bytes 1769480 | tf_op jit(solution)/shard_map/ppermute | solution.py:73
  259.4 17.7 %collective-permute-start.25 = (bf16[2,2,2,2,24,768]{5,4,3,2,1,0:T(8,128)(2,1)S(1)}, bf16[2,2,2,2,24,768]{5,4,3,2,1,0:T(8,128)(2,1)S(1)}, u32[]{:S(2)}, u32[]{:S(2)}) collective-permute-start(bf16[2,2,2,2,24,768]{5,4,3,2,1,0:T(8,128)(2,1)S(1)} %get-tuple-element.187), channel_id=1, source_target_pairs={{0,16},{8,24},{16,0},{24,8},{1,17},{9,25},{17,1},{25,9},{2,18},{10... | collective-permute-start | bytes 1769480 | tf_op jit(solution)/shard_map/ppermute | solution.py:73
  272.1 12.1 %collective-permute-start.32 = (bf16[2,2,2,24,768]{4,3,1,2,0:T(8,128)(2,1)S(1)}, bf16[2,2,2,24,768]{4,3,1,2,0:T(8,128)(2,1)S(1)}, u32[]{:S(2)}, u32[]{:S(2)}) collective-permute-start(bf16[2,2,2,24,768]{4,3,1,2,0:T(8,128)(2,1)S(1)} %pad_maximum_fusion.6), channel_id=1, source_target_pairs={{0,8},{8,0},{16,24},{24,16},{1,9},{9,1},{17,25},{25,17},{2,10},{10... | collective-permute-start | bytes 884744 | tf_op jit(solution)/shard_map/ppermute | solution.py:73
  273.1 11.3 %collective-permute-start.24 = (bf16[2,2,8,128]{3,2,0,1:T(8,128)(2,1)S(1)}, bf16[2,2,8,128]{3,2,0,1:T(8,128)(2,1)S(1)}, u32[]{:S(2)}, u32[]{:S(2)}) collective-permute-start(bf16[2,2,8,128]{3,2,0,1:T(8,128)(2,1)S(1)} %get-tuple-element.238), channel_id=1, source_target_pairs={{0,8},{8,0},{16,24},{24,16},{1,9},{9,1},{17,25},{25,17},{2,10},{10... | collective-permute-start | bytes 24584 | tf_op jit(solution)/shard_map/ppermute | solution.py:73
  275.3 9.2 %collective-permute-start.35 = (bf16[4,24,768]{2,1,0:T(8,128)(2,1)S(1)}, bf16[4,24,768]{2,1,0:T(8,128)(2,1)S(1)}, u32[]{:S(2)}, u32[]{:S(2)}) collective-permute-start(bf16[4,24,768]{2,1,0:T(8,128)(2,1)S(1)} %fusion.14), channel_id=1, source_target_pairs={{0,4},{1,5},{2,6},{3,7},{4,0},{5,1},{6,2},{7,3},{8,12},{9,13},{10,... | collective-permute-start | bytes 442376 | tf_op jit(solution)/shard_map/ppermute | solution.py:73
  278.3 11.9 %collective-permute-start.30 = (bf16[2,2,2,24,768]{4,3,2,1,0:T(8,128)(2,1)S(1)}, bf16[2,2,2,24,768]{4,3,2,1,0:T(8,128)(2,1)S(1)}, u32[]{:S(2)}, u32[]{:S(2)}) collective-permute-start(bf16[2,2,2,24,768]{4,3,2,1,0:T(8,128)(2,1)S(1)} %get-tuple-element.191), channel_id=1, source_target_pairs={{0,8},{8,0},{16,24},{24,16},{1,9},{9,1},{17,25},{25,17},{2,10},{10... | collective-permute-start | bytes 884744 | tf_op jit(solution)/shard_map/ppermute | solution.py:73
  284.4 14.4 %collective-permute-start.34 = (bf16[2,2,2,2,24,768]{5,4,2,3,0,1:T(8,128)(2,1)S(1)}, bf16[2,2,2,2,24,768]{5,4,2,3,0,1:T(8,128)(2,1)S(1)}, u32[]{:S(2)}, u32[]{:S(2)}) collective-permute-start(bf16[2,2,2,2,24,768]{5,4,2,3,0,1:T(8,128)(2,1)S(1)} %pad_maximum_fusion.3), channel_id=1, source_target_pairs={{0,1},{1,0},{2,3},{3,2},{4,5},{5,4},{6,7},{7,6},{8,9},{9,8},{10,11... | collective-permute-start | bytes 1769480 | tf_op jit(solution)/shard_map/ppermute | solution.py:73
  284.5 8.8 %collective-permute-start.29 = (bf16[2,8,128]{2,1,0:T(8,128)(2,1)S(1)}, bf16[2,8,128]{2,1,0:T(8,128)(2,1)S(1)}, u32[]{:S(2)}, u32[]{:S(2)}) collective-permute-start(bf16[2,8,128]{2,1,0:T(8,128)(2,1)S(1)} %get-tuple-element.242), channel_id=1, source_target_pairs={{0,2},{1,3},{2,0},{3,1},{4,6},{5,7},{6,4},{7,5},{8,10},{9,11},{10,... | collective-permute-start | bytes 12296 | tf_op jit(solution)/shard_map/ppermute | solution.py:73
  286.0 9.2 %collective-permute-start.37 = (bf16[2,2,24,768]{3,2,1,0:T(8,128)(2,1)S(1)}, bf16[2,2,24,768]{3,2,1,0:T(8,128)(2,1)S(1)}, u32[]{:S(2)}, u32[]{:S(2)}) collective-permute-start(bf16[2,2,24,768]{3,2,1,0:T(8,128)(2,1)S(1)} %get-tuple-element.197), channel_id=1, source_target_pairs={{0,2},{1,3},{2,0},{3,1},{4,6},{5,7},{6,4},{7,5},{8,10},{9,11},{10,... | collective-permute-start | bytes 442376 | tf_op jit(solution)/shard_map/ppermute | solution.py:73
  293.3 11.7 %collective-permute-start.33 = (bf16[8,128]{1,0:T(8,128)(2,1)S(1)}, bf16[8,128]{1,0:T(8,128)(2,1)S(1)}, u32[]{:S(2)}, u32[]{:S(2)}) collective-permute-start(bf16[8,128]{1,0:T(8,128)(2,1)S(1)} %fusion.43), channel_id=1, source_target_pairs={{0,4},{1,5},{2,6},{3,7},{4,0},{5,1},{6,2},{7,3},{8,12},{9,13},{10,... | collective-permute-start | bytes 6152 | tf_op jit(solution)/shard_map/ppermute | solution.py:73
  (30 other events, 153.5 us)
Sparse Core Ops, SparseCore 0:
  11.2 99.5 all-gather.1
  169.5 55.9 reduce-scatter.2
  252.0 28.0 reduce-scatter.4

commit v7 on v6

--- a/solution.py
+++ b/solution.py
@@ -1126,65 +1126,67 @@
     )(core, normed_low, qkv_grad, mixed_low, resid_grad, near, vec, feed_sums, row_sums, *maps)
 
 
-def fc_terms_kernel(chips, core_ref, second_ref, pg_ref, keep_ref, send_ref, second_t):
-    @pl.when(pl.program_id(0) == 0)
+def far_terms_kernel(
+    outer, inner, chips, core_ref, act_ref, up_ref, second_ref, pg_ref, proj_ref, keep_ref, send_ref,
+    second_t,
+):
+    step = pl.program_id(0)
+    blocks = pl.num_programs(0) // 2
+
+    @pl.when(step == 0)
     def _():
         second_t[...] = second_ref[...].T
 
-    value = dot(second_t[...], pg_ref[...])
-    keep_and_send(value, core_ref[0], chips, keep_ref, send_ref, 0)
-
-
-def fc_terms(core, second_low, pre_grad, chips):
+    @pl.when(step < blocks)
+    def _():
+        value = dot_tn(act_ref[...], up_ref[...])
+        rows, width = value.shape
+        value = value.reshape(outer, inner, rows // (outer * inner), width)
+        for i in range(inner):
+            proj_ref[i, :, 0] = value[:, i].astype(BF16)
+
+    @pl.when(step >= blocks)
+    def _():
+        value = dot(second_t[...], pg_ref[...])
+        keep_and_send(value, core_ref[0], chips, keep_ref, send_ref, 0)
+
+
+def far_terms(core, act_low, upstream_low, second_low, pre_grad, outer, inner, chips):
+    rows, units = pre_grad.shape
     width = second_low.shape[1]
-    rows, units = pre_grad.shape
     blocks = units // width
-    own = width // (2 * len(chips))
+    own = width // (outer * inner)
+    proj = (inner, outer, blocks, own, width)
     half = jax.ShapeDtypeStruct((len(chips), blocks, own, width), BF16)
-    out = pl.BlockSpec((len(chips), 1, own, width), lambda j: (0, j, 0, 0))
+
+    def early(i):
+        return jnp.minimum(i, blocks - 1)
+
+    def late(i):
+        return jnp.maximum(i - blocks, 0)
+
+    out = pl.BlockSpec((len(chips), 1, own, width), lambda i: (0, late(i), 0, 0))
     return pl.pallas_call(
-        functools.partial(fc_terms_kernel, chips),
-        grid=(blocks,),
+        functools.partial(far_terms_kernel, outer, inner, chips),
+        grid=(2 * blocks,),
         in_specs=[
             pl.BlockSpec(memory_space=pltpu.SMEM),
-            pl.BlockSpec((rows, width), lambda j: (0, 0)),
-            pl.BlockSpec((rows, width), lambda j: (0, j)),
-        ],
-        out_specs=[out, out],
-        out_shape=[half, half],
+            pl.BlockSpec((rows, width), lambda i: (0, early(i))),
+            whole(upstream_low),
+            whole(second_low),
+            pl.BlockSpec((rows, width), lambda i: (0, late(i))),
+        ],
+        out_specs=[
+            pl.BlockSpec((inner, outer, 1, own, width), lambda i: (0, 0, early(i), 0, 0)),
+            out,
+            out,
+        ],
+        out_shape=[jax.ShapeDtypeStruct(proj, BF16), half, half],
         scratch_shapes=[pltpu.VMEM((width, rows), BF16)],
         compiler_params=pltpu.CompilerParams(vmem_limit_bytes=VMEM_LIMIT),
-        cost_estimate=cost(0.5),
-        name="fc_weight_terms",
-    )(core, second_low, pre_grad)
-
-
-def proj_terms_kernel(outer, inner, act_ref, up_ref, out_ref):
-    value = dot_tn(act_ref[...], up_ref[...])
-    rows, width = value.shape
-    value = value.reshape(outer, inner, rows // (outer * inner), width)
-    for i in range(inner):
-        out_ref[i, :, 0] = value[:, i].astype(BF16)
-
-
-def proj_terms(act_low, upstream_low, outer, inner):
-    units = act_low.shape[1]
-    rows, width = upstream_low.shape
-    blocks = units // width
-    shape = (inner, outer, blocks, width // (outer * inner), width)
-    return pl.pallas_call(
-        functools.partial(proj_terms_kernel, outer, inner),
-        grid=(blocks,),
-        in_specs=[
-            pl.BlockSpec((rows, width), lambda j: (0, j)),
-            pl.BlockSpec((rows, width), lambda j: (0, 0)),
-        ],
-        out_specs=pl.BlockSpec((inner, outer, 1) + shape[3:], lambda j: (0, 0, j, 0, 0)),
-        out_shape=jax.ShapeDtypeStruct(shape, BF16),
-        compiler_params=pltpu.CompilerParams(vmem_limit_bytes=VMEM_LIMIT),
-        cost_estimate=cost(0.5),
-        name="proj_weight_terms",
-    )(act_low, upstream_low)
+        cost_estimate=cost(1),
+        name="far_weight_terms",
+    )(core, act_low, upstream_low, second_low, pre_grad)
 
 
 def first_kernel(
@@ -1453,9 +1455,8 @@
         hidden, mixed_low, upstream_low, weights, vec, fc_bias
     )
 
-    proj_grad = comm.proj_terms(act_low, upstream_low)
+    proj_grad, *halves = comm.far_terms(act_low, upstream_low, second_low, pre_grad)
     proj_half = comm.early(proj_grad)
-    halves = fc_terms(comm.core, after(second_low, proj_grad), pre_grad, comm.chips("zyxc"))
     fc_going = comm.scatter(halves, "zyxc")
     sent = go_after([fc_going])
     row_sums, factors, mixed_grad, resid_grad = thoughts_back(
@@ -1588,8 +1589,17 @@
         core = (lax.axis_index("fsdp") % 2)[None].astype(jnp.int32)
 
         @staticmethod
-        def proj_terms(act_low, upstream_low):
-            return proj_terms(act_low, upstream_low, links.sizes["dp"], links.sizes["fsdp"])
+        def far_terms(act_low, upstream_low, second_low, pre_grad):
+            sizes_here = links.sizes["dp"], links.sizes["fsdp"]
+            return far_terms(
+                Comm.core,
+                act_low,
+                upstream_low,
+                second_low,
+                pre_grad,
+                *sizes_here,
+                links.chips("zyxc"),
+            )
 
         @staticmethod
         def early(value):

time: 319 us -> 317 us (level)
    pallas_call x2 -> x1, Pallas kernels: 16.6 us -> 14.7 us  [far_terms(): pl.pallas_call(functools.partial(far_terms_kernel, outer, inner, chips),...]
  transfers between devices with their start and end apart: 43 -> 43, of which waited for: 12 -> 13; matrix products, arithmetic and copies ran while one was open for 7% -> 7% of each run, Pallas kernels for 38% -> 36%
where the time goes in v7:
time: 317 us; the launch traced here: 313 us
  Pallas kernels  181 us (57%)
  starting transfers between devices  46.6 us (15%)
  waiting for transfers between devices  38.8 us (12%)
  other arithmetic  21.2 us (7%)
  between operations  15.9 us (5%)
  local copies, waits for them, and re-layouts  9.7 us (3%)
    ppermute x40, starting transfers between devices, swap(): lax.ppermute(value, axis, [(i, i ^ bit) for i in range(self.sizes[axis])])  46.4 us
    ppermute x40, waiting for transfers between devices, swap(): lax.ppermute(value, axis, [(i, i ^ bit) for i in range(self.sizes[axis])])  38.7 us
    pallas_call x1, Pallas kernels, feed(): pl.pallas_call(feed_kernel, grid=(seq_len // BLOCK,), in_specs=[rows(widt...  35.4 us
    pallas_call x1, Pallas kernels, attend(): pl.pallas_call(attend_kernel, grid=(pairs,), in_specs=[pl.BlockSpec(memor...  25.5 us
    pallas_call x1, Pallas kernels, attend_back(): pl.pallas_call(attend_back_kernel, grid=(width // PAIR,), in_specs=[*(col...  24.7 us
    pallas_call x1, Pallas kernels, thoughts_back(): pl.pallas_call(thoughts_back_kernel, grid=(1,), in_specs=[pl.BlockSpec(me...  19.6 us
    pallas_call x1, Pallas kernels, thoughts_forward(): pl.pallas_call(thoughts_kernel, grid=(1,), in_specs=[pl.BlockSpec(memory_...  15.1 us
    pallas_call x1, Pallas kernels, far_terms(): pl.pallas_call(functools.partial(far_terms_kernel, outer, inner, chips),...  14.7 us
  transfers between devices with their start and end apart: 43, of which 13 were waited for; matrix products, arithmetic and copies ran while one was open for 7% of the time, Pallas kernels for 36%

profile of v7, /device:TPU:0, one launch (start us, length us, event | category | flops | bytes accessed | tf_op | source)
XLA Modules:
  0.0 313.2 jit_solution(14749497059412651587)
XLA Ops:
  7.2 2.3 far_shard.1
  11.7 4.0 %collective-permute-start.10 = (bf16[8,128]{1,0:T(8,128)(2,1)S(1)}, bf16[8,128]{1,0:T(8,128)(2,1)S(1)}, u32[]{:S(2)}, u32[]{:S(2)}) collective-permute-start(bf16[8,128]{1,0:T(8,128)(2,1)S(1)} %convert_element_type.306), channel_id=1, source_target_pairs={{0,4},{1,5},{2,6},{3,7},{4,0},{5,1},{6,2},{7,3},{8,12},{9,13},{10,... | collective-permute-start | bytes 6152 | tf_op jit(solution)/shard_map/ppermute | solution.py:73
  15.9 3.0 collective-permute-start.5
  18.9 2.0 bitcast_convert_fusion.hid_in
  23.2 2.0 collective-permute-done.11
  29.0 3.9 %collective-permute-done.1 = bf16[2,3,24,384]{3,2,1,0:T(8,128)(2,1)S(1)} collective-permute-done((bf16[2,3,24,384]{3,2,1,0:T(8,128)(2,1)S(1)}, bf16[2,3,24,384]{3,2,1,0:T(8,128)(2,1)S(1)}, u32[]{:S(2)}, u32[]{:S(2)}) %collective-permute-start.1) | collective-permute-done | bytes 110624 | tf_op jit(solution)/shard_map/ppermute | solution.py:73
  32.9 3.5 %collective-permute-done.6 = bf16[2,3,24,384]{3,2,1,0:T(8,128)(2,1)S(1)} collective-permute-done((bf16[2,3,24,384]{3,2,1,0:T(8,128)(2,1)S(1)}, bf16[2,3,24,384]{3,2,1,0:T(8,128)(2,1)S(1)}, u32[]{:S(2)}, u32[]{:S(2)}) %collective-permute-start.6) | collective-permute-done | bytes 110624 | tf_op jit(solution)/shard_map/ppermute | solution.py:73
  36.5 1.7 collective-permute-start.7
  39.8 2.7 collective-permute-done.7
  44.2 3.6 %collective-permute-done.2 = bf16[4,3,24,384]{3,2,1,0:T(8,128)(2,1)S(1)} collective-permute-done((bf16[4,3,24,384]{3,2,1,0:T(8,128)(2,1)S(1)}, bf16[4,3,24,384]{3,2,1,0:T(8,128)(2,1)S(1)}, u32[]{:S(2)}, u32[]{:S(2)}) %collective-permute-start.2) | collective-permute-done | bytes 221216 | tf_op jit(solution)/shard_map/ppermute | solution.py:73
  48.0 2.0 collective-permute-start.13
  50.0 12.8 %collective-permute-done.8 = bf16[8,3,24,384]{3,2,1,0:T(8,128)(2,1)S(1)} collective-permute-done((bf16[8,3,24,384]{3,2,1,0:T(8,128)(2,1)S(1)}, bf16[8,3,24,384]{3,2,1,0:T(8,128)(2,1)S(1)}, u32[]{:S(2)}, u32[]{:S(2)}) %collective-permute-start.8) | collective-permute-done | bytes 442400 | tf_op jit(solution)/shard_map/ppermute | solution.py:73
  71.3 2.0 vectors_unpack.1
  74.5 11.1 %first_norm_forward.1 = (bf16[3,1024,768]{2,1,0:T(8,128)(2,1)}, bf16[3,768,768]{2,1,0:T(8,128)(2,1)}) custom-call(s32[1]{0:T(128)} %bitcast.2.core_ref, bf16[1024,768]{1,0:T(8,128)(2,1)} %bitcast.272, bf16[16,3,24,384]{3,2,1,0:T(8,128)(2,1)} %copy-done.2, bf16[16,3,24,384]{3,2,1,0:T(8,128)(2,1)} %copy-done.9, bf16[16,3,24,384]{3,2,1,0:T(8,128)(2,1)} %copy-done.1, ...), custom_call_target="tpu_custom_call" | custom-call | flops 770499968 | bytes 2412000 | tf_op jit(solution)/shard_map/first_norm_forward/pallas_call | solution.py:1222
  85.5 25.5 %attention_forward.1 = (bf16[1024,768]{1,0:T(8,128)(2,1)}, f32[16,1024]{1,0:T(8,128)}) custom-call(s32[2]{0:T(128)} %pad_add_fusion.info_ref, bf16[3,1024,768]{2,1,0:T(8,128)(2,1)} %get-tuple-element.99.q_ref.k_ref.v_ref.qkv_in, bf16[3,1024,768]{2,1,0:T(8,128)(2,1)} %get-tuple-element.99.q_ref.k_ref.v_ref.qkv_in, ...), custom_call_target="tpu_custom_call" | custom-call | flops 2300000000 | bytes 7200000 | tf_op jit(solution)/shard_map/attention_forward/pallas_call | solution.py:270
  111.0 15.1 %thought_rows_forward.1 = (f32[16,1024]{1,0:T(8,128)}, f32[8,3072]{1,0:T(8,128)}, f32[32,384]{1,0:T(8,128)}, f32[8,768]{1,0:T(8,128)}, bf16[3,1024,768]{2,1,0:T(...) custom-call(s32[2]{0:T(128)} %pad_add_fusion.info_ref, ...), custom_call_target="tpu_custom_call", output_to_operand_aliasing={{4}: (8, {}), {5}: (9, {}), {6}: (10, {})} | custom-call | flops 2300000000 | bytes 7200000 | tf_op jit(solution)/shard_map/thought_rows_forward/pallas_call | solution.py:626
  126.1 35.4 %feed_forward_and_back.1 = (bf16[1024,768]{1,0:T(8,128)(2,1)}, bf16[1024,768]{1,0:T(8,128)(2,1)}, bf16[768,768]{1,0:T(8,128)(2,1)}, bf16[768,3072]{1,0:T(8,128)(...) custom-call(f32[1024,768]{1,0:T(8,128)} %get-tuple-element.105.hid_ref, ...), custom_call_target="tpu_custom_call" | custom-call | flops 3449999872 | bytes 10800000 | tf_op jit(solution)/shard_map/feed_forward_and_back/pallas_call | solution.py:944
  161.6 14.7 %far_weight_terms.1 = (bf16[8,4,4,24,768]{4,3,2,1,0:T(8,128)(2,1)}, bf16[16,4,24,768]{3,2,1,0:T(8,128)(2,1)}, bf16[16,4,24,768]{3,2,1,0:T(8,128)(2,1)}) custom-call(s32[1]{0:T(128)} %bitcast.2.core_ref, bf16[768,3072]{1,0:T(8,128)(2,1)} %get-tuple-element.110.act_ref, bf16[768,768]{1,0:T(8,128)(2,1)} %bitcast_select_fusion.up_ref, ...), custom_call_target="tpu_custom_call" | custom-call | flops 1150000000 | bytes 3600000 | tf_op jit(solution)/shard_map/far_weight_terms/pallas_call | solution.py:1169
  176.8 19.6 %thought_rows_backward.1 = (f32[8,3072]{1,0:T(8,128)}, bf16[24,768]{1,0:T(8,128)(2,1)}, bf16[768,768]{1,0:T(8,128)(2,1)}, f32[768,768]{1,0:T(8,128)}) custom-call(s32[2]{0:T(128)} %pad_add_fusion.info_ref, f32[1024,768]{1,0:T(8,128)} %get-tuple-element.105.hid_ref, ...), custom_call_target="tpu_custom_call", output_to_operand_aliasing={{2}: (12, {}), {3}: (13, {})} | custom-call | flops 2300000000 | bytes 7200000 | tf_op jit(solution)/shard_map/thought_rows_backward/pallas_call | solution.py:830
  197.9 2.3 convert_add_fusion
  200.1 1.8 collective-permute-start.16
  203.2 24.7 %attention_backward.1.grad_ref = bf16[3,1024,768]{2,1,0:T(8,128)(2,1)} custom-call(bf16[3,1024,768]{2,1,0:T(8,128)(2,1)} %get-tuple-element.108.qkv_ref.qkv_in.q_ref.k_ref.v_ref, bf16[3,1024,768]{2,1,0:T(8,128)(2,1)} %get-tuple-element.108.qkv_ref.qkv_in.q_ref.k_ref.v_ref, bf16[3,1024,768]{2,1,0:T(8,128)(2,1)} %get-tuple-element.108.qkv_ref.qkv_in.q_ref.k_ref.v_ref, ...), custom_call_target="tpu_custom_call" | custom-call | flops 2495500032 | bytes 7812000 | tf_op jit(solution)/shard_map/attention_backward/pallas_call | solution.py:350
  228.4 2.4 bitcast_add_fusion
  233.4 13.6 %near_weight_terms.1 = (bf16[16,2,24,768]{3,2,1,0:T(8,128)(2,1)}, bf16[16,2,24,768]{3,2,1,0:T(8,128)(2,1)}, bf16[16,2,24,768]{3,2,1,0:T(8,128)(2,1)}, bf16[16,2,...) custom-call(s32[1]{0:T(128)} %bitcast.2.core_ref, bf16[1024,768]{1,0:T(8,128)(2,1)} %get-tuple-element.132.normed_ref, ...), custom_call_target="tpu_custom_call" | custom-call | flops 575000000 | bytes 1800000 | tf_op jit(solution)/shard_map/near_weight_terms/pallas_call | solution.py:1100
  252.2 2.0 bitcast_add_fusion.4
  259.4 10.5 %first_norm_backward.1 = f32[1024,768]{1,0:T(8,128)} custom-call(s32[2]{0:T(128)} %pad_add_fusion.info_ref, f32[1024,768]{1,0:T(8,128)} %get-tuple-element.105.hid_ref, bf16[3,1024,768]{2,1,0:T(8,128)(2,1)} %attention_backward.1.grad_ref, f32[768,768]{1,0:T(8,128)} %get-tuple-element.133.rg_ref, bf16[3,768,768]{2,1,0:T(8,128)(2,1)} %get-tuple-element.102.near_in.near_ref, ...), custom_call_target="tpu_custom_call" | custom-call | flops 954499968 | bytes 2988000 | tf_op jit(solution)/shard_map/first_norm_backward/pallas_call | solution.py:1005
  274.1 1.8 collective-permute-start.35
  278.2 4.7 %collective-permute-done.32 = bf16[2,2,2,24,768]{4,3,1,2,0:T(8,128)(2,1)S(1)} collective-permute-done((bf16[2,2,2,24,768]{4,3,1,2,0:T(8,128)(2,1)S(1)}, bf16[2,2,2,24,768]{4,3,1,2,0:T(8,128)(2,1)S(1)}, u32[]{:S(2)}, u32[]{:S(2)}) %collective-permute-start.32) | collective-permute-done | bytes 294944 | tf_op jit(solution)/shard_map/ppermute | solution.py:73
  285.4 3.6 %collective-permute-done.30 = bf16[2,2,2,24,768]{4,3,2,1,0:T(8,128)(2,1)S(1)} collective-permute-done((bf16[2,2,2,24,768]{4,3,2,1,0:T(8,128)(2,1)S(1)}, bf16[2,2,2,24,768]{4,3,2,1,0:T(8,128)(2,1)S(1)}, u32[]{:S(2)}, u32[]{:S(2)}) %collective-permute-start.30) | collective-permute-done | bytes 294944 | tf_op jit(solution)/shard_map/ppermute | solution.py:73
  290.3 1.7 bitcast_add_fusion.10.fc_ref
  292.0 1.8 collective-permute-start.33
  299.2 3.8 %thought_rows_terms.1 = (f32[4,24,768]{2,1,0:T(8,128)}, f32[24,3072]{1,0:T(8,128)}) custom-call(s32[1]{0:T(128)} %bitcast.79.index_ref, bf16[24,32,768]{2,1,0:T(8,128)(2,1)} %bitcast.275, bf16[4,24,768]{2,1,0:T(8,128)(2,1)} %bitcast.284, f32[4,24,768]{2,1,0:T(8,128)} %bitcast_add_fusion.10.fc_ref, bf16[384,384]{1,0:T(8,128)(2,1)} %constant.309.clone.swap_ref), custom_call_target="tpu_custom_call" | custom-call | flops 379500000 | bytes 1188000 | tf_op jit(solution)/shard_map/thought_rows_terms/pallas_call | solution.py:1313
  (180 shorter events, 55.7 us)
Async XLA Ops:
  7.2 103.8 %all-gather.2.cloned.1.call-start = ((), (), s32[]{:S(2)}) async-start(), calls=%async_computation.2 | async-start | bytes 10948608 | tf_op jit(solution)/shard_map/all_gather | solution.py:1572
  9.6 223.8 %reduce-scatter.3.cloned.1.call-start = ((), (), s32[]{:S(2)}) async-start(), calls=%async_computation.3 | async-start | bytes 5308416 | tf_op jit(solution)/shard_map/reduce_scatter | solution.py:1606
  11.7 9.8 %collective-permute-start.10 = (bf16[8,128]{1,0:T(8,128)(2,1)S(1)}, bf16[8,128]{1,0:T(8,128)(2,1)S(1)}, u32[]{:S(2)}, u32[]{:S(2)}) collective-permute-start(bf16[8,128]{1,0:T(8,128)(2,1)S(1)} %convert_element_type.306), channel_id=1, source_target_pairs={{0,4},{1,5},{2,6},{3,7},{4,0},{5,1},{6,2},{7,3},{8,12},{9,13},{10,... | collective-permute-start | bytes 6152 | tf_op jit(solution)/shard_map/ppermute | solution.py:73
  15.8 9.5 %collective-permute-start = (bf16[1,3,24,384]{3,2,1,0:T(8,128)(2,1)S(1)}, bf16[1,3,24,384]{3,2,1,0:T(8,128)(2,1)S(1)}, u32[]{:S(2)}, u32[]{:S(2)}) collective-permute-start(bf16[1,3,24,384]{3,2,1,0:T(8,128)(2,1)S(1)} %maximum_bitcast_fusion), channel_id=1, source_target_pairs={{0,4},{1,5},{2,6},{3,7},{4,0},{5,1},{6,2},{7,3},{8,12},{9,13},{10,... | collective-permute-start | bytes 165896 | tf_op jit(solution)/shard_map/ppermute | solution.py:73
  15.9 11.1 %collective-permute-start.5 = (bf16[1,3,24,384]{3,2,1,0:T(8,128)(2,1)S(1)}, bf16[1,3,24,384]{3,2,1,0:T(8,128)(2,1)S(1)}, u32[]{:S(2)}, u32[]{:S(2)}) collective-permute-start(bf16[1,3,24,384]{3,2,1,0:T(8,128)(2,1)S(1)} %maximum_bitcast_fusion.1), channel_id=1, source_target_pairs={{0,4},{1,5},{2,6},{3,7},{4,0},{5,1},{6,2},{7,3},{8,12},{9,13},{10,... | collective-permute-start | bytes 165896 | tf_op jit(solution)/shard_map/ppermute | solution.py:73
  27.0 9.4 %collective-permute-start.6 = (bf16[2,3,24,384]{3,2,1,0:T(8,128)(2,1)S(1)}, bf16[2,3,24,384]{3,2,1,0:T(8,128)(2,1)S(1)}, u32[]{:S(2)}, u32[]{:S(2)}) collective-permute-start(bf16[2,3,24,384]{3,2,1,0:T(8,128)(2,1)S(1)} %pad_maximum_fusion.12), channel_id=1, source_target_pairs={{0,2},{1,3},{2,0},{3,1},{4,6},{5,7},{6,4},{7,5},{8,10},{9,11},{10,... | collective-permute-start | bytes 331784 | tf_op jit(solution)/shard_map/ppermute | solution.py:73
  27.5 10.7 %collective-permute-start.12 = (bf16[2,2,8,128]{3,2,0,1:T(8,128)(2,1)S(1)}, bf16[2,2,8,128]{3,2,0,1:T(8,128)(2,1)S(1)}, u32[]{:S(2)}, u32[]{:S(2)}) collective-permute-start(bf16[2,2,8,128]{3,2,0,1:T(8,128)(2,1)S(1)} %pad_maximum_fusion.17), channel_id=1, source_target_pairs={{0,8},{8,0},{16,24},{24,16},{1,9},{9,1},{17,25},{25,17},{2,10},{10... | collective-permute-start | bytes 24584 | tf_op jit(solution)/shard_map/ppermute | solution.py:73
  38.2 9.6 %collective-permute-start.2 = (bf16[4,3,24,384]{3,2,1,0:T(8,128)(2,1)S(1)}, bf16[4,3,24,384]{3,2,1,0:T(8,128)(2,1)S(1)}, u32[]{:S(2)}, u32[]{:S(2)}) collective-permute-start(bf16[4,3,24,384]{3,2,1,0:T(8,128)(2,1)S(1)} %pad_maximum_fusion.7), channel_id=1, source_target_pairs={{0,8},{8,0},{16,24},{24,16},{1,9},{9,1},{17,25},{25,17},{2,10},{10... | collective-permute-start | bytes 663560 | tf_op jit(solution)/shard_map/ppermute | solution.py:73
  42.6 20.2 %collective-permute-start.8 = (bf16[8,3,24,384]{3,2,1,0:T(8,128)(2,1)S(1)}, bf16[8,3,24,384]{3,2,1,0:T(8,128)(2,1)S(1)}, u32[]{:S(2)}, u32[]{:S(2)}) collective-permute-start(bf16[8,3,24,384]{3,2,1,0:T(8,128)(2,1)S(1)} %pad_maximum_fusion.5), channel_id=1, source_target_pairs={{0,8},{8,0},{16,24},{24,16},{1,9},{9,1},{17,25},{25,17},{2,10},{10... | collective-permute-start | bytes 1327112 | tf_op jit(solution)/shard_map/ppermute | solution.py:73
  47.9 15.2 %collective-permute-start.3 = (bf16[8,3,24,384]{3,2,1,0:T(8,128)(2,1)S(1)}, bf16[8,3,24,384]{3,2,1,0:T(8,128)(2,1)S(1)}, u32[]{:S(2)}, u32[]{:S(2)}) collective-permute-start(bf16[8,3,24,384]{3,2,1,0:T(8,128)(2,1)S(1)} %pad_maximum_fusion.4), channel_id=1, source_target_pairs={{0,16},{8,24},{16,0},{24,8},{1,17},{9,25},{17,1},{25,9},{2,18},{10... | collective-permute-start | bytes 1327112 | tf_op jit(solution)/shard_map/ppermute | solution.py:73
  48.0 18.6 %collective-permute-start.13 = (bf16[2,2,2,8,128]{4,3,1,2,0:T(8,128)(2,1)S(1)}, bf16[2,2,2,8,128]{4,3,1,2,0:T(8,128)(2,1)S(1)}, u32[]{:S(2)}, u32[]{:S(2)}) collective-permute-start(bf16[2,2,2,8,128]{4,3,1,2,0:T(8,128)(2,1)S(1)} %pad_maximum_fusion.16), channel_id=1, source_target_pairs={{0,16},{8,24},{16,0},{24,8},{1,17},{9,25},{17,1},{25,9},{2,18},{10... | collective-permute-start | bytes 49160 | tf_op jit(solution)/shard_map/ppermute | solution.py:73
  63.0 10.2 %collective-permute-start.9 = (bf16[16,3,24,384]{3,2,1,0:T(8,128)(2,1)S(1)}, bf16[16,3,24,384]{3,2,1,0:T(8,128)(2,1)S(1)}, u32[]{:S(2)}, u32[]{:S(2)}) collective-permute-start(bf16[16,3,24,384]{3,2,1,0:T(8,128)(2,1)S(1)} %pad_maximum_fusion.2.right_mine), channel_id=1, source_target_pairs={{0,1},{1,0},{2,3},{3,2},{4,5},{5,4},{6,7},{7,6},{8,9},{9,8},{10,11... | collective-permute-start | bytes 2654216 | tf_op jit(solution)/shard_map/ppermute | solution.py:73
  64.0 9.3 %collective-permute-start.4 = (bf16[16,3,24,384]{3,2,1,0:T(8,128)(2,1)S(1)}, bf16[16,3,24,384]{3,2,1,0:T(8,128)(2,1)S(1)}, u32[]{:S(2)}, u32[]{:S(2)}) collective-permute-start(bf16[16,3,24,384]{3,2,1,0:T(8,128)(2,1)S(1)} %pad_maximum_fusion.1.left_mine), channel_id=1, source_target_pairs={{0,1},{1,0},{2,3},{3,2},{4,5},{5,4},{6,7},{7,6},{8,9},{9,8},{10,11... | collective-permute-start | bytes 2654216 | tf_op jit(solution)/shard_map/ppermute | solution.py:73
  176.3 122.9 %reduce-scatter.5.cloned.1.call-start = ((), (), s32[]{:S(2)}) async-start(), calls=%async_computation.4 | async-start | bytes 737280 | tf_op jit(solution)/shard_map/reduce_scatter | solution.py:1612
  176.4 20.0 %collective-permute-start.15 = (bf16[2,2,2,2,4,24,768]{6,5,4,3,2,1,0:T(8,128)(2,1)}, bf16[2,2,2,2,4,24,768]{6,5,4,3,2,1,0:T(8,128)(2,1)S(1)}, u32[]{:S(2)}, u32[]{:S(2)}) collective-permute-start(bf16[2,2,2,2,4,24,768]{6,5,4,3,2,1,0:T(8,128)(2,1)} %bitcast.287), channel_id=1, source_target_pairs={{0,1},{1,0},{2,3},{3,2},{4,5},{5,4},{6,7},{7,6},{8,9},{9,8},{10,11... | collective-permute-start | bytes 7077896 | tf_op jit(solution)/shard_map/ppermute | solution.py:73
  200.1 28.2 %collective-permute-start.16 = (bf16[2,2,2,4,24,768]{5,4,3,2,1,0:T(8,128)(2,1)S(1)}, bf16[2,2,2,4,24,768]{5,4,3,2,1,0:T(8,128)(2,1)}, u32[]{:S(2)}, u32[]{:S(2)}) collective-permute-start(bf16[2,2,2,4,24,768]{5,4,3,2,1,0:T(8,128)(2,1)S(1)} %get-tuple-element.181), channel_id=1, source_target_pairs={{0,8},{8,0},{16,24},{24,16},{1,9},{9,1},{17,25},{25,17},{2,10},{10... | collective-permute-start | bytes 3538952 | tf_op jit(solution)/shard_map/ppermute | solution.py:73
  201.9 26.0 %collective-permute-start.17 = (bf16[24,768]{1,0:T(8,128)(2,1)}, bf16[24,768]{1,0:T(8,128)(2,1)S(1)}, u32[]{:S(2)}, u32[]{:S(2)}) collective-permute-start(bf16[24,768]{1,0:T(8,128)(2,1)} %get-tuple-element.124), channel_id=1, source_target_pairs={{0,4},{1,5},{2,6},{3,7},{4,0},{5,1},{6,2},{7,3},{8,12},{9,13},{10,... | collective-permute-start | bytes 110600 | tf_op jit(solution)/shard_map/ppermute | solution.py:73
  230.7 16.3 %collective-permute-start.18 = (bf16[2,2,4,24,768]{4,3,2,1,0:T(8,128)(2,1)}, bf16[2,2,4,24,768]{4,3,2,1,0:T(8,128)(2,1)S(1)}, u32[]{:S(2)}, u32[]{:S(2)}) collective-permute-start(bf16[2,2,4,24,768]{4,3,2,1,0:T(8,128)(2,1)} %get-tuple-element.183), channel_id=1, source_target_pairs={{0,16},{8,24},{16,0},{24,8},{1,17},{9,25},{17,1},{25,9},{2,18},{10... | collective-permute-start | bytes 1769480 | tf_op jit(solution)/shard_map/ppermute | solution.py:73
  232.1 14.9 %collective-permute-start.19 = (bf16[2,24,768]{2,1,0:T(8,128)(2,1)S(1)}, bf16[2,24,768]{2,1,0:T(8,128)(2,1)S(1)}, u32[]{:S(2)}, u32[]{:S(2)}) collective-permute-start(bf16[2,24,768]{2,1,0:T(8,128)(2,1)S(1)} %pad_maximum_fusion.13), channel_id=1, source_target_pairs={{0,2},{1,3},{2,0},{3,1},{4,6},{5,7},{6,4},{7,5},{8,10},{9,11},{10,... | collective-permute-start | bytes 221192 | tf_op jit(solution)/shard_map/ppermute | solution.py:73
  250.6 19.4 %collective-permute-start.28 = (bf16[2,2,24,768]{3,2,0,1:T(8,128)(2,1)}, bf16[2,2,24,768]{3,2,0,1:T(8,128)(2,1)}, u32[]{:S(2)}, u32[]{:S(2)}) collective-permute-start(bf16[2,2,24,768]{3,2,0,1:T(8,128)(2,1)} %pad_maximum_fusion.10), channel_id=1, source_target_pairs={{0,16},{8,24},{16,0},{24,8},{1,17},{9,25},{17,1},{25,9},{2,18},{10... | collective-permute-start | bytes 442376 | tf_op jit(solution)/shard_map/ppermute | solution.py:73
  254.2 17.8 %collective-permute-start.27 = (bf16[2,4,24,768]{3,2,1,0:T(8,128)(2,1)}, bf16[2,4,24,768]{3,2,1,0:T(8,128)(2,1)}, u32[]{:S(2)}, u32[]{:S(2)}) collective-permute-start(bf16[2,4,24,768]{3,2,1,0:T(8,128)(2,1)} %get-tuple-element.193), channel_id=1, source_target_pairs={{0,2},{1,3},{2,0},{3,1},{4,6},{5,7},{6,4},{7,5},{8,10},{9,11},{10,... | collective-permute-start | bytes 884744 | tf_op jit(solution)/shard_map/ppermute | solution.py:73
  255.0 17.0 %collective-permute-start.23 = (bf16[2,2,2,8,128]{4,3,1,2,0:T(8,128)(2,1)S(1)}, bf16[2,2,2,8,128]{4,3,1,2,0:T(8,128)(2,1)S(1)}, u32[]{:S(2)}, u32[]{:S(2)}) collective-permute-start(bf16[2,2,2,8,128]{4,3,1,2,0:T(8,128)(2,1)S(1)} %get-tuple-element.233), channel_id=1, source_target_pairs={{0,16},{8,24},{16,0},{24,8},{1,17},{9,25},{17,1},{25,9},{2,18},{10... | collective-permute-start | bytes 49160 | tf_op jit(solution)/shard_map/ppermute | solution.py:73
  256.7 19.2 %collective-permute-start.26 = (bf16[2,2,2,2,24,768]{5,4,3,2,1,0:T(8,128)(2,1)S(1)}, bf16[2,2,2,2,24,768]{5,4,3,2,1,0:T(8,128)(2,1)S(1)}, u32[]{:S(2)}, u32[]{:S(2)}) collective-permute-start(bf16[2,2,2,2,24,768]{5,4,3,2,1,0:T(8,128)(2,1)S(1)} %get-tuple-element.185), channel_id=1, source_target_pairs={{0,8},{8,0},{16,24},{24,16},{1,9},{9,1},{17,25},{25,17},{2,10},{10... | collective-permute-start | bytes 1769480 | tf_op jit(solution)/shard_map/ppermute | solution.py:73
  258.1 17.8 %collective-permute-start.25 = (bf16[2,2,2,2,24,768]{5,4,3,2,1,0:T(8,128)(2,1)S(1)}, bf16[2,2,2,2,24,768]{5,4,3,2,1,0:T(8,128)(2,1)S(1)}, u32[]{:S(2)}, u32[]{:S(2)}) collective-permute-start(bf16[2,2,2,2,24,768]{5,4,3,2,1,0:T(8,128)(2,1)S(1)} %get-tuple-element.187), channel_id=1, source_target_pairs={{0,16},{8,24},{16,0},{24,8},{1,17},{9,25},{17,1},{25,9},{2,18},{10... | collective-permute-start | bytes 1769480 | tf_op jit(solution)/shard_map/ppermute | solution.py:73
  271.0 12.0 %collective-permute-start.32 = (bf16[2,2,2,24,768]{4,3,1,2,0:T(8,128)(2,1)S(1)}, bf16[2,2,2,24,768]{4,3,1,2,0:T(8,128)(2,1)S(1)}, u32[]{:S(2)}, u32[]{:S(2)}) collective-permute-start(bf16[2,2,2,24,768]{4,3,1,2,0:T(8,128)(2,1)S(1)} %pad_maximum_fusion.6), channel_id=1, source_target_pairs={{0,8},{8,0},{16,24},{24,16},{1,9},{9,1},{17,25},{25,17},{2,10},{10... | collective-permute-start | bytes 884744 | tf_op jit(solution)/shard_map/ppermute | solution.py:73
  272.0 11.2 %collective-permute-start.24 = (bf16[2,2,8,128]{3,2,0,1:T(8,128)(2,1)S(1)}, bf16[2,2,8,128]{3,2,0,1:T(8,128)(2,1)S(1)}, u32[]{:S(2)}, u32[]{:S(2)}) collective-permute-start(bf16[2,2,8,128]{3,2,0,1:T(8,128)(2,1)S(1)} %get-tuple-element.238), channel_id=1, source_target_pairs={{0,8},{8,0},{16,24},{24,16},{1,9},{9,1},{17,25},{25,17},{2,10},{10... | collective-permute-start | bytes 24584 | tf_op jit(solution)/shard_map/ppermute | solution.py:73
  274.1 9.1 %collective-permute-start.35 = (bf16[4,24,768]{2,1,0:T(8,128)(2,1)S(1)}, bf16[4,24,768]{2,1,0:T(8,128)(2,1)S(1)}, u32[]{:S(2)}, u32[]{:S(2)}) collective-permute-start(bf16[4,24,768]{2,1,0:T(8,128)(2,1)S(1)} %fusion.14), channel_id=1, source_target_pairs={{0,4},{1,5},{2,6},{3,7},{4,0},{5,1},{6,2},{7,3},{8,12},{9,13},{10,... | collective-permute-start | bytes 442376 | tf_op jit(solution)/shard_map/ppermute | solution.py:73
  277.3 11.7 %collective-permute-start.30 = (bf16[2,2,2,24,768]{4,3,2,1,0:T(8,128)(2,1)S(1)}, bf16[2,2,2,24,768]{4,3,2,1,0:T(8,128)(2,1)S(1)}, u32[]{:S(2)}, u32[]{:S(2)}) collective-permute-start(bf16[2,2,2,24,768]{4,3,2,1,0:T(8,128)(2,1)S(1)} %get-tuple-element.191), channel_id=1, source_target_pairs={{0,8},{8,0},{16,24},{24,16},{1,9},{9,1},{17,25},{25,17},{2,10},{10... | collective-permute-start | bytes 884744 | tf_op jit(solution)/shard_map/ppermute | solution.py:73
  283.1 14.5 %collective-permute-start.34 = (bf16[2,2,2,2,24,768]{5,4,2,3,0,1:T(8,128)(2,1)S(1)}, bf16[2,2,2,2,24,768]{5,4,2,3,0,1:T(8,128)(2,1)S(1)}, u32[]{:S(2)}, u32[]{:S(2)}) collective-permute-start(bf16[2,2,2,2,24,768]{5,4,2,3,0,1:T(8,128)(2,1)S(1)} %pad_maximum_fusion.3), channel_id=1, source_target_pairs={{0,1},{1,0},{2,3},{3,2},{4,5},{5,4},{6,7},{7,6},{8,9},{9,8},{10,11... | collective-permute-start | bytes 1769480 | tf_op jit(solution)/shard_map/ppermute | solution.py:73
  283.2 8.8 %collective-permute-start.29 = (bf16[2,8,128]{2,1,0:T(8,128)(2,1)S(1)}, bf16[2,8,128]{2,1,0:T(8,128)(2,1)S(1)}, u32[]{:S(2)}, u32[]{:S(2)}) collective-permute-start(bf16[2,8,128]{2,1,0:T(8,128)(2,1)S(1)} %get-tuple-element.242), channel_id=1, source_target_pairs={{0,2},{1,3},{2,0},{3,1},{4,6},{5,7},{6,4},{7,5},{8,10},{9,11},{10,... | collective-permute-start | bytes 12296 | tf_op jit(solution)/shard_map/ppermute | solution.py:73
  284.6 9.2 %collective-permute-start.37 = (bf16[2,2,24,768]{3,2,1,0:T(8,128)(2,1)S(1)}, bf16[2,2,24,768]{3,2,1,0:T(8,128)(2,1)S(1)}, u32[]{:S(2)}, u32[]{:S(2)}) collective-permute-start(bf16[2,2,24,768]{3,2,1,0:T(8,128)(2,1)S(1)} %get-tuple-element.197), channel_id=1, source_target_pairs={{0,2},{1,3},{2,0},{3,1},{4,6},{5,7},{6,4},{7,5},{8,10},{9,11},{10,... | collective-permute-start | bytes 442376 | tf_op jit(solution)/shard_map/ppermute | solution.py:73
  292.0 11.9 %collective-permute-start.33 = (bf16[8,128]{1,0:T(8,128)(2,1)S(1)}, bf16[8,128]{1,0:T(8,128)(2,1)S(1)}, u32[]{:S(2)}, u32[]{:S(2)}) collective-permute-start(bf16[8,128]{1,0:T(8,128)(2,1)S(1)} %fusion.43), channel_id=1, source_target_pairs={{0,4},{1,5},{2,6},{3,7},{4,0},{5,1},{6,2},{7,3},{8,12},{9,13},{10,... | collective-permute-start | bytes 6152 | tf_op jit(solution)/shard_map/ppermute | solution.py:73
  (30 other events, 154.7 us)
Sparse Core Ops, SparseCore 0:
  11.2 99.5 all-gather.1
  176.5 55.8 reduce-scatter.2
  250.7 28.0 reduce-scatter.4

commit v8 on v7

--- a/solution.py
+++ b/solution.py
@@ -1457,7 +1457,7 @@
 
     proj_grad, *halves = comm.far_terms(act_low, upstream_low, second_low, pre_grad)
     proj_half = comm.early(proj_grad)
-    fc_going = comm.scatter(halves, "zyxc")
+    fc_going = comm.scatter(halves, "zxyc")
     sent = go_after([fc_going])
     row_sums, factors, mixed_grad, resid_grad = thoughts_back(
         info,
@@ -1598,7 +1598,7 @@
                 second_low,
                 pre_grad,
                 *sizes_here,
-                links.chips("zyxc"),
+                links.chips("zxyc"),
             )
 
         @staticmethod

time: 317 us -> 317 us (level)
  transfers between devices with their start and end apart: 43 -> 43, of which waited for: 13 -> 14; matrix products, arithmetic and copies ran while one was open for 7% -> 7% of each run, Pallas kernels for 36% -> 36%
where the time goes in v8:
time: 317 us; the launch traced here: 313 us
  Pallas kernels  181 us (57%)
  starting transfers between devices  46.5 us (15%)
  waiting for transfers between devices  37.8 us (12%)
  other arithmetic  21.2 us (7%)
  between operations  15.9 us (5%)
  local copies, waits for them, and re-layouts  10.3 us (3%)
    ppermute x40, starting transfers between devices, swap(): lax.ppermute(value, axis, [(i, i ^ bit) for i in range(self.sizes[axis])])  46.3 us
    ppermute x40, waiting for transfers between devices, swap(): lax.ppermute(value, axis, [(i, i ^ bit) for i in range(self.sizes[axis])])  37.7 us
    pallas_call x1, Pallas kernels, feed(): pl.pallas_call(feed_kernel, grid=(seq_len // BLOCK,), in_specs=[rows(widt...  35.4 us
    pallas_call x1, Pallas kernels, attend(): pl.pallas_call(attend_kernel, grid=(pairs,), in_specs=[pl.BlockSpec(memor...  25.5 us
    pallas_call x1, Pallas kernels, attend_back(): pl.pallas_call(attend_back_kernel, grid=(width // PAIR,), in_specs=[*(col...  24.7 us
    pallas_call x1, Pallas kernels, thoughts_back(): pl.pallas_call(thoughts_back_kernel, grid=(1,), in_specs=[pl.BlockSpec(me...  19.6 us
    pallas_call x1, Pallas kernels, thoughts_forward(): pl.pallas_call(thoughts_kernel, grid=(1,), in_specs=[pl.BlockSpec(memory_...  15.1 us
    pallas_call x1, Pallas kernels, far_terms(): pl.pallas_call(functools.partial(far_terms_kernel, outer, inner, chips),...  14.7 us
  transfers between devices with their start and end apart: 43, of which 14 were waited for; matrix products, arithmetic and copies ran while one was open for 7% of the time, Pallas kernels for 36%

profile of v8, /device:TPU:0, one launch (start us, length us, event | category | flops | bytes accessed | tf_op | source)
XLA Modules:
  0.0 312.7 jit_solution(3578596201182512008)
XLA Ops:
  7.2 2.3 far_shard.1
  11.7 4.0 %collective-permute-start.10 = (bf16[8,128]{1,0:T(8,128)(2,1)S(1)}, bf16[8,128]{1,0:T(8,128)(2,1)S(1)}, u32[]{:S(2)}, u32[]{:S(2)}) collective-permute-start(bf16[8,128]{1,0:T(8,128)(2,1)S(1)} %convert_element_type.306), channel_id=1, source_target_pairs={{0,4},{1,5},{2,6},{3,7},{4,0},{5,1},{6,2},{7,3},{8,12},{9,13},{10,... | collective-permute-start | bytes 6152 | tf_op jit(solution)/shard_map/ppermute | solution.py:73
  15.9 3.0 collective-permute-start.5
  18.9 2.0 bitcast_convert_fusion.hid_in
  23.2 2.0 collective-permute-done.11
  29.0 3.9 %collective-permute-done.1 = bf16[2,3,24,384]{3,2,1,0:T(8,128)(2,1)S(1)} collective-permute-done((bf16[2,3,24,384]{3,2,1,0:T(8,128)(2,1)S(1)}, bf16[2,3,24,384]{3,2,1,0:T(8,128)(2,1)S(1)}, u32[]{:S(2)}, u32[]{:S(2)}) %collective-permute-start.1) | collective-permute-done | bytes 110624 | tf_op jit(solution)/shard_map/ppermute | solution.py:73
  32.9 3.5 %collective-permute-done.6 = bf16[2,3,24,384]{3,2,1,0:T(8,128)(2,1)S(1)} collective-permute-done((bf16[2,3,24,384]{3,2,1,0:T(8,128)(2,1)S(1)}, bf16[2,3,24,384]{3,2,1,0:T(8,128)(2,1)S(1)}, u32[]{:S(2)}, u32[]{:S(2)}) %collective-permute-start.6) | collective-permute-done | bytes 110624 | tf_op jit(solution)/shard_map/ppermute | solution.py:73
  36.5 1.7 collective-permute-start.7
  39.8 2.7 collective-permute-done.7
  44.2 3.6 %collective-permute-done.2 = bf16[4,3,24,384]{3,2,1,0:T(8,128)(2,1)S(1)} collective-permute-done((bf16[4,3,24,384]{3,2,1,0:T(8,128)(2,1)S(1)}, bf16[4,3,24,384]{3,2,1,0:T(8,128)(2,1)S(1)}, u32[]{:S(2)}, u32[]{:S(2)}) %collective-permute-start.2) | collective-permute-done | bytes 221216 | tf_op jit(solution)/shard_map/ppermute | solution.py:73
  48.0 2.0 collective-permute-start.13
  50.0 12.8 %collective-permute-done.8 = bf16[8,3,24,384]{3,2,1,0:T(8,128)(2,1)S(1)} collective-permute-done((bf16[8,3,24,384]{3,2,1,0:T(8,128)(2,1)S(1)}, bf16[8,3,24,384]{3,2,1,0:T(8,128)(2,1)S(1)}, u32[]{:S(2)}, u32[]{:S(2)}) %collective-permute-start.8) | collective-permute-done | bytes 442400 | tf_op jit(solution)/shard_map/ppermute | solution.py:73
  71.3 2.0 vectors_unpack.1
  74.5 11.1 %first_norm_forward.1 = (bf16[3,1024,768]{2,1,0:T(8,128)(2,1)}, bf16[3,768,768]{2,1,0:T(8,128)(2,1)}) custom-call(s32[1]{0:T(128)} %bitcast.2.core_ref, bf16[1024,768]{1,0:T(8,128)(2,1)} %bitcast.272, bf16[16,3,24,384]{3,2,1,0:T(8,128)(2,1)} %copy-done.2, bf16[16,3,24,384]{3,2,1,0:T(8,128)(2,1)} %copy-done.9, bf16[16,3,24,384]{3,2,1,0:T(8,128)(2,1)} %copy-done.1, ...), custom_call_target="tpu_custom_call" | custom-call | flops 770499968 | bytes 2412000 | tf_op jit(solution)/shard_map/first_norm_forward/pallas_call | solution.py:1222
  85.5 25.5 %attention_forward.1 = (bf16[1024,768]{1,0:T(8,128)(2,1)}, f32[16,1024]{1,0:T(8,128)}) custom-call(s32[2]{0:T(128)} %pad_add_fusion.info_ref, bf16[3,1024,768]{2,1,0:T(8,128)(2,1)} %get-tuple-element.99.q_ref.k_ref.v_ref.qkv_in, bf16[3,1024,768]{2,1,0:T(8,128)(2,1)} %get-tuple-element.99.q_ref.k_ref.v_ref.qkv_in, ...), custom_call_target="tpu_custom_call" | custom-call | flops 2300000000 | bytes 7200000 | tf_op jit(solution)/shard_map/attention_forward/pallas_call | solution.py:270
  111.0 15.1 %thought_rows_forward.1 = (f32[16,1024]{1,0:T(8,128)}, f32[8,3072]{1,0:T(8,128)}, f32[32,384]{1,0:T(8,128)}, f32[8,768]{1,0:T(8,128)}, bf16[3,1024,768]{2,1,0:T(...) custom-call(s32[2]{0:T(128)} %pad_add_fusion.info_ref, ...), custom_call_target="tpu_custom_call", output_to_operand_aliasing={{4}: (8, {}), {5}: (9, {}), {6}: (10, {})} | custom-call | flops 2300000000 | bytes 7200000 | tf_op jit(solution)/shard_map/thought_rows_forward/pallas_call | solution.py:626
  126.1 35.4 %feed_forward_and_back.1 = (bf16[1024,768]{1,0:T(8,128)(2,1)}, bf16[1024,768]{1,0:T(8,128)(2,1)}, bf16[768,768]{1,0:T(8,128)(2,1)}, bf16[768,3072]{1,0:T(8,128)(...) custom-call(f32[1024,768]{1,0:T(8,128)} %get-tuple-element.105.hid_ref, ...), custom_call_target="tpu_custom_call" | custom-call | flops 3449999872 | bytes 10800000 | tf_op jit(solution)/shard_map/feed_forward_and_back/pallas_call | solution.py:944
  161.6 14.7 %far_weight_terms.1 = (bf16[8,4,4,24,768]{4,3,2,1,0:T(8,128)(2,1)}, bf16[16,4,24,768]{3,2,1,0:T(8,128)(2,1)}, bf16[16,4,24,768]{3,2,1,0:T(8,128)(2,1)}) custom-call(s32[1]{0:T(128)} %bitcast.2.core_ref, bf16[768,3072]{1,0:T(8,128)(2,1)} %get-tuple-element.110.act_ref, bf16[768,768]{1,0:T(8,128)(2,1)} %bitcast_select_fusion.up_ref, ...), custom_call_target="tpu_custom_call" | custom-call | flops 1150000000 | bytes 3600000 | tf_op jit(solution)/shard_map/far_weight_terms/pallas_call | solution.py:1169
  176.8 19.6 %thought_rows_backward.1 = (f32[8,3072]{1,0:T(8,128)}, bf16[24,768]{1,0:T(8,128)(2,1)}, bf16[768,768]{1,0:T(8,128)(2,1)}, f32[768,768]{1,0:T(8,128)}) custom-call(s32[2]{0:T(128)} %pad_add_fusion.info_ref, f32[1024,768]{1,0:T(8,128)} %get-tuple-element.105.hid_ref, ...), custom_call_target="tpu_custom_call", output_to_operand_aliasing={{2}: (12, {}), {3}: (13, {})} | custom-call | flops 2300000000 | bytes 7200000 | tf_op jit(solution)/shard_map/thought_rows_backward/pallas_call | solution.py:830
  197.9 2.3 convert_add_fusion
  201.5 1.8 collective-permute-start.17
  203.2 24.7 %attention_backward.1.grad_ref = bf16[3,1024,768]{2,1,0:T(8,128)(2,1)} custom-call(bf16[3,1024,768]{2,1,0:T(8,128)(2,1)} %get-tuple-element.108.qkv_ref.qkv_in.q_ref.k_ref.v_ref, bf16[3,1024,768]{2,1,0:T(8,128)(2,1)} %get-tuple-element.108.qkv_ref.qkv_in.q_ref.k_ref.v_ref, bf16[3,1024,768]{2,1,0:T(8,128)(2,1)} %get-tuple-element.108.qkv_ref.qkv_in.q_ref.k_ref.v_ref, ...), custom_call_target="tpu_custom_call" | custom-call | flops 2495500032 | bytes 7812000 | tf_op jit(solution)/shard_map/attention_backward/pallas_call | solution.py:350
  228.4 2.4 bitcast_add_fusion
  230.7 1.7 collective-permute-start.18
  233.4 13.6 %near_weight_terms.1 = (bf16[16,2,24,768]{3,2,1,0:T(8,128)(2,1)}, bf16[16,2,24,768]{3,2,1,0:T(8,128)(2,1)}, bf16[16,2,24,768]{3,2,1,0:T(8,128)(2,1)}, bf16[16,2,...) custom-call(s32[1]{0:T(128)} %bitcast.2.core_ref, bf16[1024,768]{1,0:T(8,128)(2,1)} %get-tuple-element.132.normed_ref, ...), custom_call_target="tpu_custom_call" | custom-call | flops 575000000 | bytes 1800000 | tf_op jit(solution)/shard_map/near_weight_terms/pallas_call | solution.py:1100
  252.2 2.0 bitcast_add_fusion.4
  259.1 10.6 %first_norm_backward.1 = f32[1024,768]{1,0:T(8,128)} custom-call(s32[2]{0:T(128)} %pad_add_fusion.info_ref, f32[1024,768]{1,0:T(8,128)} %get-tuple-element.105.hid_ref, bf16[3,1024,768]{2,1,0:T(8,128)(2,1)} %attention_backward.1.grad_ref, f32[768,768]{1,0:T(8,128)} %get-tuple-element.133.rg_ref, bf16[3,768,768]{2,1,0:T(8,128)(2,1)} %get-tuple-element.102.near_in.near_ref, ...), custom_call_target="tpu_custom_call" | custom-call | flops 954499968 | bytes 2988000 | tf_op jit(solution)/shard_map/first_norm_backward/pallas_call | solution.py:1005
  278.4 4.3 %collective-permute-done.32 = bf16[2,2,2,24,768]{4,3,1,2,0:T(8,128)(2,1)S(1)} collective-permute-done((bf16[2,2,2,24,768]{4,3,1,2,0:T(8,128)(2,1)S(1)}, bf16[2,2,2,24,768]{4,3,1,2,0:T(8,128)(2,1)S(1)}, u32[]{:S(2)}, u32[]{:S(2)}) %collective-permute-start.32) | collective-permute-done | bytes 294944 | tf_op jit(solution)/shard_map/ppermute | solution.py:73
  285.1 3.0 collective-permute-done.30
  291.4 2.5 collective-permute-start.33
  293.9 2.2 collective-permute-start.38
  298.6 3.8 %thought_rows_terms.1 = (f32[4,24,768]{2,1,0:T(8,128)}, f32[24,3072]{1,0:T(8,128)}) custom-call(s32[1]{0:T(128)} %bitcast.79.index_ref, bf16[24,32,768]{2,1,0:T(8,128)(2,1)} %bitcast.275, bf16[4,24,768]{2,1,0:T(8,128)(2,1)} %bitcast.284, f32[4,24,768]{2,1,0:T(8,128)} %bitcast_add_fusion.10.fc_ref, bf16[384,384]{1,0:T(8,128)(2,1)} %constant.309.clone.swap_ref), custom_call_target="tpu_custom_call" | custom-call | flops 379500000 | bytes 1188000 | tf_op jit(solution)/shard_map/thought_rows_terms/pallas_call | solution.py:1313
  (180 shorter events, 55.1 us)
Async XLA Ops:
  7.2 103.8 %all-gather.2.cloned.1.call-start = ((), (), s32[]{:S(2)}) async-start(), calls=%async_computation.2 | async-start | bytes 10948608 | tf_op jit(solution)/shard_map/all_gather | solution.py:1572
  9.6 223.8 %reduce-scatter.3.cloned.1.call-start = ((), (), s32[]{:S(2)}) async-start(), calls=%async_computation.3 | async-start | bytes 5308416 | tf_op jit(solution)/shard_map/reduce_scatter | solution.py:1606
  11.7 9.8 %collective-permute-start.10 = (bf16[8,128]{1,0:T(8,128)(2,1)S(1)}, bf16[8,128]{1,0:T(8,128)(2,1)S(1)}, u32[]{:S(2)}, u32[]{:S(2)}) collective-permute-start(bf16[8,128]{1,0:T(8,128)(2,1)S(1)} %convert_element_type.306), channel_id=1, source_target_pairs={{0,4},{1,5},{2,6},{3,7},{4,0},{5,1},{6,2},{7,3},{8,12},{9,13},{10,... | collective-permute-start | bytes 6152 | tf_op jit(solution)/shard_map/ppermute | solution.py:73
  15.8 9.5 %collective-permute-start = (bf16[1,3,24,384]{3,2,1,0:T(8,128)(2,1)S(1)}, bf16[1,3,24,384]{3,2,1,0:T(8,128)(2,1)S(1)}, u32[]{:S(2)}, u32[]{:S(2)}) collective-permute-start(bf16[1,3,24,384]{3,2,1,0:T(8,128)(2,1)S(1)} %maximum_bitcast_fusion), channel_id=1, source_target_pairs={{0,4},{1,5},{2,6},{3,7},{4,0},{5,1},{6,2},{7,3},{8,12},{9,13},{10,... | collective-permute-start | bytes 165896 | tf_op jit(solution)/shard_map/ppermute | solution.py:73
  15.9 11.1 %collective-permute-start.5 = (bf16[1,3,24,384]{3,2,1,0:T(8,128)(2,1)S(1)}, bf16[1,3,24,384]{3,2,1,0:T(8,128)(2,1)S(1)}, u32[]{:S(2)}, u32[]{:S(2)}) collective-permute-start(bf16[1,3,24,384]{3,2,1,0:T(8,128)(2,1)S(1)} %maximum_bitcast_fusion.1), channel_id=1, source_target_pairs={{0,4},{1,5},{2,6},{3,7},{4,0},{5,1},{6,2},{7,3},{8,12},{9,13},{10,... | collective-permute-start | bytes 165896 | tf_op jit(solution)/shard_map/ppermute | solution.py:73
  27.0 9.4 %collective-permute-start.6 = (bf16[2,3,24,384]{3,2,1,0:T(8,128)(2,1)S(1)}, bf16[2,3,24,384]{3,2,1,0:T(8,128)(2,1)S(1)}, u32[]{:S(2)}, u32[]{:S(2)}) collective-permute-start(bf16[2,3,24,384]{3,2,1,0:T(8,128)(2,1)S(1)} %pad_maximum_fusion.12), channel_id=1, source_target_pairs={{0,2},{1,3},{2,0},{3,1},{4,6},{5,7},{6,4},{7,5},{8,10},{9,11},{10,... | collective-permute-start | bytes 331784 | tf_op jit(solution)/shard_map/ppermute | solution.py:73
  27.5 10.7 %collective-permute-start.12 = (bf16[2,2,8,128]{3,2,0,1:T(8,128)(2,1)S(1)}, bf16[2,2,8,128]{3,2,0,1:T(8,128)(2,1)S(1)}, u32[]{:S(2)}, u32[]{:S(2)}) collective-permute-start(bf16[2,2,8,128]{3,2,0,1:T(8,128)(2,1)S(1)} %pad_maximum_fusion.17), channel_id=1, source_target_pairs={{0,8},{8,0},{16,24},{24,16},{1,9},{9,1},{17,25},{25,17},{2,10},{10... | collective-permute-start | bytes 24584 | tf_op jit(solution)/shard_map/ppermute | solution.py:73
  38.2 9.6 %collective-permute-start.2 = (bf16[4,3,24,384]{3,2,1,0:T(8,128)(2,1)S(1)}, bf16[4,3,24,384]{3,2,1,0:T(8,128)(2,1)S(1)}, u32[]{:S(2)}, u32[]{:S(2)}) collective-permute-start(bf16[4,3,24,384]{3,2,1,0:T(8,128)(2,1)S(1)} %pad_maximum_fusion.7), channel_id=1, source_target_pairs={{0,8},{8,0},{16,24},{24,16},{1,9},{9,1},{17,25},{25,17},{2,10},{10... | collective-permute-start | bytes 663560 | tf_op jit(solution)/shard_map/ppermute | solution.py:73
  42.6 20.2 %collective-permute-start.8 = (bf16[8,3,24,384]{3,2,1,0:T(8,128)(2,1)S(1)}, bf16[8,3,24,384]{3,2,1,0:T(8,128)(2,1)S(1)}, u32[]{:S(2)}, u32[]{:S(2)}) collective-permute-start(bf16[8,3,24,384]{3,2,1,0:T(8,128)(2,1)S(1)} %pad_maximum_fusion.5), channel_id=1, source_target_pairs={{0,8},{8,0},{16,24},{24,16},{1,9},{9,1},{17,25},{25,17},{2,10},{10... | collective-permute-start | bytes 1327112 | tf_op jit(solution)/shard_map/ppermute | solution.py:73
  47.9 15.2 %collective-permute-start.3 = (bf16[8,3,24,384]{3,2,1,0:T(8,128)(2,1)S(1)}, bf16[8,3,24,384]{3,2,1,0:T(8,128)(2,1)S(1)}, u32[]{:S(2)}, u32[]{:S(2)}) collective-permute-start(bf16[8,3,24,384]{3,2,1,0:T(8,128)(2,1)S(1)} %pad_maximum_fusion.4), channel_id=1, source_target_pairs={{0,16},{8,24},{16,0},{24,8},{1,17},{9,25},{17,1},{25,9},{2,18},{10... | collective-permute-start | bytes 1327112 | tf_op jit(solution)/shard_map/ppermute | solution.py:73
  48.0 18.6 %collective-permute-start.13 = (bf16[2,2,2,8,128]{4,3,1,2,0:T(8,128)(2,1)S(1)}, bf16[2,2,2,8,128]{4,3,1,2,0:T(8,128)(2,1)S(1)}, u32[]{:S(2)}, u32[]{:S(2)}) collective-permute-start(bf16[2,2,2,8,128]{4,3,1,2,0:T(8,128)(2,1)S(1)} %pad_maximum_fusion.16), channel_id=1, source_target_pairs={{0,16},{8,24},{16,0},{24,8},{1,17},{9,25},{17,1},{25,9},{2,18},{10... | collective-permute-start | bytes 49160 | tf_op jit(solution)/shard_map/ppermute | solution.py:73
  63.0 10.2 %collective-permute-start.9 = (bf16[16,3,24,384]{3,2,1,0:T(8,128)(2,1)S(1)}, bf16[16,3,24,384]{3,2,1,0:T(8,128)(2,1)S(1)}, u32[]{:S(2)}, u32[]{:S(2)}) collective-permute-start(bf16[16,3,24,384]{3,2,1,0:T(8,128)(2,1)S(1)} %pad_maximum_fusion.2.right_mine), channel_id=1, source_target_pairs={{0,1},{1,0},{2,3},{3,2},{4,5},{5,4},{6,7},{7,6},{8,9},{9,8},{10,11... | collective-permute-start | bytes 2654216 | tf_op jit(solution)/shard_map/ppermute | solution.py:73
  64.0 9.3 %collective-permute-start.4 = (bf16[16,3,24,384]{3,2,1,0:T(8,128)(2,1)S(1)}, bf16[16,3,24,384]{3,2,1,0:T(8,128)(2,1)S(1)}, u32[]{:S(2)}, u32[]{:S(2)}) collective-permute-start(bf16[16,3,24,384]{3,2,1,0:T(8,128)(2,1)S(1)} %pad_maximum_fusion.1.left_mine), channel_id=1, source_target_pairs={{0,1},{1,0},{2,3},{3,2},{4,5},{5,4},{6,7},{7,6},{8,9},{9,8},{10,11... | collective-permute-start | bytes 2654216 | tf_op jit(solution)/shard_map/ppermute | solution.py:73
  176.3 122.3 %reduce-scatter.5.cloned.1.call-start = ((), (), s32[]{:S(2)}) async-start(), calls=%async_computation.4 | async-start | bytes 737280 | tf_op jit(solution)/shard_map/reduce_scatter | solution.py:1612
  176.4 20.0 %collective-permute-start.15 = (bf16[2,2,2,2,4,24,768]{6,5,4,3,2,1,0:T(8,128)(2,1)}, bf16[2,2,2,2,4,24,768]{6,5,4,3,2,1,0:T(8,128)(2,1)S(1)}, u32[]{:S(2)}, u32[]{:S(2)}) collective-permute-start(bf16[2,2,2,2,4,24,768]{6,5,4,3,2,1,0:T(8,128)(2,1)} %bitcast.287), channel_id=1, source_target_pairs={{0,1},{1,0},{2,3},{3,2},{4,5},{5,4},{6,7},{7,6},{8,9},{9,8},{10,11... | collective-permute-start | bytes 7077896 | tf_op jit(solution)/shard_map/ppermute | solution.py:73
  200.2 28.2 %collective-permute-start.16 = (bf16[2,2,2,4,24,768]{5,4,3,2,1,0:T(8,128)(2,1)S(1)}, bf16[2,2,2,4,24,768]{5,4,3,2,1,0:T(8,128)(2,1)}, u32[]{:S(2)}, u32[]{:S(2)}) collective-permute-start(bf16[2,2,2,4,24,768]{5,4,3,2,1,0:T(8,128)(2,1)S(1)} %get-tuple-element.181), channel_id=1, source_target_pairs={{0,16},{8,24},{16,0},{24,8},{1,17},{9,25},{17,1},{25,9},{2,18},{10... | collective-permute-start | bytes 3538952 | tf_op jit(solution)/shard_map/ppermute | solution.py:73
  201.5 26.5 %collective-permute-start.17 = (bf16[24,768]{1,0:T(8,128)(2,1)}, bf16[24,768]{1,0:T(8,128)(2,1)S(1)}, u32[]{:S(2)}, u32[]{:S(2)}) collective-permute-start(bf16[24,768]{1,0:T(8,128)(2,1)} %get-tuple-element.124), channel_id=1, source_target_pairs={{0,4},{1,5},{2,6},{3,7},{4,0},{5,1},{6,2},{7,3},{8,12},{9,13},{10,... | collective-permute-start | bytes 110600 | tf_op jit(solution)/shard_map/ppermute | solution.py:73
  230.7 16.3 %collective-permute-start.18 = (bf16[2,2,4,24,768]{4,3,2,1,0:T(8,128)(2,1)}, bf16[2,2,4,24,768]{4,3,2,1,0:T(8,128)(2,1)S(1)}, u32[]{:S(2)}, u32[]{:S(2)}) collective-permute-start(bf16[2,2,4,24,768]{4,3,2,1,0:T(8,128)(2,1)} %get-tuple-element.183), channel_id=1, source_target_pairs={{0,8},{8,0},{16,24},{24,16},{1,9},{9,1},{17,25},{25,17},{2,10},{10... | collective-permute-start | bytes 1769480 | tf_op jit(solution)/shard_map/ppermute | solution.py:73
  232.5 14.5 %collective-permute-start.19 = (bf16[2,24,768]{2,1,0:T(8,128)(2,1)S(1)}, bf16[2,24,768]{2,1,0:T(8,128)(2,1)S(1)}, u32[]{:S(2)}, u32[]{:S(2)}) collective-permute-start(bf16[2,24,768]{2,1,0:T(8,128)(2,1)S(1)} %pad_maximum_fusion.13), channel_id=1, source_target_pairs={{0,2},{1,3},{2,0},{3,1},{4,6},{5,7},{6,4},{7,5},{8,10},{9,11},{10,... | collective-permute-start | bytes 221192 | tf_op jit(solution)/shard_map/ppermute | solution.py:73
  247.7 8.9 %collective-permute-start.21 = (bf16[2,2,2,2,2,24,768]{6,5,4,3,2,1,0:T(8,128)(2,1)}, bf16[2,2,2,2,2,24,768]{6,5,4,3,2,1,0:T(8,128)(2,1)S(1)}, u32[]{:S(2)}, u32[]{:S(2)}) collective-permute-start(bf16[2,2,2,2,2,24,768]{6,5,4,3,2,1,0:T(8,128)(2,1)} %bitcast.290), channel_id=1, source_target_pairs={{0,1},{1,0},{2,3},{3,2},{4,5},{5,4},{6,7},{7,6},{8,9},{9,8},{10,11... | collective-permute-start | bytes 3538952 | tf_op jit(solution)/shard_map/ppermute | solution.py:73
  250.6 19.2 %collective-permute-start.28 = (bf16[2,2,24,768]{3,2,0,1:T(8,128)(2,1)}, bf16[2,2,24,768]{3,2,0,1:T(8,128)(2,1)}, u32[]{:S(2)}, u32[]{:S(2)}) collective-permute-start(bf16[2,2,24,768]{3,2,0,1:T(8,128)(2,1)} %pad_maximum_fusion.10), channel_id=1, source_target_pairs={{0,16},{8,24},{16,0},{24,8},{1,17},{9,25},{17,1},{25,9},{2,18},{10... | collective-permute-start | bytes 442376 | tf_op jit(solution)/shard_map/ppermute | solution.py:73
  254.2 17.7 %collective-permute-start.27 = (bf16[2,4,24,768]{3,2,1,0:T(8,128)(2,1)}, bf16[2,4,24,768]{3,2,1,0:T(8,128)(2,1)}, u32[]{:S(2)}, u32[]{:S(2)}) collective-permute-start(bf16[2,4,24,768]{3,2,1,0:T(8,128)(2,1)} %get-tuple-element.193), channel_id=1, source_target_pairs={{0,2},{1,3},{2,0},{3,1},{4,6},{5,7},{6,4},{7,5},{8,10},{9,11},{10,... | collective-permute-start | bytes 884744 | tf_op jit(solution)/shard_map/ppermute | solution.py:73
  255.4 16.5 %collective-permute-start.23 = (bf16[2,2,2,8,128]{4,3,1,2,0:T(8,128)(2,1)S(1)}, bf16[2,2,2,8,128]{4,3,1,2,0:T(8,128)(2,1)S(1)}, u32[]{:S(2)}, u32[]{:S(2)}) collective-permute-start(bf16[2,2,2,8,128]{4,3,1,2,0:T(8,128)(2,1)S(1)} %get-tuple-element.233), channel_id=1, source_target_pairs={{0,16},{8,24},{16,0},{24,8},{1,17},{9,25},{17,1},{25,9},{2,18},{10... | collective-permute-start | bytes 49160 | tf_op jit(solution)/shard_map/ppermute | solution.py:73
  257.0 19.2 %collective-permute-start.26 = (bf16[2,2,2,2,24,768]{5,4,3,2,1,0:T(8,128)(2,1)S(1)}, bf16[2,2,2,2,24,768]{5,4,3,2,1,0:T(8,128)(2,1)S(1)}, u32[]{:S(2)}, u32[]{:S(2)}) collective-permute-start(bf16[2,2,2,2,24,768]{5,4,3,2,1,0:T(8,128)(2,1)S(1)} %get-tuple-element.185), channel_id=1, source_target_pairs={{0,8},{8,0},{16,24},{24,16},{1,9},{9,1},{17,25},{25,17},{2,10},{10... | collective-permute-start | bytes 1769480 | tf_op jit(solution)/shard_map/ppermute | solution.py:73
  258.2 18.0 %collective-permute-start.25 = (bf16[2,2,2,2,24,768]{5,4,3,2,1,0:T(8,128)(2,1)S(1)}, bf16[2,2,2,2,24,768]{5,4,3,2,1,0:T(8,128)(2,1)S(1)}, u32[]{:S(2)}, u32[]{:S(2)}) collective-permute-start(bf16[2,2,2,2,24,768]{5,4,3,2,1,0:T(8,128)(2,1)S(1)} %get-tuple-element.187), channel_id=1, source_target_pairs={{0,16},{8,24},{16,0},{24,8},{1,17},{9,25},{17,1},{25,9},{2,18},{10... | collective-permute-start | bytes 1769480 | tf_op jit(solution)/shard_map/ppermute | solution.py:73
  270.7 11.9 %collective-permute-start.32 = (bf16[2,2,2,24,768]{4,3,1,2,0:T(8,128)(2,1)S(1)}, bf16[2,2,2,24,768]{4,3,1,2,0:T(8,128)(2,1)S(1)}, u32[]{:S(2)}, u32[]{:S(2)}) collective-permute-start(bf16[2,2,2,24,768]{4,3,1,2,0:T(8,128)(2,1)S(1)} %pad_maximum_fusion.6), channel_id=1, source_target_pairs={{0,8},{8,0},{16,24},{24,16},{1,9},{9,1},{17,25},{25,17},{2,10},{10... | collective-permute-start | bytes 884744 | tf_op jit(solution)/shard_map/ppermute | solution.py:73
  271.9 10.9 %collective-permute-start.24 = (bf16[2,2,8,128]{3,2,0,1:T(8,128)(2,1)S(1)}, bf16[2,2,8,128]{3,2,0,1:T(8,128)(2,1)S(1)}, u32[]{:S(2)}, u32[]{:S(2)}) collective-permute-start(bf16[2,2,8,128]{3,2,0,1:T(8,128)(2,1)S(1)} %get-tuple-element.238), channel_id=1, source_target_pairs={{0,8},{8,0},{16,24},{24,16},{1,9},{9,1},{17,25},{25,17},{2,10},{10... | collective-permute-start | bytes 24584 | tf_op jit(solution)/shard_map/ppermute | solution.py:73
  273.8 9.0 %collective-permute-start.35 = (bf16[4,24,768]{2,1,0:T(8,128)(2,1)S(1)}, bf16[4,24,768]{2,1,0:T(8,128)(2,1)S(1)}, u32[]{:S(2)}, u32[]{:S(2)}) collective-permute-start(bf16[4,24,768]{2,1,0:T(8,128)(2,1)S(1)} %fusion.14), channel_id=1, source_target_pairs={{0,4},{1,5},{2,6},{3,7},{4,0},{5,1},{6,2},{7,3},{8,12},{9,13},{10,... | collective-permute-start | bytes 442376 | tf_op jit(solution)/shard_map/ppermute | solution.py:73
  277.4 10.7 %collective-permute-start.30 = (bf16[2,2,2,24,768]{4,3,2,1,0:T(8,128)(2,1)S(1)}, bf16[2,2,2,24,768]{4,3,2,1,0:T(8,128)(2,1)S(1)}, u32[]{:S(2)}, u32[]{:S(2)}) collective-permute-start(bf16[2,2,2,24,768]{4,3,2,1,0:T(8,128)(2,1)S(1)} %get-tuple-element.191), channel_id=1, source_target_pairs={{0,8},{8,0},{16,24},{24,16},{1,9},{9,1},{17,25},{25,17},{2,10},{10... | collective-permute-start | bytes 884744 | tf_op jit(solution)/shard_map/ppermute | solution.py:73
  282.8 14.2 %collective-permute-start.34 = (bf16[2,2,2,2,24,768]{5,4,2,3,0,1:T(8,128)(2,1)S(1)}, bf16[2,2,2,2,24,768]{5,4,2,3,0,1:T(8,128)(2,1)S(1)}, u32[]{:S(2)}, u32[]{:S(2)}) collective-permute-start(bf16[2,2,2,2,24,768]{5,4,2,3,0,1:T(8,128)(2,1)S(1)} %pad_maximum_fusion.3), channel_id=1, source_target_pairs={{0,1},{1,0},{2,3},{3,2},{4,5},{5,4},{6,7},{7,6},{8,9},{9,8},{10,11... | collective-permute-start | bytes 1769480 | tf_op jit(solution)/shard_map/ppermute | solution.py:73
  284.1 9.8 %collective-permute-start.37 = (bf16[2,2,24,768]{3,2,1,0:T(8,128)(2,1)S(1)}, bf16[2,2,24,768]{3,2,1,0:T(8,128)(2,1)S(1)}, u32[]{:S(2)}, u32[]{:S(2)}) collective-permute-start(bf16[2,2,24,768]{3,2,1,0:T(8,128)(2,1)S(1)} %get-tuple-element.197), channel_id=1, source_target_pairs={{0,2},{1,3},{2,0},{3,1},{4,6},{5,7},{6,4},{7,5},{8,10},{9,11},{10,... | collective-permute-start | bytes 442376 | tf_op jit(solution)/shard_map/ppermute | solution.py:73
  291.4 12.0 %collective-permute-start.33 = (bf16[8,128]{1,0:T(8,128)(2,1)S(1)}, bf16[8,128]{1,0:T(8,128)(2,1)S(1)}, u32[]{:S(2)}, u32[]{:S(2)}) collective-permute-start(bf16[8,128]{1,0:T(8,128)(2,1)S(1)} %fusion.43), channel_id=1, source_target_pairs={{0,4},{1,5},{2,6},{3,7},{4,0},{5,1},{6,2},{7,3},{8,12},{9,13},{10,... | collective-permute-start | bytes 6152 | tf_op jit(solution)/shard_map/ppermute | solution.py:73
  (30 other events, 154.9 us)
Sparse Core Ops, SparseCore 0:
  11.2 99.5 all-gather.1
  176.5 55.8 reduce-scatter.2
  250.7 26.7 reduce-scatter.4
